TPU v7x, 32 devices: a whole 2x2x4 slice. The times are simulated.
32 devices in a mesh: wide: 16 (over z, y, core), narrow: 2 (over x).
Axes of the slice: x: 2, y: 2, z: 4, core: 2. Of those that a mesh axis runs over, the one named last changes fastest.
Arguments:
- inputs: bfloat16 [64, 256, 1152], P(('wide', 'narrow')), may hold values from -6 to 6
- cotangent: bfloat16 [64, 256, 1152], P(('wide', 'narrow')), may hold values from -6 to 6
- class_ids: int32 [64], P(('wide', 'narrow')), may hold values from 0 to 999
- step_ids: int32 [64], P(('wide', 'narrow')), may hold values from 0 to 999
- image_counts: int32 [32], P(('wide', 'narrow')), may hold values from 0 to 2, as said below
- w_qkv: bfloat16 [1152, 3456], P('wide', 'narrow'), may hold values from -0.1875 to 0.1875
- w_out: bfloat16 [1152, 1152], P('wide', 'narrow'), may hold values from -0.75 to 0.75
- w_gate: bfloat16 [1152, 3072], P('wide', 'narrow'), may hold values from -0.1875 to 0.1875
- w_up: bfloat16 [1152, 3072], P('wide', 'narrow'), may hold values from -0.1875 to 0.1875
- w_down: bfloat16 [3072, 1152], P('wide', 'narrow'), may hold values from -0.109375 to 0.109375
- ada_weight: bfloat16 [1152, 6912], P('wide', 'narrow'), may hold values from -0.1875 to 0.1875
- ada_bias: bfloat16 [6912], P(('wide', 'narrow')), may hold values from -3 to 3
- class_table: bfloat16 [1000, 1152], P('narrow', 'wide'), may hold values from -6 to 6
- norm_gains: float32 [2, 72], replicated, may hold values from 0.6 to 1.8
Outputs:
- block_output: bfloat16 [64, 256, 1152], P(('wide', 'narrow'))
- input_grad: bfloat16 [64, 256, 1152], P(('wide', 'narrow'))
- grad_qkv: float32 [1152, 3456], P('wide', 'narrow')
- grad_out: float32 [1152, 1152], P('wide', 'narrow')
- grad_gate: float32 [1152, 3072], P('wide', 'narrow')
- grad_up: float32 [1152, 3072], P('wide', 'narrow')
- grad_down: float32 [3072, 1152], P('wide', 'narrow')
- grad_ada_weight: float32 [1152, 6912], P('wide', 'narrow')
- grad_ada_bias: float32 [6912], P(('wide', 'narrow'))
- grad_table: float32 [1000, 1152], P('narrow', 'wide')
- grad_gains: float32 [2, 72], replicated
Inputs may be any that keep to these rules, and one draw needn't show every extreme that they name: image_counts[d] real images fill the first slots of device d, numbered wide index times the size of narrow plus narrow index; its other slots hold padding images. Some device has all 2 slots real and some has none.
All inputs are finite; a program needn't handle non-finite values.
Results may differ from a plain program's by a relative error of at most 0.018.
Values may be sent and summed in bfloat16 or wider, within the bound.
No kernel may reach another device: no remote copies, remote signals or barrier semaphores. Data moves between devices by JAX's collectives and lax.ppermute only.
A program may use at most 256 MiB of HBM per device.

v0:
```python
import math

import jax
import jax.numpy as jnp
from jax import lax
from jax.sharding import PartitionSpec as P

H = 16
HD = 72
CLASSES = 1000
GRID = 16
MB = 2
IMG_MB = 1


EPSILON = 1e-06
HIGHEST = lax.Precision.HIGHEST


def sinusoid(steps, width):
    half_width = width // 2
    frequency = jnp.exp(-math.log(10000.0) * jnp.arange(half_width, dtype=jnp.float32) / half_width)
    angles = steps.astype(jnp.float32)[:, None] * frequency[None, :]
    return jnp.concatenate([jnp.cos(angles), jnp.sin(angles)], axis=-1)


def rope_tables(length, grid_side, head):
    quarter = head // 4
    frequency = 10000.0 ** (-jnp.arange(quarter, dtype=jnp.float32) / quarter)
    patch_index = jnp.arange(length, dtype=jnp.int32)
    row_place = (patch_index // grid_side).astype(jnp.float32)
    col_place = (patch_index % grid_side).astype(jnp.float32)
    row_angle = row_place[:, None] * frequency[None, :]
    col_angle = col_place[:, None] * frequency[None, :]
    angles = jnp.concatenate([row_angle, row_angle, col_angle, col_angle], axis=-1)
    return (jnp.cos(angles)[:, None, :], jnp.sin(angles)[:, None, :])


def rotate_half(vector):
    quarter = vector.shape[-1] // 4
    part_one = vector[..., :quarter]
    part_two = vector[..., quarter : 2 * quarter]
    part_three = vector[..., 2 * quarter : 3 * quarter]
    part_four = vector[..., 3 * quarter :]
    return jnp.concatenate([-part_two, part_one, -part_four, part_three], axis=-1)


def rotary(vector, cosine_table, sine_table):
    return vector * cosine_table + rotate_half(vector) * sine_table


def rotary_back(gradient, cosine_table, sine_table):
    return gradient * cosine_table - rotate_half(gradient * sine_table)


def layer_norm(values):
    centre = values - jnp.mean(values, axis=-1, keepdims=True)
    inverse = lax.rsqrt(jnp.mean(centre * centre, axis=-1, keepdims=True) + EPSILON)
    return (centre * inverse, inverse)


def layer_norm_back(gradient, normed, inverse):
    return inverse * (
        gradient
        - jnp.mean(gradient, axis=-1, keepdims=True)
        - normed * jnp.mean(gradient * normed, axis=-1, keepdims=True)
    )


def rms_norm(values):
    inverse = lax.rsqrt(jnp.mean(values * values, axis=-1, keepdims=True) + EPSILON)
    return (values * inverse, inverse)


def rms_back(gradient, normed, inverse):
    return inverse * (gradient - normed * jnp.mean(gradient * normed, axis=-1, keepdims=True))


def fetch_weights(shards):
    qkv_part, out_part, gate_part, up_part, down_part, ada_part, bias_part, table_part = shards
    qkv_part, out_part, gate_part, up_part, down_part, ada_part, bias_part, table_part = (
        lax.all_gather(qkv_part, "narrow", axis=1, tiled=True),
        lax.all_gather(out_part, "narrow", axis=1, tiled=True),
        lax.all_gather(gate_part, "narrow", axis=1, tiled=True),
        lax.all_gather(up_part, "narrow", axis=1, tiled=True),
        lax.all_gather(down_part, "narrow", axis=1, tiled=True),
        lax.all_gather(ada_part, "narrow", axis=1, tiled=True),
        lax.all_gather(bias_part, "narrow", axis=0, tiled=True),
        lax.all_gather(table_part, "narrow", axis=0, tiled=True),
    )
    qkv_part, out_part, gate_part, up_part, down_part, ada_part, bias_part, table_part = (
        lax.all_gather(qkv_part, "wide", axis=0, tiled=True),
        lax.all_gather(out_part, "wide", axis=0, tiled=True),
        lax.all_gather(gate_part, "wide", axis=0, tiled=True),
        lax.all_gather(up_part, "wide", axis=0, tiled=True),
        lax.all_gather(down_part, "wide", axis=0, tiled=True),
        lax.all_gather(ada_part, "wide", axis=0, tiled=True),
        lax.all_gather(bias_part, "wide", axis=0, tiled=True),
        lax.all_gather(table_part, "wide", axis=1, tiled=True),
    )
    return (qkv_part, out_part, gate_part, up_part, down_part, ada_part, bias_part, table_part)


def reduce_grads(grads):
    g_qkv, g_out, g_gate, g_up, g_down, g_ada, g_bias, g_table = grads
    g_bias = g_bias.reshape(lax.axis_size("wide"), -1)
    g_qkv, g_out, g_gate, g_up, g_down, g_ada, g_bias, g_table = (
        lax.psum_scatter(
            g_qkv.astype(jnp.bfloat16), "wide", scatter_dimension=0, tiled=True
        ).astype(jnp.float32),
        lax.psum_scatter(
            g_out.astype(jnp.bfloat16), "wide", scatter_dimension=0, tiled=True
        ).astype(jnp.float32),
        lax.psum_scatter(
            g_gate.astype(jnp.bfloat16), "wide", scatter_dimension=0, tiled=True
        ).astype(jnp.float32),
        lax.psum_scatter(g_up.astype(jnp.bfloat16), "wide", scatter_dimension=0, tiled=True).astype(
            jnp.float32
        ),
        lax.psum_scatter(
            g_down.astype(jnp.bfloat16), "wide", scatter_dimension=0, tiled=True
        ).astype(jnp.float32),
        lax.psum_scatter(
            g_ada.astype(jnp.bfloat16), "wide", scatter_dimension=0, tiled=True
        ).astype(jnp.float32),
        lax.psum_scatter(
            g_bias.astype(jnp.bfloat16), "wide", scatter_dimension=0, tiled=True
        ).astype(jnp.float32),
        lax.psum_scatter(
            g_table.astype(jnp.bfloat16), "wide", scatter_dimension=1, tiled=True
        ).astype(jnp.float32),
    )
    g_qkv, g_out, g_gate, g_up, g_down, g_ada, g_bias, g_table = (
        lax.psum_scatter(
            g_qkv.astype(jnp.bfloat16), "narrow", scatter_dimension=1, tiled=True
        ).astype(jnp.float32),
        lax.psum_scatter(
            g_out.astype(jnp.bfloat16), "narrow", scatter_dimension=1, tiled=True
        ).astype(jnp.float32),
        lax.psum_scatter(
            g_gate.astype(jnp.bfloat16), "narrow", scatter_dimension=1, tiled=True
        ).astype(jnp.float32),
        lax.psum_scatter(
            g_up.astype(jnp.bfloat16), "narrow", scatter_dimension=1, tiled=True
        ).astype(jnp.float32),
        lax.psum_scatter(
            g_down.astype(jnp.bfloat16), "narrow", scatter_dimension=1, tiled=True
        ).astype(jnp.float32),
        lax.psum_scatter(
            g_ada.astype(jnp.bfloat16), "narrow", scatter_dimension=1, tiled=True
        ).astype(jnp.float32),
        lax.psum_scatter(
            g_bias.astype(jnp.bfloat16), "narrow", scatter_dimension=1, tiled=True
        ).astype(jnp.float32),
        lax.psum_scatter(
            g_table.astype(jnp.bfloat16), "narrow", scatter_dimension=0, tiled=True
        ).astype(jnp.float32),
    )
    return (g_qkv, g_out, g_gate, g_up, g_down, g_ada, g_bias.reshape(-1), g_table)


def forward_pass(weights, norm_gains, tokens, class_ids, step_ids, cosine_table, sine_table):
    w_qkv, w_out, w_gate, w_up, w_down, ada_weight, ada_bias, class_table = weights
    images, length, width = tokens.shape
    score_scale = HD ** (-0.5)
    condition = class_table[class_ids].astype(jnp.float32) + sinusoid(step_ids, width)
    cond_act = jax.nn.silu(condition).astype(jnp.bfloat16)
    modulation = jnp.dot(
        cond_act, ada_weight, preferred_element_type=jnp.float32
    ) + ada_bias.astype(jnp.float32)
    pieces = jnp.split(modulation[:, None, :], 6, axis=-1)
    source = tokens.astype(jnp.float32)
    normed, inverse = layer_norm(source)
    attn_in = (normed * (1.0 + pieces[1]) + pieces[0]).astype(jnp.bfloat16)
    packed = jnp.einsum("bsd,de->bse", attn_in, w_qkv, preferred_element_type=jnp.float32)
    packed = packed.reshape(images, length, 3, H, HD)
    query_normed, query_inverse = rms_norm(packed[:, :, 0])
    key_normed, key_inverse = rms_norm(packed[:, :, 1])
    queries = rotary(query_normed * norm_gains[0], cosine_table, sine_table).astype(jnp.bfloat16)
    key_rows = rotary(key_normed * norm_gains[1], cosine_table, sine_table).astype(jnp.bfloat16)
    value_rows = packed[:, :, 2].astype(jnp.bfloat16)
    scores = (
        jnp.einsum("bshe,bthe->bhst", queries, key_rows, preferred_element_type=jnp.float32)
        * score_scale
    )
    row_max = jnp.max(scores, axis=-1, keepdims=True)
    exponent = jnp.exp(scores - row_max)
    row_total = jnp.sum(exponent, axis=-1, keepdims=True)
    attention = (exponent / row_total).astype(jnp.bfloat16)
    log_total = row_max + jnp.log(row_total)
    mixed = jnp.einsum("bhst,bthe->bshe", attention, value_rows, preferred_element_type=jnp.float32)
    mixed = mixed.reshape(images, length, width).astype(jnp.bfloat16)
    attn_out = jnp.einsum("bsd,de->bse", mixed, w_out, preferred_element_type=jnp.float32)
    hidden_one = source + pieces[2] * attn_out
    normed_two, inverse_two = layer_norm(hidden_one)
    mlp_in = (normed_two * (1.0 + pieces[4]) + pieces[3]).astype(jnp.bfloat16)
    gate_val = jnp.einsum("bsd,df->bsf", mlp_in, w_gate, preferred_element_type=jnp.float32)
    up_val = jnp.einsum("bsd,df->bsf", mlp_in, w_up, preferred_element_type=jnp.float32)
    hidden_mid = (jax.nn.silu(gate_val) * up_val).astype(jnp.bfloat16)
    mlp_out = jnp.einsum("bsf,fd->bsd", hidden_mid, w_down, preferred_element_type=jnp.float32)
    output = hidden_one + pieces[5] * mlp_out
    stored = (
        condition,
        cond_act,
        pieces,
        normed,
        inverse,
        attn_in,
        query_normed,
        query_inverse,
        key_normed,
        key_inverse,
        queries,
        key_rows,
        value_rows,
        log_total,
        mixed,
        attn_out,
        normed_two,
        inverse_two,
        mlp_in,
        gate_val,
        up_val,
        hidden_mid,
        mlp_out,
    )
    return (output, stored)


def backward_pass(weights, norm_gains, stored, grad_y, cosine_table, sine_table):
    w_qkv, w_out, w_gate, w_up, w_down, ada_weight, ada_bias, class_table = weights
    (
        condition,
        cond_act,
        pieces,
        normed,
        inverse,
        attn_in,
        query_normed,
        query_inverse,
        key_normed,
        key_inverse,
        queries,
        key_rows,
        value_rows,
        log_total,
        mixed,
        attn_out,
        normed_two,
        inverse_two,
        mlp_in,
        gate_val,
        up_val,
        hidden_mid,
        mlp_out,
    ) = stored
    images, length, width = grad_y.shape
    score_scale = HD ** (-0.5)
    d_gate_b = jnp.sum(grad_y * mlp_out, axis=1)
    d_mlp = (pieces[5] * grad_y).astype(jnp.bfloat16)
    d_mid = jnp.einsum("bsd,fd->bsf", d_mlp, w_down, preferred_element_type=jnp.float32)
    gate_sigmoid = jax.nn.sigmoid(gate_val)
    d_gate = (d_mid * up_val * gate_sigmoid * (1.0 + gate_val * (1.0 - gate_sigmoid))).astype(
        jnp.bfloat16
    )
    d_up = (d_mid * gate_val * gate_sigmoid).astype(jnp.bfloat16)
    d_mlp_in = jnp.einsum(
        "bsf,df->bsd", d_gate, w_gate, preferred_element_type=jnp.float32
    ) + jnp.einsum("bsf,df->bsd", d_up, w_up, preferred_element_type=jnp.float32)
    d_scale_b = jnp.sum(d_mlp_in * normed_two, axis=1)
    d_shift_b = jnp.sum(d_mlp_in, axis=1)
    d_hidden = grad_y + layer_norm_back(d_mlp_in * (1.0 + pieces[4]), normed_two, inverse_two)
    d_gate_a = jnp.sum(d_hidden * attn_out, axis=1)
    d_attn = (pieces[2] * d_hidden).astype(jnp.bfloat16)
    d_mixed = jnp.einsum("bse,de->bsd", d_attn, w_out, preferred_element_type=jnp.float32)
    d_mixed = d_mixed.astype(jnp.bfloat16).reshape(images, length, H, HD)
    scores = (
        jnp.einsum("bshe,bthe->bhst", queries, key_rows, preferred_element_type=jnp.float32)
        * score_scale
    )
    softmax_out = jnp.exp(scores - log_total)
    attention = softmax_out.astype(jnp.bfloat16)
    d_values = jnp.einsum("bhst,bshe->bthe", attention, d_mixed, preferred_element_type=jnp.float32)
    d_soft = jnp.einsum("bshe,bthe->bhst", d_mixed, value_rows, preferred_element_type=jnp.float32)
    row_inner = jnp.sum(softmax_out * d_soft, axis=-1, keepdims=True)
    d_scores = (softmax_out * (d_soft - row_inner) * score_scale).astype(jnp.bfloat16)
    d_queries = jnp.einsum(
        "bhst,bthe->bshe", d_scores, key_rows, preferred_element_type=jnp.float32
    )
    d_keys = jnp.einsum("bhst,bshe->bthe", d_scores, queries, preferred_element_type=jnp.float32)
    query_scaled = rotary_back(d_queries, cosine_table, sine_table)
    key_scaled = rotary_back(d_keys, cosine_table, sine_table)
    grad_gains = jnp.stack(
        [
            jnp.sum(query_scaled * query_normed, axis=(0, 1, 2)),
            jnp.sum(key_scaled * key_normed, axis=(0, 1, 2)),
        ],
        axis=0,
    )
    d_query_raw = rms_back(query_scaled * norm_gains[0], query_normed, query_inverse)
    d_key_raw = rms_back(key_scaled * norm_gains[1], key_normed, key_inverse)
    d_packed = jnp.stack([d_query_raw, d_key_raw, d_values], axis=2)
    d_packed = d_packed.reshape(images, length, 3 * width).astype(jnp.bfloat16)
    d_attn_in = jnp.einsum("bse,de->bsd", d_packed, w_qkv, preferred_element_type=jnp.float32)
    d_scale_a = jnp.sum(d_attn_in * normed, axis=1)
    d_shift_a = jnp.sum(d_attn_in, axis=1)
    d_tokens = d_hidden + layer_norm_back(d_attn_in * (1.0 + pieces[1]), normed, inverse)
    d_modulation = jnp.concatenate(
        [d_shift_a, d_scale_a, d_gate_a, d_shift_b, d_scale_b, d_gate_b], axis=-1
    ).astype(jnp.bfloat16)
    d_cond_act = jnp.einsum(
        "be,de->bd", d_modulation, ada_weight, preferred_element_type=jnp.float32
    )
    cond_sigmoid = jax.nn.sigmoid(condition)
    d_condition = d_cond_act * cond_sigmoid * (1.0 + condition * (1.0 - cond_sigmoid))
    operands = (
        attn_in,
        d_packed,
        mixed,
        d_attn,
        mlp_in,
        d_gate,
        d_up,
        hidden_mid,
        d_mlp,
        cond_act,
        d_modulation,
        d_condition,
    )
    return (d_tokens, grad_gains, operands)


def on_device(
    inputs,
    cotangent,
    class_ids,
    step_ids,
    image_counts,
    w_qkv,
    w_out,
    w_gate,
    w_up,
    w_down,
    ada_weight,
    ada_bias,
    class_table,
    norm_gains,
):
    shards = (w_qkv, w_out, w_gate, w_up, w_down, ada_weight, ada_bias, class_table)
    length = inputs.shape[1]
    cosine_table, sine_table = rope_tables(length, GRID, HD)
    local_count = image_counts[0]
    gathered = fetch_weights(shards)
    outputs = []
    input_grads = []
    operand_lists = [[] for member in range(12)]
    gain_total = jnp.zeros((2, HD), jnp.float32)
    for micro_step in range(MB):
        offset = micro_step * IMG_MB
        tokens = inputs[offset : offset + IMG_MB]
        slot_real = (offset + jnp.arange(IMG_MB, dtype=jnp.int32) < local_count).astype(jnp.float32)
        batch_classes = class_ids[offset : offset + IMG_MB]
        batch_steps = step_ids[offset : offset + IMG_MB]
        weights = gathered
        output, stored = forward_pass(
            weights, norm_gains, tokens, batch_classes, batch_steps, cosine_table, sine_table
        )
        grad_y = cotangent[offset : offset + IMG_MB].astype(jnp.float32) * slot_real[:, None, None]
        weights = gathered
        d_tokens, gain_grads, operands = backward_pass(
            weights, norm_gains, stored, grad_y, cosine_table, sine_table
        )
        outputs.append(output.astype(jnp.bfloat16))
        input_grads.append(d_tokens.astype(jnp.bfloat16))
        for position in range(12):
            operand_lists[position].append(operands[position])
        gain_total = gain_total + gain_grads
    (
        attn_in,
        d_packed,
        mixed,
        d_attn,
        mlp_in,
        d_gate,
        d_up,
        hidden_mid,
        d_mlp,
        cond_act,
        d_modulation,
        d_condition,
    ) = [jnp.concatenate(member, axis=0) for member in operand_lists]
    grad_qkv = jnp.einsum("bsd,bse->de", attn_in, d_packed, preferred_element_type=jnp.float32)
    grad_out = jnp.einsum("bsd,bse->de", mixed, d_attn, preferred_element_type=jnp.float32)
    grad_gate = jnp.einsum("bsd,bsf->df", mlp_in, d_gate, preferred_element_type=jnp.float32)
    grad_up = jnp.einsum("bsd,bsf->df", mlp_in, d_up, preferred_element_type=jnp.float32)
    grad_down = jnp.einsum("bsf,bsd->fd", hidden_mid, d_mlp, preferred_element_type=jnp.float32)
    grad_ada = jnp.einsum("bd,be->de", cond_act, d_modulation, preferred_element_type=jnp.float32)
    grad_bias = jnp.sum(d_modulation.astype(jnp.float32), axis=0)
    class_hot = (class_ids[:, None] == jnp.arange(CLASSES, dtype=jnp.int32)[None, :]).astype(
        jnp.float32
    )
    grad_table = jnp.dot(class_hot.T, d_condition, precision=HIGHEST)
    real_count, gain_sum = lax.psum(
        (local_count.astype(jnp.float32), gain_total), ("wide", "narrow")
    )
    reduced = reduce_grads(
        (grad_qkv, grad_out, grad_gate, grad_up, grad_down, grad_ada, grad_bias, grad_table)
    )
    return (
        jnp.concatenate(outputs, axis=0),
        jnp.concatenate(input_grads, axis=0),
        reduced[0] / real_count,
        reduced[1] / real_count,
        reduced[2] / real_count,
        reduced[3] / real_count,
        reduced[4] / real_count,
        reduced[5] / real_count,
        reduced[6] / real_count,
        reduced[7] / real_count,
        gain_sum / real_count,
    )


def solution(mesh):
    placed = (
        P(("wide", "narrow"), None, None),
        P(("wide", "narrow"), None, None),
        P(("wide", "narrow")),
        P(("wide", "narrow")),
        P(("wide", "narrow")),
        P("wide", "narrow"),
        P("wide", "narrow"),
        P("wide", "narrow"),
        P("wide", "narrow"),
        P("wide", "narrow"),
        P("wide", "narrow"),
        P(("wide", "narrow")),
        P("narrow", "wide"),
        P(),
    )
    return jax.shard_map(
        on_device,
        mesh=mesh,
        in_specs=placed,
        out_specs=(
            P(("wide", "narrow"), None, None),
            P(("wide", "narrow"), None, None),
            P("wide", "narrow"),
            P("wide", "narrow"),
            P("wide", "narrow"),
            P("wide", "narrow"),
            P("wide", "narrow"),
            P("wide", "narrow"),
            P(("wide", "narrow")),
            P("narrow", "wide"),
            P(),
        ),
        check_vma=False,
    )
```

profile of v0, /device:TPU:0, one launch (start us, length us, event | category | flops | bytes accessed | tf_op | source)
XLA Modules:
  0.0 1530.1 jit_solution(7064572114600391413)
XLA Ops:
  24.1 12.1 all_gather.50
  82.5 58.9 %all-reduce.1 = bf16[6912]{0:T(1024)(128)(2,1)S(1)} all-reduce(bf16[6912]{0:T(1024)(128)(2,1)S(1)} %dynamic-update-slice.3), channel_id=1, replica_groups=mesh['wide'=16,'narrow'=2] {'wide'}, use_global_device_ids=true, to_apply=%add.1 | all-reduce | flops 6912 | bytes 27648
  148.5 11.6 copy.141
  160.1 95.2 %all-gather.14.cloned.1.call-done = bf16[1152,6912]{1,0:T(8,128)(2,1)} async-done(((bf16[72,6912]{1,0:T(8,128)(2,1)}), bf16[1152,6912]{1,0:T(8,128)(2,1)}) %all-gather.14.cloned.1.call-update) | async-done | bytes 15925264 | tf_op jit(solution)/shard_map/all_gather | solution.py:97
  280.4 18.9 %all-gather.18.cloned.1.call-done = bf16[1152,1152]{1,0:T(8,128)(2,1)} async-done(((bf16[72,1152]{1,0:T(8,128)(2,1)}), bf16[1152,1152]{1,0:T(8,128)(2,1)}) %all-gather.18.cloned.1.call-update) | async-done | bytes 2654224 | tf_op jit(solution)/shard_map/all_gather | solution.py:93
  307.4 59.5 %all-gather.20.cloned.1.call-done = bf16[1152,3072]{1,0:T(8,128)(2,1)} async-done(((bf16[72,3072]{1,0:T(8,128)(2,1)}), bf16[1152,3072]{1,0:T(8,128)(2,1)}) %all-gather.20.cloned.1.call-update) | async-done | bytes 7077904 | tf_op jit(solution)/shard_map/all_gather | solution.py:94
  374.1 60.5 %all-gather.24.cloned.1.call-done = bf16[3072,1152]{1,0:T(8,128)(2,1)} async-done(((bf16[192,1152]{1,0:T(8,128)(2,1)}), bf16[3072,1152]{1,0:T(8,128)(2,1)}) %all-gather.24.cloned.1.call-update) | async-done | bytes 7077904 | tf_op jit(solution)/shard_map/all_gather | solution.py:96
  441.9 60.2 %all-gather.22.cloned.1.call-done = bf16[1152,3072]{1,0:T(8,128)(2,1)} async-done(((bf16[72,3072]{1,0:T(8,128)(2,1)}), bf16[1152,3072]{1,0:T(8,128)(2,1)}) %all-gather.22.cloned.1.call-update) | async-done | bytes 7077904 | tf_op jit(solution)/shard_map/all_gather | solution.py:95
  545.6 10.3 broadcast_multiply_fusion.2
  637.9 10.2 broadcast_multiply_fusion
  751.7 67.2 %reduce-scatter.52.cloned.1.call-done = bf16[72,1152]{1,0:T(8,128)(2,1)} async-done(((bf16[1152,1152]{1,0:T(8,128)(2,1)}), bf16[72,1152]{1,0:T(8,128)(2,1)}) %reduce-scatter.52.cloned.1.call-update) | async-done | bytes 165904
  820.8 90.9 %reduce-scatter.36.cloned.1.call-done = bf16[192,1152]{1,0:T(8,128)(2,1)} async-done(((bf16[3072,1152]{1,0:T(8,128)(2,1)}), bf16[192,1152]{1,0:T(8,128)(2,1)}) %reduce-scatter.36.cloned.1.call-update) | async-done | bytes 442384 | tf_op jit(solution)/shard_map/reduce_scatter | solution.py:120
  913.8 92.0 %reduce-scatter.28.cloned.1.call-done = bf16[72,3072]{1,0:T(8,128)(2,1)} async-done(((bf16[1152,3072]{1,0:T(8,128)(2,1)}), bf16[72,3072]{1,0:T(8,128)(2,1)}) %reduce-scatter.28.cloned.1.call-update) | async-done | bytes 442384 | tf_op jit(solution)/shard_map/reduce_scatter | solution.py:114
  1007.2 41.0 %all-reduce.7 = (f32[]{:T(128)}, f32[2,72]{1,0:T(2,128)S(1)}) all-reduce(f32[]{:T(128)} %bitcast.109, f32[2,72]{1,0:T(2,128)S(1)} %maximum_add_fusion.4), channel_id=1, replica_groups=mesh['wide'=16,'narrow'=2] {'wide','narrow'}, use_global_device_ids=true, to_apply=%region_32.33 | all-reduce | flops 145 | bytes 1160 | tf_op jit(solution)/shard_map/psum | solution.py:403
  1048.4 60.9 %all-reduce.4 = bf16[16,432]{1,0:T(8,128)(2,1)S(1)} all-reduce(bf16[16,432]{1,0:T(8,128)(2,1)S(1)} %convert_element_type.520), channel_id=14, replica_groups=mesh['wide'=16,'narrow'=2] {'wide'}, use_global_device_ids=true, to_apply=%region_55.56.clone | all-reduce | flops 6912 | bytes 27648
  1118.9 86.5 %reduce-scatter.50.cloned.1.call-done = bf16[72,3456]{1,0:T(8,128)(2,1)} async-done(((bf16[1152,3456]{1,0:T(8,128)(2,1)}), bf16[72,3456]{1,0:T(8,128)(2,1)}) %reduce-scatter.50.cloned.1.call-update) | async-done | bytes 497680
  1212.0 169.1 %reduce-scatter.38.cloned.1.call-done = bf16[72,6912]{1,0:T(8,128)(2,1)} async-done(((bf16[1152,6912]{1,0:T(8,128)(2,1)}), bf16[72,6912]{1,0:T(8,128)(2,1)}) %reduce-scatter.38.cloned.1.call-update) | async-done | bytes 995344 | tf_op jit(solution)/shard_map/reduce_scatter | solution.py:123
  1383.7 20.3 %all-reduce.10.cloned.1.call-done = bf16[1000,72]{0,1:T(8,128)(2,1)} async-done(((bf16[1000,72]{0,1:T(8,128)(2,1)}), bf16[1000,72]{0,1:T(8,128)(2,1)}) %all-reduce.10.cloned.1.call-update) | async-done | bytes 144016
  1406.2 12.5 reduce-scatter.44.cloned.1.call-done
  1421.0 15.1 reduce-scatter.46.cloned.1.call-done
  1438.7 13.4 reduce-scatter.30.cloned.1.call-done
  1454.3 13.7 reduce-scatter.34.cloned.1.call-done
  1470.3 19.1 %reduce-scatter.42.cloned.1.call-done = bf16[1728,72]{1,0:T(8,128)(2,1)} async-done(((bf16[3456,72]{1,0:T(8,128)(2,1)}), bf16[1728,72]{1,0:T(8,128)(2,1)}) %reduce-scatter.42.cloned.1.call-update) | async-done | bytes 248848
  1491.9 28.0 %reduce-scatter.48.cloned.1.call-done = bf16[3456,72]{1,0:T(8,128)(2,1)} async-done(((bf16[6912,72]{1,0:T(8,128)(2,1)}), bf16[3456,72]{1,0:T(8,128)(2,1)}) %reduce-scatter.48.cloned.1.call-update) | async-done | bytes 497680
  (642 shorter events, 377.7 us)
Async XLA Ops:
  7.2 136.9 %all-gather.12.cloned.1.call-start = ((), (), s32[]{:S(2)}) async-start(), calls=%async_computation.13 | async-start | bytes 2506752 | tf_op jit(solution)/shard_map/all_gather | solution.py:99
  14.4 134.1 %all-gather.16.cloned.1.call-start = ((), (), s32[]{:S(2)}) async-start(), calls=%async_computation.15 | async-start | bytes 8460288 | tf_op jit(solution)/shard_map/all_gather | solution.py:92
  24.0 231.3 %all-gather.14.cloned.1.call-start = ((), (), s32[]{:S(2)}) async-start(), calls=%async_computation.14 | async-start | bytes 16920576 | tf_op jit(solution)/shard_map/all_gather | solution.py:97
  36.2 263.2 %all-gather.18.cloned.1.call-start = ((), (), s32[]{:S(2)}) async-start(), calls=%async_computation.16 | async-start | bytes 2820096 | tf_op jit(solution)/shard_map/all_gather | solution.py:93
  42.6 324.3 %all-gather.20.cloned.1.call-start = ((), (), s32[]{:S(2)}) async-start(), calls=%async_computation.17 | async-start | bytes 7520256 | tf_op jit(solution)/shard_map/all_gather | solution.py:94
  50.8 383.8 %all-gather.24.cloned.1.call-start = ((), (), s32[]{:S(2)}) async-start(), calls=%async_computation.19 | async-start | bytes 7520256 | tf_op jit(solution)/shard_map/all_gather | solution.py:96
  60.4 441.7 %all-gather.22.cloned.1.call-start = ((), (), s32[]{:S(2)}) async-start(), calls=%async_computation.18 | async-start | bytes 7520256 | tf_op jit(solution)/shard_map/all_gather | solution.py:95
  67.7 683.9 %reduce-scatter.40.cloned.1.call-start = ((), (), s32[]{:S(2)}) async-start(), calls=%async_computation.26 | async-start | bytes 2506752 | tf_op jit(solution)/shard_map/reduce_scatter | solution.py:129
  690.0 128.9 %reduce-scatter.52.cloned.1.call-start = ((), (), s32[]{:S(2)}) async-start(), calls=%async_computation.33 | async-start | bytes 2820096
  694.8 216.9 %reduce-scatter.36.cloned.1.call-start = ((), (), s32[]{:S(2)}) async-start(), calls=%async_computation.24 | async-start | bytes 7520256 | tf_op jit(solution)/shard_map/reduce_scatter | solution.py:120
  705.0 300.8 %reduce-scatter.28.cloned.1.call-start = ((), (), s32[]{:S(2)}) async-start(), calls=%async_computation.20 | async-start | bytes 7520256 | tf_op jit(solution)/shard_map/reduce_scatter | solution.py:114
  713.9 401.5 %reduce-scatter.32.cloned.1.call-start = ((), (), s32[]{:S(2)}) async-start(), calls=%async_computation.22 | async-start | bytes 7520256 | tf_op jit(solution)/shard_map/reduce_scatter | solution.py:117
  721.9 483.5 %reduce-scatter.50.cloned.1.call-start = ((), (), s32[]{:S(2)}) async-start(), calls=%async_computation.32 | async-start | bytes 8460288
  738.2 642.8 %reduce-scatter.38.cloned.1.call-start = ((), (), s32[]{:S(2)}) async-start(), calls=%async_computation.25 | async-start | bytes 16920576 | tf_op jit(solution)/shard_map/reduce_scatter | solution.py:123
  747.0 657.0 %all-reduce.10.cloned.1.call-start = ((), (), s32[]{:S(2)}) async-start(), calls=%async_computation.31 | async-start | bytes 294912
  751.6 667.1 %reduce-scatter.44.cloned.1.call-start = ((), (), s32[]{:S(2)}) async-start(), calls=%async_computation.28 | async-start | bytes 442368
  820.8 295.3 %copy-start.155 = (f32[256]{0:T(256)S(1)}, f32[256]{0:T(256)}, u32[]{:S(2)}) copy-start(f32[256]{0:T(256)} %get-tuple-element.67) | copy-start | bytes 3076
  820.8 297.0 %copy-start.56 = (bf16[1,256,1152]{2,1,0:T(8,128)(2,1)S(1)}, bf16[1,256,1152]{2,1,0:T(8,128)(2,1)}, u32[]{:S(2)}) copy-start(bf16[1,256,1152]{2,1,0:T(8,128)(2,1)} %get-tuple-element.116) | copy-start | bytes 1769476
  820.8 297.0 %copy-start.57 = (bf16[1,256,1152]{2,1,0:T(8,128)(2,1)S(1)}, bf16[1,256,1152]{2,1,0:T(8,128)(2,1)}, u32[]{:S(2)}) copy-start(bf16[1,256,1152]{2,1,0:T(8,128)(2,1)} %get-tuple-element.119) | copy-start | bytes 1769476
  820.8 615.4 %reduce-scatter.46.cloned.1.call-start = ((), (), s32[]{:S(2)}) async-start(), calls=%async_computation.29 | async-start | bytes 884736
  913.8 538.3 %reduce-scatter.30.cloned.1.call-start = ((), (), s32[]{:S(2)}) async-start(), calls=%async_computation.21 | async-start | bytes 663552 | tf_op jit(solution)/shard_map/reduce_scatter | solution.py:140
  1005.8 462.2 %reduce-scatter.34.cloned.1.call-start = ((), (), s32[]{:S(2)}) async-start(), calls=%async_computation.23 | async-start | bytes 663552 | tf_op jit(solution)/shard_map/reduce_scatter | solution.py:143
  1115.4 373.9 %reduce-scatter.42.cloned.1.call-start = ((), (), s32[]{:S(2)}) async-start(), calls=%async_computation.27 | async-start | bytes 1327104
  1207.7 312.3 %reduce-scatter.48.cloned.1.call-start = ((), (), s32[]{:S(2)}) async-start(), calls=%async_computation.30 | async-start | bytes 2654208
  (185 other events, 2764.2 us)
Sparse Core Ops, SparseCore 0:
  14.5 44.0 all-gather.11
  61.3 71.9 all-gather.15
  135.5 119.7 all-gather.13
  257.8 41.5 all-gather.17
  301.5 65.2 all-gather.19
  369.6 65.0 all-gather.23
  437.0 65.0 all-gather.21
  690.1 61.4 reduce-scatter.39
  756.0 62.8 reduce-scatter.51
  822.8 88.8 reduce-scatter.35
  916.2 89.5 reduce-scatter.27
  1009.7 90.5 reduce-scatter.31
  1104.9 100.4 reduce-scatter.49
  1209.4 171.6 reduce-scatter.37
  1383.2 20.7 all-reduce.9
  1406.7 12.0 reduce-scatter.43
  1420.9 15.2 reduce-scatter.45
  1438.4 13.6 reduce-scatter.29
  1454.3 13.6 reduce-scatter.33
  1470.8 18.5 reduce-scatter.41
  1491.7 28.2 reduce-scatter.47
where the time goes:
time: 1540 us; the launch traced here: 1530 us
  waiting for transfers between devices  927 us (60%)
  blocking collectives  226 us (15%)
  matrix products  223 us (14%)
  local copies, waits for them, and re-layouts  75.1 us (5%)
  other arithmetic  52.7 us (3%)
  between operations  25.2 us (2%)
    unnamed x28, waiting for transfers between devices  249 us
    reduce_scatter x1, waiting for transfers between devices, reduce_grads(): lax.psum_scatter(g_ada.astype(jnp.bfloat16), 'wide', scatter_dimension=0,...  169 us
    unnamed x4, blocking collectives  130 us
    all_gather x1, waiting for transfers between devices, fetch_weights(): lax.all_gather(ada_part, 'wide', axis=0, tiled=True)  95.2 us
    reduce_scatter x1, waiting for transfers between devices, reduce_grads(): lax.psum_scatter(g_gate.astype(jnp.bfloat16), 'wide', scatter_dimension=0...  92 us
    reduce_scatter x1, waiting for transfers between devices, reduce_grads(): lax.psum_scatter(g_down.astype(jnp.bfloat16), 'wide', scatter_dimension=0...  90.9 us
    all_gather x1, waiting for transfers between devices, fetch_weights(): lax.all_gather(down_part, 'wide', axis=0, tiled=True)  60.5 us
    all_gather x1, waiting for transfers between devices, fetch_weights(): lax.all_gather(up_part, 'wide', axis=0, tiled=True)  60.2 us
  transfers between devices with their start and end apart: 21, of which 18 were waited for; matrix products, arithmetic and copies ran while one was open for 10% of the time, Pallas kernels for 0%

commit v1 on v0

v1 whole, which is shorter than its diff:
```python
import math

import jax
import jax.numpy as jnp
from jax import lax
from jax.experimental import pallas as pl
from jax.experimental.pallas import tpu as pltpu
from jax.sharding import PartitionSpec as P

H = 16
HD = 72
CLASSES = 1000
GRID = 16

EPSILON = 1e-06
HIGHEST = lax.Precision.HIGHEST
ALL = ("wide", "narrow")
BF = jnp.bfloat16
F32 = jnp.float32


def rope_tables(length, grid_side, head):
    quarter = head // 4
    frequency = 10000.0 ** (-jnp.arange(quarter, dtype=jnp.float32) / quarter)
    patch_index = jnp.arange(length, dtype=jnp.int32)
    row_place = (patch_index // grid_side).astype(jnp.float32)
    col_place = (patch_index % grid_side).astype(jnp.float32)
    row_angle = row_place[:, None] * frequency[None, :]
    col_angle = col_place[:, None] * frequency[None, :]
    angles = jnp.concatenate([row_angle, row_angle, col_angle, col_angle], axis=-1)
    return (jnp.cos(angles)[:, None, :], jnp.sin(angles)[:, None, :])


def rotate_half(vector):
    quarter = vector.shape[-1] // 4
    part_one = vector[..., :quarter]
    part_two = vector[..., quarter : 2 * quarter]
    part_three = vector[..., 2 * quarter : 3 * quarter]
    part_four = vector[..., 3 * quarter :]
    return jnp.concatenate([-part_two, part_one, -part_four, part_three], axis=-1)


def rotary(vector, cosine_table, sine_table):
    return vector * cosine_table + rotate_half(vector) * sine_table


def rotary_back(gradient, cosine_table, sine_table):
    return gradient * cosine_table - rotate_half(gradient * sine_table)


def layer_norm(values):
    centre = values - jnp.mean(values, axis=-1, keepdims=True)
    inverse = lax.rsqrt(jnp.mean(centre * centre, axis=-1, keepdims=True) + EPSILON)
    return (centre * inverse, inverse)


def layer_norm_back(gradient, normed, inverse):
    return inverse * (
        gradient
        - jnp.mean(gradient, axis=-1, keepdims=True)
        - normed * jnp.mean(gradient * normed, axis=-1, keepdims=True)
    )


def rms_norm(values):
    inverse = lax.rsqrt(jnp.mean(values * values, axis=-1, keepdims=True) + EPSILON)
    return (values * inverse, inverse)


def rms_back(gradient, normed, inverse):
    return inverse * (gradient - normed * jnp.mean(gradient * normed, axis=-1, keepdims=True))


class Places:
    def __init__(self):
        self.wide, self.narrow = lax.axis_size("wide"), lax.axis_size("narrow")
        self.z = self.wide // 4
        w = lax.axis_index("wide")
        self.w, self.x = w, lax.axis_index("narrow")
        self.at_z, self.at_y, self.at_c = w // 4, (w // 2) % 2, w % 2
        self.z_bits = [1 << i for i in range(self.z.bit_length() - 1)]
        self.x_bits = [1 << i for i in range(self.narrow.bit_length() - 1)]
        x_masks = [(0, bit) for bit in self.x_bits]
        self.orders = ([(1, 0)] + x_masks, x_masks + [(1, 0)])

    def swap(self, value, flip):
        pairs = []
        for w in range(self.wide):
            for x in range(self.narrow):
                dz, dy, dc, dx = flip(w % 2)
                to = (w // 4 ^ dz) * 4 + (w // 2 % 2 ^ dy) * 2 + (w % 2 ^ dc)
                pairs.append((w * self.narrow + x, to * self.narrow + (x ^ dx)))
        return lax.ppermute(value, ALL, pairs)

    def step_flip(self, i):
        return lambda core: (0, self.orders[core][i][0], 0, self.orders[core][i][1])

    def masks(self, core):
        out = [(0, 0)]
        for dy, dx in self.orders[core]:
            out = out + [(y ^ dy, x ^ dx) for y, x in out]
        return out

    def all_bits(self):
        out = [(0, (bit, 0, 0, 0), self.at_z // bit % 2) for bit in self.z_bits]
        out.append((1, (0, 1, 0, 0), self.at_y))
        out += [(3, (0, 0, 0, bit), self.x // bit % 2) for bit in self.x_bits]
        out.append((2, (0, 0, 1, 0), self.at_c))
        return out

    def gather_small(self, value):
        value = value[None, None, None, None]
        for axis, flip, bit in self.all_bits():
            other = self.swap(value, lambda core: flip)
            low = jnp.where(bit == 0, value, other)
            high = jnp.where(bit == 0, other, value)
            value = jnp.concatenate([low, high], axis)
        return value.reshape(self.wide * self.narrow, *value.shape[4:])

    def add_all(self, value):
        for _, flip, _ in self.all_bits():
            value = value + self.swap(value, lambda core: flip)
        return value

    def add_narrow(self, value):
        for bit in self.x_bits:
            value = value + self.swap(value, lambda core: (0, 0, 0, bit))
        return value

    def scatter_wide(self, value):
        value = value.reshape(self.z, 2, 2, *value.shape[1:])
        other = self.swap(take(value, 2, 1 - self.at_c), lambda core: (0, 0, 1, 0))
        value = take(value, 2, self.at_c) + other
        other = self.swap(take(value, 1, 1 - self.at_y), lambda core: (0, 1, 0, 0))
        value = take(value, 1, self.at_y) + other
        for bit in reversed(self.z_bits):
            value = value.reshape(2, bit, *value.shape[1:])
            here = self.at_z // bit % 2
            other = self.swap(take(value, 0, 1 - here), lambda core: (bit, 0, 0, 0))
            value = take(value, 0, here) + other
        return value[0]


def pick(parts, index):
    if len(parts) == 1:
        return parts[0]
    if len(parts) == 2:
        return jnp.where(index == 0, parts[0], parts[1])
    return lax.dynamic_index_in_dim(jnp.stack(parts), index, 0, keepdims=False)


def take(value, axis, index):
    return lax.dynamic_index_in_dim(value, index, axis, keepdims=False)


def after(value, *before):
    return lax.optimization_barrier((value,) + before)[0]


def assemble(places, parts):
    half, z, rows, columns = parts[0].shape
    masks = [places.masks(0), places.masks(1)]

    def kernel(at, s0, s1, t0, t1, out, held, sem, out_sem):
        core, y, x, here_z = at[0], at[1], at[2], at[3]
        copies = []
        for i, src in enumerate((s0, s1, t0, t1)):
            owner = core ^ (i // 2)
            for j in range(half):
                k = j + half * (i % 2)
                dy = jnp.where(owner == 0, masks[0][k][0], masks[1][k][0])
                dx = jnp.where(owner == 0, masks[0][k][1], masks[1][k][1])
                for d in range(z):
                    to = held.at[x ^ dx, here_z ^ d, y ^ dy, owner]
                    copies.append(pltpu.make_async_copy(src.at[j, d], to, sem.at[len(copies)]))
        for copy in copies:
            copy.start()
        for copy in copies:
            copy.wait()
        whole = pltpu.make_async_copy(held, out, out_sem)
        whole.start()
        whole.wait()

    shape = (places.narrow, z, 2, 2, rows, columns)
    at = jnp.stack([places.at_c, places.at_y, places.x, places.at_z]).astype(jnp.int32)
    size = 2 * math.prod(shape)
    return pl.pallas_call(
        kernel,
        out_shape=jax.ShapeDtypeStruct(shape, BF),
        in_specs=[pl.BlockSpec(memory_space=pltpu.SMEM)] + [pl.BlockSpec(memory_space=pl.ANY)] * 4,
        out_specs=pl.BlockSpec(memory_space=pl.ANY),
        scratch_shapes=[
            pltpu.VMEM(shape, BF),
            pltpu.SemaphoreType.DMA((4 * half * z,)),
            pltpu.SemaphoreType.DMA,
        ],
        compiler_params=pltpu.CompilerParams(vmem_limit_bytes=24 * 2**20),
        cost_estimate=pl.CostEstimate(flops=0, bytes_accessed=2 * size, transcendentals=0),
        name="assemble",
    )(at, *parts)


def gather_weights(places, shards):
    outs, last = [], {}

    def swap(kind, value, flip):
        if kind in last:
            value = after(value, last[kind])
        last[kind] = places.swap(value, flip)
        return last[kind]

    steps = len(places.orders[0])
    for shard in shards:
        held = shard[None]
        for bit in places.z_bits:
            held = jnp.concatenate([held, swap("z", held, lambda core: (bit, 0, 0, 0))], 0)
        held = held[None]
        for i in range(steps):
            other = swap(i, held, places.step_flip(i))
            if i < steps - 1:
                held = jnp.concatenate([held, other], 0)
        parts = [held, other]
        parts += [places.swap(part, lambda core: (0, 0, 1, 0)) for part in parts]
        whole = assemble(places, parts)
        outs.append(list(whole.reshape(places.narrow, places.wide * shard.shape[0], shard.shape[1])))
    return outs


def scatter(places, blocks):
    z = places.z
    blocks = [b.reshape(z, 2, 2, -1, b.shape[-1]) for b in blocks]
    masks = [places.masks(0), places.masks(1)]

    def stack(owner, first, count):
        out = []
        for j in range(first, first + count):
            dy = jnp.where(owner == 0, masks[0][j][0], masks[1][j][0])
            dx = jnp.where(owner == 0, masks[0][j][1], masks[1][j][1])
            rows = [
                take(take(b, 2, owner), 1, places.at_y ^ dy) for b in blocks
            ]
            out.append(pick(rows, places.x ^ dx))
        return jnp.stack(out)

    total = len(masks[0])
    arrived = places.swap(stack(1 - places.at_c, 0, total), lambda core: (0, 0, 1, 0))
    half = total // 2
    send = (stack(places.at_c, half, half).astype(F32) + arrived[half:].astype(F32)).astype(BF)
    other = places.swap(send, places.step_flip(len(places.orders[0]) - 1))
    held = stack(places.at_c, 0, half).astype(F32) + arrived[:half].astype(F32) + other.astype(F32)
    for i in reversed(range(len(places.orders[0]) - 1)):
        half //= 2
        other = places.swap(held[half:].astype(BF), places.step_flip(i))
        held = held[:half] + other.astype(F32)
    held = held[0]
    held = jnp.stack([take(held, 0, places.at_z ^ d) for d in range(z)])
    for bit in reversed(places.z_bits):
        other = places.swap(held[bit:].astype(BF), lambda core: (bit, 0, 0, 0))
        held = held[:bit] + other.astype(F32)
    return held[0]


def dot(a, b, dims, out=F32):
    return lax.dot_general(a, b, (dims, ((), ())), preferred_element_type=F32).astype(out)


def times(a, blocks):
    return jnp.concatenate([dot(a, b, ((1,), (0,))) for b in blocks], axis=1)


def times_t(a, blocks):
    width = blocks[0].shape[1]
    total = None
    for n, b in enumerate(blocks):
        term = dot(a[:, n * width : (n + 1) * width], b, ((1,), (1,)))
        total = term if total is None else total + term
    return total


def grad_blocks(a, d, narrow):
    width = d.shape[1] // narrow
    return [dot(a, d[:, n * width : (n + 1) * width], ((0,), (0,)), BF) for n in range(narrow)]


def on_device(
    inputs,
    cotangent,
    class_ids,
    step_ids,
    image_counts,
    w_qkv,
    w_out,
    w_gate,
    w_up,
    w_down,
    ada_weight,
    ada_bias,
    class_table,
    norm_gains,
):
    places = Places()
    wide, narrow, at_w, at_n = places.wide, places.narrow, places.w, places.x
    images, length, width = inputs.shape
    cosine_table, sine_table = rope_tables(length, GRID, HD)
    local_count = image_counts[0]
    score_scale = HD ** (-0.5)

    small = [class_ids, step_ids, image_counts, ada_bias]
    small = places.gather_small(jnp.concatenate([v.astype(F32) for v in small])[None])[:, 0]
    ids = small[:, : 2 * images].reshape(-1, 2, images).transpose(0, 2, 1).reshape(-1, 2)
    ids = ids.astype(jnp.int32)
    real_count = jnp.sum(small[:, 2 * images])
    bias = small[:, 2 * images + 1 :].reshape(-1)
    rows_here, cols_here = class_table.shape
    class_hot = ids[:, :1] - at_n * rows_here == jnp.arange(rows_here, dtype=jnp.int32)[None, :]
    picked = dot(class_hot.astype(BF), class_table, ((1,), (0,)))
    column = at_w * cols_here + jnp.arange(cols_here, dtype=jnp.int32)
    half_width = width // 2
    frequency = jnp.exp(-math.log(10000.0) * (column % half_width).astype(F32) / half_width)
    angles = ids[:, 1:].astype(F32) * frequency[None, :]
    wave = jnp.where(column[None, :] < half_width, jnp.cos(angles), jnp.sin(angles))
    condition = places.add_narrow(picked) + wave
    cond_act = jax.nn.silu(condition).astype(BF)
    mod_part = dot(cond_act, ada_weight, ((1,), (0,)))
    mod_part = places.scatter_wide(mod_part.reshape(wide, narrow, images, -1))
    modulation = lax.all_to_all(mod_part, "narrow", 0, 0, tiled=True)
    modulation = modulation.transpose(1, 0, 2).reshape(images, -1) + bias
    pieces = jnp.split(modulation[:, None, :], 6, axis=-1)

    qkv_b, out_b, gate_b, up_b, down_b = gather_weights(
        places, [w_qkv, w_out, w_gate, w_up, w_down]
    )
    tokens = images * length

    def flat(v):
        return v.reshape(tokens, -1)

    def deep(v):
        return v.reshape(images, length, -1)

    source = inputs.astype(F32)
    normed, inverse = layer_norm(source)
    attn_in = flat((normed * (1.0 + pieces[1]) + pieces[0]).astype(BF))
    packed = times(attn_in, qkv_b).reshape(images, length, 3, H, HD)
    query_normed, query_inverse = rms_norm(packed[:, :, 0])
    key_normed, key_inverse = rms_norm(packed[:, :, 1])
    queries = rotary(query_normed * norm_gains[0], cosine_table, sine_table).astype(BF)
    key_rows = rotary(key_normed * norm_gains[1], cosine_table, sine_table).astype(BF)
    value_rows = packed[:, :, 2].astype(BF)
    scores = (
        jnp.einsum("bshe,bthe->bhst", queries, key_rows, preferred_element_type=F32) * score_scale
    )
    row_max = jnp.max(scores, axis=-1, keepdims=True)
    exponent = jnp.exp(scores - row_max)
    softmax_out = exponent / jnp.sum(exponent, axis=-1, keepdims=True)
    attention = softmax_out.astype(BF)
    mixed = jnp.einsum("bhst,bthe->bshe", attention, value_rows, preferred_element_type=F32)
    mixed = mixed.reshape(tokens, width).astype(BF)
    attn_out = deep(times(mixed, out_b))
    hidden_one = source + pieces[2] * attn_out
    normed_two, inverse_two = layer_norm(hidden_one)
    mlp_in = flat((normed_two * (1.0 + pieces[4]) + pieces[3]).astype(BF))
    gate_val = times(mlp_in, gate_b)
    up_val = times(mlp_in, up_b)
    gate_sigmoid = jax.nn.sigmoid(gate_val)
    hidden_mid = (gate_val * gate_sigmoid * up_val).astype(BF)
    mlp_out = deep(times(hidden_mid, down_b))
    block_output = (hidden_one + pieces[5] * mlp_out).astype(BF)

    slot_real = (jnp.arange(images, dtype=jnp.int32) < local_count).astype(F32)
    grad_y = cotangent.astype(F32) * slot_real[:, None, None]
    d_gate_b = jnp.sum(grad_y * mlp_out, axis=1)
    d_mlp = flat((pieces[5] * grad_y).astype(BF))

    r_down = scatter(places, grad_blocks(hidden_mid, d_mlp, narrow))
    d_mid = times_t(d_mlp, down_b)
    d_gate = (d_mid * up_val * gate_sigmoid * (1.0 + gate_val * (1.0 - gate_sigmoid))).astype(BF)
    d_up = (d_mid * gate_val * gate_sigmoid).astype(BF)
    r_up = scatter(places, grad_blocks(mlp_in, d_up, narrow))
    r_gate = scatter(places, grad_blocks(mlp_in, d_gate, narrow))
    d_mlp_in = deep(times_t(d_gate, gate_b) + times_t(d_up, up_b))
    d_scale_b = jnp.sum(d_mlp_in * normed_two, axis=1)
    d_shift_b = jnp.sum(d_mlp_in, axis=1)
    d_hidden = grad_y + layer_norm_back(d_mlp_in * (1.0 + pieces[4]), normed_two, inverse_two)
    d_gate_a = jnp.sum(d_hidden * attn_out, axis=1)
    d_attn = flat((pieces[2] * d_hidden).astype(BF))
    r_out = scatter(places, grad_blocks(mixed, d_attn, narrow))
    d_mixed = times_t(d_attn, out_b).astype(BF).reshape(images, length, H, HD)
    d_values = jnp.einsum("bhst,bshe->bthe", attention, d_mixed, preferred_element_type=F32)
    d_soft = jnp.einsum("bshe,bthe->bhst", d_mixed, value_rows, preferred_element_type=F32)
    row_inner = jnp.sum(softmax_out * d_soft, axis=-1, keepdims=True)
    d_scores = (softmax_out * (d_soft - row_inner) * score_scale).astype(BF)
    d_queries = jnp.einsum("bhst,bthe->bshe", d_scores, key_rows, preferred_element_type=F32)
    d_keys = jnp.einsum("bhst,bshe->bthe", d_scores, queries, preferred_element_type=F32)
    query_scaled = rotary_back(d_queries, cosine_table, sine_table)
    key_scaled = rotary_back(d_keys, cosine_table, sine_table)
    grad_gains = jnp.stack(
        [
            jnp.sum(query_scaled * query_normed, axis=(0, 1, 2)),
            jnp.sum(key_scaled * key_normed, axis=(0, 1, 2)),
        ],
        axis=0,
    )
    d_query_raw = rms_back(query_scaled * norm_gains[0], query_normed, query_inverse)
    d_key_raw = rms_back(key_scaled * norm_gains[1], key_normed, key_inverse)
    d_packed = jnp.stack([d_query_raw, d_key_raw, d_values], axis=2)
    d_packed = d_packed.reshape(tokens, 3 * width).astype(BF)
    r_qkv = scatter(places, grad_blocks(attn_in, d_packed, narrow))
    d_attn_in = deep(times_t(d_packed, qkv_b))
    d_scale_a = jnp.sum(d_attn_in * normed, axis=1)
    d_shift_a = jnp.sum(d_attn_in, axis=1)
    d_tokens = d_hidden + layer_norm_back(d_attn_in * (1.0 + pieces[1]), normed, inverse)
    d_modulation = jnp.concatenate(
        [d_shift_a, d_scale_a, d_gate_a, d_shift_b, d_scale_b, d_gate_b], axis=-1
    ).astype(BF)

    d_mod = places.gather_small(d_modulation).reshape(-1, d_modulation.shape[1])
    ada_cols = ada_weight.shape[1]
    d_mod_here = lax.dynamic_slice_in_dim(d_mod, at_n * ada_cols, ada_cols, 1)
    g_ada = dot(cond_act, d_mod_here, ((0,), (0,)))
    bias_cols = ada_bias.shape[0]
    bias_at = (at_w * narrow + at_n) * bias_cols
    g_bias = jnp.sum(lax.dynamic_slice_in_dim(d_mod, bias_at, bias_cols, 1).astype(F32), axis=0)
    d_cond_act = places.add_narrow(dot(d_mod_here, ada_weight, ((1,), (1,))))
    cond_sigmoid = jax.nn.sigmoid(condition)
    d_condition = d_cond_act * cond_sigmoid * (1.0 + condition * (1.0 - cond_sigmoid))
    g_table = jnp.dot(class_hot.astype(F32).T, d_condition, precision=HIGHEST)
    gain_sum = places.add_all(grad_gains)
    return (
        block_output,
        d_tokens.astype(BF),
        r_qkv / real_count,
        r_out / real_count,
        r_gate / real_count,
        r_up / real_count,
        r_down / real_count,
        g_ada / real_count,
        g_bias / real_count,
        g_table / real_count,
        gain_sum / real_count,
    )


def solution(mesh):
    split = P("wide", "narrow")
    images = P(ALL, None, None)
    return jax.shard_map(
        on_device,
        mesh=mesh,
        in_specs=(
            images,
            images,
            P(ALL),
            P(ALL),
            P(ALL),
            split,
            split,
            split,
            split,
            split,
            split,
            P(ALL),
            P("narrow", "wide"),
            P(),
        ),
        out_specs=(
            images,
            images,
            split,
            split,
            split,
            split,
            split,
            split,
            P(ALL),
            P("narrow", "wide"),
            P(),
        ),
        check_vma=False,
    )
```

time: 1540 us -> 867 us (0.56)
  waiting for transfers between devices: 927 us -> 331 us
  blocking collectives: 226 us -> 0 us
  other arithmetic: 52.7 us -> 156 us
  starting transfers between devices: 0.86 us -> 65.4 us
  matrix products: 223 us -> 171 us
  Pallas kernels: 0 us -> 33.6 us
  local copies, waits for them, and re-layouts: 75.1 us -> 98.8 us
  between operations: 25.2 us -> 3.8 us
    reduce_scatter x7 -> x0, waiting for transfers between devices: 384 us -> none  [the longest x1 169 us: reduce_grads(): lax.psum_scatter(g_ada.astype(jnp.bfloat16), 'wide', scatter_dimension=0,...]
    ppermute x0 -> x76, waiting for transfers between devices: none -> 331 us  [swap(): return lax.ppermute(value, ALL, pairs)]
    all_gather x7 -> x0, waiting for transfers between devices: 294 us -> none  [the longest x1 95.2 us: fetch_weights(): lax.all_gather(ada_part, 'wide', axis=0, tiled=True)]
    unnamed x28 -> x0, waiting for transfers between devices: 249 us -> none
    unnamed x4 -> x0, blocking collectives: 130 us -> none
    ppermute x0 -> x76, starting transfers between devices: none -> 61.3 us  [swap(): return lax.ppermute(value, ALL, pairs)]
    dot_general x43 -> x40, matrix products: 223 us -> 163 us  [the longest x34 116 us: dot(): lax.dot_general(a, b, (dims, ((), ())), preferred_element_type=F32)]
    all_gather x7 -> x0, blocking collectives: 54.8 us -> none  [the longest x1 12.1 us: fetch_weights(): lax.all_gather(ada_part, 'narrow', axis=1, tiled=True)]
  transfers between devices with their start and end apart: 21 -> 77, of which waited for: 18 -> 38; matrix products, arithmetic and copies ran while one was open for 10% -> 28% of each run, Pallas kernels for 0% -> 3%
where the time goes in v1:
time: 867 us; the launch traced here: 860 us
  waiting for transfers between devices  331 us (38%)
  matrix products  171 us (20%)
  other arithmetic  156 us (18%)
  local copies, waits for them, and re-layouts  98.8 us (11%)
  starting transfers between devices  65.4 us (8%)
  Pallas kernels  33.6 us (4%)
    ppermute x76, waiting for transfers between devices, swap(): return lax.ppermute(value, ALL, pairs)  331 us
    dot_general x34, matrix products, dot(): lax.dot_general(a, b, (dims, ((), ())), preferred_element_type=F32)  116 us
    ppermute x76, starting transfers between devices, swap(): return lax.ppermute(value, ALL, pairs)  61.3 us
    select_n x8, other arithmetic, pick(): return jnp.where(index == 0, parts[0], parts[1])  36.6 us
    pallas_call x5, Pallas kernels, assemble(): pl.pallas_call(kernel, out_shape=jax.ShapeDtypeStruct(shape, BF), in_spec...  33.6 us
    convert_element_type x6, local copies, waits for them, and re-layouts, dot(): lax.dot_general(a, b, (dims, ((), ())), preferred_element_type=F32)  29.9 us
    unnamed x276, local copies, waits for them, and re-layouts  19.8 us
  transfers between devices with their start and end apart: 77, of which 38 were waited for; matrix products, arithmetic and copies ran while one was open for 28% of the time, Pallas kernels for 3%

profile of v1, /device:TPU:0, one launch (start us, length us, event | category | flops | bytes accessed | tf_op | source)
XLA Modules:
  0.0 859.8 jit_solution(11952288875101349805)
XLA Ops:
  39.4 19.6 %collective-permute-done.11 = bf16[2,72,1728]{2,1,0:T(8,128)(2,1)S(1)} collective-permute-done((bf16[2,72,1728]{2,1,0:T(8,128)(2,1)S(1)}, bf16[2,72,1728]{2,1,0:T(8,128)(2,1)S(1)}, u32[]{:S(2)}, u32[]{:S(2)}) %collective-permute-start.11) | collective-permute-done | bytes 497696 | tf_op jit(solution)/shard_map/ppermute | solution.py:93
  67.3 9.1 %collective-permute-done.17 = bf16[2,72,576]{2,1,0:T(8,128)(2,1)S(1)} collective-permute-done((bf16[2,72,576]{2,1,0:T(8,128)(2,1)S(1)}, bf16[2,72,576]{2,1,0:T(8,128)(2,1)S(1)}, u32[]{:S(2)}, u32[]{:S(2)}) %collective-permute-start.17) | collective-permute-done | bytes 165920 | tf_op jit(solution)/shard_map/ppermute | solution.py:93
  86.1 18.3 %collective-permute-done.23 = bf16[2,72,1536]{2,1,0:T(8,128)(2,1)S(1)} collective-permute-done((bf16[2,72,1536]{2,1,0:T(8,128)(2,1)S(1)}, bf16[2,72,1536]{2,1,0:T(8,128)(2,1)S(1)}, u32[]{:S(2)}, u32[]{:S(2)}) %collective-permute-start.23) | collective-permute-done | bytes 442400 | tf_op jit(solution)/shard_map/ppermute | solution.py:93
  122.3 12.1 %collective-permute-done.29 = bf16[2,72,1536]{2,1,0:T(8,128)(2,1)} collective-permute-done((bf16[2,72,1536]{2,1,0:T(8,128)(2,1)}, bf16[2,72,1536]{2,1,0:T(8,128)(2,1)}, u32[]{:S(2)}, u32[]{:S(2)}) %collective-permute-start.29) | collective-permute-done | bytes 442400 | tf_op jit(solution)/shard_map/ppermute | solution.py:93
  145.1 10.1 %collective-permute-done.13.s1 = bf16[2,4,72,1728]{3,2,1,0:T(8,128)(2,1)} collective-permute-done((bf16[2,4,72,1728]{3,2,1,0:T(8,128)(2,1)S(1)}, bf16[2,4,72,1728]{3,2,1,0:T(8,128)(2,1)}, u32[]{:S(2)}, u32[]{:S(2)}) %collective-permute-start.13) | collective-permute-done | bytes 1990688 | tf_op jit(solution)/shard_map/ppermute | solution.py:93
  159.4 8.1 collective-permute-done.35
  193.7 10.2 %assemble.5 = bf16[2,4,2,2,72,1728]{5,4,3,2,1,0:T(8,128)(2,1)S(1)} custom-call(s32[4]{0:T(128)S(1)} %pad_add_fusion.at, bf16[2,4,72,1728]{3,2,1,0:T(8,128)(2,1)S(1)} %pad_maximum_fusion.10.s0, bf16[2,4,72,1728]{3,2,1,0:T(8,128)(2,1)} %collective-permute-done.13.s1, bf16[2,4,72,1728]{3,2,1,0:T(8,128)(2,1)S(1)} %collective-permute-done.14.t0, ...), custom_call_target="tpu_custom_call" | custom-call | bytes 15925248 | tf_op jit(solution)/shard_map/assemble/pallas_call | solution.py:187
  214.1 9.8 %reshape.1455 = f32[2,256,3,16,72]{1,0,4,3,2:T(2,128)} reshape(f32[512,3456]{0,1:T(8,128)} %pad_maximum_fusion) | data formatting | bytes 14155776 | tf_op jit(solution)/shard_map/reshape | solution.py:344
  236.5 8.0 fusion.198
  262.3 13.6 %collective-permute-done.31.s1 = bf16[2,4,72,1536]{3,2,1,0:T(8,128)(2,1)S(1)} collective-permute-done((bf16[2,4,72,1536]{3,2,1,0:T(8,128)(2,1)}, bf16[2,4,72,1536]{3,2,1,0:T(8,128)(2,1)S(1)}, u32[]{:S(2)}, u32[]{:S(2)}) %collective-permute-start.31) | collective-permute-done | bytes 1769504 | tf_op jit(solution)/shard_map/ppermute | solution.py:93
  309.9 7.2 fusion.209
  334.0 11.4 %multiply_convert_fusion.2 = (bf16[512,3072]{1,0:T(8,128)(2,1)}, bf16[512,3072]{1,0:T(8,128)(2,1)}, bf16[512,3072]{1,0:T(8,128)(2,1)}) fusion(f32[512,1536]{1,0:T(8,128)} %fusion.209, f32[512,1536]{1,0:T(8,128)} %fusion.208, f32[512,1536]{1,0:T(8,128)} %fusion.207, f32[512,1536]{1,0:T(8,128)} %fusion.206, f32[512,3072]{1,0:T(8,128)} %fusion.117, ...), kind=kOutput, calls=%fused_computation.18 | convolution fusion | flops 1841823744 | bytes 32505856 | tf_op jit(solution)/shard_map/dot_general | solution.py:264
  432.5 13.6 %fusion.9 = f32[2,16,72,256]{3,2,1,0:T(8,128)} fusion(bf16[2,256,16,72]{1,3,2,0:T(8,128)(2,1)S(1)} %copy-done.73, f32[2,16,256,256]{2,3,1,0:T(8,128)} %fusion.125, f32[2,16,256,256]{2,3,1,0:T(8,128)} %get-tuple-element.193, f32[2,16,256]{2,1,0:T(8,128)S(1)} %get-tuple-element.192), kind=kOutput, calls=%fused_computation.25 | convolution fusion | flops 316678400 | bytes 20348928 | tf_op jit(solution)/shard_map/bhst,bshe->bthe/dot_general | solution.py:394
  446.1 16.6 %bitcast_multiply_fusion.3 = (f32[2,256,16,72]{1,3,2,0:T(8,128)}, f32[2,256,16,72]{1,3,2,0:T(8,128)S(1)}, f32[2,16,72,256]{3,2,1,0:T(8,128)}) fusion(f32[256,72]{0,1:T(8,128)S(1)} %copy-done.96, f32[2,16,72,256]{3,2,1,0:T(8,128)} %fusion.9, bf16[2,256,16,72]{1,3,2,0:T(8,128)(2,1)} %copy-done.72, f32[2,16,256,256]{2,3,1,0:T(8,128)} %fusion.125, ...), kind=kOutput, calls=%fused_computation.88 | convolution fusion | flops 317858048 | bytes 27500544 | tf_op jit(solution)/shard_map/bhst,bthe->bshe/dot_general | solution.py:393
  515.8 7.7 fusion.110
  552.7 8.1 fusion.94
  618.5 7.4 collective-permute-done.46
  667.0 25.6 %collective-permute-done.51 = bf16[2,4,72,1536]{3,2,1,0:T(8,128)(2,1)S(1)} collective-permute-done((bf16[2,4,72,1536]{3,2,1,0:T(8,128)(2,1)S(1)}, bf16[2,4,72,1536]{3,2,1,0:T(8,128)(2,1)S(1)}, u32[]{:S(2)}, u32[]{:S(2)}) %collective-permute-start.51) | collective-permute-done | bytes 1769504 | tf_op jit(solution)/shard_map/ppermute | solution.py:93
  695.8 27.4 %collective-permute-done.61 = bf16[2,4,192,576]{3,2,1,0:T(8,128)(2,1)S(1)} collective-permute-done((bf16[2,4,192,576]{3,2,1,0:T(8,128)(2,1)S(1)}, bf16[2,4,192,576]{3,2,1,0:T(8,128)(2,1)S(1)}, u32[]{:S(2)}, u32[]{:S(2)}) %collective-permute-start.61) | collective-permute-done | bytes 1769504 | tf_op jit(solution)/shard_map/ppermute | solution.py:93
  726.1 29.8 %collective-permute-done.41 = bf16[2,4,72,1728]{3,2,1,0:T(8,128)(2,1)S(1)} collective-permute-done((bf16[2,4,72,1728]{3,2,1,0:T(8,128)(2,1)S(1)}, bf16[2,4,72,1728]{3,2,1,0:T(8,128)(2,1)S(1)}, u32[]{:S(2)}, u32[]{:S(2)}) %collective-permute-start.41) | collective-permute-done | bytes 1990688 | tf_op jit(solution)/shard_map/ppermute | solution.py:93
  764.4 33.8 %collective-permute-done.58 = bf16[2,72,1536]{2,1,0:T(8,128)(2,1)S(1)} collective-permute-done((bf16[2,72,1536]{2,1,0:T(8,128)(2,1)S(1)}, bf16[2,72,1536]{2,1,0:T(8,128)(2,1)S(1)}, u32[]{:S(2)}, u32[]{:S(2)}) %collective-permute-start.58) | collective-permute-done | bytes 442400 | tf_op jit(solution)/shard_map/ppermute | solution.py:93
  798.4 9.4 %collective-permute-done.53 = bf16[2,72,1536]{2,1,0:T(8,128)(2,1)S(1)} collective-permute-done((bf16[2,72,1536]{2,1,0:T(8,128)(2,1)S(1)}, bf16[2,72,1536]{2,1,0:T(8,128)(2,1)S(1)}, u32[]{:S(2)}, u32[]{:S(2)}) %collective-permute-start.53) | collective-permute-done | bytes 442400 | tf_op jit(solution)/shard_map/ppermute | solution.py:93
  808.0 10.2 %collective-permute-done.63 = bf16[2,192,576]{2,1,0:T(8,128)(2,1)S(1)} collective-permute-done((bf16[2,192,576]{2,1,0:T(8,128)(2,1)S(1)}, bf16[2,192,576]{2,1,0:T(8,128)(2,1)S(1)}, u32[]{:S(2)}, u32[]{:S(2)}) %collective-permute-start.63) | collective-permute-done | bytes 442400 | tf_op jit(solution)/shard_map/ppermute | solution.py:93
  829.2 20.5 %collective-permute-done.43 = bf16[2,72,1728]{2,1,0:T(8,128)(2,1)S(1)} collective-permute-done((bf16[2,72,1728]{2,1,0:T(8,128)(2,1)S(1)}, bf16[2,72,1728]{2,1,0:T(8,128)(2,1)S(1)}, u32[]{:S(2)}, u32[]{:S(2)}) %collective-permute-start.43) | collective-permute-done | bytes 497696 | tf_op jit(solution)/shard_map/ppermute | solution.py:93
  (654 shorter events, 508.5 us)
Async XLA Ops:
  66.8 37.7 %collective-permute-start.12 = (bf16[1,4,72,1728]{3,2,1,0:T(8,128)(2,1)S(1)}, bf16[1,4,72,1728]{3,2,1,0:T(8,128)(2,1)S(1)}, u32[]{:S(2)}, u32[]{:S(2)}) collective-permute-start(bf16[1,4,72,1728]{3,2,1,0:T(8,128)(2,1)S(1)} %maximum_bitcast_fusion), channel_id=1, source_target_pairs={{0,4},{1,5},{2,3},{3,2},{4,0},{5,1},{6,7},{7,6},{8,12},{9,13},{10,... | collective-permute-start | bytes 2985992 | tf_op jit(solution)/shard_map/ppermute | solution.py:93
  120.3 34.9 %collective-permute-start.13 = (bf16[2,4,72,1728]{3,2,1,0:T(8,128)(2,1)S(1)}, bf16[2,4,72,1728]{3,2,1,0:T(8,128)(2,1)}, u32[]{:S(2)}, u32[]{:S(2)}) collective-permute-start(bf16[2,4,72,1728]{3,2,1,0:T(8,128)(2,1)S(1)} %pad_maximum_fusion.10.s0), channel_id=1, source_target_pairs={{0,1},{1,0},{2,6},{3,7},{4,5},{5,4},{6,2},{7,3},{8,9},{9,8},{10,14... | collective-permute-start | bytes 5971976 | tf_op jit(solution)/shard_map/ppermute | solution.py:93
  145.1 48.6 %collective-permute-start.14 = (bf16[2,4,72,1728]{3,2,1,0:T(8,128)(2,1)S(1)}, bf16[2,4,72,1728]{3,2,1,0:T(8,128)(2,1)S(1)}, u32[]{:S(2)}, u32[]{:S(2)}) collective-permute-start(bf16[2,4,72,1728]{3,2,1,0:T(8,128)(2,1)S(1)} %pad_maximum_fusion.10.s0), channel_id=1, source_target_pairs={{0,2},{1,3},{2,0},{3,1},{4,6},{5,7},{6,4},{7,5},{8,10},{9,11},{10,... | collective-permute-start | bytes 5971976 | tf_op jit(solution)/shard_map/ppermute | solution.py:93
  155.2 38.5 %collective-permute-start.15 = (bf16[2,4,72,1728]{3,2,1,0:T(8,128)(2,1)}, bf16[2,4,72,1728]{3,2,1,0:T(8,128)(2,1)S(1)}, u32[]{:S(2)}, u32[]{:S(2)}) collective-permute-start(bf16[2,4,72,1728]{3,2,1,0:T(8,128)(2,1)} %collective-permute-done.13.s1), channel_id=1, source_target_pairs={{0,2},{1,3},{2,0},{3,1},{4,6},{5,7},{6,4},{7,5},{8,10},{9,11},{10,... | collective-permute-start | bytes 5971976 | tf_op jit(solution)/shard_map/ppermute | solution.py:93
  182.8 93.7 %collective-permute-start.26 = (bf16[2,4,72,1536]{3,2,1,0:T(8,128)(2,1)}, bf16[2,4,72,1536]{3,2,1,0:T(8,128)(2,1)}, u32[]{:S(2)}, u32[]{:S(2)}) collective-permute-start(bf16[2,4,72,1536]{3,2,1,0:T(8,128)(2,1)} %pad_maximum_fusion.12.s0), channel_id=1, source_target_pairs={{0,2},{1,3},{2,0},{3,1},{4,6},{5,7},{6,4},{7,5},{8,10},{9,11},{10,... | collective-permute-start | bytes 5308424 | tf_op jit(solution)/shard_map/ppermute | solution.py:93
  184.4 116.4 %collective-permute-start.32 = (bf16[2,4,72,1536]{3,2,1,0:T(8,128)(2,1)}, bf16[2,4,72,1536]{3,2,1,0:T(8,128)(2,1)}, u32[]{:S(2)}, u32[]{:S(2)}) collective-permute-start(bf16[2,4,72,1536]{3,2,1,0:T(8,128)(2,1)} %pad_maximum_fusion.13.s0), channel_id=1, source_target_pairs={{0,2},{1,3},{2,0},{3,1},{4,6},{5,7},{6,4},{7,5},{8,10},{9,11},{10,... | collective-permute-start | bytes 5308424 | tf_op jit(solution)/shard_map/ppermute | solution.py:93
  184.9 68.2 %collective-permute-start.25 = (bf16[2,4,72,1536]{3,2,1,0:T(8,128)(2,1)}, bf16[2,4,72,1536]{3,2,1,0:T(8,128)(2,1)}, u32[]{:S(2)}, u32[]{:S(2)}) collective-permute-start(bf16[2,4,72,1536]{3,2,1,0:T(8,128)(2,1)} %pad_maximum_fusion.12.s0), channel_id=1, source_target_pairs={{0,1},{1,0},{2,6},{3,7},{4,5},{5,4},{6,2},{7,3},{8,9},{9,8},{10,14... | collective-permute-start | bytes 5308424 | tf_op jit(solution)/shard_map/ppermute | solution.py:93
  193.7 127.3 %collective-permute-start.38 = (bf16[2,4,192,576]{3,2,1,0:T(8,128)(2,1)}, bf16[2,4,192,576]{3,2,1,0:T(8,128)(2,1)}, u32[]{:S(2)}, u32[]{:S(2)}) collective-permute-start(bf16[2,4,192,576]{3,2,1,0:T(8,128)(2,1)} %pad_maximum_fusion.11.s0), channel_id=1, source_target_pairs={{0,2},{1,3},{2,0},{3,1},{4,6},{5,7},{6,4},{7,5},{8,10},{9,11},{10,... | collective-permute-start | bytes 5308424 | tf_op jit(solution)/shard_map/ppermute | solution.py:93
  503.1 108.9 %collective-permute-start.45 = (bf16[4,4,72,576]{3,2,1,0:T(8,128)(2,1)}, bf16[4,4,72,576]{3,2,1,0:T(8,128)(2,1)}, u32[]{:S(2)}, u32[]{:S(2)}) collective-permute-start(bf16[4,4,72,576]{3,2,1,0:T(8,128)(2,1)} %pad_maximum_fusion.14), channel_id=1, source_target_pairs={{0,2},{1,3},{2,0},{3,1},{4,6},{5,7},{6,4},{7,5},{8,10},{9,11},{10,... | collective-permute-start | bytes 3981320 | tf_op jit(solution)/shard_map/ppermute | solution.py:93
  525.5 121.2 %collective-permute-start.50 = (bf16[4,4,72,1536]{3,2,1,0:T(8,128)(2,1)}, bf16[4,4,72,1536]{3,2,1,0:T(8,128)(2,1)}, u32[]{:S(2)}, u32[]{:S(2)}) collective-permute-start(bf16[4,4,72,1536]{3,2,1,0:T(8,128)(2,1)} %pad_maximum_fusion.6), channel_id=1, source_target_pairs={{0,2},{1,3},{2,0},{3,1},{4,6},{5,7},{6,4},{7,5},{8,10},{9,11},{10,... | collective-permute-start | bytes 10616840 | tf_op jit(solution)/shard_map/ppermute | solution.py:93
  526.1 62.8 %collective-permute-start.71 = (f32[2,72]{1,0:T(2,128)}, f32[2,72]{1,0:T(2,128)}, u32[]{:S(2)}, u32[]{:S(2)}) collective-permute-start(f32[2,72]{1,0:T(2,128)} %pad_maximum_fusion.37), channel_id=1, source_target_pairs={{0,8},{1,9},{2,10},{3,11},{4,12},{5,13},{6,14},{7,15},{8,0},{9,1},... | collective-permute-start | bytes 1736 | tf_op jit(solution)/shard_map/ppermute | solution.py:93
  539.3 46.8 %collective-permute-start.65 = (bf16[1,1,1,1,2,6912]{5,4,3,2,1,0:T(2,128)(2,1)}, bf16[1,1,1,1,2,6912]{5,4,3,2,1,0:T(2,128)(2,1)}, u32[]{:S(2)}, u32[]{:S(2)}) collective-permute-start(bf16[1,1,1,1,2,6912]{5,4,3,2,1,0:T(2,128)(2,1)} %constant_dynamic-update-slice_fusion), channel_id=1, source_target_pairs={{0,8},{1,9},{2,10},{3,11},{4,12},{5,13},{6,14},{7,15},{8,0},{9,1},... | collective-permute-start | bytes 82952 | tf_op jit(solution)/shard_map/ppermute | solution.py:93
  609.2 40.4 %collective-permute-start.60 = (bf16[4,4,192,576]{3,2,1,0:T(8,128)(2,1)}, bf16[4,4,192,576]{3,2,1,0:T(8,128)(2,1)}, u32[]{:S(2)}, u32[]{:S(2)}) collective-permute-start(bf16[4,4,192,576]{3,2,1,0:T(8,128)(2,1)} %pad_maximum_fusion.4), channel_id=1, source_target_pairs={{0,2},{1,3},{2,0},{3,1},{4,6},{5,7},{6,4},{7,5},{8,10},{9,11},{10,... | collective-permute-start | bytes 10616840 | tf_op jit(solution)/shard_map/ppermute | solution.py:93
  610.8 42.5 %collective-permute-start.40 = (bf16[4,4,72,1728]{3,2,1,0:T(8,128)(2,1)}, bf16[4,4,72,1728]{3,2,1,0:T(8,128)(2,1)}, u32[]{:S(2)}, u32[]{:S(2)}) collective-permute-start(bf16[4,4,72,1728]{3,2,1,0:T(8,128)(2,1)} %pad_maximum_fusion.3), channel_id=1, source_target_pairs={{0,2},{1,3},{2,0},{3,1},{4,6},{5,7},{6,4},{7,5},{8,10},{9,11},{10,... | collective-permute-start | bytes 11943944 | tf_op jit(solution)/shard_map/ppermute | solution.py:93
  648.9 43.8 %collective-permute-start.51 = (bf16[2,4,72,1536]{3,2,1,0:T(8,128)(2,1)S(1)}, bf16[2,4,72,1536]{3,2,1,0:T(8,128)(2,1)S(1)}, u32[]{:S(2)}, u32[]{:S(2)}) collective-permute-start(bf16[2,4,72,1536]{3,2,1,0:T(8,128)(2,1)S(1)} %add_convert_fusion.3), channel_id=1, source_target_pairs={{0,1},{1,0},{2,6},{3,7},{4,5},{5,4},{6,2},{7,3},{8,9},{9,8},{10,14... | collective-permute-start | bytes 5308424 | tf_op jit(solution)/shard_map/ppermute | solution.py:93
  651.9 71.3 %collective-permute-start.61 = (bf16[2,4,192,576]{3,2,1,0:T(8,128)(2,1)S(1)}, bf16[2,4,192,576]{3,2,1,0:T(8,128)(2,1)S(1)}, u32[]{:S(2)}, u32[]{:S(2)}) collective-permute-start(bf16[2,4,192,576]{3,2,1,0:T(8,128)(2,1)S(1)} %add_convert_fusion.1), channel_id=1, source_target_pairs={{0,1},{1,0},{2,6},{3,7},{4,5},{5,4},{6,2},{7,3},{8,9},{9,8},{10,14... | collective-permute-start | bytes 5308424 | tf_op jit(solution)/shard_map/ppermute | solution.py:93
  655.7 100.1 %collective-permute-start.41 = (bf16[2,4,72,1728]{3,2,1,0:T(8,128)(2,1)S(1)}, bf16[2,4,72,1728]{3,2,1,0:T(8,128)(2,1)S(1)}, u32[]{:S(2)}, u32[]{:S(2)}) collective-permute-start(bf16[2,4,72,1728]{3,2,1,0:T(8,128)(2,1)S(1)} %add_convert_fusion), channel_id=1, source_target_pairs={{0,1},{1,0},{2,6},{3,7},{4,5},{5,4},{6,2},{7,3},{8,9},{9,8},{10,14... | collective-permute-start | bytes 5971976 | tf_op jit(solution)/shard_map/ppermute | solution.py:93
  666.4 92.5 %collective-permute-start.57 = (bf16[1,4,72,1536]{3,2,1,0:T(8,128)(2,1)S(1)}, bf16[1,4,72,1536]{3,2,1,0:T(8,128)(2,1)S(1)}, u32[]{:S(2)}, u32[]{:S(2)}) collective-permute-start(bf16[1,4,72,1536]{3,2,1,0:T(8,128)(2,1)S(1)} %slice.485), channel_id=1, source_target_pairs={{0,4},{1,5},{2,3},{3,2},{4,0},{5,1},{6,7},{7,6},{8,12},{9,13},{10,... | collective-permute-start | bytes 2654216 | tf_op jit(solution)/shard_map/ppermute | solution.py:93
  695.2 65.3 %collective-permute-start.52 = (bf16[1,4,72,1536]{3,2,1,0:T(8,128)(2,1)S(1)}, bf16[1,4,72,1536]{3,2,1,0:T(8,128)(2,1)S(1)}, u32[]{:S(2)}, u32[]{:S(2)}) collective-permute-start(bf16[1,4,72,1536]{3,2,1,0:T(8,128)(2,1)S(1)} %slice.486), channel_id=1, source_target_pairs={{0,4},{1,5},{2,3},{3,2},{4,0},{5,1},{6,7},{7,6},{8,12},{9,13},{10,... | collective-permute-start | bytes 2654216 | tf_op jit(solution)/shard_map/ppermute | solution.py:93
  725.5 37.2 %collective-permute-start.62 = (bf16[1,4,192,576]{3,2,1,0:T(8,128)(2,1)S(1)}, bf16[1,4,192,576]{3,2,1,0:T(8,128)(2,1)S(1)}, u32[]{:S(2)}, u32[]{:S(2)}) collective-permute-start(bf16[1,4,192,576]{3,2,1,0:T(8,128)(2,1)S(1)} %slice.484), channel_id=1, source_target_pairs={{0,4},{1,5},{2,3},{3,2},{4,0},{5,1},{6,7},{7,6},{8,12},{9,13},{10,... | collective-permute-start | bytes 2654216 | tf_op jit(solution)/shard_map/ppermute | solution.py:93
  758.3 66.0 %collective-permute-start.42 = (bf16[1,4,72,1728]{3,2,1,0:T(8,128)(2,1)S(1)}, bf16[1,4,72,1728]{3,2,1,0:T(8,128)(2,1)S(1)}, u32[]{:S(2)}, u32[]{:S(2)}) collective-permute-start(bf16[1,4,72,1728]{3,2,1,0:T(8,128)(2,1)S(1)} %slice.483), channel_id=1, source_target_pairs={{0,4},{1,5},{2,3},{3,2},{4,0},{5,1},{6,7},{7,6},{8,12},{9,13},{10,... | collective-permute-start | bytes 2985992 | tf_op jit(solution)/shard_map/ppermute | solution.py:93
  759.2 38.9 %collective-permute-start.58 = (bf16[2,72,1536]{2,1,0:T(8,128)(2,1)S(1)}, bf16[2,72,1536]{2,1,0:T(8,128)(2,1)S(1)}, u32[]{:S(2)}, u32[]{:S(2)}) collective-permute-start(bf16[2,72,1536]{2,1,0:T(8,128)(2,1)S(1)} %pad_maximum_fusion.24), channel_id=1, source_target_pairs={{0,16},{1,17},{2,18},{3,19},{4,20},{5,21},{6,22},{7,23},{8,24},{9,... | collective-permute-start | bytes 1327112 | tf_op jit(solution)/shard_map/ppermute | solution.py:93
  760.8 46.9 %collective-permute-start.53 = (bf16[2,72,1536]{2,1,0:T(8,128)(2,1)S(1)}, bf16[2,72,1536]{2,1,0:T(8,128)(2,1)S(1)}, u32[]{:S(2)}, u32[]{:S(2)}) collective-permute-start(bf16[2,72,1536]{2,1,0:T(8,128)(2,1)S(1)} %pad_maximum_fusion.23), channel_id=1, source_target_pairs={{0,16},{1,17},{2,18},{3,19},{4,20},{5,21},{6,22},{7,23},{8,24},{9,... | collective-permute-start | bytes 1327112 | tf_op jit(solution)/shard_map/ppermute | solution.py:93
  763.0 55.1 %collective-permute-start.63 = (bf16[2,192,576]{2,1,0:T(8,128)(2,1)S(1)}, bf16[2,192,576]{2,1,0:T(8,128)(2,1)S(1)}, u32[]{:S(2)}, u32[]{:S(2)}) collective-permute-start(bf16[2,192,576]{2,1,0:T(8,128)(2,1)S(1)} %pad_maximum_fusion.20), channel_id=1, source_target_pairs={{0,16},{1,17},{2,18},{3,19},{4,20},{5,21},{6,22},{7,23},{8,24},{9,... | collective-permute-start | bytes 1327112 | tf_op jit(solution)/shard_map/ppermute | solution.py:93
  (187 other events, 2171.9 us)

commit v2 on v1

v2 whole, which is shorter than its diff:
```python
import math

import jax
import jax.numpy as jnp
from jax import lax
from jax.experimental import pallas as pl
from jax.experimental.pallas import tpu as pltpu
from jax.sharding import PartitionSpec as P

H = 16
HD = 72
CLASSES = 1000
GRID = 16

EPSILON = 1e-06
HIGHEST = lax.Precision.HIGHEST
ALL = ("wide", "narrow")
BF = jnp.bfloat16
F32 = jnp.float32
SHORT = pl.CostEstimate(flops=10**6, bytes_accessed=10**6, transcendentals=0)


def layer_norm(values):
    centre = values - jnp.mean(values, axis=-1, keepdims=True)
    inverse = lax.rsqrt(jnp.mean(centre * centre, axis=-1, keepdims=True) + EPSILON)
    return (centre * inverse, inverse)


def head_tables(length):
    quarter = HD // 4
    frequency = 10000.0 ** (-jnp.arange(quarter, dtype=F32) / quarter)
    patch = jnp.arange(length, dtype=jnp.int32)
    row_angle = (patch // GRID).astype(F32)[:, None] * frequency[None, :]
    col_angle = (patch % GRID).astype(F32)[:, None] * frequency[None, :]
    angles = jnp.concatenate([row_angle, row_angle, col_angle, col_angle], axis=-1)
    cosine, sine = jnp.cos(angles), jnp.sin(angles)
    first = (jnp.arange(HD) // quarter) % 2 == 0
    above = jnp.where(first[None, :], -sine, 0.0)
    below = jnp.where(first[None, :], 0.0, sine)
    return [jnp.tile(t, (1, H)) for t in (cosine, above, below)]


def head_sums():
    lane = lax.broadcasted_iota(jnp.int32, (H * HD, 128), 0) // HD
    return (lane == lax.broadcasted_iota(jnp.int32, (H * HD, 128), 1)).astype(BF)


def exact_dot(a, b, dims):
    total = None
    for _ in range(3):
        term = a.astype(BF)
        a = a - term.astype(F32)
        part = lax.dot_general(term, b, (dims, ((), ())), preferred_element_type=F32)
        total = part if total is None else total + part
    return total


def head_mean(values, sums):
    mean = exact_dot(values, sums, ((1,), (0,))) * (1.0 / HD)
    return exact_dot(mean, sums, ((1,), (1,)))


def shifted(values, cosine, above, below, sign):
    quarter, width = HD // 4, values.shape[1]
    up = pltpu.roll(values, width - quarter, 1)
    down = pltpu.roll(values, quarter, 1)
    return values * cosine + sign * (up * above + down * below)


def window(head):
    first, last = head * HD // 128 * 128, ((head + 1) * HD + 127) // 128 * 128
    return first, last


def only(values, head):
    first, last = window(head)
    part = values[:, first:last]
    lane = first + lax.broadcasted_iota(jnp.int32, (1, last - first), 1)
    mine = ((lane >= head * HD) & (lane < (head + 1) * HD)).astype(values.dtype)
    return part * mine


class Tiles:
    def __init__(self, store):
        self.store, self.held = store, {}

    def add(self, head, value):
        first, last = window(head)
        for tile in range(first // 128, last // 128):
            part = value[:, tile * 128 - first : tile * 128 - first + 128]
            self.held[tile] = self.held[tile] + part if tile in self.held else part
        done = (head + 1) * HD // 128
        for tile in sorted(self.held):
            if tile < done or head == H - 1:
                self.store(tile * 128, self.held.pop(tile))


def mm(a, b, dims):
    return lax.dot_general(a, b, (dims, ((), ())), preferred_element_type=F32)


def softmax_of(queries, keys, head):
    first, last = window(head)
    scores = mm(queries[:, first:last], only(keys, head), ((1,), (1,))) * (HD ** (-0.5))
    exponent = jnp.exp(scores - jnp.max(scores, axis=1, keepdims=True))
    return exponent / jnp.sum(exponent, axis=1, keepdims=True)


def attention_forward(packed, gains, tables, sums, images):
    tokens = packed[0].shape[0]
    length, width, blocks = tokens // images, H * HD, len(packed)

    def kernel(*refs):
        parts, refs = refs[:blocks], refs[blocks:]
        gain, cosine, above, below, sums_ref, q_ref, k_ref, v_ref, mixed_ref = refs
        whole = jnp.concatenate([p[...] for p in parts], axis=1)
        sums_here = sums_ref[...]
        for i, ref in enumerate((q_ref, k_ref)):
            raw = whole[:, i * width : (i + 1) * width]
            normed = raw * lax.rsqrt(head_mean(raw * raw, sums_here) + EPSILON)
            turned = shifted(normed * gain[i : i + 1, :], cosine[...], above[...], below[...], 1.0)
            ref[...] = turned.astype(BF)
        v_ref[...] = whole[:, 2 * width :].astype(BF)

        def store(first, value):
            mixed_ref[:, first : first + 128] = value.astype(BF)

        mixed = Tiles(store)
        for head in range(H):
            attention = softmax_of(q_ref, k_ref, head).astype(BF)
            mixed.add(head, mm(attention, only(v_ref, head), ((1,), (0,))))

    def rows(n):
        return pl.BlockSpec((length, n), lambda i: (i, 0))

    def all_of(a):
        return pl.BlockSpec(a.shape, lambda i: (0, 0))

    out = jax.ShapeDtypeStruct((tokens, width), BF)
    return pl.pallas_call(
        kernel,
        grid=(images,),
        out_shape=[out] * 4,
        in_specs=[rows(p.shape[1]) for p in packed] + [all_of(a) for a in (gains, *tables, sums)],
        out_specs=[rows(width)] * 4,
        compiler_params=pltpu.CompilerParams(vmem_limit_bytes=48 * 2**20),
        cost_estimate=SHORT,
        name="attention_forward",
    )(*packed, gains, *tables, sums)


def attention_backward(packed, queries, keys, values, d_mixed, gains, tables, sums, images):
    tokens = queries.shape[0]
    length, width, blocks = tokens // images, H * HD, len(packed)
    block = packed[0].shape[1]

    def kernel(*refs):
        parts, refs = refs[:blocks], refs[blocks:]
        q_ref, k_ref, v_ref, d_ref, gain, cosine, above, below, sums_ref = refs[:9]
        outs, (gain_ref, d_q, d_k, d_v) = refs[9 : 9 + blocks], refs[9 + blocks :]

        def store_to(ref):
            def store(first, value):
                ref[:, first : first + 128] = value

            return store

        all_q, all_k, all_v = [Tiles(store_to(ref)) for ref in (d_q, d_k, d_v)]
        for head in range(H):
            first, last = window(head)
            soft = softmax_of(q_ref, k_ref, head)
            d_here = only(d_ref, head)
            all_v.add(head, mm(soft.astype(BF), d_here, ((0,), (0,))))
            d_soft = mm(d_here, v_ref[:, first:last], ((1,), (1,)))
            inner = jnp.sum(soft * d_soft, axis=1, keepdims=True)
            d_scores = (soft * (d_soft - inner) * (HD ** (-0.5))).astype(BF)
            all_q.add(head, mm(d_scores, only(k_ref, head), ((1,), (0,))))
            all_k.add(head, mm(d_scores, only(q_ref, head), ((0,), (0,))))
        whole = jnp.concatenate([p[...] for p in parts], axis=1)
        sums_here = sums_ref[...]
        done = []
        for i, ref in enumerate((d_q, d_k)):
            raw = whole[:, i * width : (i + 1) * width]
            inverse = lax.rsqrt(head_mean(raw * raw, sums_here) + EPSILON)
            normed = raw * inverse
            scaled = shifted(ref[...], cosine[...], above[...], below[...], -1.0)
            gain_ref[0, i : i + 1, :] = jnp.sum(scaled * normed, axis=0, keepdims=True)
            incoming = scaled * gain[i : i + 1, :]
            mean = head_mean(incoming * normed, sums_here)
            done.append((inverse * (incoming - normed * mean)).astype(BF))
        done.append(d_v[...].astype(BF))
        done = jnp.concatenate(done, axis=1)
        for j, out in enumerate(outs):
            out[...] = done[:, j * block : (j + 1) * block]

    def rows(n):
        return pl.BlockSpec((length, n), lambda i: (i, 0))

    def all_of(a):
        return pl.BlockSpec(a.shape, lambda i: (0, 0))

    outs = pl.pallas_call(
        kernel,
        grid=(images,),
        out_shape=[jax.ShapeDtypeStruct((tokens, block), BF)] * blocks
        + [jax.ShapeDtypeStruct((images, 2, width), F32)],
        in_specs=[rows(block)] * blocks
        + [rows(width)] * 4
        + [all_of(a) for a in (gains, *tables, sums)],
        out_specs=[rows(block)] * blocks + [pl.BlockSpec((1, 2, width), lambda i: (i, 0, 0))],
        scratch_shapes=[pltpu.VMEM((length, width), F32)] * 3,
        compiler_params=pltpu.CompilerParams(vmem_limit_bytes=56 * 2**20),
        cost_estimate=SHORT,
        name="attention_backward",
    )(*packed, queries, keys, values, d_mixed, gains, *tables, sums)
    return outs[:blocks], outs[blocks]

def whole_block(a):
    return pl.BlockSpec(a.shape, lambda *i: (0,) * a.ndim)


def chunk_of(columns, most):
    count = -(-columns // most)
    return columns if count == 1 else -(-columns // (128 * count)) * 128


def project(a, blocks):
    tokens, depth = a.shape
    columns = blocks[0].shape[1]
    count, chunk = len(blocks), chunk_of(columns, 640)

    def kernel(a_ref, *refs):
        for w_ref, out_ref in zip(refs[:count], refs[count:]):
            out_ref[...] = mm(a_ref[...], w_ref[...], ((1,), (0,)))

    return pl.pallas_call(
        kernel,
        grid=(-(-columns // chunk),),
        out_shape=[jax.ShapeDtypeStruct((tokens, columns), F32)] * count,
        in_specs=[whole_block(a)] + [pl.BlockSpec((depth, chunk), lambda i: (0, i))] * count,
        out_specs=[pl.BlockSpec((tokens, chunk), lambda i: (0, i))] * count,
        compiler_params=pltpu.CompilerParams(vmem_limit_bytes=40 * 2**20),
        cost_estimate=SHORT,
        name="project",
    )(a, *blocks)


def gated(a, w_gate, w_up):
    tokens, depth = a.shape
    columns = w_gate.shape[1]
    chunk = 512

    def kernel(a_ref, g_ref, u_ref, gate_ref, up_ref, mid_ref):
        gate = mm(a_ref[...], g_ref[...], ((1,), (0,)))
        up = mm(a_ref[...], u_ref[...], ((1,), (0,)))
        gate_ref[...] = gate
        up_ref[...] = up
        mid_ref[...] = (gate * jax.nn.sigmoid(gate) * up).astype(BF)

    weight = pl.BlockSpec((depth, chunk), lambda i: (0, i))
    out = pl.BlockSpec((tokens, chunk), lambda i: (0, i))
    return pl.pallas_call(
        kernel,
        grid=(columns // chunk,),
        out_shape=[jax.ShapeDtypeStruct((tokens, columns), t) for t in (F32, F32, BF)],
        in_specs=[whole_block(a), weight, weight],
        out_specs=[out] * 3,
        compiler_params=pltpu.CompilerParams(vmem_limit_bytes=40 * 2**20),
        cost_estimate=SHORT,
        name="gated",
    )(a, w_gate, w_up)


def gated_back(d_parts, down, gate_val, up_val, w_gate, w_up):
    tokens, columns = gate_val.shape
    depth, count, chunk = w_gate.shape[0], len(down), 512

    def kernel(*refs):
        d_refs, w_refs, refs = refs[:count], refs[count : 2 * count], refs[2 * count :]
        gate_ref, up_ref, g_ref, u_ref, d_gate_ref, d_up_ref, in_ref = refs
        d_mid = None
        for d_ref, w_ref in zip(d_refs, w_refs):
            term = mm(d_ref[...], w_ref[...], ((1,), (1,)))
            d_mid = term if d_mid is None else d_mid + term
        gate, up = gate_ref[...], up_ref[...]
        sigmoid = jax.nn.sigmoid(gate)
        silu = gate * sigmoid
        d_gate = (d_mid * up * (sigmoid + silu * (1.0 - sigmoid))).astype(BF)
        d_up = (d_mid * silu).astype(BF)
        d_gate_ref[...] = d_gate
        d_up_ref[...] = d_up
        term = mm(d_gate, g_ref[...], ((1,), (1,))) + mm(d_up, u_ref[...], ((1,), (1,)))

        @pl.when(pl.program_id(0) == 0)
        def _():
            in_ref[...] = term

        @pl.when(pl.program_id(0) > 0)
        def _():
            in_ref[...] += term

    width = down[0].shape[1]
    token = pl.BlockSpec((tokens, chunk), lambda i: (0, i))
    weight = pl.BlockSpec((depth, chunk), lambda i: (0, i))
    return pl.pallas_call(
        kernel,
        grid=(columns // chunk,),
        out_shape=[jax.ShapeDtypeStruct((tokens, columns), BF)] * 2
        + [jax.ShapeDtypeStruct((tokens, depth), F32)],
        in_specs=[whole_block(d) for d in d_parts]
        + [pl.BlockSpec((chunk, width), lambda i: (i, 0))] * count
        + [token, token, weight, weight],
        out_specs=[token, token, pl.BlockSpec((tokens, depth), lambda i: (0, 0))],
        compiler_params=pltpu.CompilerParams(vmem_limit_bytes=48 * 2**20),
        cost_estimate=SHORT,
        name="gated_back",
    )(*d_parts, *down, gate_val, up_val, w_gate, w_up)


def normal(values):
    centre = values - jnp.mean(values, axis=1, keepdims=True)
    inverse = lax.rsqrt(jnp.mean(centre * centre, axis=1, keepdims=True) + EPSILON)
    return centre * inverse, inverse


def normal_back(gradient, normed, inverse):
    mean = jnp.mean(gradient, axis=1, keepdims=True)
    return inverse * (
        gradient - mean - normed * jnp.mean(gradient * normed, axis=1, keepdims=True)
    )


def per_image(kernel, images, by_image, whole, outs, vmem, name, scalar=None):
    def spec(rows, rest):
        return pl.BlockSpec((rows, *rest), lambda i: (i,) + (0,) * len(rest))

    in_specs = [spec(a.shape[0] // images, a.shape[1:]) for a in by_image]
    in_specs += [whole_block(a) for a in whole]
    args = [*by_image, *whole]
    if scalar is not None:
        in_specs.append(pl.BlockSpec(memory_space=pltpu.SMEM))
        args.append(scalar)
    return pl.pallas_call(
        kernel,
        grid=(images,),
        out_shape=[jax.ShapeDtypeStruct((images * rows, *rest), t) for rows, rest, t in outs],
        in_specs=in_specs,
        out_specs=[spec(rows, rest) for rows, rest, _ in outs],
        compiler_params=pltpu.CompilerParams(vmem_limit_bytes=vmem * 2**20),
        cost_estimate=SHORT,
        name=name,
    )(*args)


def attention_tail(mixed, out_b, inputs, pieces, images):
    tokens, width = mixed.shape

    def kernel(mixed_ref, in_ref, piece, *refs):
        w_refs, (attn_ref, hidden_ref, mlp_ref) = refs[:-3], refs[-3:]
        attn = [mm(mixed_ref[...], w[...], ((1,), (0,))) for w in w_refs]
        attn = jnp.concatenate(attn, axis=1)
        attn_ref[...] = attn
        hidden = in_ref[...].astype(F32) + piece[0, 2:3, :] * attn
        hidden_ref[...] = hidden
        normed, _ = normal(hidden)
        mlp_ref[...] = (normed * (1.0 + piece[0, 4:5, :]) + piece[0, 3:4, :]).astype(BF)

    rows = tokens // images
    outs = [(rows, (width,), F32), (rows, (width,), F32), (rows, (width,), BF)]
    return per_image(kernel, images, [mixed, inputs, pieces], out_b, outs, 32, "attention_tail")


def block_tail(hidden_mid, down_b, hidden_one, cotangent, pieces, count, images):
    tokens, width = hidden_one.shape

    def kernel(mid_ref, hidden_ref, cot_ref, piece, *refs):
        w_refs, (count_ref, out_ref, gate_ref) = refs[:-3], refs[-3:]
        mlp = [mm(mid_ref[...], w[...], ((1,), (0,))) for w in w_refs]
        mlp = jnp.concatenate(mlp, axis=1)
        out_ref[...] = (hidden_ref[...] + piece[0, 5:6, :] * mlp).astype(BF)
        real = (pl.program_id(0) < count_ref[0]).astype(F32)
        grad = cot_ref[...].astype(F32) * real
        gate_ref[0] = jnp.sum(grad * mlp, axis=0, keepdims=True)

    rows = tokens // images
    outs = [(rows, (width,), BF), (1, (1, width), F32)]
    by_image = [hidden_mid, hidden_one, cotangent, pieces]
    return per_image(kernel, images, by_image, down_b, outs, 40, "block_tail", count)


def middle_back(d_mlp_in, hidden_one, attn_out, cotangent, pieces, out_b, count, images):
    tokens, width = d_mlp_in.shape
    blocks, columns = len(out_b), out_b[0].shape[1]

    def kernel(in_ref, hidden_ref, attn_ref, cot_ref, piece, *refs):
        w_refs, count_ref, refs = refs[:blocks], refs[blocks], refs[blocks + 1 :]
        d_hidden_ref, d_mixed_ref, sums_ref = refs[:3]
        d_in = in_ref[...]
        normed, inverse = normal(hidden_ref[...])
        sums_ref[0, 0:1] = jnp.sum(d_in, axis=0, keepdims=True)
        sums_ref[0, 1:2] = jnp.sum(d_in * normed, axis=0, keepdims=True)
        real = (pl.program_id(0) < count_ref[0]).astype(F32)
        grad = cot_ref[...].astype(F32) * real
        d_hidden = grad + normal_back(d_in * (1.0 + piece[0, 4:5, :]), normed, inverse)
        d_hidden_ref[...] = d_hidden
        sums_ref[0, 2:3] = jnp.sum(d_hidden * attn_ref[...], axis=0, keepdims=True)
        d_attn = (piece[0, 2:3, :] * d_hidden).astype(BF)
        d_mixed = None
        for j, (w, out) in enumerate(zip(w_refs, refs[3:])):
            part = d_attn[:, j * columns : (j + 1) * columns]
            out[...] = part
            term = mm(part, w[...], ((1,), (1,)))
            d_mixed = term if d_mixed is None else d_mixed + term
        d_mixed_ref[...] = d_mixed.astype(BF)

    rows = tokens // images
    outs = [(rows, (width,), F32), (rows, (width,), BF), (1, (3, width), F32)]
    outs += [(rows, (columns,), BF)] * blocks
    by_image = [d_mlp_in, hidden_one, attn_out, cotangent, pieces]
    return per_image(kernel, images, by_image, out_b, outs, 40, "middle_back", count)


def block_head_back(d_packed, d_hidden, inputs, pieces, qkv_b, images):
    tokens, width = d_hidden.shape
    blocks = len(qkv_b)

    def kernel(*refs):
        d_refs, (d_hidden_ref, in_ref, piece) = refs[:blocks], refs[blocks : blocks + 3]
        w_refs, (out_ref, sums_ref) = refs[blocks + 3 : -2], refs[-2:]
        d_in = None
        for d, w in zip(d_refs, w_refs):
            term = mm(d[...], w[...], ((1,), (1,)))
            d_in = term if d_in is None else d_in + term
        normed, inverse = normal(in_ref[...].astype(F32))
        sums_ref[0, 0:1] = jnp.sum(d_in, axis=0, keepdims=True)
        sums_ref[0, 1:2] = jnp.sum(d_in * normed, axis=0, keepdims=True)
        back = normal_back(d_in * (1.0 + piece[0, 1:2, :]), normed, inverse)
        out_ref[...] = (d_hidden_ref[...] + back).astype(BF)

    outs = [(tokens // images, (width,), BF), (1, (2, width), F32)]
    by_image = [*d_packed, d_hidden, inputs, pieces]
    return per_image(kernel, images, by_image, qkv_b, outs, 48, "block_head_back")


def grad_stacks(places, a, parts):
    tokens, features = a.shape
    columns = parts[0].shape[1]
    z, count = places.z, len(parts)
    rows = features // (4 * z)
    chunk = chunk_of(columns, 900)
    masks = [places.masks(0), places.masks(1)]
    total = len(masks[0])

    def kernel(at, a_ref, *refs):
        d_refs, (own_ref, send_ref, turned, product) = refs[:count], refs[count:]

        @pl.when(pl.program_id(0) == 0)
        def _():
            turned[...] = a_ref[...].T

        for i, d_ref in enumerate(d_refs):
            whole = mm(turned[...], d_ref[...], ((1,), (0,)))
            for k in range(4 * z):
                product[i, k] = whole[k * rows : (k + 1) * rows].astype(BF)
        core, y, x = at[0], at[1], at[2]
        for out, owner in ((own_ref, core), (send_ref, 1 - core)):
            for j in range(total):
                dy = jnp.where(owner == 0, masks[0][j][0], masks[1][j][0])
                dx = jnp.where(owner == 0, masks[0][j][1], masks[1][j][1])
                for k in range(z):
                    out[j, k] = product[x ^ dx, (k * 2 + (y ^ dy)) * 2 + owner]

    at = jnp.stack([places.at_c, places.at_y, places.x]).astype(jnp.int32)
    shape = (total, z, rows, columns)
    out = pl.BlockSpec((total, z, rows, chunk), lambda i: (0, 0, 0, i))
    return pl.pallas_call(
        kernel,
        grid=(-(-columns // chunk),),
        out_shape=[jax.ShapeDtypeStruct(shape, BF)] * 2,
        in_specs=[pl.BlockSpec(memory_space=pltpu.SMEM), whole_block(a)]
        + [pl.BlockSpec((tokens, chunk), lambda i: (0, i))] * count,
        out_specs=[out, out],
        scratch_shapes=[
            pltpu.VMEM((features, tokens), BF),
            pltpu.VMEM((count, 4 * z, rows, chunk), BF),
        ],
        compiler_params=pltpu.CompilerParams(vmem_limit_bytes=56 * 2**20),
        cost_estimate=SHORT,
        name="grad_stacks",
    )(at, a, *parts)


class Places:
    def __init__(self):
        self.wide, self.narrow = lax.axis_size("wide"), lax.axis_size("narrow")
        self.z = self.wide // 4
        w = lax.axis_index("wide")
        self.w, self.x = w, lax.axis_index("narrow")
        self.at_z, self.at_y, self.at_c = w // 4, (w // 2) % 2, w % 2
        self.z_bits = [1 << i for i in range(self.z.bit_length() - 1)]
        self.x_bits = [1 << i for i in range(self.narrow.bit_length() - 1)]
        x_masks = [(0, bit) for bit in self.x_bits]
        self.orders = ([(1, 0)] + x_masks, x_masks + [(1, 0)])

    def swap(self, value, flip):
        pairs = []
        for w in range(self.wide):
            for x in range(self.narrow):
                dz, dy, dc, dx = flip(w % 2)
                to = (w // 4 ^ dz) * 4 + (w // 2 % 2 ^ dy) * 2 + (w % 2 ^ dc)
                pairs.append((w * self.narrow + x, to * self.narrow + (x ^ dx)))
        return lax.ppermute(value, ALL, pairs)

    def step_flip(self, i):
        return lambda core: (0, self.orders[core][i][0], 0, self.orders[core][i][1])

    def masks(self, core):
        out = [(0, 0)]
        for dy, dx in self.orders[core]:
            out = out + [(y ^ dy, x ^ dx) for y, x in out]
        return out

    def all_bits(self):
        out = [(0, (bit, 0, 0, 0), self.at_z // bit % 2) for bit in self.z_bits]
        out.append((1, (0, 1, 0, 0), self.at_y))
        out += [(3, (0, 0, 0, bit), self.x // bit % 2) for bit in self.x_bits]
        out.append((2, (0, 0, 1, 0), self.at_c))
        return out

    def gather_small(self, value):
        value = value[None, None, None, None]
        for axis, flip, bit in self.all_bits():
            other = self.swap(value, lambda core: flip)
            low = jnp.where(bit == 0, value, other)
            high = jnp.where(bit == 0, other, value)
            value = jnp.concatenate([low, high], axis)
        return value.reshape(self.wide * self.narrow, *value.shape[4:])

    def add_all(self, value):
        for _, flip, _ in self.all_bits():
            value = value + self.swap(value, lambda core: flip)
        return value

    def add_narrow(self, value):
        for bit in self.x_bits:
            value = value + self.swap(value, lambda core: (0, 0, 0, bit))
        return value

    def scatter_chip_row(self, value):
        value = value.reshape(self.z, 2, 2, *value.shape[1:])
        other = self.swap(take(value, 2, 1 - self.at_c), lambda core: (0, 0, 1, 0))
        value = take(value, 2, self.at_c) + other
        other = self.swap(take(value, 1, 1 - self.at_y), lambda core: (0, 1, 0, 0))
        return take(value, 1, self.at_y) + other

    def scatter_z(self, value):
        for bit in reversed(self.z_bits):
            value = value.reshape(2, bit, *value.shape[1:])
            here = self.at_z // bit % 2
            other = self.swap(take(value, 0, 1 - here), lambda core: (bit, 0, 0, 0))
            value = take(value, 0, here) + other
        return value[0]

    def trade_narrow(self, value):
        if self.narrow != 2:
            return lax.all_to_all(value, "narrow", 0, 0, tiled=True)
        other = self.swap(take(value, 0, 1 - self.x), lambda core: (0, 0, 0, 1))
        own = take(value, 0, self.x)
        return jnp.stack([pick([own, other], self.x), pick([other, own], self.x)])


def pick(parts, index):
    if len(parts) == 1:
        return parts[0]
    if len(parts) == 2:
        return jnp.where(index == 0, parts[0], parts[1])
    return lax.dynamic_index_in_dim(jnp.stack(parts), index, 0, keepdims=False)


def take(value, axis, index):
    return lax.dynamic_index_in_dim(value, index, axis, keepdims=False)


def after(value, *before):
    return lax.optimization_barrier((value,) + before)[0]


def assemble(places, parts):
    half, z, rows, columns = parts[0].shape
    joined = columns % 128 == 0
    masks = [places.masks(0), places.masks(1)]

    def kernel(at, s0, s1, t0, t1, out, held, sem, out_sem):
        core, y, x, here_z = at[0], at[1], at[2], at[3]
        copies = []
        for i, src in enumerate((s0, s1, t0, t1)):
            owner = core ^ (i // 2)
            for j in range(half):
                k = j + half * (i % 2)
                dy = jnp.where(owner == 0, masks[0][k][0], masks[1][k][0])
                dx = jnp.where(owner == 0, masks[0][k][1], masks[1][k][1])
                for d in range(z):
                    if joined:
                        lanes = pl.ds(pl.multiple_of((x ^ dx) * columns, 128), columns)
                        to = held.at[here_z ^ d, y ^ dy, owner, :, lanes]
                    else:
                        to = held.at[x ^ dx, here_z ^ d, y ^ dy, owner]
                    copies.append(pltpu.make_async_copy(src.at[j, d], to, sem.at[len(copies)]))
        for copy in copies:
            copy.start()
        for copy in copies:
            copy.wait()
        whole = pltpu.make_async_copy(held, out, out_sem)
        whole.start()
        whole.wait()

    shape = (places.narrow, z, 2, 2, rows, columns)
    if joined:
        shape = (z, 2, 2, rows, places.narrow * columns)
    at = jnp.stack([places.at_c, places.at_y, places.x, places.at_z]).astype(jnp.int32)
    return pl.pallas_call(
        kernel,
        out_shape=jax.ShapeDtypeStruct(shape, BF),
        in_specs=[pl.BlockSpec(memory_space=pltpu.SMEM)] + [pl.BlockSpec(memory_space=pl.ANY)] * 4,
        out_specs=pl.BlockSpec(memory_space=pl.ANY),
        scratch_shapes=[
            pltpu.VMEM(shape, BF),
            pltpu.SemaphoreType.DMA((4 * half * z,)),
            pltpu.SemaphoreType.DMA,
        ],
        compiler_params=pltpu.CompilerParams(vmem_limit_bytes=24 * 2**20),
        cost_estimate=SHORT,
        name="assemble",
    )(at, *parts)


class Slots:
    def __init__(self):
        self.before, self.now = (), []

    def tie(self, value):
        return after(value, *self.before) if self.before else value

    def note(self, *values):
        self.now += values

    def next(self, *values):
        self.note(*values)
        self.before, self.now = tuple(self.now), []


class Gather:
    def __init__(self, places, shard):
        self.places, self.rows = places, places.wide * shard.shape[0]
        self.held, self.other = shard[None], None

    def step_z(self, bit, *before):
        other = self.places.swap(after(self.held, *before), lambda core: (bit, 0, 0, 0))
        self.held = jnp.concatenate([self.held, other], 0)
        if bit == self.places.z_bits[-1]:
            self.held = self.held[None]
        return other

    def all_z(self, *before):
        other = None
        for i, bit in enumerate(self.places.z_bits):
            other = self.step_z(bit, *(before if i == 0 else ()))
        return other

    def step(self, i, *before):
        if self.other is not None:
            self.held = jnp.concatenate([self.held, self.other], 0)
        self.other = self.places.swap(after(self.held, *before), self.places.step_flip(i))
        return self.other

    def first(self, *before):
        for i in range(len(self.places.orders[0]) - 1):
            other = self.step(i, *(before if i == 0 else ()))
        return other

    def last(self, *before):
        return self.step(len(self.places.orders[0]) - 1, *before)

    def cores(self, *before):
        parts = after((self.held, self.other), *before)
        parts = list(parts)
        self.parts = parts + [self.places.swap(p, lambda core: (0, 0, 1, 0)) for p in parts]
        return self.parts[2:]

    def whole(self, *before):
        whole = assemble(self.places, after(tuple(self.parts), *before))
        return list(whole.reshape(-1, self.rows, whole.shape[-1]))


class Scatter:
    def __init__(self, places, a, parts):
        self.places = places
        self.stack, self.to_core = grad_stacks(places, a, parts)
        self.half = self.stack.shape[0]

    def cores(self, *before):
        self.arrived = self.places.swap(after(self.to_core, *before), lambda core: (0, 0, 1, 0))
        return self.arrived

    def first(self, *before):
        places, arrived = self.places, self.arrived
        self.half = half = self.half // 2
        send = self.stack[half:].astype(F32) + arrived[half:].astype(F32)
        flip = places.step_flip(len(places.orders[0]) - 1)
        self.other = places.swap(after(send.astype(BF), *before), flip)
        self.own = self.stack[:half].astype(F32) + arrived[:half].astype(F32)
        return self.other

    def last(self, *before):
        places = self.places
        for i in reversed(range(len(places.orders[0]) - 1)):
            held = self.own + self.other.astype(F32)
            self.half = half = self.half // 2
            send = after(held[half:].astype(BF), *before)
            self.own, self.other = held[:half], places.swap(send, places.step_flip(i))
        return self.other

    def step_z(self, bit, *before):
        places = self.places
        held = self.own + self.other.astype(F32)
        if bit == places.z_bits[-1]:
            held = held[0]
            held = jnp.stack([take(held, 0, places.at_z ^ d) for d in range(places.z)])
        send = after(held[bit:].astype(BF), *before)
        self.own, self.other = held[:bit], places.swap(send, lambda core: (bit, 0, 0, 0))
        return self.other

    def all_z(self, *before):
        for i, bit in enumerate(reversed(self.places.z_bits)):
            other = self.step_z(bit, *(before if i == 0 else ()))
        return other

    def result(self):
        return (self.own + self.other.astype(F32))[0]


def dot(a, b, dims, out=F32):
    return lax.dot_general(a, b, (dims, ((), ())), preferred_element_type=F32).astype(out)


def split(a, count):
    width = a.shape[1] // count
    return [a[:, n * width : (n + 1) * width] for n in range(count)]


def on_device(
    inputs,
    cotangent,
    class_ids,
    step_ids,
    image_counts,
    w_qkv,
    w_out,
    w_gate,
    w_up,
    w_down,
    ada_weight,
    ada_bias,
    class_table,
    norm_gains,
):
    places = Places()
    wide, narrow, at_w, at_n = places.wide, places.narrow, places.w, places.x
    images, length, width = inputs.shape
    tables, sums = head_tables(length), head_sums()
    gains = jnp.tile(norm_gains, (1, H))
    local_count = image_counts[0]

    tokens = images * length

    def flat(v):
        return v.reshape(tokens, -1)

    def deep(v):
        return v.reshape(images, length, -1)

    t = Slots()
    z_low, z_high = places.z_bits[0], places.z_bits[1:]
    qkv, out, gate, up, down = [
        Gather(places, shard) for shard in (w_qkv, w_out, w_gate, w_up, w_down)
    ]

    def high_z(weight):
        for i, bit in enumerate(z_high):
            other = weight.step_z(bit, *(t.before if i == 0 else ()))
        return other

    def high_sum(grad):
        for i, bit in enumerate(reversed(z_high)):
            other = grad.step_z(bit, *(t.before if i == 0 else ()))
        return other

    small = [class_ids, step_ids, image_counts, ada_bias]
    small = jnp.concatenate([v.astype(F32) for v in small])[None]
    small = places.gather_small(small)[:, 0]
    t.next(qkv.step_z(z_low), small)

    ids = small[:, : 2 * images].reshape(-1, 2, images).transpose(0, 2, 1).reshape(-1, 2)
    ids = t.tie(ids).astype(jnp.int32)
    real_count = jnp.sum(small[:, 2 * images])
    bias = small[:, 2 * images + 1 :].reshape(-1)
    rows_here, cols_here = class_table.shape
    class_hot = ids[:, :1] - at_n * rows_here == jnp.arange(rows_here, dtype=jnp.int32)[None, :]
    picked = dot(class_hot.astype(BF), class_table, ((1,), (0,)))
    column = at_w * cols_here + jnp.arange(cols_here, dtype=jnp.int32)
    half_width = width // 2
    frequency = jnp.exp(-math.log(10000.0) * (column % half_width).astype(F32) / half_width)
    angles = ids[:, 1:].astype(F32) * frequency[None, :]
    wave = jnp.where(column[None, :] < half_width, jnp.cos(angles), jnp.sin(angles))
    condition = places.add_narrow(picked) + wave
    cond_act = jax.nn.silu(condition).astype(BF)
    mod_part = dot(cond_act, ada_weight, ((1,), (0,)))
    mod_part = places.scatter_chip_row(mod_part.reshape(wide, narrow, images, -1))
    t.next(high_z(qkv), mod_part)

    mod_part = places.trade_narrow(places.scatter_z(t.tie(mod_part)))
    modulation = mod_part.transpose(1, 0, 2).reshape(images, -1) + bias
    t.next(qkv.first(*t.before), out.all_z(*t.before), modulation)

    pieces = t.tie(modulation).reshape(images, 6, width)
    normed, _ = layer_norm(inputs.astype(F32))
    attn_in = flat((normed * (1.0 + pieces[:, 1:2]) + pieces[:, 0:1]).astype(BF))
    t.next(qkv.last(*t.before), gate.all_z(*t.before), attn_in, *tables, sums)

    t.note(*qkv.cores(*t.before))
    t.next(out.first(*t.before), gate.first(*t.before), up.step_z(z_low, *t.before))

    qkv_b = qkv.whole(*t.before)
    packed = project(attn_in, qkv_b)
    t.next(out.last(*t.before), gate.last(*t.before), high_z(up), *packed)

    t.note(*out.cores(*t.before), *gate.cores(*t.before))
    packed = t.tie(packed)
    queries, key_rows, value_rows, mixed = attention_forward(packed, gains, tables, sums, images)
    t.next(up.first(*t.before), down.step_z(z_low, *t.before), mixed)

    out_b = out.whole(*t.before)
    attn_out, hidden_one, mlp_in = attention_tail(mixed, out_b, flat(inputs), pieces, images)
    t.next(up.last(*t.before), high_z(down), mlp_in)

    t.note(*up.cores(*t.before))
    (gate_b,) = gate.whole(*t.before)
    t.next(down.first(*t.before), gate_b)

    (up_b,) = up.whole(*t.before)
    gate_val, up_val, hidden_mid = gated(mlp_in, gate_b, up_b)
    slot_real = (jnp.arange(images, dtype=jnp.int32) < local_count).astype(F32)
    grad_y = cotangent.astype(F32) * slot_real[:, None, None]
    d_mlp = flat((pieces[:, 5:6] * grad_y).astype(BF))
    t.next(down.last(*t.before), hidden_mid)

    t.note(*down.cores(*t.before))
    g_down = Scatter(places, t.tie(hidden_mid), split(d_mlp, narrow))
    t.next(g_down.cores())

    g_down_1 = g_down.first(*t.before)
    down_b = down.whole(*t.before)
    d_gate, d_up, d_mlp_in = gated_back(
        split(d_mlp, narrow), down_b, gate_val, up_val, gate_b, up_b
    )
    t.next(g_down_1, d_mlp_in)

    g_down_2 = g_down.last(*t.before)
    g_gate = Scatter(places, mlp_in, split(t.tie(d_gate), narrow))
    t.next(g_down_2, g_gate.cores())

    g_gate_1 = g_gate.first(*t.before)
    t.note(g_gate_1, high_sum(g_down))
    g_up = Scatter(places, mlp_in, split(t.tie(d_up), narrow))
    t.note(g_up.cores())
    d_hidden, d_mixed, sums_b, *d_attn = middle_back(
        t.tie(d_mlp_in), hidden_one, attn_out, flat(cotangent), pieces, out_b, image_counts, images
    )
    g_out = Scatter(places, mixed, d_attn)
    t.note(g_out.cores())
    t.next(d_mixed)

    t.note(g_up.first(*t.before), g_gate.last(*t.before), g_down.step_z(z_low, *t.before))
    d_packed, gain_terms = attention_backward(
        packed, queries, key_rows, value_rows, t.tie(d_mixed), gains, tables, sums, images
    )
    t.next(*d_packed)

    t.note(g_up.last(*t.before), g_out.first(*t.before), high_sum(g_gate))
    g_qkv = Scatter(places, attn_in, t.tie(d_packed))
    grad_gains = gain_terms.sum(0).reshape(2, H, HD).sum(1)
    t.next(g_qkv.cores())

    t.note(g_qkv.first(*t.before), g_out.last(*t.before), high_sum(g_up))
    t.note(g_gate.step_z(z_low, *t.before))
    d_tokens, sums_a = block_head_back(
        t.tie(d_packed), d_hidden, flat(inputs), pieces, qkv_b, images
    )
    block_output, sums_gate = block_tail(
        t.tie(hidden_mid), down_b, hidden_one, flat(cotangent), pieces, image_counts, images
    )
    d_modulation = jnp.concatenate([sums_a, sums_b[:, 2:], sums_b[:, :2], sums_gate], axis=1)
    d_modulation = d_modulation.astype(BF).reshape(images, -1)
    t.next(d_modulation, d_tokens, block_output)

    t.note(high_sum(g_out), g_up.step_z(z_low, *t.before))
    gain_sum = places.add_all(t.tie(grad_gains))
    t.next(g_qkv.last(*t.before))

    t.note(high_sum(g_qkv), g_out.step_z(z_low, *t.before))
    d_mod = places.gather_small(t.tie(d_modulation)).reshape(-1, d_modulation.shape[1])
    g_qkv.step_z(z_low)
    r_qkv, r_out, r_gate, r_up, r_down = [
        g.result() for g in (g_qkv, g_out, g_gate, g_up, g_down)
    ]

    ada_cols = ada_weight.shape[1]
    d_mod_here = lax.dynamic_slice_in_dim(d_mod, at_n * ada_cols, ada_cols, 1)
    g_ada = dot(cond_act, d_mod_here, ((0,), (0,)))
    bias_cols = ada_bias.shape[0]
    bias_at = (at_w * narrow + at_n) * bias_cols
    g_bias = jnp.sum(lax.dynamic_slice_in_dim(d_mod, bias_at, bias_cols, 1).astype(F32), axis=0)
    d_cond_act = places.add_narrow(dot(d_mod_here, ada_weight, ((1,), (1,))))
    cond_sigmoid = jax.nn.sigmoid(condition)
    d_condition = d_cond_act * cond_sigmoid * (1.0 + condition * (1.0 - cond_sigmoid))
    g_table = jnp.dot(class_hot.astype(F32).T, d_condition, precision=HIGHEST)
    return (
        deep(block_output),
        deep(d_tokens),
        r_qkv / real_count,
        r_out / real_count,
        r_gate / real_count,
        r_up / real_count,
        r_down / real_count,
        g_ada / real_count,
        g_bias / real_count,
        g_table / real_count,
        gain_sum / real_count,
    )


def solution(mesh):
    split = P("wide", "narrow")
    images = P(ALL, None, None)
    return jax.shard_map(
        on_device,
        mesh=mesh,
        in_specs=(
            images,
            images,
            P(ALL),
            P(ALL),
            P(ALL),
            split,
            split,
            split,
            split,
            split,
            split,
            P(ALL),
            P("narrow", "wide"),
            P(),
        ),
        out_specs=(
            images,
            images,
            split,
            split,
            split,
            split,
            split,
            split,
            P(ALL),
            P("narrow", "wide"),
            P(),
        ),
        check_vma=False,
    )
```

time: 867 us -> 649 us (0.75)
  matrix products: 171 us -> 5.32 us
  Pallas kernels: 33.6 us -> 193 us
  waiting for transfers between devices: 331 us -> 242 us
  other arithmetic: 156 us -> 72.7 us
  local copies, waits for them, and re-layouts: 98.8 us -> 63.1 us
    pallas_call x0 -> x14, Pallas kernels: none -> 166 us  [the longest x5 43.3 us: grad_stacks(): pl.pallas_call(kernel, grid=(-(-columns // chunk),), out_shape=[jax.Shape...]
    dot_general x34 -> x4, matrix products: 116 us -> 3.57 us  [dot(): lax.dot_general(a, b, (dims, ((), ())), preferred_element_type=F32)]
    ppermute x76 -> x77, waiting for transfers between devices: 331 us -> 242 us  [swap(): return lax.ppermute(value, ALL, pairs)]
    dot_general x5 -> x0, matrix products: 45.5 us -> none  [the longest x1 16.6 us: on_device(): jnp.einsum('bhst,bthe->bshe', d_scores, key_rows, preferred_element_type=...]
    select_n x8 -> x1, other arithmetic: 36.6 us -> 0.97 us  [head_tables(): below = jnp.where(first[None, :], 0.0, sine)]
    convert_element_type x9 -> x0, local copies, waits for them, and re-layouts: 31.3 us -> none  [the longest x6 29.9 us: dot(): lax.dot_general(a, b, (dims, ((), ())), preferred_element_type=F32)]
    reshape x5 -> x3, local copies, waits for them, and re-layouts: 23.7 us -> 0.24 us  [the longest x1 0.11 us: on_device(): small[:, :2 * images].reshape(-1, 2, images).transpose(0, 2, 1)]
    reduce_sum x6 -> x2, other arithmetic: 15.5 us -> 0.04 us  [on_device(): grad_gains = gain_terms.sum(0).reshape(2, H, HD).sum(1)]
  transfers between devices with their start and end apart: 77 -> 77, of which waited for: 38 -> 41; matrix products, arithmetic and copies ran while one was open for 28% -> 14% of each run, Pallas kernels for 3% -> 24%
where the time goes in v2:
time: 649 us; the launch traced here: 645 us
  waiting for transfers between devices  242 us (37%)
  Pallas kernels  193 us (30%)
  other arithmetic  72.7 us (11%)
  starting transfers between devices  64.9 us (10%)
  local copies, waits for them, and re-layouts  63.1 us (10%)
    ppermute x77, waiting for transfers between devices, swap(): return lax.ppermute(value, ALL, pairs)  242 us
    ppermute x77, starting transfers between devices, swap(): return lax.ppermute(value, ALL, pairs)  64.9 us
    pallas_call x5, Pallas kernels, grad_stacks(): pl.pallas_call(kernel, grid=(-(-columns // chunk),), out_shape=[jax.Shape...  43.3 us
    pallas_call x1, Pallas kernels, attention_backward(): pl.pallas_call(kernel, grid=(images,), out_shape=[jax.ShapeDtypeStruct((t...  34.3 us
    unnamed x200, local copies, waits for them, and re-layouts  30.5 us
    pallas_call x4, Pallas kernels, per_image(): pl.pallas_call(kernel, grid=(images,), out_shape=[jax.ShapeDtypeStruct((i...  28.3 us
    pallas_call x5, Pallas kernels, assemble(): pl.pallas_call(kernel, out_shape=jax.ShapeDtypeStruct(shape, BF), in_spec...  27.1 us
    pallas_call x1, Pallas kernels, gated_back(): pl.pallas_call(kernel, grid=(columns // chunk,), out_shape=[jax.ShapeDtyp...  22.7 us
  transfers between devices with their start and end apart: 77, of which 41 were waited for; matrix products, arithmetic and copies ran while one was open for 14% of the time, Pallas kernels for 24%

profile of v2, /device:TPU:0, one launch (start us, length us, event | category | flops | bytes accessed | tf_op | source)
XLA Modules:
  0.0 644.8 jit_solution(16866563624593369493)
XLA Ops:
  40.3 19.7 %collective-permute-done.9 = bf16[2,72,1728]{2,1,0:T(8,128)(2,1)S(1)} collective-permute-done((bf16[2,72,1728]{2,1,0:T(8,128)(2,1)S(1)}, bf16[2,72,1728]{2,1,0:T(8,128)(2,1)S(1)}, u32[]{:S(2)}, u32[]{:S(2)}) %collective-permute-start.9) | collective-permute-done | bytes 497696 | tf_op jit(solution)/shard_map/ppermute | solution.py:512
  77.9 8.0 %collective-permute-done.13 = bf16[1,4,72,1728]{3,2,1,0:T(8,128)(2,1)S(1)} collective-permute-done((bf16[1,4,72,1728]{3,2,1,0:T(8,128)(2,1)S(1)}, bf16[1,4,72,1728]{3,2,1,0:T(8,128)(2,1)S(1)}, u32[]{:S(2)}, u32[]{:S(2)}) %collective-permute-start.13) | collective-permute-done | bytes 995360 | tf_op jit(solution)/shard_map/ppermute | solution.py:512
  98.3 14.7 %collective-permute-done.18 = bf16[2,72,1536]{2,1,0:T(8,128)(2,1)S(1)} collective-permute-done((bf16[2,72,1536]{2,1,0:T(8,128)(2,1)S(1)}, bf16[2,72,1536]{2,1,0:T(8,128)(2,1)S(1)}, u32[]{:S(2)}, u32[]{:S(2)}) %collective-permute-start.18) | collective-permute-done | bytes 442400 | tf_op jit(solution)/shard_map/ppermute | solution.py:512
  119.0 10.5 %collective-permute-done.22 = bf16[1,4,72,1536]{3,2,1,0:T(8,128)(2,1)S(1)} collective-permute-done((bf16[1,4,72,1536]{3,2,1,0:T(8,128)(2,1)S(1)}, bf16[1,4,72,1536]{3,2,1,0:T(8,128)(2,1)S(1)}, u32[]{:S(2)}, u32[]{:S(2)}) %collective-permute-start.22) | collective-permute-done | bytes 884768 | tf_op jit(solution)/shard_map/ppermute | solution.py:512
  136.7 7.6 %assemble.5 = bf16[2,4,2,2,72,1728]{5,4,3,2,1,0:T(8,128)(2,1)S(1)} custom-call(s32[4]{0:T(128)S(1)} %pad_add_fusion.at, bf16[2,4,72,1728]{3,2,1,0:T(8,128)(2,1)} %pad_maximum_fusion.s0, bf16[2,4,72,1728]{3,2,1,0:T(8,128)(2,1)} %collective-permute-done.16.s1, bf16[2,4,72,1728]{3,2,1,0:T(8,128)(2,1)S(1)} %collective-permute-done.19.t0, ...), custom_call_target="tpu_custom_call" | custom-call | flops 1000000 | bytes 1000000 | tf_op jit(solution)/shard_map/assemble/pallas_call | solution.py:621
  146.5 9.9 %project.1 = (f32[512,1728]{1,0:T(8,128)S(1)}, f32[512,1728]{1,0:T(8,128)S(1)}) custom-call(bf16[512,1152]{1,0:T(8,128)(2,1)S(1)} %bitcast.156, bf16[1152,1728]{1,0:T(8,128)(2,1)S(1)} %bitcast.146, bf16[1152,1728]{1,0:T(8,128)(2,1)} %bitcast.160), custom_call_target="tpu_custom_call" | custom-call | flops 1000000 | bytes 1000000 | tf_op jit(solution)/shard_map/project/pallas_call | solution.py:236
  173.6 14.1 %attention_forward.1 = (bf16[512,1152]{1,0:T(8,128)(2,1)S(1)}, bf16[512,1152]{1,0:T(8,128)(2,1)S(1)}, bf16[512,1152]{1,0:T(8,128)(2,1)S(1)}, bf16[512,1152]{1,0:T(8,128)(2,1)S(1)}) custom-call(f32[512,1728]{1,0:T(8,128)} %copy-done.6, f32[512,1728]{1,0:T(8,128)} %copy-done.7, f32[2,1152]{1,0:T(2,128)S(1)} %tile.43.refs_2_.refs_6_, ...), custom_call_target="tpu_custom_call" | custom-call | flops 1000000 | bytes 1000000 | tf_op jit(solution)/shard_map/attention_forward/pallas_call | solution.py:140
  210.6 12.1 %collective-permute-done.34 = bf16[2,192,576]{2,1,0:T(8,128)(2,1)S(1)} collective-permute-done((bf16[2,192,576]{2,1,0:T(8,128)(2,1)S(1)}, bf16[2,192,576]{2,1,0:T(8,128)(2,1)S(1)}, u32[]{:S(2)}, u32[]{:S(2)}) %collective-permute-start.34) | collective-permute-done | bytes 442400 | tf_op jit(solution)/shard_map/ppermute | solution.py:512
  245.9 13.5 %gated.1 = (f32[512,3072]{1,0:T(8,128)S(1)}, f32[512,3072]{1,0:T(8,128)}, bf16[512,3072]{1,0:T(8,128)(2,1)S(1)}) custom-call(bf16[512,1152]{1,0:T(8,128)(2,1)S(1)} %get-tuple-element.166.a_ref, bf16[1152,3072]{1,0:T(8,128)(2,1)} %bitcast.142, bf16[1152,3072]{1,0:T(8,128)(2,1)} %bitcast.144), custom_call_target="tpu_custom_call" | custom-call | flops 1000000 | bytes 1000000 | tf_op jit(solution)/shard_map/gated/pallas_call | solution.py:262
  263.8 10.7 %grad_stacks.5 = (bf16[4,4,192,576]{3,2,1,0:T(8,128)(2,1)}, bf16[4,4,192,576]{3,2,1,0:T(8,128)(2,1)}) custom-call(s32[3]{0:T(128)} %pad_add_fusion.1.at, bf16[512,3072]{1,0:T(8,128)(2,1)} %copy-done.8, bf16[512,576]{1,0:T(8,128)(2,1)} %get-tuple-element.278.refs_0_, bf16[512,576]{1,0:T(8,128)(2,1)} %get-tuple-element.277.refs_1_), custom_call_target="tpu_custom_call" | custom-call | flops 1000000 | bytes 1000000 | tf_op jit(solution)/shard_map/grad_stacks/pallas_call | solution.py:476
  289.0 9.6 %assemble.9 = bf16[2,4,2,2,192,576]{5,4,3,2,1,0:T(8,128)(2,1)S(1)} custom-call(s32[4]{0:T(128)S(1)} %pad_add_fusion.at, bf16[2,4,192,576]{3,2,1,0:T(8,128)(2,1)S(1)} %copy-done.18, bf16[2,4,192,576]{3,2,1,0:T(8,128)(2,1)} %collective-permute-done.38.s1, bf16[2,4,192,576]{3,2,1,0:T(8,128)(2,1)S(1)} %collective-permute-done.39.t0, ...), custom_call_target="tpu_custom_call" | custom-call | flops 1000000 | bytes 1000000 | tf_op jit(solution)/shard_map/assemble/pallas_call | solution.py:621
  302.1 22.7 %gated_back.1 = (bf16[512,3072]{1,0:T(8,128)(2,1)}, bf16[512,3072]{1,0:T(8,128)(2,1)}, f32[512,1152]{1,0:T(8,128)S(1)}) custom-call(bf16[512,576]{1,0:T(8,128)(2,1)S(1)} %copy-done.23, bf16[512,576]{1,0:T(8,128)(2,1)S(1)} %copy-done.22, bf16[3072,576]{1,0:T(8,128)(2,1)} %bitcast.148, bf16[3072,576]{1,0:T(8,128)(2,1)} %bitcast.162, f32[512,3072]{1,0:T(8,128)} %copy-done.21, ...), custom_call_target="tpu_custom_call" | custom-call | flops 1000000 | bytes 1000000 | tf_op jit(solution)/shard_map/gated_back/pallas_call | solution.py:305
  330.1 8.7 %grad_stacks.6 = (bf16[4,4,72,1536]{3,2,1,0:T(8,128)(2,1)}, bf16[4,4,72,1536]{3,2,1,0:T(8,128)(2,1)}) custom-call(s32[3]{0:T(128)} %pad_add_fusion.1.at, bf16[512,1152]{1,0:T(8,128)(2,1)} %copy-done.13, bf16[512,1536]{1,0:T(8,128)(2,1)} %get-tuple-element.258.refs_0_, bf16[512,1536]{1,0:T(8,128)(2,1)} %get-tuple-element.257.refs_1_), custom_call_target="tpu_custom_call" | custom-call | flops 1000000 | bytes 1000000 | tf_op jit(solution)/shard_map/grad_stacks/pallas_call | solution.py:476
  344.9 13.8 %collective-permute-done.43 = bf16[1,4,192,576]{3,2,1,0:T(8,128)(2,1)S(1)} collective-permute-done((bf16[1,4,192,576]{3,2,1,0:T(8,128)(2,1)S(1)}, bf16[1,4,192,576]{3,2,1,0:T(8,128)(2,1)S(1)}, u32[]{:S(2)}, u32[]{:S(2)}) %collective-permute-start.43) | collective-permute-done | bytes 884768 | tf_op jit(solution)/shard_map/ppermute | solution.py:512
  361.8 8.4 %grad_stacks.7 = (bf16[4,4,72,1536]{3,2,1,0:T(8,128)(2,1)}, bf16[4,4,72,1536]{3,2,1,0:T(8,128)(2,1)}) custom-call(s32[3]{0:T(128)} %pad_add_fusion.1.at, bf16[512,1152]{1,0:T(8,128)(2,1)} %copy-done.13, bf16[512,1536]{1,0:T(8,128)(2,1)} %get-tuple-element.256.refs_0_, bf16[512,1536]{1,0:T(8,128)(2,1)} %get-tuple-element.255.refs_1_), custom_call_target="tpu_custom_call" | custom-call | flops 1000000 | bytes 1000000 | tf_op jit(solution)/shard_map/grad_stacks/pallas_call | solution.py:476
  397.3 20.8 %collective-permute-done.47 = bf16[2,192,576]{2,1,0:T(8,128)(2,1)S(1)} collective-permute-done((bf16[2,192,576]{2,1,0:T(8,128)(2,1)S(1)}, bf16[2,192,576]{2,1,0:T(8,128)(2,1)S(1)}, u32[]{:S(2)}, u32[]{:S(2)}) %collective-permute-start.47) | collective-permute-done | bytes 442400 | tf_op jit(solution)/shard_map/ppermute | solution.py:512
  429.0 34.3 %attention_backward.1 = (bf16[512,1728]{1,0:T(8,128)(2,1)}, bf16[512,1728]{1,0:T(8,128)(2,1)}, f32[2,2,1152]{2,1,0:T(2,128)}) custom-call(f32[512,1728]{1,0:T(8,128)} %copy-done.6, f32[512,1728]{1,0:T(8,128)} %copy-done.7, bf16[512,1152]{1,0:T(8,128)(2,1)} %copy-done.30, bf16[512,1152]{1,0:T(8,128)(2,1)} %copy-done.31, bf16[512,1152]{1,0:T(8,128)(2,1)} %copy-done.32, ...), custom_call_target="tpu_custom_call" | custom-call | flops 1000000 | bytes 1000000 | tf_op jit(solution)/shard_map/attention_backward/pallas_call | solution.py:202
  463.4 10.1 %grad_stacks.9 = (bf16[4,4,72,1728]{3,2,1,0:T(8,128)(2,1)}, bf16[4,4,72,1728]{3,2,1,0:T(8,128)(2,1)}) custom-call(s32[3]{0:T(128)} %pad_add_fusion.1.at, bf16[512,1152]{1,0:T(8,128)(2,1)} %bitcast.157, bf16[512,1728]{1,0:T(8,128)(2,1)} %get-tuple-element.231.refs_0_, bf16[512,1728]{1,0:T(8,128)(2,1)} %get-tuple-element.232.refs_1_), custom_call_target="tpu_custom_call" | custom-call | flops 1000000 | bytes 1000000 | tf_op jit(solution)/shard_map/grad_stacks/pallas_call | solution.py:476
  488.5 16.0 %collective-permute-done.54 = bf16[2,72,1536]{2,1,0:T(8,128)(2,1)S(1)} collective-permute-done((bf16[2,72,1536]{2,1,0:T(8,128)(2,1)S(1)}, bf16[2,72,1536]{2,1,0:T(8,128)(2,1)S(1)}, u32[]{:S(2)}, u32[]{:S(2)}) %collective-permute-start.54) | collective-permute-done | bytes 442400 | tf_op jit(solution)/shard_map/ppermute | solution.py:512
  515.4 10.7 %block_head_back.1 = (bf16[512,1152]{1,0:T(8,128)(2,1)}, f32[2,2,1152]{2,1,0:T(2,128)S(1)}) custom-call(bf16[512,1728]{1,0:T(8,128)(2,1)S(1)} %copy-done.19, bf16[512,1728]{1,0:T(8,128)(2,1)S(1)} %copy-done.20, f32[512,1152]{1,0:T(8,128)} %copy-done.26, bf16[512,1152]{1,0:T(8,128)(2,1)S(1)} %bitcast.151, f32[2,6,1152]{2,1,0:T(8,128)S(1)} %reshape.383.piece.refs_4_, ...), custom_call_target="tpu_custom_call" | custom-call | flops 1000000 | bytes 1000000 | tf_op jit(solution)/shard_map/block_head_back/pallas_call | solution.py:343
  527.9 8.8 %block_tail.1 = (bf16[512,1152]{1,0:T(8,128)(2,1)}, f32[2,1,1152]{2,1,0:T(1,128)S(1)}) custom-call(bf16[512,3072]{1,0:T(8,128)(2,1)S(1)} %copy-done.9, f32[512,1152]{1,0:T(8,128)S(1)} %copy-done.16, bf16[512,1152]{1,0:T(8,128)(2,1)S(1)} %bitcast.159, f32[2,6,1152]{2,1,0:T(8,128)S(1)} %reshape.383.piece.refs_4_, bf16[3072,576]{1,0:T(8,128)(2,1)S(1)} %bitcast.149, ...), custom_call_target="tpu_custom_call" | custom-call | flops 1000000 | bytes 1000000 | tf_op jit(solution)/shard_map/block_tail/pallas_call | solution.py:343
  539.6 7.9 %collective-permute-done.59 = bf16[1,72,1536]{2,1,0:T(8,128)(2,1)S(1)} collective-permute-done((bf16[1,72,1536]{2,1,0:T(8,128)(2,1)S(1)}, bf16[1,72,1536]{2,1,0:T(8,128)(2,1)S(1)}, u32[]{:S(2)}, u32[]{:S(2)}) %collective-permute-start.59) | collective-permute-done | bytes 221216 | tf_op jit(solution)/shard_map/ppermute | solution.py:512
  549.1 10.1 %collective-permute-done.58 = bf16[2,72,1536]{2,1,0:T(8,128)(2,1)S(1)} collective-permute-done((bf16[2,72,1536]{2,1,0:T(8,128)(2,1)S(1)}, bf16[2,72,1536]{2,1,0:T(8,128)(2,1)S(1)}, u32[]{:S(2)}, u32[]{:S(2)}) %collective-permute-start.58) | collective-permute-done | bytes 442400 | tf_op jit(solution)/shard_map/ppermute | solution.py:512
  611.8 12.0 %collective-permute-done.63 = bf16[2,72,1728]{2,1,0:T(8,128)(2,1)S(1)} collective-permute-done((bf16[2,72,1728]{2,1,0:T(8,128)(2,1)S(1)}, bf16[2,72,1728]{2,1,0:T(8,128)(2,1)S(1)}, u32[]{:S(2)}, u32[]{:S(2)}) %collective-permute-start.63) | collective-permute-done | bytes 497696 | tf_op jit(solution)/shard_map/ppermute | solution.py:512
  (522 shorter events, 326.3 us)
Async XLA Ops:
  34.5 25.6 %collective-permute-start.9 = (bf16[2,72,1728]{2,1,0:T(8,128)(2,1)S(1)}, bf16[2,72,1728]{2,1,0:T(8,128)(2,1)S(1)}, u32[]{:S(2)}, u32[]{:S(2)}) collective-permute-start(bf16[2,72,1728]{2,1,0:T(8,128)(2,1)S(1)} %pad_maximum_fusion.6), channel_id=1, source_target_pairs={{0,16},{1,17},{2,18},{3,19},{4,20},{5,21},{6,22},{7,23},{8,24},{9,... | collective-permute-start | bytes 1493000 | tf_op jit(solution)/shard_map/ppermute | solution.py:512
  87.4 26.1 %collective-permute-start.16 = (bf16[2,4,72,1728]{3,2,1,0:T(8,128)(2,1)}, bf16[2,4,72,1728]{3,2,1,0:T(8,128)(2,1)}, u32[]{:S(2)}, u32[]{:S(2)}) collective-permute-start(bf16[2,4,72,1728]{3,2,1,0:T(8,128)(2,1)} %pad_maximum_fusion.s0), channel_id=1, source_target_pairs={{0,1},{1,0},{2,6},{3,7},{4,5},{5,4},{6,2},{7,3},{8,9},{9,8},{10,14... | collective-permute-start | bytes 5971976 | tf_op jit(solution)/shard_map/ppermute | solution.py:512
  133.5 30.7 %collective-permute-start.25 = (bf16[2,4,72,1536]{3,2,1,0:T(8,128)(2,1)}, bf16[2,4,72,1536]{3,2,1,0:T(8,128)(2,1)}, u32[]{:S(2)}, u32[]{:S(2)}) collective-permute-start(bf16[2,4,72,1536]{3,2,1,0:T(8,128)(2,1)} %pad_maximum_fusion.2.s0), channel_id=1, source_target_pairs={{0,1},{1,0},{2,6},{3,7},{4,5},{5,4},{6,2},{7,3},{8,9},{9,8},{10,14... | collective-permute-start | bytes 5308424 | tf_op jit(solution)/shard_map/ppermute | solution.py:512
  136.1 24.0 %collective-permute-start.26 = (bf16[2,72,1536]{2,1,0:T(8,128)(2,1)S(1)}, bf16[2,72,1536]{2,1,0:T(8,128)(2,1)S(1)}, u32[]{:S(2)}, u32[]{:S(2)}) collective-permute-start(bf16[2,72,1536]{2,1,0:T(8,128)(2,1)S(1)} %pad_maximum_fusion.11), channel_id=1, source_target_pairs={{0,16},{1,17},{2,18},{3,19},{4,20},{5,21},{6,22},{7,23},{8,24},{9,... | collective-permute-start | bytes 1327112 | tf_op jit(solution)/shard_map/ppermute | solution.py:512
  136.1 28.1 %collective-permute-start.24 = (bf16[2,4,72,576]{3,2,1,0:T(8,128)(2,1)}, bf16[2,4,72,576]{3,2,1,0:T(8,128)(2,1)}, u32[]{:S(2)}, u32[]{:S(2)}) collective-permute-start(bf16[2,4,72,576]{3,2,1,0:T(8,128)(2,1)} %pad_maximum_fusion.5.s0), channel_id=1, source_target_pairs={{0,1},{1,0},{2,6},{3,7},{4,5},{5,4},{6,2},{7,3},{8,9},{9,8},{10,14... | collective-permute-start | bytes 1990664 | tf_op jit(solution)/shard_map/ppermute | solution.py:512
  164.2 32.6 %collective-permute-start.29 = (bf16[2,4,72,1536]{3,2,1,0:T(8,128)(2,1)}, bf16[2,4,72,1536]{3,2,1,0:T(8,128)(2,1)}, u32[]{:S(2)}, u32[]{:S(2)}) collective-permute-start(bf16[2,4,72,1536]{3,2,1,0:T(8,128)(2,1)} %pad_maximum_fusion.2.s0), channel_id=1, source_target_pairs={{0,2},{1,3},{2,0},{3,1},{4,6},{5,7},{6,4},{7,5},{8,10},{9,11},{10,... | collective-permute-start | bytes 5308424 | tf_op jit(solution)/shard_map/ppermute | solution.py:512
  164.2 32.6 %collective-permute-start.30 = (bf16[2,4,72,1536]{3,2,1,0:T(8,128)(2,1)}, bf16[2,4,72,1536]{3,2,1,0:T(8,128)(2,1)}, u32[]{:S(2)}, u32[]{:S(2)}) collective-permute-start(bf16[2,4,72,1536]{3,2,1,0:T(8,128)(2,1)} %collective-permute-done.25.s1), channel_id=1, source_target_pairs={{0,2},{1,3},{2,0},{3,1},{4,6},{5,7},{6,4},{7,5},{8,10},{9,11},{10,... | collective-permute-start | bytes 5308424 | tf_op jit(solution)/shard_map/ppermute | solution.py:512
  165.7 23.1 %collective-permute-start.31 = (bf16[1,4,72,1536]{3,2,1,0:T(8,128)(2,1)}, bf16[1,4,72,1536]{3,2,1,0:T(8,128)(2,1)}, u32[]{:S(2)}, u32[]{:S(2)}) collective-permute-start(bf16[1,4,72,1536]{3,2,1,0:T(8,128)(2,1)} %maximum_bitcast_fusion.3), channel_id=1, source_target_pairs={{0,4},{1,5},{2,3},{3,2},{4,0},{5,1},{6,7},{7,6},{8,12},{9,13},{10,... | collective-permute-start | bytes 2654216 | tf_op jit(solution)/shard_map/ppermute | solution.py:512
  167.2 29.6 %collective-permute-start.27 = (bf16[2,4,72,576]{3,2,1,0:T(8,128)(2,1)}, bf16[2,4,72,576]{3,2,1,0:T(8,128)(2,1)}, u32[]{:S(2)}, u32[]{:S(2)}) collective-permute-start(bf16[2,4,72,576]{3,2,1,0:T(8,128)(2,1)} %pad_maximum_fusion.5.s0), channel_id=1, source_target_pairs={{0,2},{1,3},{2,0},{3,1},{4,6},{5,7},{6,4},{7,5},{8,10},{9,11},{10,... | collective-permute-start | bytes 1990664 | tf_op jit(solution)/shard_map/ppermute | solution.py:512
  167.2 29.6 %collective-permute-start.28 = (bf16[2,4,72,576]{3,2,1,0:T(8,128)(2,1)}, bf16[2,4,72,576]{3,2,1,0:T(8,128)(2,1)}, u32[]{:S(2)}, u32[]{:S(2)}) collective-permute-start(bf16[2,4,72,576]{3,2,1,0:T(8,128)(2,1)} %collective-permute-done.24.s1), channel_id=1, source_target_pairs={{0,2},{1,3},{2,0},{3,1},{4,6},{5,7},{6,4},{7,5},{8,10},{9,11},{10,... | collective-permute-start | bytes 1990664 | tf_op jit(solution)/shard_map/ppermute | solution.py:512
  196.8 26.0 %collective-permute-start.33 = (bf16[2,4,72,1536]{3,2,1,0:T(8,128)(2,1)S(1)}, bf16[2,4,72,1536]{3,2,1,0:T(8,128)(2,1)S(1)}, u32[]{:S(2)}, u32[]{:S(2)}) collective-permute-start(bf16[2,4,72,1536]{3,2,1,0:T(8,128)(2,1)S(1)} %pad_maximum_fusion.3.s0), channel_id=1, source_target_pairs={{0,1},{1,0},{2,6},{3,7},{4,5},{5,4},{6,2},{7,3},{8,9},{9,8},{10,14... | collective-permute-start | bytes 5308424 | tf_op jit(solution)/shard_map/ppermute | solution.py:512
  199.0 23.8 %collective-permute-start.34 = (bf16[2,192,576]{2,1,0:T(8,128)(2,1)S(1)}, bf16[2,192,576]{2,1,0:T(8,128)(2,1)S(1)}, u32[]{:S(2)}, u32[]{:S(2)}) collective-permute-start(bf16[2,192,576]{2,1,0:T(8,128)(2,1)S(1)} %pad_maximum_fusion.8), channel_id=1, source_target_pairs={{0,16},{1,17},{2,18},{3,19},{4,20},{5,21},{6,22},{7,23},{8,24},{9,... | collective-permute-start | bytes 1327112 | tf_op jit(solution)/shard_map/ppermute | solution.py:512
  237.9 25.9 %collective-permute-start.38 = (bf16[2,4,192,576]{3,2,1,0:T(8,128)(2,1)S(1)}, bf16[2,4,192,576]{3,2,1,0:T(8,128)(2,1)}, u32[]{:S(2)}, u32[]{:S(2)}) collective-permute-start(bf16[2,4,192,576]{3,2,1,0:T(8,128)(2,1)S(1)} %pad_maximum_fusion.1.s0), channel_id=1, source_target_pairs={{0,1},{1,0},{2,6},{3,7},{4,5},{5,4},{6,2},{7,3},{8,9},{9,8},{10,14... | collective-permute-start | bytes 5308424 | tf_op jit(solution)/shard_map/ppermute | solution.py:512
  287.1 37.7 %collective-permute-start.42 = (bf16[2,4,192,576]{3,2,1,0:T(8,128)(2,1)S(1)}, bf16[2,4,192,576]{3,2,1,0:T(8,128)(2,1)S(1)}, u32[]{:S(2)}, u32[]{:S(2)}) collective-permute-start(bf16[2,4,192,576]{3,2,1,0:T(8,128)(2,1)S(1)} %add_convert_fusion.1), channel_id=1, source_target_pairs={{0,1},{1,0},{2,6},{3,7},{4,5},{5,4},{6,2},{7,3},{8,9},{9,8},{10,14... | collective-permute-start | bytes 5308424 | tf_op jit(solution)/shard_map/ppermute | solution.py:512
  370.2 23.6 %collective-permute-start.45 = (bf16[4,4,72,1536]{3,2,1,0:T(8,128)(2,1)}, bf16[4,4,72,1536]{3,2,1,0:T(8,128)(2,1)}, u32[]{:S(2)}, u32[]{:S(2)}) collective-permute-start(bf16[4,4,72,1536]{3,2,1,0:T(8,128)(2,1)} %get-tuple-element.202), channel_id=1, source_target_pairs={{0,2},{1,3},{2,0},{3,1},{4,6},{5,7},{6,4},{7,5},{8,10},{9,11},{10,... | collective-permute-start | bytes 10616840 | tf_op jit(solution)/shard_map/ppermute | solution.py:512
  374.1 44.0 %collective-permute-start.46 = (bf16[2,4,72,1536]{3,2,1,0:T(8,128)(2,1)}, bf16[2,4,72,1536]{3,2,1,0:T(8,128)(2,1)}, u32[]{:S(2)}, u32[]{:S(2)}) collective-permute-start(bf16[2,4,72,1536]{3,2,1,0:T(8,128)(2,1)} %add_convert_fusion.2), channel_id=1, source_target_pairs={{0,1},{1,0},{2,6},{3,7},{4,5},{5,4},{6,2},{7,3},{8,9},{9,8},{10,14... | collective-permute-start | bytes 5308424 | tf_op jit(solution)/shard_map/ppermute | solution.py:512
  389.3 28.7 %collective-permute-start.48 = (bf16[4,4,72,576]{3,2,1,0:T(8,128)(2,1)}, bf16[4,4,72,576]{3,2,1,0:T(8,128)(2,1)}, u32[]{:S(2)}, u32[]{:S(2)}) collective-permute-start(bf16[4,4,72,576]{3,2,1,0:T(8,128)(2,1)} %get-tuple-element.211), channel_id=1, source_target_pairs={{0,2},{1,3},{2,0},{3,1},{4,6},{5,7},{6,4},{7,5},{8,10},{9,11},{10,... | collective-permute-start | bytes 3981320 | tf_op jit(solution)/shard_map/ppermute | solution.py:512
  393.2 24.8 %collective-permute-start.47 = (bf16[2,192,576]{2,1,0:T(8,128)(2,1)S(1)}, bf16[2,192,576]{2,1,0:T(8,128)(2,1)S(1)}, u32[]{:S(2)}, u32[]{:S(2)}) collective-permute-start(bf16[2,192,576]{2,1,0:T(8,128)(2,1)S(1)} %pad_maximum_fusion.9), channel_id=1, source_target_pairs={{0,16},{1,17},{2,18},{3,19},{4,20},{5,21},{6,22},{7,23},{8,24},{9,... | collective-permute-start | bytes 1327112 | tf_op jit(solution)/shard_map/ppermute | solution.py:512
  418.0 45.4 %collective-permute-start.49 = (bf16[2,4,72,1536]{3,2,1,0:T(8,128)(2,1)}, bf16[2,4,72,1536]{3,2,1,0:T(8,128)(2,1)}, u32[]{:S(2)}, u32[]{:S(2)}) collective-permute-start(bf16[2,4,72,1536]{3,2,1,0:T(8,128)(2,1)} %add_convert_fusion.3), channel_id=1, source_target_pairs={{0,1},{1,0},{2,6},{3,7},{4,5},{5,4},{6,2},{7,3},{8,9},{9,8},{10,14... | collective-permute-start | bytes 5308424 | tf_op jit(solution)/shard_map/ppermute | solution.py:512
  426.3 37.1 %collective-permute-start.50 = (bf16[1,4,72,1536]{3,2,1,0:T(8,128)(2,1)}, bf16[1,4,72,1536]{3,2,1,0:T(8,128)(2,1)}, u32[]{:S(2)}, u32[]{:S(2)}) collective-permute-start(bf16[1,4,72,1536]{3,2,1,0:T(8,128)(2,1)} %slice.370), channel_id=1, source_target_pairs={{0,4},{1,5},{2,3},{3,2},{4,0},{5,1},{6,7},{7,6},{8,12},{9,13},{10,... | collective-permute-start | bytes 2654216 | tf_op jit(solution)/shard_map/ppermute | solution.py:512
  429.0 34.4 %collective-permute-start.51 = (bf16[1,192,576]{2,1,0:T(8,128)(2,1)S(1)}, bf16[1,192,576]{2,1,0:T(8,128)(2,1)S(1)}, u32[]{:S(2)}, u32[]{:S(2)}) collective-permute-start(bf16[1,192,576]{2,1,0:T(8,128)(2,1)S(1)} %slice.374), channel_id=1, source_target_pairs={{0,8},{1,9},{2,10},{3,11},{4,12},{5,13},{6,14},{7,15},{8,0},{9,1},... | collective-permute-start | bytes 663560 | tf_op jit(solution)/shard_map/ppermute | solution.py:512
  473.5 34.4 %collective-permute-start.55 = (bf16[4,4,72,1728]{3,2,1,0:T(8,128)(2,1)}, bf16[4,4,72,1728]{3,2,1,0:T(8,128)(2,1)}, u32[]{:S(2)}, u32[]{:S(2)}) collective-permute-start(bf16[4,4,72,1728]{3,2,1,0:T(8,128)(2,1)} %get-tuple-element.228), channel_id=1, source_target_pairs={{0,2},{1,3},{2,0},{3,1},{4,6},{5,7},{6,4},{7,5},{8,10},{9,11},{10,... | collective-permute-start | bytes 11943944 | tf_op jit(solution)/shard_map/ppermute | solution.py:512
  487.6 23.9 %collective-permute-start.52 = (bf16[1,4,72,1536]{3,2,1,0:T(8,128)(2,1)S(1)}, bf16[1,4,72,1536]{3,2,1,0:T(8,128)(2,1)S(1)}, u32[]{:S(2)}, u32[]{:S(2)}) collective-permute-start(bf16[1,4,72,1536]{3,2,1,0:T(8,128)(2,1)S(1)} %slice.371), channel_id=1, source_target_pairs={{0,4},{1,5},{2,3},{3,2},{4,0},{5,1},{6,7},{7,6},{8,12},{9,13},{10,... | collective-permute-start | bytes 2654216 | tf_op jit(solution)/shard_map/ppermute | solution.py:512
  511.5 47.7 %collective-permute-start.56 = (bf16[2,4,72,1728]{3,2,1,0:T(8,128)(2,1)}, bf16[2,4,72,1728]{3,2,1,0:T(8,128)(2,1)}, u32[]{:S(2)}, u32[]{:S(2)}) collective-permute-start(bf16[2,4,72,1728]{3,2,1,0:T(8,128)(2,1)} %add_convert_fusion), channel_id=1, source_target_pairs={{0,1},{1,0},{2,6},{3,7},{4,5},{5,4},{6,2},{7,3},{8,9},{9,8},{10,14... | collective-permute-start | bytes 5971976 | tf_op jit(solution)/shard_map/ppermute | solution.py:512
  (152 other events, 1597.7 us)

commit v3 on v2

--- a/solution.py
+++ b/solution.py
@@ -17,7 +17,7 @@
 ALL = ("wide", "narrow")
 BF = jnp.bfloat16
 F32 = jnp.float32
-SHORT = pl.CostEstimate(flops=10**6, bytes_accessed=10**6, transcendentals=0)
+LONG = pl.CostEstimate(flops=10**12, bytes_accessed=1, transcendentals=0)
 
 
 def layer_norm(values):
@@ -28,16 +28,14 @@
 
 def head_tables(length):
     quarter = HD // 4
-    frequency = 10000.0 ** (-jnp.arange(quarter, dtype=F32) / quarter)
-    patch = jnp.arange(length, dtype=jnp.int32)
-    row_angle = (patch // GRID).astype(F32)[:, None] * frequency[None, :]
-    col_angle = (patch % GRID).astype(F32)[:, None] * frequency[None, :]
-    angles = jnp.concatenate([row_angle, row_angle, col_angle, col_angle], axis=-1)
+    lane = jnp.arange(H * HD, dtype=jnp.int32) % HD
+    frequency = 10000.0 ** (-(lane % quarter).astype(F32) / quarter)
+    patch = jnp.arange(length, dtype=jnp.int32)[:, None]
+    place = jnp.where(lane[None, :] < 2 * quarter, patch // GRID, patch % GRID)
+    angles = place.astype(F32) * frequency[None, :]
     cosine, sine = jnp.cos(angles), jnp.sin(angles)
-    first = (jnp.arange(HD) // quarter) % 2 == 0
-    above = jnp.where(first[None, :], -sine, 0.0)
-    below = jnp.where(first[None, :], 0.0, sine)
-    return [jnp.tile(t, (1, H)) for t in (cosine, above, below)]
+    first = (lane // quarter % 2 == 0)[None, :]
+    return [cosine, jnp.where(first, -sine, 0.0), jnp.where(first, 0.0, sine)]
 
 
 def head_sums():
@@ -144,7 +142,7 @@
         in_specs=[rows(p.shape[1]) for p in packed] + [all_of(a) for a in (gains, *tables, sums)],
         out_specs=[rows(width)] * 4,
         compiler_params=pltpu.CompilerParams(vmem_limit_bytes=48 * 2**20),
-        cost_estimate=SHORT,
+        cost_estimate=LONG,
         name="attention_forward",
     )(*packed, gains, *tables, sums)
 
@@ -168,14 +166,16 @@
         all_q, all_k, all_v = [Tiles(store_to(ref)) for ref in (d_q, d_k, d_v)]
         for head in range(H):
             first, last = window(head)
-            soft = softmax_of(q_ref, k_ref, head)
-            d_here = only(d_ref, head)
-            all_v.add(head, mm(soft.astype(BF), d_here, ((0,), (0,))))
-            d_soft = mm(d_here, v_ref[:, first:last], ((1,), (1,)))
-            inner = jnp.sum(soft * d_soft, axis=1, keepdims=True)
+            q_here, k_here, d_here = [only(ref, head) for ref in (q_ref, k_ref, d_ref)]
+            scores = mm(k_here, q_ref[:, first:last], ((1,), (1,))) * (HD ** (-0.5))
+            exponent = jnp.exp(scores - jnp.max(scores, axis=0, keepdims=True))
+            soft = exponent / jnp.sum(exponent, axis=0, keepdims=True)
+            all_v.add(head, mm(soft.astype(BF), d_here, ((1,), (0,))))
+            d_soft = mm(v_ref[:, first:last], d_here, ((1,), (1,)))
+            inner = jnp.sum(soft * d_soft, axis=0, keepdims=True)
             d_scores = (soft * (d_soft - inner) * (HD ** (-0.5))).astype(BF)
-            all_q.add(head, mm(d_scores, only(k_ref, head), ((1,), (0,))))
-            all_k.add(head, mm(d_scores, only(q_ref, head), ((0,), (0,))))
+            all_k.add(head, mm(d_scores, q_here, ((1,), (0,))))
+            all_q.add(head, mm(d_scores, k_here, ((0,), (0,))))
         whole = jnp.concatenate([p[...] for p in parts], axis=1)
         sums_here = sums_ref[...]
         done = []
@@ -210,7 +210,7 @@
         out_specs=[rows(block)] * blocks + [pl.BlockSpec((1, 2, width), lambda i: (i, 0, 0))],
         scratch_shapes=[pltpu.VMEM((length, width), F32)] * 3,
         compiler_params=pltpu.CompilerParams(vmem_limit_bytes=56 * 2**20),
-        cost_estimate=SHORT,
+        cost_estimate=LONG,
         name="attention_backward",
     )(*packed, queries, keys, values, d_mixed, gains, *tables, sums)
     return outs[:blocks], outs[blocks]
@@ -226,8 +226,8 @@
 
 def project(a, blocks):
     tokens, depth = a.shape
-    columns = blocks[0].shape[1]
-    count, chunk = len(blocks), chunk_of(columns, 640)
+    count, _, columns = blocks.shape
+    chunk = chunk_of(columns, 640)
 
     def kernel(a_ref, *refs):
         for w_ref, out_ref in zip(refs[:count], refs[count:]):
@@ -237,12 +237,13 @@
         kernel,
         grid=(-(-columns // chunk),),
         out_shape=[jax.ShapeDtypeStruct((tokens, columns), F32)] * count,
-        in_specs=[whole_block(a)] + [pl.BlockSpec((depth, chunk), lambda i: (0, i))] * count,
+        in_specs=[whole_block(a)]
+        + [pl.BlockSpec((None, depth, chunk), lambda i, j=j: (j, 0, i)) for j in range(count)],
         out_specs=[pl.BlockSpec((tokens, chunk), lambda i: (0, i))] * count,
         compiler_params=pltpu.CompilerParams(vmem_limit_bytes=40 * 2**20),
-        cost_estimate=SHORT,
+        cost_estimate=LONG,
         name="project",
-    )(a, *blocks)
+    )(a, *[blocks] * count)
 
 
 def gated(a, w_gate, w_up):
@@ -266,14 +267,14 @@
         in_specs=[whole_block(a), weight, weight],
         out_specs=[out] * 3,
         compiler_params=pltpu.CompilerParams(vmem_limit_bytes=40 * 2**20),
-        cost_estimate=SHORT,
+        cost_estimate=LONG,
         name="gated",
     )(a, w_gate, w_up)
 
 
 def gated_back(d_parts, down, gate_val, up_val, w_gate, w_up):
     tokens, columns = gate_val.shape
-    depth, count, chunk = w_gate.shape[0], len(down), 512
+    depth, count, chunk = w_gate.shape[0], down.shape[0], 512
 
     def kernel(*refs):
         d_refs, w_refs, refs = refs[:count], refs[count : 2 * count], refs[2 * count :]
@@ -299,7 +300,7 @@
         def _():
             in_ref[...] += term
 
-    width = down[0].shape[1]
+    width = down.shape[2]
     token = pl.BlockSpec((tokens, chunk), lambda i: (0, i))
     weight = pl.BlockSpec((depth, chunk), lambda i: (0, i))
     return pl.pallas_call(
@@ -308,13 +309,13 @@
         out_shape=[jax.ShapeDtypeStruct((tokens, columns), BF)] * 2
         + [jax.ShapeDtypeStruct((tokens, depth), F32)],
         in_specs=[whole_block(d) for d in d_parts]
-        + [pl.BlockSpec((chunk, width), lambda i: (i, 0))] * count
+        + [pl.BlockSpec((None, chunk, width), lambda i, j=j: (j, i, 0)) for j in range(count)]
         + [token, token, weight, weight],
         out_specs=[token, token, pl.BlockSpec((tokens, depth), lambda i: (0, 0))],
         compiler_params=pltpu.CompilerParams(vmem_limit_bytes=48 * 2**20),
-        cost_estimate=SHORT,
+        cost_estimate=LONG,
         name="gated_back",
-    )(*d_parts, *down, gate_val, up_val, w_gate, w_up)
+    )(*d_parts, *[down] * count, gate_val, up_val, w_gate, w_up)
 
 
 def normal(values):
@@ -347,7 +348,7 @@
         in_specs=in_specs,
         out_specs=[spec(rows, rest) for rows, rest, _ in outs],
         compiler_params=pltpu.CompilerParams(vmem_limit_bytes=vmem * 2**20),
-        cost_estimate=SHORT,
+        cost_estimate=LONG,
         name=name,
     )(*args)
 
@@ -356,8 +357,8 @@
     tokens, width = mixed.shape
 
     def kernel(mixed_ref, in_ref, piece, *refs):
-        w_refs, (attn_ref, hidden_ref, mlp_ref) = refs[:-3], refs[-3:]
-        attn = [mm(mixed_ref[...], w[...], ((1,), (0,))) for w in w_refs]
+        w_ref, attn_ref, hidden_ref, mlp_ref = refs
+        attn = [mm(mixed_ref[...], w_ref[j], ((1,), (0,))) for j in range(out_b.shape[0])]
         attn = jnp.concatenate(attn, axis=1)
         attn_ref[...] = attn
         hidden = in_ref[...].astype(F32) + piece[0, 2:3, :] * attn
@@ -367,15 +368,15 @@
 
     rows = tokens // images
     outs = [(rows, (width,), F32), (rows, (width,), F32), (rows, (width,), BF)]
-    return per_image(kernel, images, [mixed, inputs, pieces], out_b, outs, 32, "attention_tail")
+    return per_image(kernel, images, [mixed, inputs, pieces], [out_b], outs, 32, "attention_tail")
 
 
 def block_tail(hidden_mid, down_b, hidden_one, cotangent, pieces, count, images):
     tokens, width = hidden_one.shape
 
     def kernel(mid_ref, hidden_ref, cot_ref, piece, *refs):
-        w_refs, (count_ref, out_ref, gate_ref) = refs[:-3], refs[-3:]
-        mlp = [mm(mid_ref[...], w[...], ((1,), (0,))) for w in w_refs]
+        w_ref, count_ref, out_ref, gate_ref = refs
+        mlp = [mm(mid_ref[...], w_ref[j], ((1,), (0,))) for j in range(down_b.shape[0])]
         mlp = jnp.concatenate(mlp, axis=1)
         out_ref[...] = (hidden_ref[...] + piece[0, 5:6, :] * mlp).astype(BF)
         real = (pl.program_id(0) < count_ref[0]).astype(F32)
@@ -385,15 +386,15 @@
     rows = tokens // images
     outs = [(rows, (width,), BF), (1, (1, width), F32)]
     by_image = [hidden_mid, hidden_one, cotangent, pieces]
-    return per_image(kernel, images, by_image, down_b, outs, 40, "block_tail", count)
+    return per_image(kernel, images, by_image, [down_b], outs, 40, "block_tail", count)
 
 
 def middle_back(d_mlp_in, hidden_one, attn_out, cotangent, pieces, out_b, count, images):
     tokens, width = d_mlp_in.shape
-    blocks, columns = len(out_b), out_b[0].shape[1]
+    blocks, _, columns = out_b.shape
 
     def kernel(in_ref, hidden_ref, attn_ref, cot_ref, piece, *refs):
-        w_refs, count_ref, refs = refs[:blocks], refs[blocks], refs[blocks + 1 :]
+        w_ref, count_ref, refs = refs[0], refs[1], refs[2:]
         d_hidden_ref, d_mixed_ref, sums_ref = refs[:3]
         d_in = in_ref[...]
         normed, inverse = normal(hidden_ref[...])
@@ -406,10 +407,10 @@
         sums_ref[0, 2:3] = jnp.sum(d_hidden * attn_ref[...], axis=0, keepdims=True)
         d_attn = (piece[0, 2:3, :] * d_hidden).astype(BF)
         d_mixed = None
-        for j, (w, out) in enumerate(zip(w_refs, refs[3:])):
+        for j, out in enumerate(refs[3:]):
             part = d_attn[:, j * columns : (j + 1) * columns]
             out[...] = part
-            term = mm(part, w[...], ((1,), (1,)))
+            term = mm(part, w_ref[j], ((1,), (1,)))
             d_mixed = term if d_mixed is None else d_mixed + term
         d_mixed_ref[...] = d_mixed.astype(BF)
 
@@ -417,19 +418,19 @@
     outs = [(rows, (width,), F32), (rows, (width,), BF), (1, (3, width), F32)]
     outs += [(rows, (columns,), BF)] * blocks
     by_image = [d_mlp_in, hidden_one, attn_out, cotangent, pieces]
-    return per_image(kernel, images, by_image, out_b, outs, 40, "middle_back", count)
+    return per_image(kernel, images, by_image, [out_b], outs, 40, "middle_back", count)
 
 
 def block_head_back(d_packed, d_hidden, inputs, pieces, qkv_b, images):
     tokens, width = d_hidden.shape
-    blocks = len(qkv_b)
+    blocks = qkv_b.shape[0]
 
     def kernel(*refs):
         d_refs, (d_hidden_ref, in_ref, piece) = refs[:blocks], refs[blocks : blocks + 3]
-        w_refs, (out_ref, sums_ref) = refs[blocks + 3 : -2], refs[-2:]
+        w_ref, out_ref, sums_ref = refs[blocks + 3 :]
         d_in = None
-        for d, w in zip(d_refs, w_refs):
-            term = mm(d[...], w[...], ((1,), (1,)))
+        for j, d in enumerate(d_refs):
+            term = mm(d[...], w_ref[j], ((1,), (1,)))
             d_in = term if d_in is None else d_in + term
         normed, inverse = normal(in_ref[...].astype(F32))
         sums_ref[0, 0:1] = jnp.sum(d_in, axis=0, keepdims=True)
@@ -439,13 +440,14 @@
 
     outs = [(tokens // images, (width,), BF), (1, (2, width), F32)]
     by_image = [*d_packed, d_hidden, inputs, pieces]
-    return per_image(kernel, images, by_image, qkv_b, outs, 48, "block_head_back")
+    return per_image(kernel, images, by_image, [qkv_b], outs, 48, "block_head_back")
 
 
 def grad_stacks(places, a, parts):
     tokens, features = a.shape
-    columns = parts[0].shape[1]
-    z, count = places.z, len(parts)
+    z, count = places.z, places.narrow
+    joined = len(parts) < count
+    columns = parts[0].shape[1] // (count if joined else 1)
     rows = features // (4 * z)
     chunk = chunk_of(columns, 900)
     masks = [places.masks(0), places.masks(1)]
@@ -478,16 +480,19 @@
         grid=(-(-columns // chunk),),
         out_shape=[jax.ShapeDtypeStruct(shape, BF)] * 2,
         in_specs=[pl.BlockSpec(memory_space=pltpu.SMEM), whole_block(a)]
-        + [pl.BlockSpec((tokens, chunk), lambda i: (0, i))] * count,
+        + [
+            pl.BlockSpec((tokens, chunk), lambda i, j=j: (0, j * (columns // chunk) + i if joined else i))
+            for j in range(count)
+        ],
         out_specs=[out, out],
         scratch_shapes=[
             pltpu.VMEM((features, tokens), BF),
             pltpu.VMEM((count, 4 * z, rows, chunk), BF),
         ],
         compiler_params=pltpu.CompilerParams(vmem_limit_bytes=56 * 2**20),
-        cost_estimate=SHORT,
+        cost_estimate=LONG,
         name="grad_stacks",
-    )(at, a, *parts)
+    )(at, a, *(parts * count if joined else parts))
 
 
 class Places:
@@ -527,18 +532,15 @@
         out.append((2, (0, 0, 1, 0), self.at_c))
         return out
 
-    def gather_small(self, value):
-        value = value[None, None, None, None]
-        for axis, flip, bit in self.all_bits():
+    def open_small(self, value):
+        return value[None, None, None, None]
+
+    def gather_bits(self, value, bits):
+        for axis, flip, bit in bits:
             other = self.swap(value, lambda core: flip)
             low = jnp.where(bit == 0, value, other)
             high = jnp.where(bit == 0, other, value)
             value = jnp.concatenate([low, high], axis)
-        return value.reshape(self.wide * self.narrow, *value.shape[4:])
-
-    def add_all(self, value):
-        for _, flip, _ in self.all_bits():
-            value = value + self.swap(value, lambda core: flip)
         return value
 
     def add_narrow(self, value):
@@ -629,114 +631,190 @@
             pltpu.SemaphoreType.DMA,
         ],
         compiler_params=pltpu.CompilerParams(vmem_limit_bytes=24 * 2**20),
-        cost_estimate=SHORT,
+        cost_estimate=LONG,
         name="assemble",
     )(at, *parts)
 
 
+def join(parts):
+    counts = [p.shape[0] for p in parts]
+
+    def kernel(*refs):
+        first = 0
+        for ref, count in zip(refs[:-1], counts):
+            refs[-1][first : first + count] = ref[...]
+            first += count
+
+    shape = jax.ShapeDtypeStruct((sum(counts), *parts[0].shape[1:]), BF)
+    return pl.pallas_call(
+        kernel,
+        grid=(1,),
+        out_shape=shape,
+        in_specs=[whole_block(p) for p in parts],
+        out_specs=whole_block(shape),
+        compiler_params=pltpu.CompilerParams(vmem_limit_bytes=24 * 2**20),
+        cost_estimate=LONG,
+        name="join",
+    )(*parts)
+
+
+def add_stacks(terms, half):
+    shape = (half, *terms[0].shape[1:])
+
+    def kernel(*refs):
+        total = refs[0][...].astype(F32)
+        for ref in refs[1:-1]:
+            total += ref[...].astype(F32)
+        refs[-1][...] = total.astype(BF)
+
+    deep = 2 if shape[1] % 2 == 0 else 1
+    block = (1, deep, *shape[2:])
+    return pl.pallas_call(
+        kernel,
+        grid=(half, shape[1] // deep),
+        out_shape=jax.ShapeDtypeStruct(shape, BF),
+        in_specs=[pl.BlockSpec(block, lambda i, j: (half + i, j, 0, 0))] * len(terms),
+        out_specs=pl.BlockSpec(block, lambda i, j: (i, j, 0, 0)),
+        compiler_params=pltpu.CompilerParams(vmem_limit_bytes=24 * 2**20),
+        cost_estimate=LONG,
+        name="add_stacks",
+    )(*terms)
+
+
+def add_slabs(places, terms, z_terms, first, count, divisor=None):
+    rows, columns = terms[0].shape[2:]
+    late = [(at, term) for at, term in z_terms if at <= first < at + term.shape[0]]
+
+    def kernel(at_ref, *refs):
+        out, refs = refs[-1], refs[:-1]
+        total = None
+        for i, ref in enumerate(refs[: len(terms) + len(late)]):
+            value = (ref[0, 0] if i < len(terms) else ref[0]).astype(F32)
+            total = value if total is None else total + value
+        if divisor is not None:
+            total = total / refs[-1][0]
+        out[0] = total.astype(out.dtype)
+
+    in_specs = [
+        pl.BlockSpec((1, 1, rows, columns), lambda i, at: (0, at[0] ^ (first + i), 0, 0))
+        for _ in terms
+    ]
+    in_specs += [
+        pl.BlockSpec((1, rows, columns), lambda i, at, f=first - at_first: (f + i, 0, 0))
+        for at_first, _ in late
+    ]
+    args = [*terms, *[term for _, term in late]]
+    if divisor is not None:
+        in_specs.append(pl.BlockSpec(memory_space=pltpu.SMEM))
+        args.append(divisor.reshape(1))
+    kind = BF if divisor is None else F32
+    return pl.pallas_call(
+        kernel,
+        grid_spec=pltpu.PrefetchScalarGridSpec(
+            num_scalar_prefetch=1,
+            grid=(count,),
+            in_specs=in_specs,
+            out_specs=pl.BlockSpec((1, rows, columns), lambda i, at: (i, 0, 0)),
+        ),
+        out_shape=jax.ShapeDtypeStruct((count, rows, columns), kind),
+        compiler_params=pltpu.CompilerParams(vmem_limit_bytes=24 * 2**20),
+        cost_estimate=LONG,
+        name="add_slabs",
+    )(places.at_z.astype(jnp.int32).reshape(1), *args)
+
+
 class Slots:
-    def __init__(self):
-        self.before, self.now = (), []
+    def __init__(self, places):
+        self.places = places
+        self.before, self.now, self.ready = (), [], []
 
     def tie(self, value):
-        return after(value, *self.before) if self.before else value
+        return after(value, *self.before, *self.ready)
 
     def note(self, *values):
         self.now += values
 
     def next(self, *values):
         self.note(*values)
-        self.before, self.now = tuple(self.now), []
+        self.before, self.now, self.ready = tuple(self.now), [], []
+
+    def send(self, value, flip):
+        value = after(value, *self.before)
+        self.ready.append(value)
+        return self.follow(value, flip)
+
+    def follow(self, value, flip):
+        other = self.places.swap(value, flip)
+        self.note(other)
+        return other
 
 
 class Gather:
-    def __init__(self, places, shard):
-        self.places, self.rows = places, places.wide * shard.shape[0]
-        self.held, self.other = shard[None], None
-
-    def step_z(self, bit, *before):
-        other = self.places.swap(after(self.held, *before), lambda core: (bit, 0, 0, 0))
-        self.held = jnp.concatenate([self.held, other], 0)
-        if bit == self.places.z_bits[-1]:
-            self.held = self.held[None]
-        return other
-
-    def all_z(self, *before):
-        other = None
-        for i, bit in enumerate(self.places.z_bits):
-            other = self.step_z(bit, *(before if i == 0 else ()))
-        return other
-
-    def step(self, i, *before):
-        if self.other is not None:
-            self.held = jnp.concatenate([self.held, self.other], 0)
-        self.other = self.places.swap(after(self.held, *before), self.places.step_flip(i))
-        return self.other
-
-    def first(self, *before):
+    def __init__(self, slots, shard):
+        self.slots, self.places = slots, slots.places
+        self.rows = self.places.wide * shard.shape[0]
+        self.parts = [shard[None]]
+
+    def all_z(self):
+        for d in range(1, self.places.z):
+            self.parts.append(self.slots.send(self.parts[0], lambda core: (d, 0, 0, 0)))
+
+    def step(self, i, exchange):
+        joined = join([p.reshape(-1, *p.shape[-2:]) for p in self.parts])
+        self.parts = [joined]
+        self.parts.append(exchange(joined, self.places.step_flip(i)))
+
+    def first(self):
         for i in range(len(self.places.orders[0]) - 1):
-            other = self.step(i, *(before if i == 0 else ()))
-        return other
-
-    def last(self, *before):
-        return self.step(len(self.places.orders[0]) - 1, *before)
-
-    def cores(self, *before):
-        parts = after((self.held, self.other), *before)
-        parts = list(parts)
-        self.parts = parts + [self.places.swap(p, lambda core: (0, 0, 1, 0)) for p in parts]
-        return self.parts[2:]
-
-    def whole(self, *before):
-        whole = assemble(self.places, after(tuple(self.parts), *before))
-        return list(whole.reshape(-1, self.rows, whole.shape[-1]))
+            self.step(i, self.slots.follow if i else self.slots.send)
+
+    def last(self):
+        self.step(len(self.places.orders[0]) - 1, self.slots.send)
+
+    def cores(self):
+        parts = [p.reshape(-1, self.places.z, *p.shape[-2:]) for p in self.parts]
+        self.parts = parts + [self.slots.send(p, lambda core: (0, 0, 1, 0)) for p in parts]
+
+    def whole(self):
+        whole = assemble(self.places, self.slots.tie(tuple(self.parts)))
+        return whole.reshape(-1, self.rows, whole.shape[-1])
 
 
 class Scatter:
-    def __init__(self, places, a, parts):
-        self.places = places
-        self.stack, self.to_core = grad_stacks(places, a, parts)
-        self.half = self.stack.shape[0]
-
-    def cores(self, *before):
-        self.arrived = self.places.swap(after(self.to_core, *before), lambda core: (0, 0, 1, 0))
-        return self.arrived
-
-    def first(self, *before):
-        places, arrived = self.places, self.arrived
-        self.half = half = self.half // 2
-        send = self.stack[half:].astype(F32) + arrived[half:].astype(F32)
-        flip = places.step_flip(len(places.orders[0]) - 1)
-        self.other = places.swap(after(send.astype(BF), *before), flip)
-        self.own = self.stack[:half].astype(F32) + arrived[:half].astype(F32)
-        return self.other
-
-    def last(self, *before):
-        places = self.places
-        for i in reversed(range(len(places.orders[0]) - 1)):
-            held = self.own + self.other.astype(F32)
-            self.half = half = self.half // 2
-            send = after(held[half:].astype(BF), *before)
-            self.own, self.other = held[:half], places.swap(send, places.step_flip(i))
-        return self.other
-
-    def step_z(self, bit, *before):
-        places = self.places
-        held = self.own + self.other.astype(F32)
-        if bit == places.z_bits[-1]:
-            held = held[0]
-            held = jnp.stack([take(held, 0, places.at_z ^ d) for d in range(places.z)])
-        send = after(held[bit:].astype(BF), *before)
-        self.own, self.other = held[:bit], places.swap(send, lambda core: (bit, 0, 0, 0))
-        return self.other
-
-    def all_z(self, *before):
-        for i, bit in enumerate(reversed(self.places.z_bits)):
-            other = self.step_z(bit, *(before if i == 0 else ()))
-        return other
-
-    def result(self):
-        return (self.own + self.other.astype(F32))[0]
+    def __init__(self, slots, a, parts):
+        self.slots, self.places = slots, slots.places
+        stack, self.to_core = grad_stacks(self.places, a, parts)
+        self.terms, self.z_terms, self.half = [stack], [], stack.shape[0]
+
+    def cores(self, exchange):
+        self.terms.append(exchange(self.to_core, lambda core: (0, 0, 1, 0)))
+
+    def step(self, i, exchange):
+        self.half //= 2
+        send = add_stacks(self.terms, self.half)
+        self.terms.append(exchange(send, self.places.step_flip(i)))
+
+    def first(self):
+        self.step(len(self.places.orders[0]) - 1, self.slots.send)
+
+    def last(self):
+        for i in reversed(range(len(self.places.orders[0]) - 1)):
+            chained = i < len(self.places.orders[0]) - 2
+            self.step(i, self.slots.follow if chained else self.slots.send)
+
+    def step_z(self, *bits):
+        for i, bit in enumerate(bits):
+            exchange = self.slots.follow if i else self.slots.send
+            send = add_slabs(self.places, self.terms, self.z_terms, bit, bit)
+            self.z_terms.append((0, exchange(send, lambda core: (bit, 0, 0, 0))))
+
+    def direct_z(self):
+        for d in reversed(range(1, self.places.z)):
+            send = add_slabs(self.places, self.terms, self.z_terms, d, 1)
+            self.z_terms.append((0, self.slots.send(send, lambda core: (d, 0, 0, 0))))
+
+    def result(self, divisor):
+        return add_slabs(self.places, self.terms, self.z_terms, 0, 1, divisor)[0]
 
 
 def dot(a, b, dims, out=F32):
@@ -779,29 +857,26 @@
     def deep(v):
         return v.reshape(images, length, -1)
 
-    t = Slots()
-    z_low, z_high = places.z_bits[0], places.z_bits[1:]
+    t = Slots(places)
+    z_low, z_high = places.z_bits[:1], places.z_bits[1:]
+    z_down = z_high[::-1]
     qkv, out, gate, up, down = [
-        Gather(places, shard) for shard in (w_qkv, w_out, w_gate, w_up, w_down)
+        Gather(t, shard) for shard in (w_qkv, w_out, w_gate, w_up, w_down)
     ]
 
-    def high_z(weight):
-        for i, bit in enumerate(z_high):
-            other = weight.step_z(bit, *(t.before if i == 0 else ()))
-        return other
-
-    def high_sum(grad):
-        for i, bit in enumerate(reversed(z_high)):
-            other = grad.step_z(bit, *(t.before if i == 0 else ()))
-        return other
-
+    qkv.all_z()
     small = [class_ids, step_ids, image_counts, ada_bias]
     small = jnp.concatenate([v.astype(F32) for v in small])[None]
-    small = places.gather_small(small)[:, 0]
-    t.next(qkv.step_z(z_low), small)
-
+    bits = places.all_bits()
+    small = places.gather_bits(places.open_small(small), bits)
+    small = small.reshape(wide * narrow, -1)
+    t.next(small)
+
+    qkv.first()
+    out.all_z()
+    small = t.tie(small)
     ids = small[:, : 2 * images].reshape(-1, 2, images).transpose(0, 2, 1).reshape(-1, 2)
-    ids = t.tie(ids).astype(jnp.int32)
+    ids = ids.astype(jnp.int32)
     real_count = jnp.sum(small[:, 2 * images])
     bias = small[:, 2 * images + 1 :].reshape(-1)
     rows_here, cols_here = class_table.shape
@@ -814,128 +889,160 @@
     wave = jnp.where(column[None, :] < half_width, jnp.cos(angles), jnp.sin(angles))
     condition = places.add_narrow(picked) + wave
     cond_act = jax.nn.silu(condition).astype(BF)
-    mod_part = dot(cond_act, ada_weight, ((1,), (0,)))
+    t.next(cond_act)
+
+    qkv.last()
+    gate.all_z()
+    mod_part = dot(t.tie(cond_act), ada_weight, ((1,), (0,)))
     mod_part = places.scatter_chip_row(mod_part.reshape(wide, narrow, images, -1))
-    t.next(high_z(qkv), mod_part)
-
+    t.next(mod_part, *tables, sums)
+
+    qkv.cores()
+    out.first()
+    gate.first()
     mod_part = places.trade_narrow(places.scatter_z(t.tie(mod_part)))
-    modulation = mod_part.transpose(1, 0, 2).reshape(images, -1) + bias
-    t.next(qkv.first(*t.before), out.all_z(*t.before), modulation)
-
-    pieces = t.tie(modulation).reshape(images, 6, width)
+    t.next(mod_part)
+
+    out.last()
+    gate.last()
+    up.all_z()
+    qkv_b = qkv.whole()
+    modulation = t.tie(mod_part).transpose(1, 0, 2).reshape(images, -1) + bias
+    pieces = modulation.reshape(images, 6, width)
     normed, _ = layer_norm(inputs.astype(F32))
     attn_in = flat((normed * (1.0 + pieces[:, 1:2]) + pieces[:, 0:1]).astype(BF))
-    t.next(qkv.last(*t.before), gate.all_z(*t.before), attn_in, *tables, sums)
-
-    t.note(*qkv.cores(*t.before))
-    t.next(out.first(*t.before), gate.first(*t.before), up.step_z(z_low, *t.before))
-
-    qkv_b = qkv.whole(*t.before)
-    packed = project(attn_in, qkv_b)
-    t.next(out.last(*t.before), gate.last(*t.before), high_z(up), *packed)
-
-    t.note(*out.cores(*t.before), *gate.cores(*t.before))
+    t.next(attn_in, qkv_b)
+
+    out.cores()
+    gate.cores()
+    up.first()
+    packed = project(t.tie(attn_in), qkv_b)
+    t.next(*packed)
+
+    up.last()
+    down.all_z()
     packed = t.tie(packed)
     queries, key_rows, value_rows, mixed = attention_forward(packed, gains, tables, sums, images)
-    t.next(up.first(*t.before), down.step_z(z_low, *t.before), mixed)
-
-    out_b = out.whole(*t.before)
-    attn_out, hidden_one, mlp_in = attention_tail(mixed, out_b, flat(inputs), pieces, images)
-    t.next(up.last(*t.before), high_z(down), mlp_in)
-
-    t.note(*up.cores(*t.before))
-    (gate_b,) = gate.whole(*t.before)
-    t.next(down.first(*t.before), gate_b)
-
-    (up_b,) = up.whole(*t.before)
-    gate_val, up_val, hidden_mid = gated(mlp_in, gate_b, up_b)
     slot_real = (jnp.arange(images, dtype=jnp.int32) < local_count).astype(F32)
     grad_y = cotangent.astype(F32) * slot_real[:, None, None]
-    d_mlp = flat((pieces[:, 5:6] * grad_y).astype(BF))
-    t.next(down.last(*t.before), hidden_mid)
-
-    t.note(*down.cores(*t.before))
-    g_down = Scatter(places, t.tie(hidden_mid), split(d_mlp, narrow))
-    t.next(g_down.cores())
-
-    g_down_1 = g_down.first(*t.before)
-    down_b = down.whole(*t.before)
-    d_gate, d_up, d_mlp_in = gated_back(
-        split(d_mlp, narrow), down_b, gate_val, up_val, gate_b, up_b
-    )
-    t.next(g_down_1, d_mlp_in)
-
-    g_down_2 = g_down.last(*t.before)
-    g_gate = Scatter(places, mlp_in, split(t.tie(d_gate), narrow))
-    t.next(g_down_2, g_gate.cores())
-
-    g_gate_1 = g_gate.first(*t.before)
-    t.note(g_gate_1, high_sum(g_down))
-    g_up = Scatter(places, mlp_in, split(t.tie(d_up), narrow))
-    t.note(g_up.cores())
+    d_mlp = split(flat((pieces[:, 5:6] * grad_y).astype(BF)), narrow)
+    t.next(mixed, *d_mlp)
+
+    up.cores()
+    down.first()
+    out_b = out.whole()
+    attn_out, hidden_one, mlp_in = attention_tail(mixed, out_b, flat(inputs), pieces, images)
+    gate_b = gate.whole()[0]
+    t.next(mlp_in, gate_b)
+
+    down.last()
+    up_b = up.whole()[0]
+    gate_val, up_val, hidden_mid = gated(mlp_in, gate_b, up_b)
+    t.next(hidden_mid)
+
+    down.cores()
+    g_down = Scatter(t, t.tie(hidden_mid), d_mlp)
+    t.next(g_down.to_core)
+
+    g_down.cores(t.send)
+    down_b = down.whole()
+    t.next(down_b)
+
+    g_down.first()
+    d_gate, d_up, d_mlp_in = gated_back(t.tie(d_mlp), down_b, gate_val, up_val, gate_b, up_b)
+    t.next(d_mlp_in)
+
+    g_down.last()
+    g_gate = Scatter(t, mlp_in, [t.tie(d_gate)])
+    g_gate.cores(t.follow)
+    t.next()
+
+    g_gate.first()
+    g_down.step_z(*z_down)
+    g_up = Scatter(t, mlp_in, [t.tie(d_up)])
+    g_up.cores(t.follow)
     d_hidden, d_mixed, sums_b, *d_attn = middle_back(
         t.tie(d_mlp_in), hidden_one, attn_out, flat(cotangent), pieces, out_b, image_counts, images
     )
-    g_out = Scatter(places, mixed, d_attn)
-    t.note(g_out.cores())
-    t.next(d_mixed)
-
-    t.note(g_up.first(*t.before), g_gate.last(*t.before), g_down.step_z(z_low, *t.before))
+    g_out = Scatter(t, mixed, d_attn)
+    t.next(g_out.to_core, d_mixed)
+
+    g_gate.last()
+    g_up.first()
+    g_out.cores(t.send)
+    g_down.step_z(*z_low)
     d_packed, gain_terms = attention_backward(
         packed, queries, key_rows, value_rows, t.tie(d_mixed), gains, tables, sums, images
     )
     t.next(*d_packed)
 
-    t.note(g_up.last(*t.before), g_out.first(*t.before), high_sum(g_gate))
-    g_qkv = Scatter(places, attn_in, t.tie(d_packed))
-    grad_gains = gain_terms.sum(0).reshape(2, H, HD).sum(1)
-    t.next(g_qkv.cores())
-
-    t.note(g_qkv.first(*t.before), g_out.last(*t.before), high_sum(g_up))
-    t.note(g_gate.step_z(z_low, *t.before))
+    g_up.last()
+    g_out.first()
+    g_gate.step_z(*z_down)
+    g_qkv = Scatter(t, attn_in, t.tie(d_packed))
+    g_qkv.cores(t.follow)
+    t.next()
+
+    g_qkv.first()
+    g_out.last()
+    g_up.step_z(*z_down)
+    g_gate.step_z(*z_low)
     d_tokens, sums_a = block_head_back(
         t.tie(d_packed), d_hidden, flat(inputs), pieces, qkv_b, images
     )
     block_output, sums_gate = block_tail(
         t.tie(hidden_mid), down_b, hidden_one, flat(cotangent), pieces, image_counts, images
     )
+    grad_gains = gain_terms.sum(0).reshape(2, H, HD).sum(1).reshape(1, -1)
+    gains_high = grad_gains.astype(BF)
+    gains_low = (grad_gains - gains_high.astype(F32)).astype(BF)
+    rest = jnp.zeros((images - 2, 2 * HD), BF)
+    grad_gains = jnp.concatenate([gains_high, gains_low, rest], axis=0)
     d_modulation = jnp.concatenate([sums_a, sums_b[:, 2:], sums_b[:, :2], sums_gate], axis=1)
     d_modulation = d_modulation.astype(BF).reshape(images, -1)
-    t.next(d_modulation, d_tokens, block_output)
-
-    t.note(high_sum(g_out), g_up.step_z(z_low, *t.before))
-    gain_sum = places.add_all(t.tie(grad_gains))
-    t.next(g_qkv.last(*t.before))
-
-    t.note(high_sum(g_qkv), g_out.step_z(z_low, *t.before))
-    d_mod = places.gather_small(t.tie(d_modulation)).reshape(-1, d_modulation.shape[1])
-    g_qkv.step_z(z_low)
-    r_qkv, r_out, r_gate, r_up, r_down = [
-        g.result() for g in (g_qkv, g_out, g_gate, g_up, g_down)
-    ]
-
+    rest = jnp.zeros((images, 65 * 128 - 6 * width - 2 * HD), BF)
+    d_modulation = jnp.concatenate([d_modulation, grad_gains, rest], axis=1)
+    t.next(d_modulation)
+
+    g_qkv.last()
+    g_up.step_z(*z_low)
+    g_out.step_z(*z_down)
+    d_all = lax.all_gather(t.tie(d_modulation), ALL, axis=0, tiled=True)
+    t.next()
+
+    g_qkv.direct_z()
+    g_out.step_z(*z_low)
+    gain_sum = d_all[:, 6 * width : 6 * width + 2 * HD].astype(F32)
+    gain_sum = jnp.sum(gain_sum, axis=0).reshape(2, HD) / real_count
+    d_mod = d_all[:, : 6 * width]
     ada_cols = ada_weight.shape[1]
     d_mod_here = lax.dynamic_slice_in_dim(d_mod, at_n * ada_cols, ada_cols, 1)
-    g_ada = dot(cond_act, d_mod_here, ((0,), (0,)))
+    g_ada = dot(cond_act, d_mod_here, ((0,), (0,))) / real_count
     bias_cols = ada_bias.shape[0]
     bias_at = (at_w * narrow + at_n) * bias_cols
     g_bias = jnp.sum(lax.dynamic_slice_in_dim(d_mod, bias_at, bias_cols, 1).astype(F32), axis=0)
+    g_bias = g_bias / real_count
     d_cond_act = places.add_narrow(dot(d_mod_here, ada_weight, ((1,), (1,))))
     cond_sigmoid = jax.nn.sigmoid(condition)
     d_condition = d_cond_act * cond_sigmoid * (1.0 + condition * (1.0 - cond_sigmoid))
-    g_table = jnp.dot(class_hot.astype(F32).T, d_condition, precision=HIGHEST)
+    g_table = jnp.dot(class_hot.astype(F32).T, d_condition, precision=HIGHEST) / real_count
+    r_out, r_gate, r_up, r_down = [g.result(real_count) for g in (g_out, g_gate, g_up, g_down)]
+    at, late = g_qkv.z_terms[-1]
+    g_qkv.z_terms[-1] = (at, after(late, g_ada, g_table, r_out, r_gate, r_up, r_down))
+    r_qkv = g_qkv.result(real_count)
+
     return (
         deep(block_output),
         deep(d_tokens),
-        r_qkv / real_count,
-        r_out / real_count,
-        r_gate / real_count,
-        r_up / real_count,
-        r_down / real_count,
-        g_ada / real_count,
-        g_bias / real_count,
-        g_table / real_count,
-        gain_sum / real_count,
+        r_qkv,
+        r_out,
+        r_gate,
+        r_up,
+        r_down,
+        g_ada,
+        g_bias,
+        g_table,
+        gain_sum,
     )
 
 

time: 649 us -> 584 us (0.90)
  waiting for transfers between devices: 242 us -> 137 us
  Pallas kernels: 193 us -> 277 us
  other arithmetic: 72.7 us -> 24.8 us
  local copies, waits for them, and re-layouts: 63.1 us -> 40.2 us
  between operations: 3.7 us -> 16.4 us
  starting transfers between devices: 64.9 us -> 73.2 us
    ppermute x77 -> x73, waiting for transfers between devices: 242 us -> 109 us  [swap(): return lax.ppermute(value, ALL, pairs)]
    pallas_call x0 -> x36, Pallas kernels: none -> 90.3 us  [the longest x16 38.4 us: add_slabs(): pl.pallas_call(kernel, grid_spec=pltpu.PrefetchScalarGridSpec(num_scalar_...]
    all_gather x0 -> x1, waiting for transfers between devices: none -> 28.5 us  [on_device(): d_all = lax.all_gather(t.tie(d_modulation), ALL, axis=0, tiled=True)]
    add x20 -> x1, other arithmetic: 19.9 us -> 0.01 us  [on_device(): modulation = t.tie(mod_part).transpose(1, 0, 2).reshape(images, -1) + bias]
    convert_element_type x8 -> x3, other arithmetic: 17.1 us -> 1.41 us  [the longest x1 1.4 us: on_device(): d_mlp = split(flat((pieces[:, 5:6] * grad_y).astype(BF)), narrow)]
    another operation x11 -> x0, local copies, waits for them, and re-layouts: 14.4 us -> none  [the longest x6 8 us: head_tables(): return [jnp.tile(t, (1, H)) for t in (cosine, above, below)]]
    div x7 -> x2, other arithmetic: 10.6 us -> 1.66 us  [the longest x1 1.11 us: on_device(): g_bias = g_bias / real_count]
    ppermute x77 -> x73, starting transfers between devices: 64.9 us -> 73.1 us  [swap(): return lax.ppermute(value, ALL, pairs)]
  transfers between devices with their start and end apart: 77 -> 74, of which waited for: 41 -> 27; matrix products, arithmetic and copies ran while one was open for 14% -> 6% of each run, Pallas kernels for 24% -> 46%
where the time goes in v3:
time: 584 us; the launch traced here: 574 us
  Pallas kernels  277 us (47%)
  waiting for transfers between devices  137 us (23%)
  starting transfers between devices  73.2 us (13%)
  local copies, waits for them, and re-layouts  40.2 us (7%)
  other arithmetic  24.8 us (4%)
  between operations  16.4 us (3%)
    ppermute x73, waiting for transfers between devices, swap(): return lax.ppermute(value, ALL, pairs)  109 us
    ppermute x73, starting transfers between devices, swap(): return lax.ppermute(value, ALL, pairs)  73.1 us
    pallas_call x5, Pallas kernels, grad_stacks(): pl.pallas_call(kernel, grid=(-(-columns // chunk),), out_shape=[jax.Shape...  43.2 us
    pallas_call x16, Pallas kernels, add_slabs(): pl.pallas_call(kernel, grid_spec=pltpu.PrefetchScalarGridSpec(num_scalar_...  38.4 us
    pallas_call x10, Pallas kernels, add_stacks(): pl.pallas_call(kernel, grid=(half, shape[1] // deep), out_shape=jax.Shape...  32.8 us
    pallas_call x1, Pallas kernels, attention_backward(): pl.pallas_call(kernel, grid=(images,), out_shape=[jax.ShapeDtypeStruct((t...  31.1 us
    unnamed x211, local copies, waits for them, and re-layouts  30.9 us
    pallas_call x4, Pallas kernels, per_image(): pl.pallas_call(kernel, grid=(images,), out_shape=[jax.ShapeDtypeStruct((i...  29.9 us
  transfers between devices with their start and end apart: 74, of which 27 were waited for; matrix products, arithmetic and copies ran while one was open for 6% of the time, Pallas kernels for 46%

profile of v3, /device:TPU:0, one launch (start us, length us, event | category | flops | bytes accessed | tf_op | source)
XLA Modules:
  0.0 573.7 jit_solution(15695947765861100578)
XLA Ops:
  7.2 5.1 collective-permute-start.7
  19.7 6.2 %fusion.8 = (f32[256,1152]{1,0:T(8,128)}, f32[256,1152]{1,0:T(8,128)}, f32[256,1152]{1,0:T(8,128)}) fusion(f32[1152]{0:T(1024)S(1)} %fusion.29, s32[256]{0:T(256)S(1)} %get-tuple-element.285, s32[256]{0:T(256)S(1)} %get-tuple-element.286, pred[1152]{0:T(1024)(128)(4,1)S(1)} %get-tuple-element.287, pred[1152]{0:T(1024)(128)(4,1)S(1)} %get-tuple-element.288), kind=kLoop, calls=%fused_computation.14 | loop fusion | flops 1769472 | bytes 3547904 | tf_op jit(solution)/shard_map/jit(_where)/select_n | solution.py:38
  77.5 12.5 %collective-permute-done.17.refs_2_ = bf16[1,72,1536]{2,1,0:T(8,128)(2,1)S(1)} collective-permute-done((bf16[1,72,1536]{2,1,0:T(8,128)(2,1)S(1)}, bf16[1,72,1536]{2,1,0:T(8,128)(2,1)S(1)}, u32[]{:S(2)}, u32[]{:S(2)}) %collective-permute-start.17) | collective-permute-done | bytes 221216 | tf_op jit(solution)/shard_map/ppermute | solution.py:517
  92.2 5.6 collective-permute-done.15
  98.9 5.7 collective-permute-done.19
  120.4 8.7 %collective-permute-done.25.refs_1_ = bf16[4,72,1536]{2,1,0:T(8,128)(2,1)} collective-permute-done((bf16[4,72,1536]{2,1,0:T(8,128)(2,1)}, bf16[4,72,1536]{2,1,0:T(8,128)(2,1)}, u32[]{:S(2)}, u32[]{:S(2)}) %collective-permute-start.25) | collective-permute-done | bytes 884768 | tf_op jit(solution)/shard_map/ppermute | solution.py:517
  148.0 5.8 %collective-permute-done.29.refs_2_ = bf16[1,72,1536]{2,1,0:T(8,128)(2,1)} collective-permute-done((bf16[1,72,1536]{2,1,0:T(8,128)(2,1)}, bf16[1,72,1536]{2,1,0:T(8,128)(2,1)}, u32[]{:S(2)}, u32[]{:S(2)}) %collective-permute-start.29) | collective-permute-done | bytes 221216 | tf_op jit(solution)/shard_map/ppermute | solution.py:517
  156.0 11.1 %collective-permute-done.27 = bf16[8,72,1536]{2,1,0:T(8,128)(2,1)} collective-permute-done((bf16[8,72,1536]{2,1,0:T(8,128)(2,1)}, bf16[8,72,1536]{2,1,0:T(8,128)(2,1)}, u32[]{:S(2)}, u32[]{:S(2)}) %collective-permute-start.27) | collective-permute-done | bytes 1769504 | tf_op jit(solution)/shard_map/ppermute | solution.py:517
  169.7 9.0 %project.1 = (f32[512,1728]{1,0:T(8,128)S(1)}, f32[512,1728]{1,0:T(8,128)S(1)}) custom-call(bf16[512,1152]{1,0:T(8,128)(2,1)S(1)} %bitcast.93, bf16[2,1152,1728]{2,1,0:T(8,128)(2,1)} %bitcast.107, bf16[2,1152,1728]{2,1,0:T(8,128)(2,1)} %bitcast.108), custom_call_target="tpu_custom_call" | custom-call | flops 999999995904 | bytes 1 | tf_op jit(solution)/shard_map/project/pallas_call | solution.py:236
  189.8 14.4 %attention_forward.1 = (bf16[512,1152]{1,0:T(8,128)(2,1)S(1)}, bf16[512,1152]{1,0:T(8,128)(2,1)S(1)}, bf16[512,1152]{1,0:T(8,128)(2,1)S(1)}, bf16[512,1152]{1,0:T(8,128)(2,1)S(1)}) custom-call(f32[512,1728]{1,0:T(8,128)} %copy-done.35, f32[512,1728]{1,0:T(8,128)} %copy-done.36, f32[2,1152]{1,0:T(2,128)S(1)} %tile.10.refs_2_.refs_6_, ...), custom_call_target="tpu_custom_call" | custom-call | flops 999999995904 | bytes 1 | tf_op jit(solution)/shard_map/attention_forward/pallas_call | solution.py:138
  240.1 13.7 %gated.1 = (f32[512,3072]{1,0:T(8,128)S(1)}, f32[512,3072]{1,0:T(8,128)}, bf16[512,3072]{1,0:T(8,128)(2,1)S(1)}) custom-call(bf16[512,1152]{1,0:T(8,128)(2,1)S(1)} %get-tuple-element.175.a_ref, bf16[1152,3072]{1,0:T(8,128)(2,1)} %bitcast.113, bf16[1152,3072]{1,0:T(8,128)(2,1)} %bitcast.115), custom_call_target="tpu_custom_call" | custom-call | flops 999999995904 | bytes 1 | tf_op jit(solution)/shard_map/gated/pallas_call | solution.py:263
  258.6 10.8 %grad_stacks.5 = (bf16[4,4,192,576]{3,2,1,0:T(8,128)(2,1)}, bf16[4,4,192,576]{3,2,1,0:T(8,128)(2,1)}) custom-call(s32[3]{0:T(128)} %pad_add_fusion.1.at, bf16[512,3072]{1,0:T(8,128)(2,1)} %copy-done.47, bf16[512,576]{1,0:T(8,128)(2,1)} %get-tuple-element.197.refs_0_, bf16[512,576]{1,0:T(8,128)(2,1)} %get-tuple-element.198.refs_1_), custom_call_target="tpu_custom_call" | custom-call | flops 999999995904 | bytes 1 | tf_op jit(solution)/shard_map/grad_stacks/pallas_call | solution.py:478
  283.2 22.8 %gated_back.1 = (bf16[512,3072]{1,0:T(8,128)(2,1)}, bf16[512,3072]{1,0:T(8,128)(2,1)}, f32[512,1152]{1,0:T(8,128)S(1)}) custom-call(bf16[512,576]{1,0:T(8,128)(2,1)S(1)} %copy-done.7, bf16[512,576]{1,0:T(8,128)(2,1)S(1)} %copy-done.6, bf16[2,3072,576]{2,1,0:T(8,128)(2,1)} %bitcast.110, bf16[2,3072,576]{2,1,0:T(8,128)(2,1)} %bitcast.111, ...), custom_call_target="tpu_custom_call" | custom-call | flops 999999995904 | bytes 1 | tf_op jit(solution)/shard_map/gated_back/pallas_call | solution.py:306
  310.6 8.5 %grad_stacks.6 = (bf16[4,4,72,1536]{3,2,1,0:T(8,128)(2,1)}, bf16[4,4,72,1536]{3,2,1,0:T(8,128)(2,1)}) custom-call(s32[3]{0:T(128)} %pad_add_fusion.1.at, bf16[512,1152]{1,0:T(8,128)(2,1)} %copy-done.67, bf16[512,3072]{1,0:T(8,128)(2,1)} %get-tuple-element.205.refs_0_.refs_1_, bf16[512,3072]{1,0:T(8,128)(2,1)} %get-tuple-element.205.refs_0_.refs_1_), custom_call_target="tpu_custom_call" | custom-call | flops 999999995904 | bytes 1 | tf_op jit(solution)/shard_map/grad_stacks/pallas_call | solution.py:478
  331.8 6.4 %middle_back.1 = (f32[512,1152]{1,0:T(8,128)S(1)}, bf16[512,1152]{1,0:T(8,128)(2,1)S(1)}, f32[2,3,1152]{2,1,0:T(4,128)S(1)}, bf16[512,576]{1,0:T(8,128)(2,1)S(1)}, bf16[512,576]{1,0:T(8,128)(2,1)S(1)}) custom-call(f32[512,1152]{1,0:T(8,128)S(1)} %copy-done.50, f32[512,1152]{1,0:T(8,128)S(1)} %copy-done.53, f32[512,1152]{1,0:T(8,128)S(1)} %copy-done.56, ...), custom_call_target="tpu_custom_call" | custom-call | flops 999999995904 | bytes 1 | tf_op jit(solution)/shard_map/middle_back/pallas_call | solution.py:344
  343.1 8.4 %grad_stacks.7 = (bf16[4,4,72,1536]{3,2,1,0:T(8,128)(2,1)}, bf16[4,4,72,1536]{3,2,1,0:T(8,128)(2,1)}) custom-call(s32[3]{0:T(128)} %pad_add_fusion.1.at, bf16[512,1152]{1,0:T(8,128)(2,1)} %copy-done.67, bf16[512,3072]{1,0:T(8,128)(2,1)} %get-tuple-element.210.refs_0_.refs_1_, bf16[512,3072]{1,0:T(8,128)(2,1)} %get-tuple-element.210.refs_0_.refs_1_), custom_call_target="tpu_custom_call" | custom-call | flops 999999995904 | bytes 1 | tf_op jit(solution)/shard_map/grad_stacks/pallas_call | solution.py:478
  351.6 5.4 grad_stacks.8
  359.3 5.7 collective-permute-done.51.refs_2_
  375.7 31.1 %attention_backward.1 = (bf16[512,1728]{1,0:T(8,128)(2,1)}, bf16[512,1728]{1,0:T(8,128)(2,1)}, f32[2,2,1152]{2,1,0:T(2,128)}) custom-call(f32[512,1728]{1,0:T(8,128)} %copy-done.35, f32[512,1728]{1,0:T(8,128)} %copy-done.36, bf16[512,1152]{1,0:T(8,128)(2,1)} %copy-done.63, bf16[512,1152]{1,0:T(8,128)(2,1)} %copy-done.64, bf16[512,1152]{1,0:T(8,128)(2,1)} %copy-done.65, ...), custom_call_target="tpu_custom_call" | custom-call | flops 999999995904 | bytes 1 | tf_op jit(solution)/shard_map/attention_backward/pallas_call | solution.py:202
  424.1 10.1 %grad_stacks.9 = (bf16[4,4,72,1728]{3,2,1,0:T(8,128)(2,1)}, bf16[4,4,72,1728]{3,2,1,0:T(8,128)(2,1)}) custom-call(s32[3]{0:T(128)} %pad_add_fusion.1.at, bf16[512,1152]{1,0:T(8,128)(2,1)} %bitcast.94, bf16[512,1728]{1,0:T(8,128)(2,1)} %get-tuple-element.244.refs_0_, bf16[512,1728]{1,0:T(8,128)(2,1)} %get-tuple-element.245.refs_1_), custom_call_target="tpu_custom_call" | custom-call | flops 999999995904 | bytes 1 | tf_op jit(solution)/shard_map/grad_stacks/pallas_call | solution.py:478
  434.2 7.5 %collective-permute-done.59.refs_4_ = bf16[2,72,1536]{2,1,0:T(8,128)(2,1)} collective-permute-done((bf16[2,72,1536]{2,1,0:T(8,128)(2,1)}, bf16[2,72,1536]{2,1,0:T(8,128)(2,1)}, u32[]{:S(2)}, u32[]{:S(2)}) %collective-permute-start.59) | collective-permute-done | bytes 442400 | tf_op jit(solution)/shard_map/ppermute | solution.py:517
  458.0 9.8 %block_tail.1 = (bf16[512,1152]{1,0:T(8,128)(2,1)}, f32[2,1,1152]{2,1,0:T(1,128)S(1)}) custom-call(bf16[512,3072]{1,0:T(8,128)(2,1)S(1)} %copy-done.48, f32[512,1152]{1,0:T(8,128)S(1)} %copy-done.54, bf16[512,1152]{1,0:T(8,128)(2,1)S(1)} %bitcast.92, f32[2,6,1152]{2,1,0:T(8,128)S(1)} %copy-done.12, bf16[2,3072,576]{2,1,0:T(8,128)(2,1)} %bitcast.112, ...), custom_call_target="tpu_custom_call" | custom-call | flops 999999995904 | bytes 1 | tf_op jit(solution)/shard_map/block_tail/pallas_call | solution.py:344
  468.4 10.6 %block_head_back.1 = (bf16[512,1152]{1,0:T(8,128)(2,1)}, f32[2,2,1152]{2,1,0:T(2,128)S(1)}) custom-call(bf16[512,1728]{1,0:T(8,128)(2,1)S(1)} %copy-done.57, bf16[512,1728]{1,0:T(8,128)(2,1)S(1)} %copy-done.58, f32[512,1152]{1,0:T(8,128)} %copy-done.51, bf16[512,1152]{1,0:T(8,128)(2,1)S(1)} %bitcast.90, f32[2,6,1152]{2,1,0:T(8,128)S(1)} %copy-done.12, ...), custom_call_target="tpu_custom_call" | custom-call | flops 999999995904 | bytes 1 | tf_op jit(solution)/shard_map/block_head_back/pallas_call | solution.py:344
  522.6 28.5 %all-gather.3.cloned.1.call-done = bf16[32,2,8320]{2,1,0:T(2,128)(2,1)} async-done(((bf16[1,2,8320]{2,1,0:T(2,128)(2,1)}), bf16[32,2,8320]{2,1,0:T(2,128)(2,1)}) %all-gather.3.cloned.1.call-update) | async-done | bytes 1064976 | tf_op jit(solution)/shard_map/all_gather | solution.py:1010
  (479 shorter events, 294.2 us)
Async XLA Ops:
  7.2 543.8 %all-gather.3.cloned.1.call-start = ((), (), s32[]{:S(2)}) async-start(), calls=%async_computation | async-start | bytes 1098240 | tf_op jit(solution)/shard_map/all_gather | solution.py:1010
  7.2 36.9 %collective-permute-start.7 = (bf16[1,72,1728]{2,1,0:T(8,128)(2,1)}, bf16[1,72,1728]{2,1,0:T(8,128)(2,1)S(1)}, u32[]{:S(2)}, u32[]{:S(2)}) collective-permute-start(bf16[1,72,1728]{2,1,0:T(8,128)(2,1)} %bitcast.95), channel_id=1, source_target_pairs={{0,24},{1,25},{2,26},{3,27},{4,28},{5,29},{6,30},{7,31},{8,16},{9,... | collective-permute-start | bytes 746504 | tf_op jit(solution)/shard_map/ppermute | solution.py:517
  12.4 31.8 %collective-permute-start.6 = (bf16[1,72,1728]{2,1,0:T(8,128)(2,1)}, bf16[1,72,1728]{2,1,0:T(8,128)(2,1)S(1)}, u32[]{:S(2)}, u32[]{:S(2)}) collective-permute-start(bf16[1,72,1728]{2,1,0:T(8,128)(2,1)} %bitcast.96), channel_id=1, source_target_pairs={{0,16},{1,17},{2,18},{3,19},{4,20},{5,21},{6,22},{7,23},{8,24},{9,... | collective-permute-start | bytes 746504 | tf_op jit(solution)/shard_map/ppermute | solution.py:517
  12.4 31.8 %collective-permute-start.5 = (bf16[1,72,1728]{2,1,0:T(8,128)(2,1)}, bf16[1,72,1728]{2,1,0:T(8,128)(2,1)S(1)}, u32[]{:S(2)}, u32[]{:S(2)}) collective-permute-start(bf16[1,72,1728]{2,1,0:T(8,128)(2,1)} %bitcast.97), channel_id=1, source_target_pairs={{0,8},{1,9},{2,10},{3,11},{4,12},{5,13},{6,14},{7,15},{8,0},{9,1},... | collective-permute-start | bytes 746504 | tf_op jit(solution)/shard_map/ppermute | solution.py:517
  71.7 26.0 %collective-permute-start.15 = (bf16[8,72,1728]{2,1,0:T(8,128)(2,1)}, bf16[8,72,1728]{2,1,0:T(8,128)(2,1)}, u32[]{:S(2)}, u32[]{:S(2)}) collective-permute-start(bf16[8,72,1728]{2,1,0:T(8,128)(2,1)} %join.11), channel_id=1, source_target_pairs={{0,1},{1,0},{2,6},{3,7},{4,5},{5,4},{6,2},{7,3},{8,9},{9,8},{10,14... | collective-permute-start | bytes 5971976 | tf_op jit(solution)/shard_map/ppermute | solution.py:517
  137.0 30.2 %collective-permute-start.27 = (bf16[8,72,1536]{2,1,0:T(8,128)(2,1)}, bf16[8,72,1536]{2,1,0:T(8,128)(2,1)}, u32[]{:S(2)}, u32[]{:S(2)}) collective-permute-start(bf16[8,72,1536]{2,1,0:T(8,128)(2,1)} %join.15), channel_id=1, source_target_pairs={{0,1},{1,0},{2,6},{3,7},{4,5},{5,4},{6,2},{7,3},{8,9},{9,8},{10,14... | collective-permute-start | bytes 5308424 | tf_op jit(solution)/shard_map/ppermute | solution.py:517
  189.2 22.8 %collective-permute-start.36 = (bf16[8,72,1536]{2,1,0:T(8,128)(2,1)}, bf16[8,72,1536]{2,1,0:T(8,128)(2,1)}, u32[]{:S(2)}, u32[]{:S(2)}) collective-permute-start(bf16[8,72,1536]{2,1,0:T(8,128)(2,1)} %join.17), channel_id=1, source_target_pairs={{0,1},{1,0},{2,6},{3,7},{4,5},{5,4},{6,2},{7,3},{8,9},{9,8},{10,14... | collective-permute-start | bytes 5308424 | tf_op jit(solution)/shard_map/ppermute | solution.py:517
  232.2 25.8 %collective-permute-start.43 = (bf16[8,192,576]{2,1,0:T(8,128)(2,1)}, bf16[8,192,576]{2,1,0:T(8,128)(2,1)}, u32[]{:S(2)}, u32[]{:S(2)}) collective-permute-start(bf16[8,192,576]{2,1,0:T(8,128)(2,1)} %join.19), channel_id=1, source_target_pairs={{0,1},{1,0},{2,6},{3,7},{4,5},{5,4},{6,2},{7,3},{8,9},{9,8},{10,14... | collective-permute-start | bytes 5308424 | tf_op jit(solution)/shard_map/ppermute | solution.py:517
  282.2 24.9 %collective-permute-start.47 = (bf16[2,4,192,576]{3,2,1,0:T(8,128)(2,1)}, bf16[2,4,192,576]{3,2,1,0:T(8,128)(2,1)}, u32[]{:S(2)}, u32[]{:S(2)}) collective-permute-start(bf16[2,4,192,576]{3,2,1,0:T(8,128)(2,1)} %add_stacks.10), channel_id=1, source_target_pairs={{0,1},{1,0},{2,6},{3,7},{4,5},{5,4},{6,2},{7,3},{8,9},{9,8},{10,14... | collective-permute-start | bytes 5308424 | tf_op jit(solution)/shard_map/ppermute | solution.py:517
  326.5 30.5 %collective-permute-start.52 = (bf16[2,192,576]{2,1,0:T(8,128)(2,1)}, bf16[2,192,576]{2,1,0:T(8,128)(2,1)}, u32[]{:S(2)}, u32[]{:S(2)}) collective-permute-start(bf16[2,192,576]{2,1,0:T(8,128)(2,1)} %add_slabs.16), channel_id=1, source_target_pairs={{0,16},{1,17},{2,18},{3,19},{4,20},{5,21},{6,22},{7,23},{8,24},{9,... | collective-permute-start | bytes 1327112 | tf_op jit(solution)/shard_map/ppermute | solution.py:517
  342.1 22.8 %collective-permute-start.51 = (bf16[2,4,72,1536]{3,2,1,0:T(8,128)(2,1)}, bf16[2,4,72,1536]{3,2,1,0:T(8,128)(2,1)}, u32[]{:S(2)}, u32[]{:S(2)}) collective-permute-start(bf16[2,4,72,1536]{3,2,1,0:T(8,128)(2,1)} %add_stacks.12), channel_id=1, source_target_pairs={{0,1},{1,0},{2,6},{3,7},{4,5},{5,4},{6,2},{7,3},{8,9},{9,8},{10,14... | collective-permute-start | bytes 5308424 | tf_op jit(solution)/shard_map/ppermute | solution.py:517
  367.5 40.9 %collective-permute-start.56 = (bf16[1,192,576]{2,1,0:T(8,128)(2,1)}, bf16[1,192,576]{2,1,0:T(8,128)(2,1)}, u32[]{:S(2)}, u32[]{:S(2)}) collective-permute-start(bf16[1,192,576]{2,1,0:T(8,128)(2,1)} %add_slabs.17), channel_id=1, source_target_pairs={{0,8},{1,9},{2,10},{3,11},{4,12},{5,13},{6,14},{7,15},{8,0},{9,1},... | collective-permute-start | bytes 663560 | tf_op jit(solution)/shard_map/ppermute | solution.py:517
  369.5 44.2 %collective-permute-start.54 = (bf16[1,4,72,1536]{3,2,1,0:T(8,128)(2,1)}, bf16[1,4,72,1536]{3,2,1,0:T(8,128)(2,1)}, u32[]{:S(2)}, u32[]{:S(2)}) collective-permute-start(bf16[1,4,72,1536]{3,2,1,0:T(8,128)(2,1)} %add_stacks.15), channel_id=1, source_target_pairs={{0,4},{1,5},{2,3},{3,2},{4,0},{5,1},{6,7},{7,6},{8,12},{9,13},{10,... | collective-permute-start | bytes 2654216 | tf_op jit(solution)/shard_map/ppermute | solution.py:517
  370.5 45.5 %collective-permute-start.55 = (bf16[4,4,72,576]{3,2,1,0:T(8,128)(2,1)}, bf16[4,4,72,576]{3,2,1,0:T(8,128)(2,1)}, u32[]{:S(2)}, u32[]{:S(2)}) collective-permute-start(bf16[4,4,72,576]{3,2,1,0:T(8,128)(2,1)} %get-tuple-element.222), channel_id=1, source_target_pairs={{0,2},{1,3},{2,0},{3,1},{4,6},{5,7},{6,4},{7,5},{8,10},{9,11},{10,... | collective-permute-start | bytes 3981320 | tf_op jit(solution)/shard_map/ppermute | solution.py:517
  374.4 45.1 %collective-permute-start.53 = (bf16[2,4,72,1536]{3,2,1,0:T(8,128)(2,1)}, bf16[2,4,72,1536]{3,2,1,0:T(8,128)(2,1)}, u32[]{:S(2)}, u32[]{:S(2)}) collective-permute-start(bf16[2,4,72,1536]{3,2,1,0:T(8,128)(2,1)} %add_stacks.13), channel_id=1, source_target_pairs={{0,1},{1,0},{2,6},{3,7},{4,5},{5,4},{6,2},{7,3},{8,9},{9,8},{10,14... | collective-permute-start | bytes 5308424 | tf_op jit(solution)/shard_map/ppermute | solution.py:517
  420.0 23.9 %collective-permute-start.58 = (bf16[2,4,72,576]{3,2,1,0:T(8,128)(2,1)}, bf16[2,4,72,576]{3,2,1,0:T(8,128)(2,1)}, u32[]{:S(2)}, u32[]{:S(2)}) collective-permute-start(bf16[2,4,72,576]{3,2,1,0:T(8,128)(2,1)} %add_stacks.16), channel_id=1, source_target_pairs={{0,1},{1,0},{2,6},{3,7},{4,5},{5,4},{6,2},{7,3},{8,9},{9,8},{10,14... | collective-permute-start | bytes 1990664 | tf_op jit(solution)/shard_map/ppermute | solution.py:517
  423.1 22.9 %collective-permute-start.57 = (bf16[1,4,72,1536]{3,2,1,0:T(8,128)(2,1)}, bf16[1,4,72,1536]{3,2,1,0:T(8,128)(2,1)}, u32[]{:S(2)}, u32[]{:S(2)}) collective-permute-start(bf16[1,4,72,1536]{3,2,1,0:T(8,128)(2,1)} %add_stacks.14), channel_id=1, source_target_pairs={{0,4},{1,5},{2,3},{3,2},{4,0},{5,1},{6,7},{7,6},{8,12},{9,13},{10,... | collective-permute-start | bytes 2654216 | tf_op jit(solution)/shard_map/ppermute | solution.py:517
  448.7 31.2 %collective-permute-start.64 = (bf16[1,72,1536]{2,1,0:T(8,128)(2,1)}, bf16[1,72,1536]{2,1,0:T(8,128)(2,1)}, u32[]{:S(2)}, u32[]{:S(2)}) collective-permute-start(bf16[1,72,1536]{2,1,0:T(8,128)(2,1)} %add_slabs.20), channel_id=1, source_target_pairs={{0,8},{1,9},{2,10},{3,11},{4,12},{5,13},{6,14},{7,15},{8,0},{9,1},... | collective-permute-start | bytes 663560 | tf_op jit(solution)/shard_map/ppermute | solution.py:517
  448.7 36.2 %collective-permute-start.62 = (bf16[1,4,72,576]{3,2,1,0:T(8,128)(2,1)}, bf16[1,4,72,576]{3,2,1,0:T(8,128)(2,1)}, u32[]{:S(2)}, u32[]{:S(2)}) collective-permute-start(bf16[1,4,72,576]{3,2,1,0:T(8,128)(2,1)} %add_stacks.18), channel_id=1, source_target_pairs={{0,4},{1,5},{2,3},{3,2},{4,0},{5,1},{6,7},{7,6},{8,12},{9,13},{10,... | collective-permute-start | bytes 995336 | tf_op jit(solution)/shard_map/ppermute | solution.py:517
  449.7 37.1 %collective-permute-start.63 = (bf16[2,72,1536]{2,1,0:T(8,128)(2,1)}, bf16[2,72,1536]{2,1,0:T(8,128)(2,1)}, u32[]{:S(2)}, u32[]{:S(2)}) collective-permute-start(bf16[2,72,1536]{2,1,0:T(8,128)(2,1)} %add_slabs.19), channel_id=1, source_target_pairs={{0,16},{1,17},{2,18},{3,19},{4,20},{5,21},{6,22},{7,23},{8,24},{9,... | collective-permute-start | bytes 1327112 | tf_op jit(solution)/shard_map/ppermute | solution.py:517
  456.7 32.7 %collective-permute-start.61 = (bf16[2,4,72,1728]{3,2,1,0:T(8,128)(2,1)}, bf16[2,4,72,1728]{3,2,1,0:T(8,128)(2,1)}, u32[]{:S(2)}, u32[]{:S(2)}) collective-permute-start(bf16[2,4,72,1728]{3,2,1,0:T(8,128)(2,1)} %add_stacks.17), channel_id=1, source_target_pairs={{0,1},{1,0},{2,6},{3,7},{4,5},{5,4},{6,2},{7,3},{8,9},{9,8},{10,14... | collective-permute-start | bytes 5971976 | tf_op jit(solution)/shard_map/ppermute | solution.py:517
  515.8 45.3 %collective-permute-start.68 = (bf16[1,72,1728]{2,1,0:T(8,128)(2,1)}, bf16[1,72,1728]{2,1,0:T(8,128)(2,1)}, u32[]{:S(2)}, u32[]{:S(2)}) collective-permute-start(bf16[1,72,1728]{2,1,0:T(8,128)(2,1)} %add_slabs.21), channel_id=1, source_target_pairs={{0,24},{1,25},{2,26},{3,27},{4,28},{5,29},{6,30},{7,31},{8,16},{9,... | collective-permute-start | bytes 746504 | tf_op jit(solution)/shard_map/ppermute | solution.py:517
  517.7 43.5 %collective-permute-start.69 = (bf16[1,72,1728]{2,1,0:T(8,128)(2,1)}, bf16[1,72,1728]{2,1,0:T(8,128)(2,1)}, u32[]{:S(2)}, u32[]{:S(2)}) collective-permute-start(bf16[1,72,1728]{2,1,0:T(8,128)(2,1)} %add_slabs.24), channel_id=1, source_target_pairs={{0,16},{1,17},{2,18},{3,19},{4,20},{5,21},{6,22},{7,23},{8,24},{9,... | collective-permute-start | bytes 746504 | tf_op jit(solution)/shard_map/ppermute | solution.py:517
  519.2 41.9 %collective-permute-start.70 = (bf16[1,72,1728]{2,1,0:T(8,128)(2,1)}, bf16[1,72,1728]{2,1,0:T(8,128)(2,1)}, u32[]{:S(2)}, u32[]{:S(2)}) collective-permute-start(bf16[1,72,1728]{2,1,0:T(8,128)(2,1)} %add_slabs.25), channel_id=1, source_target_pairs={{0,8},{1,9},{2,10},{3,11},{4,12},{5,13},{6,14},{7,15},{8,0},{9,1},... | collective-permute-start | bytes 746504 | tf_op jit(solution)/shard_map/ppermute | solution.py:517
  (154 other events, 1686.4 us)
Sparse Core Ops, SparseCore 0:
  495.3 55.6 all-gather.2

commit v4 on v3

--- a/solution.py
+++ b/solution.py
@@ -18,6 +18,7 @@
 BF = jnp.bfloat16
 F32 = jnp.float32
 LONG = pl.CostEstimate(flops=10**12, bytes_accessed=1, transcendentals=0)
+SHORT = pl.CostEstimate(flops=1, bytes_accessed=1, transcendentals=0)
 
 
 def layer_norm(values):
@@ -97,9 +98,17 @@
     return lax.dot_general(a, b, (dims, ((), ())), preferred_element_type=F32)
 
 
-def softmax_of(queries, keys, head):
+def only_turned(values, head):
     first, last = window(head)
-    scores = mm(queries[:, first:last], only(keys, head), ((1,), (1,))) * (HD ** (-0.5))
+    part = values[first:last, :]
+    row = first + lax.broadcasted_iota(jnp.int32, (last - first, 1), 0)
+    mine = ((row >= head * HD) & (row < (head + 1) * HD)).astype(values.dtype)
+    return part * mine
+
+
+def softmax_of(queries, keys_turned, head):
+    first, last = window(head)
+    scores = mm(only(queries, head), keys_turned[first:last, :], ((1,), (0,))) * (HD ** (-0.5))
     exponent = jnp.exp(scores - jnp.max(scores, axis=1, keepdims=True))
     return exponent / jnp.sum(exponent, axis=1, keepdims=True)
 
@@ -110,7 +119,7 @@
 
     def kernel(*refs):
         parts, refs = refs[:blocks], refs[blocks:]
-        gain, cosine, above, below, sums_ref, q_ref, k_ref, v_ref, mixed_ref = refs
+        gain, cosine, above, below, sums_ref, q_ref, k_ref, v_ref, mixed_ref, k_turned = refs
         whole = jnp.concatenate([p[...] for p in parts], axis=1)
         sums_here = sums_ref[...]
         for i, ref in enumerate((q_ref, k_ref)):
@@ -123,9 +132,10 @@
         def store(first, value):
             mixed_ref[:, first : first + 128] = value.astype(BF)
 
+        k_turned[...] = k_ref[...].T
         mixed = Tiles(store)
         for head in range(H):
-            attention = softmax_of(q_ref, k_ref, head).astype(BF)
+            attention = softmax_of(q_ref, k_turned, head).astype(BF)
             mixed.add(head, mm(attention, only(v_ref, head), ((1,), (0,))))
 
     def rows(n):
@@ -141,7 +151,8 @@
         out_shape=[out] * 4,
         in_specs=[rows(p.shape[1]) for p in packed] + [all_of(a) for a in (gains, *tables, sums)],
         out_specs=[rows(width)] * 4,
-        compiler_params=pltpu.CompilerParams(vmem_limit_bytes=48 * 2**20),
+        scratch_shapes=[pltpu.VMEM((width, length), BF)],
+        compiler_params=pltpu.CompilerParams(vmem_limit_bytes=60 * 2**20),
         cost_estimate=LONG,
         name="attention_forward",
     )(*packed, gains, *tables, sums)
@@ -155,7 +166,8 @@
     def kernel(*refs):
         parts, refs = refs[:blocks], refs[blocks:]
         q_ref, k_ref, v_ref, d_ref, gain, cosine, above, below, sums_ref = refs[:9]
-        outs, (gain_ref, d_q, d_k, d_v) = refs[9 : 9 + blocks], refs[9 + blocks :]
+        outs, refs = refs[9 : 9 + blocks], refs[9 + blocks :]
+        gain_ref, d_q_turned, d_k, d_v, q_turned, k_turned, d_turned = refs
 
         def store_to(ref):
             def store(first, value):
@@ -163,27 +175,35 @@
 
             return store
 
-        all_q, all_k, all_v = [Tiles(store_to(ref)) for ref in (d_q, d_k, d_v)]
+        for ref, turned in ((q_ref, q_turned), (k_ref, k_turned), (d_ref, d_turned)):
+            turned[...] = ref[...].T
+        all_k, all_v = [Tiles(store_to(ref)) for ref in (d_k, d_v)]
+        rows_q = {}
         for head in range(H):
             first, last = window(head)
-            q_here, k_here, d_here = [only(ref, head) for ref in (q_ref, k_ref, d_ref)]
-            scores = mm(k_here, q_ref[:, first:last], ((1,), (1,))) * (HD ** (-0.5))
+            scores = mm(only(k_ref, head), q_turned[first:last, :], ((1,), (0,))) * (HD ** (-0.5))
             exponent = jnp.exp(scores - jnp.max(scores, axis=0, keepdims=True))
             soft = exponent / jnp.sum(exponent, axis=0, keepdims=True)
-            all_v.add(head, mm(soft.astype(BF), d_here, ((1,), (0,))))
-            d_soft = mm(v_ref[:, first:last], d_here, ((1,), (1,)))
+            all_v.add(head, mm(soft.astype(BF), only(d_ref, head), ((1,), (0,))))
+            d_soft = mm(only(v_ref, head), d_turned[first:last, :], ((1,), (0,)))
             inner = jnp.sum(soft * d_soft, axis=0, keepdims=True)
             d_scores = (soft * (d_soft - inner) * (HD ** (-0.5))).astype(BF)
-            all_k.add(head, mm(d_scores, q_here, ((1,), (0,))))
-            all_q.add(head, mm(d_scores, k_here, ((0,), (0,))))
+            all_k.add(head, mm(d_scores, only(q_ref, head), ((1,), (0,))))
+            part = mm(only_turned(k_turned, head), d_scores, ((1,), (0,)))
+            for tile in range(first // 128, last // 128):
+                rows = part[tile * 128 - first : tile * 128 - first + 128]
+                rows_q[tile] = rows_q[tile] + rows if tile in rows_q else rows
+            for tile in sorted(rows_q):
+                if tile < (head + 1) * HD // 128 or head == H - 1:
+                    d_q_turned[tile * 128 : tile * 128 + 128, :] = rows_q.pop(tile)
         whole = jnp.concatenate([p[...] for p in parts], axis=1)
         sums_here = sums_ref[...]
         done = []
-        for i, ref in enumerate((d_q, d_k)):
+        for i, value in enumerate((d_q_turned[...].T, d_k[...])):
             raw = whole[:, i * width : (i + 1) * width]
             inverse = lax.rsqrt(head_mean(raw * raw, sums_here) + EPSILON)
             normed = raw * inverse
-            scaled = shifted(ref[...], cosine[...], above[...], below[...], -1.0)
+            scaled = shifted(value, cosine[...], above[...], below[...], -1.0)
             gain_ref[0, i : i + 1, :] = jnp.sum(scaled * normed, axis=0, keepdims=True)
             incoming = scaled * gain[i : i + 1, :]
             mean = head_mean(incoming * normed, sums_here)
@@ -208,8 +228,10 @@
         + [rows(width)] * 4
         + [all_of(a) for a in (gains, *tables, sums)],
         out_specs=[rows(block)] * blocks + [pl.BlockSpec((1, 2, width), lambda i: (i, 0, 0))],
-        scratch_shapes=[pltpu.VMEM((length, width), F32)] * 3,
-        compiler_params=pltpu.CompilerParams(vmem_limit_bytes=56 * 2**20),
+        scratch_shapes=[pltpu.VMEM((width, length), F32)]
+        + [pltpu.VMEM((length, width), F32)] * 2
+        + [pltpu.VMEM((width, length), BF)] * 3,
+        compiler_params=pltpu.CompilerParams(vmem_limit_bytes=60 * 2**20),
         cost_estimate=LONG,
         name="attention_backward",
     )(*packed, queries, keys, values, d_mixed, gains, *tables, sums)
@@ -240,7 +262,7 @@
         in_specs=[whole_block(a)]
         + [pl.BlockSpec((None, depth, chunk), lambda i, j=j: (j, 0, i)) for j in range(count)],
         out_specs=[pl.BlockSpec((tokens, chunk), lambda i: (0, i))] * count,
-        compiler_params=pltpu.CompilerParams(vmem_limit_bytes=40 * 2**20),
+        compiler_params=pltpu.CompilerParams(vmem_limit_bytes=60 * 2**20),
         cost_estimate=LONG,
         name="project",
     )(a, *[blocks] * count)
@@ -266,7 +288,7 @@
         out_shape=[jax.ShapeDtypeStruct((tokens, columns), t) for t in (F32, F32, BF)],
         in_specs=[whole_block(a), weight, weight],
         out_specs=[out] * 3,
-        compiler_params=pltpu.CompilerParams(vmem_limit_bytes=40 * 2**20),
+        compiler_params=pltpu.CompilerParams(vmem_limit_bytes=60 * 2**20),
         cost_estimate=LONG,
         name="gated",
     )(a, w_gate, w_up)
@@ -312,7 +334,7 @@
         + [pl.BlockSpec((None, chunk, width), lambda i, j=j: (j, i, 0)) for j in range(count)]
         + [token, token, weight, weight],
         out_specs=[token, token, pl.BlockSpec((tokens, depth), lambda i: (0, 0))],
-        compiler_params=pltpu.CompilerParams(vmem_limit_bytes=48 * 2**20),
+        compiler_params=pltpu.CompilerParams(vmem_limit_bytes=60 * 2**20),
         cost_estimate=LONG,
         name="gated_back",
     )(*d_parts, *[down] * count, gate_val, up_val, w_gate, w_up)
@@ -347,7 +369,7 @@
         out_shape=[jax.ShapeDtypeStruct((images * rows, *rest), t) for rows, rest, t in outs],
         in_specs=in_specs,
         out_specs=[spec(rows, rest) for rows, rest, _ in outs],
-        compiler_params=pltpu.CompilerParams(vmem_limit_bytes=vmem * 2**20),
+        compiler_params=pltpu.CompilerParams(vmem_limit_bytes=60 * 2**20),
         cost_estimate=LONG,
         name=name,
     )(*args)
@@ -489,7 +511,7 @@
             pltpu.VMEM((features, tokens), BF),
             pltpu.VMEM((count, 4 * z, rows, chunk), BF),
         ],
-        compiler_params=pltpu.CompilerParams(vmem_limit_bytes=56 * 2**20),
+        compiler_params=pltpu.CompilerParams(vmem_limit_bytes=60 * 2**20),
         cost_estimate=LONG,
         name="grad_stacks",
     )(at, a, *(parts * count if joined else parts))
@@ -630,7 +652,7 @@
             pltpu.SemaphoreType.DMA((4 * half * z,)),
             pltpu.SemaphoreType.DMA,
         ],
-        compiler_params=pltpu.CompilerParams(vmem_limit_bytes=24 * 2**20),
+        compiler_params=pltpu.CompilerParams(vmem_limit_bytes=60 * 2**20),
         cost_estimate=LONG,
         name="assemble",
     )(at, *parts)
@@ -652,8 +674,8 @@
         out_shape=shape,
         in_specs=[whole_block(p) for p in parts],
         out_specs=whole_block(shape),
-        compiler_params=pltpu.CompilerParams(vmem_limit_bytes=24 * 2**20),
-        cost_estimate=LONG,
+        compiler_params=pltpu.CompilerParams(vmem_limit_bytes=60 * 2**20),
+        cost_estimate=SHORT,
         name="join",
     )(*parts)
 
@@ -675,8 +697,8 @@
         out_shape=jax.ShapeDtypeStruct(shape, BF),
         in_specs=[pl.BlockSpec(block, lambda i, j: (half + i, j, 0, 0))] * len(terms),
         out_specs=pl.BlockSpec(block, lambda i, j: (i, j, 0, 0)),
-        compiler_params=pltpu.CompilerParams(vmem_limit_bytes=24 * 2**20),
-        cost_estimate=LONG,
+        compiler_params=pltpu.CompilerParams(vmem_limit_bytes=60 * 2**20),
+        cost_estimate=SHORT,
         name="add_stacks",
     )(*terms)
 
@@ -717,8 +739,8 @@
             out_specs=pl.BlockSpec((1, rows, columns), lambda i, at: (i, 0, 0)),
         ),
         out_shape=jax.ShapeDtypeStruct((count, rows, columns), kind),
-        compiler_params=pltpu.CompilerParams(vmem_limit_bytes=24 * 2**20),
-        cost_estimate=LONG,
+        compiler_params=pltpu.CompilerParams(vmem_limit_bytes=60 * 2**20),
+        cost_estimate=SHORT,
         name="add_slabs",
     )(places.at_z.astype(jnp.int32).reshape(1), *args)
 
@@ -814,6 +836,7 @@
             self.z_terms.append((0, self.slots.send(send, lambda core: (d, 0, 0, 0))))
 
     def result(self, divisor):
+        divisor = self.slots.tie(divisor)
         return add_slabs(self.places, self.terms, self.z_terms, 0, 1, divisor)[0]
 
 
@@ -955,17 +978,17 @@
     g_down.last()
     g_gate = Scatter(t, mlp_in, [t.tie(d_gate)])
     g_gate.cores(t.follow)
-    t.next()
+    d_hidden, d_mixed, sums_b, *d_attn = middle_back(
+        t.tie(d_mlp_in), hidden_one, attn_out, flat(cotangent), pieces, out_b, image_counts, images
+    )
+    t.next(d_mixed)
 
     g_gate.first()
     g_down.step_z(*z_down)
     g_up = Scatter(t, mlp_in, [t.tie(d_up)])
     g_up.cores(t.follow)
-    d_hidden, d_mixed, sums_b, *d_attn = middle_back(
-        t.tie(d_mlp_in), hidden_one, attn_out, flat(cotangent), pieces, out_b, image_counts, images
-    )
-    g_out = Scatter(t, mixed, d_attn)
-    t.next(g_out.to_core, d_mixed)
+    g_out = Scatter(t, mixed, t.tie(d_attn))
+    t.next(g_out.to_core)
 
     g_gate.last()
     g_up.first()
@@ -981,7 +1004,16 @@
     g_gate.step_z(*z_down)
     g_qkv = Scatter(t, attn_in, t.tie(d_packed))
     g_qkv.cores(t.follow)
-    t.next()
+    block_output, sums_gate = block_tail(
+        after(hidden_mid, g_qkv.to_core),
+        down_b,
+        hidden_one,
+        flat(cotangent),
+        pieces,
+        image_counts,
+        images,
+    )
+    t.next(sums_gate)
 
     g_qkv.first()
     g_out.last()
@@ -989,9 +1021,6 @@
     g_gate.step_z(*z_low)
     d_tokens, sums_a = block_head_back(
         t.tie(d_packed), d_hidden, flat(inputs), pieces, qkv_b, images
-    )
-    block_output, sums_gate = block_tail(
-        t.tie(hidden_mid), down_b, hidden_one, flat(cotangent), pieces, image_counts, images
     )
     grad_gains = gain_terms.sum(0).reshape(2, H, HD).sum(1).reshape(1, -1)
     gains_high = grad_gains.astype(BF)
@@ -1000,18 +1029,20 @@
     grad_gains = jnp.concatenate([gains_high, gains_low, rest], axis=0)
     d_modulation = jnp.concatenate([sums_a, sums_b[:, 2:], sums_b[:, :2], sums_gate], axis=1)
     d_modulation = d_modulation.astype(BF).reshape(images, -1)
-    rest = jnp.zeros((images, 65 * 128 - 6 * width - 2 * HD), BF)
-    d_modulation = jnp.concatenate([d_modulation, grad_gains, rest], axis=1)
+    d_modulation = jnp.concatenate([d_modulation, grad_gains], axis=1)
     t.next(d_modulation)
 
     g_qkv.last()
     g_up.step_z(*z_low)
     g_out.step_z(*z_down)
-    d_all = lax.all_gather(t.tie(d_modulation), ALL, axis=0, tiled=True)
-    t.next()
+    d_all = places.open_small(t.tie(d_modulation))
+    d_all = places.gather_bits(d_all, bits[: len(places.z_bits)])
+    t.next(d_all)
 
     g_qkv.direct_z()
     g_out.step_z(*z_low)
+    d_all = places.gather_bits(t.tie(d_all), bits[len(places.z_bits) :])
+    d_all = d_all.reshape(wide * narrow * images, -1)
     gain_sum = d_all[:, 6 * width : 6 * width + 2 * HD].astype(F32)
     gain_sum = jnp.sum(gain_sum, axis=0).reshape(2, HD) / real_count
     d_mod = d_all[:, : 6 * width]

time: 584 us -> 561 us (0.961)
  Pallas kernels: 277 us -> 307 us
  local copies, waits for them, and re-layouts: 40.2 us -> 12.6 us
  waiting for transfers between devices: 137 us -> 112 us
  between operations: 16.4 us -> 2.8 us
  starting transfers between devices: 73.2 us -> 82.1 us
  other arithmetic: 24.8 us -> 30.9 us
    all_gather x1 -> x0, waiting for transfers between devices: 28.5 us -> none  [on_device(): d_all = lax.all_gather(t.tie(d_modulation), ALL, axis=0, tiled=True)]
    unnamed x211 -> x114, local copies, waits for them, and re-layouts: 30.9 us -> 6.39 us
    pallas_call x5, Pallas kernels: 22.6 us -> 33.6 us  [assemble(): pl.pallas_call(kernel, out_shape=jax.ShapeDtypeStruct(shape, BF), in_spec...]
    pallas_call x4, Pallas kernels: 29.9 us -> 39.1 us  [per_image(): pl.pallas_call(kernel, grid=(images,), out_shape=[jax.ShapeDtypeStruct((i...]
    ppermute x73 -> x78, starting transfers between devices: 73.1 us -> 82.1 us  [swap(): return lax.ppermute(value, ALL, pairs)]
    ppermute x73 -> x78, waiting for transfers between devices: 109 us -> 112 us  [swap(): return lax.ppermute(value, ALL, pairs)]
  transfers between devices with their start and end apart: 74 -> 78, of which waited for: 27 -> 32; matrix products, arithmetic and copies ran while one was open for 6% -> 7% of each run, Pallas kernels for 46% -> 51%
where the time goes in v4:
time: 561 us; the launch traced here: 551 us
  Pallas kernels  307 us (55%)
  waiting for transfers between devices  112 us (20%)
  starting transfers between devices  82.1 us (15%)
  other arithmetic  30.9 us (6%)
  local copies, waits for them, and re-layouts  12.6 us (2%)
    ppermute x78, waiting for transfers between devices, swap(): return lax.ppermute(value, ALL, pairs)  112 us
    ppermute x78, starting transfers between devices, swap(): return lax.ppermute(value, ALL, pairs)  82.1 us
    pallas_call x5, Pallas kernels, grad_stacks(): pl.pallas_call(kernel, grid=(-(-columns // chunk),), out_shape=[jax.Shape...  43.2 us
    pallas_call x4, Pallas kernels, per_image(): pl.pallas_call(kernel, grid=(images,), out_shape=[jax.ShapeDtypeStruct((i...  39.1 us
    pallas_call x16, Pallas kernels, add_slabs(): pl.pallas_call(kernel, grid_spec=pltpu.PrefetchScalarGridSpec(num_scalar_...  38.4 us
    pallas_call x5, Pallas kernels, assemble(): pl.pallas_call(kernel, out_shape=jax.ShapeDtypeStruct(shape, BF), in_spec...  33.6 us
    pallas_call x10, Pallas kernels, add_stacks(): pl.pallas_call(kernel, grid=(half, shape[1] // deep), out_shape=jax.Shape...  33.3 us
    pallas_call x1, Pallas kernels, attention_backward(): pl.pallas_call(kernel, grid=(images,), out_shape=[jax.ShapeDtypeStruct((t...  29.3 us
  transfers between devices with their start and end apart: 78, of which 32 were waited for; matrix products, arithmetic and copies ran while one was open for 7% of the time, Pallas kernels for 51%

profile of v4, /device:TPU:0, one launch (start us, length us, event | category | flops | bytes accessed | tf_op | source)
XLA Modules:
  0.0 551.1 jit_solution(18341724009755146916)
XLA Ops:
  12.1 6.1 %fusion.8 = (f32[256,1152]{1,0:T(8,128)}, f32[256,1152]{1,0:T(8,128)}, f32[256,1152]{1,0:T(8,128)}) fusion(f32[1152]{0:T(1024)S(1)} %fusion.29, s32[256]{0:T(256)S(1)} %get-tuple-element.303, s32[256]{0:T(256)S(1)} %get-tuple-element.304, pred[1152]{0:T(1024)(128)(4,1)S(1)} %get-tuple-element.305, pred[1152]{0:T(1024)(128)(4,1)S(1)} %get-tuple-element.306), kind=kLoop, calls=%fused_computation.14 | loop fusion | flops 1769472 | bytes 3547904 | tf_op jit(solution)/shard_map/jit(_where)/select_n | solution.py:39
  72.6 12.2 %collective-permute-done.17.refs_2_ = bf16[1,72,1536]{2,1,0:T(8,128)(2,1)} collective-permute-done((bf16[1,72,1536]{2,1,0:T(8,128)(2,1)S(1)}, bf16[1,72,1536]{2,1,0:T(8,128)(2,1)}, u32[]{:S(2)}, u32[]{:S(2)}) %collective-permute-start.17) | collective-permute-done | bytes 221216 | tf_op jit(solution)/shard_map/ppermute | solution.py:539
  116.9 6.8 %collective-permute-done.25.refs_1_ = bf16[4,72,1536]{2,1,0:T(8,128)(2,1)} collective-permute-done((bf16[4,72,1536]{2,1,0:T(8,128)(2,1)}, bf16[4,72,1536]{2,1,0:T(8,128)(2,1)}, u32[]{:S(2)}, u32[]{:S(2)}) %collective-permute-start.25) | collective-permute-done | bytes 884768 | tf_op jit(solution)/shard_map/ppermute | solution.py:539
  133.5 7.8 %assemble.5 = bf16[2,4,2,2,72,1728]{5,4,3,2,1,0:T(8,128)(2,1)} custom-call(s32[4]{0:T(128)} %pad_add_fusion.at, bf16[2,4,72,1728]{3,2,1,0:T(8,128)(2,1)} %bitcast.94, bf16[2,4,72,1728]{3,2,1,0:T(8,128)(2,1)} %bitcast.13.s1, bf16[2,4,72,1728]{3,2,1,0:T(8,128)(2,1)} %collective-permute-done.22.t0, bf16[2,4,72,1728]{3,2,1,0:T(8,128)(2,1)} %collective-permute-done.23.t1), custom_call_target="tpu_custom_call" | custom-call | flops 999999995904 | bytes 1 | tf_op jit(solution)/shard_map/assemble/pallas_call | solution.py:645
  150.8 10.7 %collective-permute-done.27 = bf16[8,72,1536]{2,1,0:T(8,128)(2,1)} collective-permute-done((bf16[8,72,1536]{2,1,0:T(8,128)(2,1)}, bf16[8,72,1536]{2,1,0:T(8,128)(2,1)}, u32[]{:S(2)}, u32[]{:S(2)}) %collective-permute-start.27) | collective-permute-done | bytes 1769504 | tf_op jit(solution)/shard_map/ppermute | solution.py:539
  164.1 10.4 %project.1 = (f32[512,1728]{1,0:T(8,128)}, f32[512,1728]{1,0:T(8,128)}) custom-call(bf16[512,1152]{1,0:T(8,128)(2,1)} %bitcast.98, bf16[2,1152,1728]{2,1,0:T(8,128)(2,1)} %bitcast.128, bf16[2,1152,1728]{2,1,0:T(8,128)(2,1)} %bitcast.129), custom_call_target="tpu_custom_call" | custom-call | flops 999999995904 | bytes 1 | tf_op jit(solution)/shard_map/project/pallas_call | solution.py:258
  183.2 15.4 %attention_forward.1 = (bf16[512,1152]{1,0:T(8,128)(2,1)}, bf16[512,1152]{1,0:T(8,128)(2,1)}, bf16[512,1152]{1,0:T(8,128)(2,1)}, bf16[512,1152]{1,0:T(8,128)(2,1)}) custom-call(f32[512,1728]{1,0:T(8,128)} %get-tuple-element.169.refs_0_, f32[512,1728]{1,0:T(8,128)} %get-tuple-element.170.refs_1_, f32[2,1152]{1,0:T(2,128)} %tile.10.refs_2_.refs_6_, ...), custom_call_target="tpu_custom_call" | custom-call | flops 999999995904 | bytes 1 | tf_op jit(solution)/shard_map/attention_forward/pallas_call | solution.py:148
  212.0 6.9 %attention_tail.1 = (f32[512,1152]{1,0:T(8,128)}, f32[512,1152]{1,0:T(8,128)}, bf16[512,1152]{1,0:T(8,128)(2,1)}) custom-call(bf16[512,1152]{1,0:T(8,128)(2,1)} %get-tuple-element.171.mixed_ref.a_ref, bf16[512,1152]{1,0:T(8,128)(2,1)} %bitcast.91, f32[2,6,1152]{2,1,0:T(8,128)} %broadcast_add_fusion.piece.refs_4_, bf16[2,1152,576]{2,1,0:T(8,128)(2,1)} %bitcast.138), custom_call_target="tpu_custom_call" | custom-call | flops 999999995904 | bytes 1 | tf_op jit(solution)/shard_map/attention_tail/pallas_call | solution.py:366
  218.9 6.9 %assemble.7 = bf16[4,2,2,72,3072]{4,3,2,1,0:T(8,128)(2,1)} custom-call(s32[4]{0:T(128)} %pad_add_fusion.at, bf16[2,4,72,1536]{3,2,1,0:T(8,128)(2,1)} %bitcast.30.s0, bf16[2,4,72,1536]{3,2,1,0:T(8,128)(2,1)} %bitcast.31.s1, bf16[2,4,72,1536]{3,2,1,0:T(8,128)(2,1)} %collective-permute-done.33.t0, bf16[2,4,72,1536]{3,2,1,0:T(8,128)(2,1)} %collective-permute-done.34.t1), custom_call_target="tpu_custom_call" | custom-call | flops 999999995904 | bytes 1 | tf_op jit(solution)/shard_map/assemble/pallas_call | solution.py:645
  229.4 7.0 %assemble.8 = bf16[4,2,2,72,3072]{4,3,2,1,0:T(8,128)(2,1)} custom-call(s32[4]{0:T(128)} %pad_add_fusion.at, bf16[2,4,72,1536]{3,2,1,0:T(8,128)(2,1)} %bitcast.36.s0, bf16[2,4,72,1536]{3,2,1,0:T(8,128)(2,1)} %bitcast.37.s1, bf16[2,4,72,1536]{3,2,1,0:T(8,128)(2,1)} %collective-permute-done.40.t0, bf16[2,4,72,1536]{3,2,1,0:T(8,128)(2,1)} %collective-permute-done.41.t1), custom_call_target="tpu_custom_call" | custom-call | flops 999999995904 | bytes 1 | tf_op jit(solution)/shard_map/assemble/pallas_call | solution.py:645
  236.4 15.3 %gated.1 = (f32[512,3072]{1,0:T(8,128)}, f32[512,3072]{1,0:T(8,128)}, bf16[512,3072]{1,0:T(8,128)(2,1)}) custom-call(bf16[512,1152]{1,0:T(8,128)(2,1)} %get-tuple-element.179.a_ref, bf16[1152,3072]{1,0:T(8,128)(2,1)} %bitcast.134, bf16[1152,3072]{1,0:T(8,128)(2,1)} %bitcast.136), custom_call_target="tpu_custom_call" | custom-call | flops 999999995904 | bytes 1 | tf_op jit(solution)/shard_map/gated/pallas_call | solution.py:285
  254.3 10.7 %grad_stacks.5 = (bf16[4,4,192,576]{3,2,1,0:T(8,128)(2,1)}, bf16[4,4,192,576]{3,2,1,0:T(8,128)(2,1)}) custom-call(s32[3]{0:T(128)} %pad_add_fusion.1.at, bf16[512,3072]{1,0:T(8,128)(2,1)} %get-tuple-element.243.a_ref.mid_ref, bf16[512,576]{1,0:T(8,128)(2,1)} %get-tuple-element.204.refs_0_, bf16[512,576]{1,0:T(8,128)(2,1)} %get-tuple-element.205.refs_1_), custom_call_target="tpu_custom_call" | custom-call | flops 999999995904 | bytes 1 | tf_op jit(solution)/shard_map/grad_stacks/pallas_call | solution.py:500
  265.1 7.4 %assemble.9 = bf16[2,4,2,2,192,576]{5,4,3,2,1,0:T(8,128)(2,1)} custom-call(s32[4]{0:T(128)} %pad_add_fusion.at, bf16[2,4,192,576]{3,2,1,0:T(8,128)(2,1)} %bitcast.41.s0, bf16[2,4,192,576]{3,2,1,0:T(8,128)(2,1)} %bitcast.42.s1, bf16[2,4,192,576]{3,2,1,0:T(8,128)(2,1)} %collective-permute-done.44.t0, bf16[2,4,192,576]{3,2,1,0:T(8,128)(2,1)} %collective-permute-done.45.t1), custom_call_target="tpu_custom_call" | custom-call | flops 999999995904 | bytes 1 | tf_op jit(solution)/shard_map/assemble/pallas_call | solution.py:645
  277.3 24.1 %gated_back.1 = (bf16[512,3072]{1,0:T(8,128)(2,1)}, bf16[512,3072]{1,0:T(8,128)(2,1)}, f32[512,1152]{1,0:T(8,128)}) custom-call(bf16[512,576]{1,0:T(8,128)(2,1)} %get-tuple-element.204.refs_0_, bf16[512,576]{1,0:T(8,128)(2,1)} %get-tuple-element.205.refs_1_, bf16[2,3072,576]{2,1,0:T(8,128)(2,1)} %bitcast.131, bf16[2,3072,576]{2,1,0:T(8,128)(2,1)} %bitcast.132, ...), custom_call_target="tpu_custom_call" | custom-call | flops 999999995904 | bytes 1 | tf_op jit(solution)/shard_map/gated_back/pallas_call | solution.py:328
  305.0 8.4 %grad_stacks.6 = (bf16[4,4,72,1536]{3,2,1,0:T(8,128)(2,1)}, bf16[4,4,72,1536]{3,2,1,0:T(8,128)(2,1)}) custom-call(s32[3]{0:T(128)} %pad_add_fusion.1.at, bf16[512,1152]{1,0:T(8,128)(2,1)} %get-tuple-element.179.a_ref, bf16[512,3072]{1,0:T(8,128)(2,1)} %get-tuple-element.215.refs_0_.refs_1_, bf16[512,3072]{1,0:T(8,128)(2,1)} %get-tuple-element.215.refs_0_.refs_1_), custom_call_target="tpu_custom_call" | custom-call | flops 999999995904 | bytes 1 | tf_op jit(solution)/shard_map/grad_stacks/pallas_call | solution.py:500
  313.4 9.3 %middle_back.1 = (f32[512,1152]{1,0:T(8,128)}, bf16[512,1152]{1,0:T(8,128)(2,1)}, f32[2,3,1152]{2,1,0:T(4,128)}, bf16[512,576]{1,0:T(8,128)(2,1)}, bf16[512,576]{1,0:T(8,128)(2,1)}) custom-call(f32[512,1152]{1,0:T(8,128)} %get-tuple-element.210.in_ref, f32[512,1152]{1,0:T(8,128)} %get-tuple-element.211.hidden_ref, f32[512,1152]{1,0:T(8,128)} %get-tuple-element.212.attn_ref, ...), custom_call_target="tpu_custom_call" | custom-call | flops 999999995904 | bytes 1 | tf_op jit(solution)/shard_map/middle_back/pallas_call | solution.py:366
  332.9 8.4 %grad_stacks.7 = (bf16[4,4,72,1536]{3,2,1,0:T(8,128)(2,1)}, bf16[4,4,72,1536]{3,2,1,0:T(8,128)(2,1)}) custom-call(s32[3]{0:T(128)} %pad_add_fusion.1.at, bf16[512,1152]{1,0:T(8,128)(2,1)} %get-tuple-element.179.a_ref, bf16[512,3072]{1,0:T(8,128)(2,1)} %get-tuple-element.221.refs_0_.refs_1_, bf16[512,3072]{1,0:T(8,128)(2,1)} %get-tuple-element.221.refs_0_.refs_1_), custom_call_target="tpu_custom_call" | custom-call | flops 999999995904 | bytes 1 | tf_op jit(solution)/shard_map/grad_stacks/pallas_call | solution.py:500
  341.5 5.4 grad_stacks.8
  366.0 29.3 %attention_backward.1 = (bf16[512,1728]{1,0:T(8,128)(2,1)}, bf16[512,1728]{1,0:T(8,128)(2,1)}, f32[2,2,1152]{2,1,0:T(2,128)}) custom-call(f32[512,1728]{1,0:T(8,128)} %get-tuple-element.169.refs_0_, f32[512,1728]{1,0:T(8,128)} %get-tuple-element.170.refs_1_, bf16[512,1152]{1,0:T(8,128)(2,1)} %get-tuple-element.190.refs_2_, ...), custom_call_target="tpu_custom_call" | custom-call | flops 999999995904 | bytes 1 | tf_op jit(solution)/shard_map/attention_backward/pallas_call | solution.py:222
  407.3 10.2 %grad_stacks.9 = (bf16[4,4,72,1728]{3,2,1,0:T(8,128)(2,1)}, bf16[4,4,72,1728]{3,2,1,0:T(8,128)(2,1)}) custom-call(s32[3]{0:T(128)} %pad_add_fusion.1.at, bf16[512,1152]{1,0:T(8,128)(2,1)} %bitcast.99, bf16[512,1728]{1,0:T(8,128)(2,1)} %get-tuple-element.251.refs_0_, bf16[512,1728]{1,0:T(8,128)(2,1)} %get-tuple-element.252.refs_1_), custom_call_target="tpu_custom_call" | custom-call | flops 999999995904 | bytes 1 | tf_op jit(solution)/shard_map/grad_stacks/pallas_call | solution.py:500
  417.6 10.9 %block_tail.1 = (bf16[512,1152]{1,0:T(8,128)(2,1)}, f32[2,1,1152]{2,1,0:T(1,128)}) custom-call(bf16[512,3072]{1,0:T(8,128)(2,1)} %get-tuple-element.243.a_ref.mid_ref, f32[512,1152]{1,0:T(8,128)} %get-tuple-element.211.hidden_ref, bf16[512,1152]{1,0:T(8,128)(2,1)} %bitcast.97, f32[2,6,1152]{2,1,0:T(8,128)} %broadcast_add_fusion.piece.refs_4_, ...), custom_call_target="tpu_custom_call" | custom-call | flops 999999995904 | bytes 1 | tf_op jit(solution)/shard_map/block_tail/pallas_call | solution.py:366
  445.9 12.0 %block_head_back.1 = (bf16[512,1152]{1,0:T(8,128)(2,1)}, f32[2,2,1152]{2,1,0:T(2,128)}) custom-call(bf16[512,1728]{1,0:T(8,128)(2,1)} %get-tuple-element.251.refs_0_, bf16[512,1728]{1,0:T(8,128)(2,1)} %get-tuple-element.252.refs_1_, f32[512,1152]{1,0:T(8,128)} %get-tuple-element.253.refs_2_, bf16[512,1152]{1,0:T(8,128)(2,1)} %bitcast.92, ...), custom_call_target="tpu_custom_call" | custom-call | flops 999999995904 | bytes 1 | tf_op jit(solution)/shard_map/block_head_back/pallas_call | solution.py:366
  464.4 6.2 %collective-permute-done.61.refs_2_ = bf16[2,4,72,1728]{3,2,1,0:T(8,128)(2,1)} collective-permute-done((bf16[2,4,72,1728]{3,2,1,0:T(8,128)(2,1)}, bf16[2,4,72,1728]{3,2,1,0:T(8,128)(2,1)}, u32[]{:S(2)}, u32[]{:S(2)}) %collective-permute-start.61) | collective-permute-done | bytes 1990688 | tf_op jit(solution)/shard_map/ppermute | solution.py:539
  484.6 5.3 collective-permute-done.67.refs_4_
  (398 shorter events, 295.0 us)
Async XLA Ops:
  0.7 36.3 %collective-permute-start.7 = (bf16[1,72,1728]{2,1,0:T(8,128)(2,1)}, bf16[1,72,1728]{2,1,0:T(8,128)(2,1)S(1)}, u32[]{:S(2)}, u32[]{:S(2)}) collective-permute-start(bf16[1,72,1728]{2,1,0:T(8,128)(2,1)} %bitcast.106), channel_id=1, source_target_pairs={{0,24},{1,25},{2,26},{3,27},{4,28},{5,29},{6,30},{7,31},{8,16},{9,... | collective-permute-start | bytes 746504 | tf_op jit(solution)/shard_map/ppermute | solution.py:539
  5.8 31.2 %collective-permute-start.6 = (bf16[1,72,1728]{2,1,0:T(8,128)(2,1)}, bf16[1,72,1728]{2,1,0:T(8,128)(2,1)S(1)}, u32[]{:S(2)}, u32[]{:S(2)}) collective-permute-start(bf16[1,72,1728]{2,1,0:T(8,128)(2,1)} %bitcast.107), channel_id=1, source_target_pairs={{0,16},{1,17},{2,18},{3,19},{4,20},{5,21},{6,22},{7,23},{8,24},{9,... | collective-permute-start | bytes 746504 | tf_op jit(solution)/shard_map/ppermute | solution.py:539
  5.8 31.2 %collective-permute-start.5 = (bf16[1,72,1728]{2,1,0:T(8,128)(2,1)}, bf16[1,72,1728]{2,1,0:T(8,128)(2,1)S(1)}, u32[]{:S(2)}, u32[]{:S(2)}) collective-permute-start(bf16[1,72,1728]{2,1,0:T(8,128)(2,1)} %bitcast.108), channel_id=1, source_target_pairs={{0,8},{1,9},{2,10},{3,11},{4,12},{5,13},{6,14},{7,15},{8,0},{9,1},... | collective-permute-start | bytes 746504 | tf_op jit(solution)/shard_map/ppermute | solution.py:539
  66.3 26.0 %collective-permute-start.15 = (bf16[8,72,1728]{2,1,0:T(8,128)(2,1)}, bf16[8,72,1728]{2,1,0:T(8,128)(2,1)}, u32[]{:S(2)}, u32[]{:S(2)}) collective-permute-start(bf16[8,72,1728]{2,1,0:T(8,128)(2,1)} %join.11), channel_id=1, source_target_pairs={{0,1},{1,0},{2,6},{3,7},{4,5},{5,4},{6,2},{7,3},{8,9},{9,8},{10,14... | collective-permute-start | bytes 5971976 | tf_op jit(solution)/shard_map/ppermute | solution.py:539
  99.9 26.5 %collective-permute-start.22 = (bf16[2,4,72,1728]{3,2,1,0:T(8,128)(2,1)S(1)}, bf16[2,4,72,1728]{3,2,1,0:T(8,128)(2,1)}, u32[]{:S(2)}, u32[]{:S(2)}) collective-permute-start(bf16[2,4,72,1728]{3,2,1,0:T(8,128)(2,1)S(1)} %bitcast.95), channel_id=1, source_target_pairs={{0,2},{1,3},{2,0},{3,1},{4,6},{5,7},{6,4},{7,5},{8,10},{9,11},{10,... | collective-permute-start | bytes 5971976 | tf_op jit(solution)/shard_map/ppermute | solution.py:539
  102.8 23.6 %collective-permute-start.23 = (bf16[2,4,72,1728]{3,2,1,0:T(8,128)(2,1)}, bf16[2,4,72,1728]{3,2,1,0:T(8,128)(2,1)}, u32[]{:S(2)}, u32[]{:S(2)}) collective-permute-start(bf16[2,4,72,1728]{3,2,1,0:T(8,128)(2,1)} %bitcast.13.s1), channel_id=1, source_target_pairs={{0,2},{1,3},{2,0},{3,1},{4,6},{5,7},{6,4},{7,5},{8,10},{9,11},{10,... | collective-permute-start | bytes 5971976 | tf_op jit(solution)/shard_map/ppermute | solution.py:539
  131.3 30.2 %collective-permute-start.27 = (bf16[8,72,1536]{2,1,0:T(8,128)(2,1)}, bf16[8,72,1536]{2,1,0:T(8,128)(2,1)}, u32[]{:S(2)}, u32[]{:S(2)}) collective-permute-start(bf16[8,72,1536]{2,1,0:T(8,128)(2,1)} %join.15), channel_id=1, source_target_pairs={{0,1},{1,0},{2,6},{3,7},{4,5},{5,4},{6,2},{7,3},{8,9},{9,8},{10,14... | collective-permute-start | bytes 5308424 | tf_op jit(solution)/shard_map/ppermute | solution.py:539
  182.7 22.8 %collective-permute-start.36 = (bf16[8,72,1536]{2,1,0:T(8,128)(2,1)}, bf16[8,72,1536]{2,1,0:T(8,128)(2,1)}, u32[]{:S(2)}, u32[]{:S(2)}) collective-permute-start(bf16[8,72,1536]{2,1,0:T(8,128)(2,1)} %join.17), channel_id=1, source_target_pairs={{0,1},{1,0},{2,6},{3,7},{4,5},{5,4},{6,2},{7,3},{8,9},{9,8},{10,14... | collective-permute-start | bytes 5308424 | tf_op jit(solution)/shard_map/ppermute | solution.py:539
  228.8 24.9 %collective-permute-start.43 = (bf16[8,192,576]{2,1,0:T(8,128)(2,1)}, bf16[8,192,576]{2,1,0:T(8,128)(2,1)}, u32[]{:S(2)}, u32[]{:S(2)}) collective-permute-start(bf16[8,192,576]{2,1,0:T(8,128)(2,1)} %join.19), channel_id=1, source_target_pairs={{0,1},{1,0},{2,6},{3,7},{4,5},{5,4},{6,2},{7,3},{8,9},{9,8},{10,14... | collective-permute-start | bytes 5308424 | tf_op jit(solution)/shard_map/ppermute | solution.py:539
  276.8 24.9 %collective-permute-start.47 = (bf16[2,4,192,576]{3,2,1,0:T(8,128)(2,1)}, bf16[2,4,192,576]{3,2,1,0:T(8,128)(2,1)}, u32[]{:S(2)}, u32[]{:S(2)}) collective-permute-start(bf16[2,4,192,576]{3,2,1,0:T(8,128)(2,1)} %add_stacks.10), channel_id=1, source_target_pairs={{0,1},{1,0},{2,6},{3,7},{4,5},{5,4},{6,2},{7,3},{8,9},{9,8},{10,14... | collective-permute-start | bytes 5308424 | tf_op jit(solution)/shard_map/ppermute | solution.py:539
  327.1 24.8 %collective-permute-start.51 = (bf16[2,192,576]{2,1,0:T(8,128)(2,1)}, bf16[2,192,576]{2,1,0:T(8,128)(2,1)}, u32[]{:S(2)}, u32[]{:S(2)}) collective-permute-start(bf16[2,192,576]{2,1,0:T(8,128)(2,1)} %add_slabs.16), channel_id=1, source_target_pairs={{0,16},{1,17},{2,18},{3,19},{4,20},{5,21},{6,22},{7,23},{8,24},{9,... | collective-permute-start | bytes 1327112 | tf_op jit(solution)/shard_map/ppermute | solution.py:539
  331.7 22.8 %collective-permute-start.50 = (bf16[2,4,72,1536]{3,2,1,0:T(8,128)(2,1)}, bf16[2,4,72,1536]{3,2,1,0:T(8,128)(2,1)}, u32[]{:S(2)}, u32[]{:S(2)}) collective-permute-start(bf16[2,4,72,1536]{3,2,1,0:T(8,128)(2,1)} %add_stacks.12), channel_id=1, source_target_pairs={{0,1},{1,0},{2,6},{3,7},{4,5},{5,4},{6,2},{7,3},{8,9},{9,8},{10,14... | collective-permute-start | bytes 5308424 | tf_op jit(solution)/shard_map/ppermute | solution.py:539
  357.2 45.6 %collective-permute-start.56 = (bf16[1,192,576]{2,1,0:T(8,128)(2,1)}, bf16[1,192,576]{2,1,0:T(8,128)(2,1)}, u32[]{:S(2)}, u32[]{:S(2)}) collective-permute-start(bf16[1,192,576]{2,1,0:T(8,128)(2,1)} %add_slabs.17), channel_id=1, source_target_pairs={{0,8},{1,9},{2,10},{3,11},{4,12},{5,13},{6,14},{7,15},{8,0},{9,1},... | collective-permute-start | bytes 663560 | tf_op jit(solution)/shard_map/ppermute | solution.py:539
  359.2 37.7 %collective-permute-start.53 = (bf16[1,4,72,1536]{3,2,1,0:T(8,128)(2,1)}, bf16[1,4,72,1536]{3,2,1,0:T(8,128)(2,1)}, u32[]{:S(2)}, u32[]{:S(2)}) collective-permute-start(bf16[1,4,72,1536]{3,2,1,0:T(8,128)(2,1)} %add_stacks.13), channel_id=1, source_target_pairs={{0,4},{1,5},{2,3},{3,2},{4,0},{5,1},{6,7},{7,6},{8,12},{9,13},{10,... | collective-permute-start | bytes 2654216 | tf_op jit(solution)/shard_map/ppermute | solution.py:539
  360.7 38.6 %collective-permute-start.55 = (bf16[4,4,72,576]{3,2,1,0:T(8,128)(2,1)}, bf16[4,4,72,576]{3,2,1,0:T(8,128)(2,1)}, u32[]{:S(2)}, u32[]{:S(2)}) collective-permute-start(bf16[4,4,72,576]{3,2,1,0:T(8,128)(2,1)} %get-tuple-element.231), channel_id=1, source_target_pairs={{0,2},{1,3},{2,0},{3,1},{4,6},{5,7},{6,4},{7,5},{8,10},{9,11},{10,... | collective-permute-start | bytes 3981320 | tf_op jit(solution)/shard_map/ppermute | solution.py:539
  364.8 38.0 %collective-permute-start.54 = (bf16[2,4,72,1536]{3,2,1,0:T(8,128)(2,1)}, bf16[2,4,72,1536]{3,2,1,0:T(8,128)(2,1)}, u32[]{:S(2)}, u32[]{:S(2)}) collective-permute-start(bf16[2,4,72,1536]{3,2,1,0:T(8,128)(2,1)} %add_stacks.14), channel_id=1, source_target_pairs={{0,1},{1,0},{2,6},{3,7},{4,5},{5,4},{6,2},{7,3},{8,9},{9,8},{10,14... | collective-permute-start | bytes 5308424 | tf_op jit(solution)/shard_map/ppermute | solution.py:539
  402.8 27.0 %collective-permute-start.59 = (bf16[2,72,1536]{2,1,0:T(8,128)(2,1)}, bf16[2,72,1536]{2,1,0:T(8,128)(2,1)}, u32[]{:S(2)}, u32[]{:S(2)}) collective-permute-start(bf16[2,72,1536]{2,1,0:T(8,128)(2,1)} %add_slabs.18), channel_id=1, source_target_pairs={{0,16},{1,17},{2,18},{3,19},{4,20},{5,21},{6,22},{7,23},{8,24},{9,... | collective-permute-start | bytes 1327112 | tf_op jit(solution)/shard_map/ppermute | solution.py:539
  403.3 28.6 %collective-permute-start.58 = (bf16[2,4,72,576]{3,2,1,0:T(8,128)(2,1)}, bf16[2,4,72,576]{3,2,1,0:T(8,128)(2,1)}, u32[]{:S(2)}, u32[]{:S(2)}) collective-permute-start(bf16[2,4,72,576]{3,2,1,0:T(8,128)(2,1)} %add_stacks.16), channel_id=1, source_target_pairs={{0,1},{1,0},{2,6},{3,7},{4,5},{5,4},{6,2},{7,3},{8,9},{9,8},{10,14... | collective-permute-start | bytes 1990664 | tf_op jit(solution)/shard_map/ppermute | solution.py:539
  406.8 27.3 %collective-permute-start.57 = (bf16[1,4,72,1536]{3,2,1,0:T(8,128)(2,1)}, bf16[1,4,72,1536]{3,2,1,0:T(8,128)(2,1)}, u32[]{:S(2)}, u32[]{:S(2)}) collective-permute-start(bf16[1,4,72,1536]{3,2,1,0:T(8,128)(2,1)} %add_stacks.15), channel_id=1, source_target_pairs={{0,4},{1,5},{2,3},{3,2},{4,0},{5,1},{6,7},{7,6},{8,12},{9,13},{10,... | collective-permute-start | bytes 2654216 | tf_op jit(solution)/shard_map/ppermute | solution.py:539
  436.4 28.0 %collective-permute-start.64 = (bf16[1,72,1536]{2,1,0:T(8,128)(2,1)}, bf16[1,72,1536]{2,1,0:T(8,128)(2,1)}, u32[]{:S(2)}, u32[]{:S(2)}) collective-permute-start(bf16[1,72,1536]{2,1,0:T(8,128)(2,1)} %add_slabs.20), channel_id=1, source_target_pairs={{0,8},{1,9},{2,10},{3,11},{4,12},{5,13},{6,14},{7,15},{8,0},{9,1},... | collective-permute-start | bytes 663560 | tf_op jit(solution)/shard_map/ppermute | solution.py:539
  444.6 26.0 %collective-permute-start.61 = (bf16[2,4,72,1728]{3,2,1,0:T(8,128)(2,1)}, bf16[2,4,72,1728]{3,2,1,0:T(8,128)(2,1)}, u32[]{:S(2)}, u32[]{:S(2)}) collective-permute-start(bf16[2,4,72,1728]{3,2,1,0:T(8,128)(2,1)} %add_stacks.17), channel_id=1, source_target_pairs={{0,1},{1,0},{2,6},{3,7},{4,5},{5,4},{6,2},{7,3},{8,9},{9,8},{10,14... | collective-permute-start | bytes 5971976 | tf_op jit(solution)/shard_map/ppermute | solution.py:539
  518.5 28.2 %collective-permute-start.70 = (bf16[1,72,1728]{2,1,0:T(8,128)(2,1)S(1)}, bf16[1,72,1728]{2,1,0:T(8,128)(2,1)S(1)}, u32[]{:S(2)}, u32[]{:S(2)}) collective-permute-start(bf16[1,72,1728]{2,1,0:T(8,128)(2,1)S(1)} %copy-done.13), channel_id=1, source_target_pairs={{0,24},{1,25},{2,26},{3,27},{4,28},{5,29},{6,30},{7,31},{8,16},{9,... | collective-permute-start | bytes 746504 | tf_op jit(solution)/shard_map/ppermute | solution.py:539
  520.4 26.3 %collective-permute-start.71 = (bf16[1,72,1728]{2,1,0:T(8,128)(2,1)S(1)}, bf16[1,72,1728]{2,1,0:T(8,128)(2,1)}, u32[]{:S(2)}, u32[]{:S(2)}) collective-permute-start(bf16[1,72,1728]{2,1,0:T(8,128)(2,1)S(1)} %copy-done.12), channel_id=1, source_target_pairs={{0,16},{1,17},{2,18},{3,19},{4,20},{5,21},{6,22},{7,23},{8,24},{9,... | collective-permute-start | bytes 746504 | tf_op jit(solution)/shard_map/ppermute | solution.py:539
  522.0 24.8 %collective-permute-start.72 = (bf16[1,72,1728]{2,1,0:T(8,128)(2,1)S(1)}, bf16[1,72,1728]{2,1,0:T(8,128)(2,1)}, u32[]{:S(2)}, u32[]{:S(2)}) collective-permute-start(bf16[1,72,1728]{2,1,0:T(8,128)(2,1)S(1)} %copy-done.14), channel_id=1, source_target_pairs={{0,8},{1,9},{2,10},{3,11},{4,12},{5,13},{6,14},{7,15},{8,0},{9,1},... | collective-permute-start | bytes 746504 | tf_op jit(solution)/shard_map/ppermute | solution.py:539
  (110 other events, 1458.4 us)

commit v5 on v4

--- a/solution.py
+++ b/solution.py
@@ -658,6 +658,78 @@
     )(at, *parts)
 
 
+def turn(places, a):
+    tokens, features = a.shape
+    slabs = 4 * places.z
+    rows = features // slabs
+
+    def kernel(at, a_ref, mine_ref, other_ref, turned):
+        whole = a_ref[...].astype(F32).T
+        for k in range(slabs):
+            turned[k] = whole[k * rows : (k + 1) * rows].astype(BF)
+        for k in range(slabs // 2):
+            mine_ref[k] = turned[2 * k + at[0]]
+            other_ref[k] = turned[2 * k + 1 - at[0]]
+
+    out = jax.ShapeDtypeStruct((slabs // 2, rows, tokens), BF)
+    return pl.pallas_call(
+        kernel,
+        grid=(1,),
+        out_shape=[out, out],
+        in_specs=[pl.BlockSpec(memory_space=pltpu.SMEM), whole_block(a)],
+        out_specs=[whole_block(out)] * 2,
+        scratch_shapes=[pltpu.VMEM((slabs, rows, tokens), BF)],
+        compiler_params=pltpu.CompilerParams(vmem_limit_bytes=60 * 2**20),
+        cost_estimate=LONG,
+        name="turn",
+    )(places.at_c.astype(jnp.int32).reshape(1), a)
+
+
+def chip_stacks(places, turned, parts):
+    slabs, rows, tokens = turned[0].shape
+    z, count = places.z, places.narrow
+    joined = len(parts[0]) < count
+    columns = parts[0][0].shape[1] // (count if joined else 1)
+    chunk = chunk_of(columns, 900)
+    masks = [places.masks(0), places.masks(1)]
+    half = len(masks[0]) // 2
+
+    def kernel(at, own_ref, got_ref, *refs):
+        d_refs, (keep_ref, send_ref, product) = refs[: 2 * count], refs[2 * count :]
+        for i in range(count):
+            whole = mm(own_ref[...], d_refs[i][...], ((1,), (0,)))
+            whole += mm(got_ref[...], d_refs[count + i][...], ((1,), (0,)))
+            for k in range(slabs):
+                product[i, k] = whole[k * rows : (k + 1) * rows].astype(BF)
+        core, y, x = at[0], at[1], at[2]
+        for j in range(2 * half):
+            dy = jnp.where(core == 0, masks[0][j][0], masks[1][j][0])
+            dx = jnp.where(core == 0, masks[0][j][1], masks[1][j][1])
+            out = keep_ref if j < half else send_ref
+            for k in range(z):
+                out[j % half, k] = product[x ^ dx, k * 2 + (y ^ dy)]
+
+    at = jnp.stack([places.at_c, places.at_y, places.x]).astype(jnp.int32)
+    flat = [a.reshape(slabs * rows, tokens) for a in turned]
+    out = pl.BlockSpec((half, z, rows, chunk), lambda i: (0, 0, 0, i))
+    specs = [
+        pl.BlockSpec((tokens, chunk), lambda i, j=j: (0, j * (columns // chunk) + i if joined else i))
+        for j in range(count)
+    ]
+    args = [p for part in parts for p in (list(part) * count if joined else part)]
+    return pl.pallas_call(
+        kernel,
+        grid=(-(-columns // chunk),),
+        out_shape=[jax.ShapeDtypeStruct((half, z, rows, columns), BF)] * 2,
+        in_specs=[pl.BlockSpec(memory_space=pltpu.SMEM)] + [whole_block(a) for a in flat] + specs * 2,
+        out_specs=[out, out],
+        scratch_shapes=[pltpu.VMEM((count, slabs, rows, chunk), BF)],
+        compiler_params=pltpu.CompilerParams(vmem_limit_bytes=60 * 2**20),
+        cost_estimate=LONG,
+        name="chip_stacks",
+    )(at, *flat, *args)
+
+
 def join(parts):
     counts = [p.shape[0] for p in parts]
 
@@ -811,6 +883,9 @@
     def cores(self, exchange):
         self.terms.append(exchange(self.to_core, lambda core: (0, 0, 1, 0)))
 
+    def hold(self):
+        self.terms[0] = self.slots.tie(self.terms[0])
+
     def step(self, i, exchange):
         self.half //= 2
         send = add_stacks(self.terms, self.half)
@@ -838,6 +913,21 @@
     def result(self, divisor):
         divisor = self.slots.tie(divisor)
         return add_slabs(self.places, self.terms, self.z_terms, 0, 1, divisor)[0]
+
+
+class ChipScatter(Scatter):
+    def __init__(self, slots, turned, parts):
+        self.slots, self.places = slots, slots.places
+        keep, self.ready = chip_stacks(self.places, turned, parts)
+        self.terms, self.z_terms, self.half = [keep], [], keep.shape[0]
+
+    def first(self):
+        flip = self.places.step_flip(len(self.places.orders[0]) - 1)
+        self.terms.append(self.slots.send(self.ready, flip))
+
+
+def to_core(core):
+    return (0, 0, 1, 0)
 
 
 def dot(a, b, dims, out=F32):
@@ -940,8 +1030,10 @@
     gate.cores()
     up.first()
     packed = project(t.tie(attn_in), qkv_b)
-    t.next(*packed)
-
+    attn_turned, attn_other = turn(places, t.tie(attn_in))
+    t.next(*packed, attn_other)
+
+    attn_turned = [attn_turned, t.send(attn_other, to_core)]
     up.last()
     down.all_z()
     packed = t.tie(packed)
@@ -956,8 +1048,10 @@
     out_b = out.whole()
     attn_out, hidden_one, mlp_in = attention_tail(mixed, out_b, flat(inputs), pieces, images)
     gate_b = gate.whole()[0]
-    t.next(mlp_in, gate_b)
-
+    mlp_turned, mlp_other = turn(places, mlp_in)
+    t.next(mlp_in, gate_b, mlp_other)
+
+    mlp_turned = [mlp_turned, t.send(mlp_other, to_core)]
     down.last()
     up_b = up.whole()[0]
     gate_val, up_val, hidden_mid = gated(mlp_in, gate_b, up_b)
@@ -976,22 +1070,23 @@
     t.next(d_mlp_in)
 
     g_down.last()
-    g_gate = Scatter(t, mlp_in, [t.tie(d_gate)])
-    g_gate.cores(t.follow)
+    d_gate_got = t.send(d_gate, to_core)
+    d_up_got = t.send(d_up, to_core)
     d_hidden, d_mixed, sums_b, *d_attn = middle_back(
         t.tie(d_mlp_in), hidden_one, attn_out, flat(cotangent), pieces, out_b, image_counts, images
     )
-    t.next(d_mixed)
+    g_gate = ChipScatter(t, mlp_turned, [[after(d_gate, d_mixed)], [d_gate_got]])
+    t.next(g_gate.ready)
 
     g_gate.first()
+    g_down.hold()
     g_down.step_z(*z_down)
-    g_up = Scatter(t, mlp_in, [t.tie(d_up)])
-    g_up.cores(t.follow)
+    g_up = ChipScatter(t, mlp_turned, [[t.tie(d_up)], [d_up_got]])
     g_out = Scatter(t, mixed, t.tie(d_attn))
-    t.next(g_out.to_core)
-
+    t.next(g_up.ready, g_out.to_core)
+
+    g_up.first()
     g_gate.last()
-    g_up.first()
     g_out.cores(t.send)
     g_down.step_z(*z_low)
     d_packed, gain_terms = attention_backward(
@@ -999,13 +1094,17 @@
     )
     t.next(*d_packed)
 
+    d_packed_got = [
+        t.send(d.reshape(-1, 8, d.shape[1]), to_core).reshape(d.shape) for d in d_packed
+    ]
+    for grad in (g_up, g_out, g_gate):
+        grad.hold()
     g_up.last()
     g_out.first()
     g_gate.step_z(*z_down)
-    g_qkv = Scatter(t, attn_in, t.tie(d_packed))
-    g_qkv.cores(t.follow)
+    g_qkv = ChipScatter(t, attn_turned, [t.tie(d_packed), d_packed_got])
     block_output, sums_gate = block_tail(
-        after(hidden_mid, g_qkv.to_core),
+        after(hidden_mid, g_qkv.ready),
         down_b,
         hidden_one,
         flat(cotangent),
@@ -1016,6 +1115,8 @@
     t.next(sums_gate)
 
     g_qkv.first()
+    for grad in (g_out, g_up, g_gate):
+        grad.hold()
     g_out.last()
     g_up.step_z(*z_down)
     g_gate.step_z(*z_low)
@@ -1033,6 +1134,8 @@
     t.next(d_modulation)
 
     g_qkv.last()
+    for grad in (g_up, g_out):
+        grad.hold()
     g_up.step_z(*z_low)
     g_out.step_z(*z_down)
     d_all = places.open_small(t.tie(d_modulation))

time: 561 us -> 554 us (0.988)
  Pallas kernels: 307 us -> 296 us
    pallas_call x0 -> x5, Pallas kernels: none -> 31.1 us  [the longest x3 25.7 us: chip_stacks(): pl.pallas_call(kernel, grid=(-(-columns // chunk),), out_shape=[jax.Shape...]
    pallas_call x5 -> x2, Pallas kernels: 43.2 us -> 16.1 us  [grad_stacks(): pl.pallas_call(kernel, grid=(-(-columns // chunk),), out_shape=[jax.Shape...]
    pallas_call x10 -> x7, Pallas kernels: 33.3 us -> 19.7 us  [add_stacks(): pl.pallas_call(kernel, grid=(half, shape[1] // deep), out_shape=jax.Shape...]
    ppermute x78 -> x81, waiting for transfers between devices: 112 us -> 115 us  [swap(): return lax.ppermute(value, ALL, pairs)]
    ppermute x78 -> x81, starting transfers between devices: 82.1 us -> 80.5 us  [swap(): return lax.ppermute(value, ALL, pairs)]
  transfers between devices with their start and end apart: 78 -> 81, of which waited for: 32 -> 28; matrix products, arithmetic and copies ran while one was open for 7% -> 7% of each run, Pallas kernels for 51% -> 50%
where the time goes in v5:
time: 554 us; the launch traced here: 544 us
  Pallas kernels  296 us (53%)
  waiting for transfers between devices  115 us (21%)
  starting transfers between devices  80.5 us (15%)
  other arithmetic  30.1 us (5%)
  local copies, waits for them, and re-layouts  14.2 us (3%)
    ppermute x81, waiting for transfers between devices, swap(): return lax.ppermute(value, ALL, pairs)  115 us
    ppermute x81, starting transfers between devices, swap(): return lax.ppermute(value, ALL, pairs)  80.5 us
    pallas_call x4, Pallas kernels, per_image(): pl.pallas_call(kernel, grid=(images,), out_shape=[jax.ShapeDtypeStruct((i...  38.7 us
    pallas_call x16, Pallas kernels, add_slabs(): pl.pallas_call(kernel, grid_spec=pltpu.PrefetchScalarGridSpec(num_scalar_...  37.5 us
    pallas_call x5, Pallas kernels, assemble(): pl.pallas_call(kernel, out_shape=jax.ShapeDtypeStruct(shape, BF), in_spec...  33.8 us
    pallas_call x1, Pallas kernels, attention_backward(): pl.pallas_call(kernel, grid=(images,), out_shape=[jax.ShapeDtypeStruct((t...  29.2 us
    pallas_call x3, Pallas kernels, chip_stacks(): pl.pallas_call(kernel, grid=(-(-columns // chunk),), out_shape=[jax.Shape...  25.7 us
    pallas_call x10, Pallas kernels, join(): pl.pallas_call(kernel, grid=(1,), out_shape=shape, in_specs=[whole_block(...  24.6 us
  transfers between devices with their start and end apart: 81, of which 28 were waited for; matrix products, arithmetic and copies ran while one was open for 7% of the time, Pallas kernels for 50%

profile of v5, /device:TPU:0, one launch (start us, length us, event | category | flops | bytes accessed | tf_op | source)
XLA Modules:
  0.0 543.8 jit_solution(5484172174877810790)
XLA Ops:
  12.1 6.1 %fusion.8 = (f32[256,1152]{1,0:T(8,128)}, f32[256,1152]{1,0:T(8,128)}, f32[256,1152]{1,0:T(8,128)}) fusion(f32[1152]{0:T(1024)S(1)} %fusion.29, s32[256]{0:T(256)S(1)} %get-tuple-element.341, s32[256]{0:T(256)S(1)} %get-tuple-element.342, pred[1152]{0:T(1024)(128)(4,1)S(1)} %get-tuple-element.343, pred[1152]{0:T(1024)(128)(4,1)S(1)} %get-tuple-element.344), kind=kLoop, calls=%fused_computation.14 | loop fusion | flops 1769472 | bytes 3547904 | tf_op jit(solution)/shard_map/jit(_where)/select_n | solution.py:39
  72.8 12.1 %collective-permute-done.17.refs_2_ = bf16[1,72,1536]{2,1,0:T(8,128)(2,1)} collective-permute-done((bf16[1,72,1536]{2,1,0:T(8,128)(2,1)S(1)}, bf16[1,72,1536]{2,1,0:T(8,128)(2,1)}, u32[]{:S(2)}, u32[]{:S(2)}) %collective-permute-start.17) | collective-permute-done | bytes 221216 | tf_op jit(solution)/shard_map/ppermute | solution.py:539
  116.9 6.8 %collective-permute-done.25.refs_1_ = bf16[4,72,1536]{2,1,0:T(8,128)(2,1)} collective-permute-done((bf16[4,72,1536]{2,1,0:T(8,128)(2,1)}, bf16[4,72,1536]{2,1,0:T(8,128)(2,1)}, u32[]{:S(2)}, u32[]{:S(2)}) %collective-permute-start.25) | collective-permute-done | bytes 884768 | tf_op jit(solution)/shard_map/ppermute | solution.py:539
  133.6 7.9 %assemble.5 = bf16[2,4,2,2,72,1728]{5,4,3,2,1,0:T(8,128)(2,1)} custom-call(s32[4]{0:T(128)} %pad_add_fusion.at, bf16[2,4,72,1728]{3,2,1,0:T(8,128)(2,1)} %bitcast.102, bf16[2,4,72,1728]{3,2,1,0:T(8,128)(2,1)} %bitcast.13.s1, bf16[2,4,72,1728]{3,2,1,0:T(8,128)(2,1)} %collective-permute-done.22.t0, bf16[2,4,72,1728]{3,2,1,0:T(8,128)(2,1)} %collective-permute-done.23.t1), custom_call_target="tpu_custom_call" | custom-call | flops 999999995904 | bytes 1 | tf_op jit(solution)/shard_map/assemble/pallas_call | solution.py:645
  150.9 10.7 %collective-permute-done.27 = bf16[8,72,1536]{2,1,0:T(8,128)(2,1)} collective-permute-done((bf16[8,72,1536]{2,1,0:T(8,128)(2,1)}, bf16[8,72,1536]{2,1,0:T(8,128)(2,1)}, u32[]{:S(2)}, u32[]{:S(2)}) %collective-permute-start.27) | collective-permute-done | bytes 1769504 | tf_op jit(solution)/shard_map/ppermute | solution.py:539
  166.9 10.4 %project.1 = (f32[512,1728]{1,0:T(8,128)}, f32[512,1728]{1,0:T(8,128)}) custom-call(bf16[512,1152]{1,0:T(8,128)(2,1)} %bitcast.107, bf16[2,1152,1728]{2,1,0:T(8,128)(2,1)} %bitcast.139, bf16[2,1152,1728]{2,1,0:T(8,128)(2,1)} %bitcast.140), custom_call_target="tpu_custom_call" | custom-call | flops 999999995904 | bytes 1 | tf_op jit(solution)/shard_map/project/pallas_call | solution.py:258
  185.0 15.4 %attention_forward.1 = (bf16[512,1152]{1,0:T(8,128)(2,1)}, bf16[512,1152]{1,0:T(8,128)(2,1)}, bf16[512,1152]{1,0:T(8,128)(2,1)}, bf16[512,1152]{1,0:T(8,128)(2,1)}) custom-call(f32[512,1728]{1,0:T(8,128)} %get-tuple-element.190.refs_0_, f32[512,1728]{1,0:T(8,128)} %get-tuple-element.191.refs_1_, f32[2,1152]{1,0:T(2,128)} %tile.10.refs_2_.refs_6_, ...), custom_call_target="tpu_custom_call" | custom-call | flops 999999995904 | bytes 1 | tf_op jit(solution)/shard_map/attention_forward/pallas_call | solution.py:148
  212.8 6.9 %attention_tail.1 = (f32[512,1152]{1,0:T(8,128)}, f32[512,1152]{1,0:T(8,128)}, bf16[512,1152]{1,0:T(8,128)(2,1)}) custom-call(bf16[512,1152]{1,0:T(8,128)(2,1)} %get-tuple-element.192.mixed_ref.a_ref, bf16[512,1152]{1,0:T(8,128)(2,1)} %bitcast.99, f32[2,6,1152]{2,1,0:T(8,128)} %broadcast_add_fusion.piece.refs_4_, bf16[2,1152,576]{2,1,0:T(8,128)(2,1)} %bitcast.149), custom_call_target="tpu_custom_call" | custom-call | flops 999999995904 | bytes 1 | tf_op jit(solution)/shard_map/attention_tail/pallas_call | solution.py:366
  222.4 7.0 %assemble.7 = bf16[4,2,2,72,3072]{4,3,2,1,0:T(8,128)(2,1)} custom-call(s32[4]{0:T(128)} %pad_add_fusion.at, bf16[2,4,72,1536]{3,2,1,0:T(8,128)(2,1)} %bitcast.30.s0, bf16[2,4,72,1536]{3,2,1,0:T(8,128)(2,1)} %bitcast.31.s1, bf16[2,4,72,1536]{3,2,1,0:T(8,128)(2,1)} %collective-permute-done.33.t0, bf16[2,4,72,1536]{3,2,1,0:T(8,128)(2,1)} %collective-permute-done.34.t1), custom_call_target="tpu_custom_call" | custom-call | flops 999999995904 | bytes 1 | tf_op jit(solution)/shard_map/assemble/pallas_call | solution.py:645
  233.3 7.0 %assemble.8 = bf16[4,2,2,72,3072]{4,3,2,1,0:T(8,128)(2,1)} custom-call(s32[4]{0:T(128)} %pad_add_fusion.at, bf16[2,4,72,1536]{3,2,1,0:T(8,128)(2,1)} %bitcast.36.s0, bf16[2,4,72,1536]{3,2,1,0:T(8,128)(2,1)} %bitcast.37.s1, bf16[2,4,72,1536]{3,2,1,0:T(8,128)(2,1)} %collective-permute-done.41.t0, bf16[2,4,72,1536]{3,2,1,0:T(8,128)(2,1)} %collective-permute-done.42.t1), custom_call_target="tpu_custom_call" | custom-call | flops 999999995904 | bytes 1 | tf_op jit(solution)/shard_map/assemble/pallas_call | solution.py:645
  240.3 15.6 %gated.1 = (f32[512,3072]{1,0:T(8,128)}, f32[512,3072]{1,0:T(8,128)}, bf16[512,3072]{1,0:T(8,128)(2,1)}) custom-call(bf16[512,1152]{1,0:T(8,128)(2,1)} %get-tuple-element.200.a_ref, bf16[1152,3072]{1,0:T(8,128)(2,1)} %bitcast.145, bf16[1152,3072]{1,0:T(8,128)(2,1)} %bitcast.147), custom_call_target="tpu_custom_call" | custom-call | flops 999999995904 | bytes 1 | tf_op jit(solution)/shard_map/gated/pallas_call | solution.py:285
  257.9 10.7 %grad_stacks.2 = (bf16[4,4,192,576]{3,2,1,0:T(8,128)(2,1)}, bf16[4,4,192,576]{3,2,1,0:T(8,128)(2,1)}) custom-call(s32[3]{0:T(128)} %pad_add_fusion.1.at, bf16[512,3072]{1,0:T(8,128)(2,1)} %get-tuple-element.276.a_ref.mid_ref, bf16[512,576]{1,0:T(8,128)(2,1)} %get-tuple-element.228.refs_0_, bf16[512,576]{1,0:T(8,128)(2,1)} %get-tuple-element.229.refs_1_), custom_call_target="tpu_custom_call" | custom-call | flops 999999995904 | bytes 1 | tf_op jit(solution)/shard_map/grad_stacks/pallas_call | solution.py:500
  268.7 7.5 %assemble.9 = bf16[2,4,2,2,192,576]{5,4,3,2,1,0:T(8,128)(2,1)} custom-call(s32[4]{0:T(128)} %pad_add_fusion.at, bf16[2,4,192,576]{3,2,1,0:T(8,128)(2,1)} %bitcast.43.s0, bf16[2,4,192,576]{3,2,1,0:T(8,128)(2,1)} %bitcast.44.s1, bf16[2,4,192,576]{3,2,1,0:T(8,128)(2,1)} %collective-permute-done.46.t0, bf16[2,4,192,576]{3,2,1,0:T(8,128)(2,1)} %collective-permute-done.47.t1), custom_call_target="tpu_custom_call" | custom-call | flops 999999995904 | bytes 1 | tf_op jit(solution)/shard_map/assemble/pallas_call | solution.py:645
  281.3 24.1 %gated_back.1 = (bf16[512,3072]{1,0:T(8,128)(2,1)}, bf16[512,3072]{1,0:T(8,128)(2,1)}, f32[512,1152]{1,0:T(8,128)}) custom-call(bf16[512,576]{1,0:T(8,128)(2,1)} %get-tuple-element.228.refs_0_, bf16[512,576]{1,0:T(8,128)(2,1)} %get-tuple-element.229.refs_1_, bf16[2,3072,576]{2,1,0:T(8,128)(2,1)} %bitcast.142, bf16[2,3072,576]{2,1,0:T(8,128)(2,1)} %bitcast.143, ...), custom_call_target="tpu_custom_call" | custom-call | flops 999999995904 | bytes 1 | tf_op jit(solution)/shard_map/gated_back/pallas_call | solution.py:328
  310.2 8.9 %middle_back.1 = (f32[512,1152]{1,0:T(8,128)}, bf16[512,1152]{1,0:T(8,128)(2,1)}, f32[2,3,1152]{2,1,0:T(4,128)}, bf16[512,576]{1,0:T(8,128)(2,1)}, bf16[512,576]{1,0:T(8,128)(2,1)}) custom-call(f32[512,1152]{1,0:T(8,128)} %get-tuple-element.238.in_ref, f32[512,1152]{1,0:T(8,128)} %get-tuple-element.239.hidden_ref, f32[512,1152]{1,0:T(8,128)} %get-tuple-element.240.attn_ref, ...), custom_call_target="tpu_custom_call" | custom-call | flops 999999995904 | bytes 1 | tf_op jit(solution)/shard_map/middle_back/pallas_call | solution.py:366
  319.1 8.2 %chip_stacks.3 = (bf16[2,4,72,1536]{3,2,1,0:T(8,128)(2,1)}, bf16[2,4,72,1536]{3,2,1,0:T(8,128)(2,1)}) custom-call(s32[3]{0:T(128)} %pad_add_fusion.1.at, bf16[576,512]{1,0:T(8,128)(2,1)} %bitcast.154, bf16[576,512]{1,0:T(8,128)(2,1)} %bitcast.48.got_ref, bf16[512,3072]{1,0:T(8,128)(2,1)} %get-tuple-element.243.refs_0_.refs_1_, ...), custom_call_target="tpu_custom_call" | custom-call | flops 999999995904 | bytes 1 | tf_op jit(solution)/shard_map/chip_stacks/pallas_call | solution.py:720
  331.5 5.4 grad_stacks.3
  336.8 8.0 %chip_stacks.4 = (bf16[2,4,72,1536]{3,2,1,0:T(8,128)(2,1)}, bf16[2,4,72,1536]{3,2,1,0:T(8,128)(2,1)}) custom-call(s32[3]{0:T(128)} %pad_add_fusion.1.at, bf16[576,512]{1,0:T(8,128)(2,1)} %bitcast.155, bf16[576,512]{1,0:T(8,128)(2,1)} %bitcast.48.got_ref, bf16[512,3072]{1,0:T(8,128)(2,1)} %get-tuple-element.248.refs_0_.refs_1_, ...), custom_call_target="tpu_custom_call" | custom-call | flops 999999995904 | bytes 1 | tf_op jit(solution)/shard_map/chip_stacks/pallas_call | solution.py:720
  344.8 9.5 %collective-permute-done.54.refs_4_ = bf16[2,192,576]{2,1,0:T(8,128)(2,1)} collective-permute-done((bf16[2,192,576]{2,1,0:T(8,128)(2,1)}, bf16[2,192,576]{2,1,0:T(8,128)(2,1)}, u32[]{:S(2)}, u32[]{:S(2)}) %collective-permute-start.54) | collective-permute-done | bytes 442400 | tf_op jit(solution)/shard_map/ppermute | solution.py:539
  361.6 29.2 %attention_backward.1 = (bf16[512,1728]{1,0:T(8,128)(2,1)}, bf16[512,1728]{1,0:T(8,128)(2,1)}, f32[2,2,1152]{2,1,0:T(2,128)}) custom-call(f32[512,1728]{1,0:T(8,128)} %get-tuple-element.190.refs_0_, f32[512,1728]{1,0:T(8,128)} %get-tuple-element.191.refs_1_, bf16[512,1152]{1,0:T(8,128)(2,1)} %get-tuple-element.214.refs_2_, ...), custom_call_target="tpu_custom_call" | custom-call | flops 999999995904 | bytes 1 | tf_op jit(solution)/shard_map/attention_backward/pallas_call | solution.py:222
  408.4 9.5 %chip_stacks.5 = (bf16[2,4,72,1728]{3,2,1,0:T(8,128)(2,1)}, bf16[2,4,72,1728]{3,2,1,0:T(8,128)(2,1)}) custom-call(s32[3]{0:T(128)} %pad_add_fusion.1.at, bf16[576,512]{1,0:T(8,128)(2,1)} %bitcast.153, bf16[576,512]{1,0:T(8,128)(2,1)} %bitcast.42.got_ref, bf16[512,1728]{1,0:T(8,128)(2,1)} %get-tuple-element.286.refs_0_, ...), custom_call_target="tpu_custom_call" | custom-call | flops 999999995904 | bytes 1 | tf_op jit(solution)/shard_map/chip_stacks/pallas_call | solution.py:720
  417.9 10.9 %block_tail.1 = (bf16[512,1152]{1,0:T(8,128)(2,1)}, f32[2,1,1152]{2,1,0:T(1,128)}) custom-call(bf16[512,3072]{1,0:T(8,128)(2,1)} %get-tuple-element.276.a_ref.mid_ref, f32[512,1152]{1,0:T(8,128)} %get-tuple-element.239.hidden_ref, bf16[512,1152]{1,0:T(8,128)(2,1)} %bitcast.105, f32[2,6,1152]{2,1,0:T(8,128)} %broadcast_add_fusion.piece.refs_4_, ...), custom_call_target="tpu_custom_call" | custom-call | flops 999999995904 | bytes 1 | tf_op jit(solution)/shard_map/block_tail/pallas_call | solution.py:366
  440.8 12.0 %block_head_back.1 = (bf16[512,1152]{1,0:T(8,128)(2,1)}, f32[2,2,1152]{2,1,0:T(2,128)}) custom-call(bf16[512,1728]{1,0:T(8,128)(2,1)} %get-tuple-element.286.refs_0_, bf16[512,1728]{1,0:T(8,128)(2,1)} %get-tuple-element.287.refs_1_, f32[512,1152]{1,0:T(8,128)} %get-tuple-element.288.refs_2_, bf16[512,1152]{1,0:T(8,128)(2,1)} %bitcast.100, ...), custom_call_target="tpu_custom_call" | custom-call | flops 999999995904 | bytes 1 | tf_op jit(solution)/shard_map/block_head_back/pallas_call | solution.py:366
  453.7 6.5 %collective-permute-done.64.refs_1_ = bf16[2,4,72,1728]{3,2,1,0:T(8,128)(2,1)} collective-permute-done((bf16[2,4,72,1728]{3,2,1,0:T(8,128)(2,1)}, bf16[2,4,72,1728]{3,2,1,0:T(8,128)(2,1)}, u32[]{:S(2)}, u32[]{:S(2)}) %collective-permute-start.64) | collective-permute-done | bytes 1990688 | tf_op jit(solution)/shard_map/ppermute | solution.py:539
  (407 shorter events, 284.6 us)
Async XLA Ops:
  0.7 36.3 %collective-permute-start.7 = (bf16[1,72,1728]{2,1,0:T(8,128)(2,1)}, bf16[1,72,1728]{2,1,0:T(8,128)(2,1)S(1)}, u32[]{:S(2)}, u32[]{:S(2)}) collective-permute-start(bf16[1,72,1728]{2,1,0:T(8,128)(2,1)} %bitcast.114), channel_id=1, source_target_pairs={{0,24},{1,25},{2,26},{3,27},{4,28},{5,29},{6,30},{7,31},{8,16},{9,... | collective-permute-start | bytes 746504 | tf_op jit(solution)/shard_map/ppermute | solution.py:539
  5.8 31.2 %collective-permute-start.6 = (bf16[1,72,1728]{2,1,0:T(8,128)(2,1)}, bf16[1,72,1728]{2,1,0:T(8,128)(2,1)S(1)}, u32[]{:S(2)}, u32[]{:S(2)}) collective-permute-start(bf16[1,72,1728]{2,1,0:T(8,128)(2,1)} %bitcast.115), channel_id=1, source_target_pairs={{0,16},{1,17},{2,18},{3,19},{4,20},{5,21},{6,22},{7,23},{8,24},{9,... | collective-permute-start | bytes 746504 | tf_op jit(solution)/shard_map/ppermute | solution.py:539
  5.8 31.2 %collective-permute-start.5 = (bf16[1,72,1728]{2,1,0:T(8,128)(2,1)}, bf16[1,72,1728]{2,1,0:T(8,128)(2,1)S(1)}, u32[]{:S(2)}, u32[]{:S(2)}) collective-permute-start(bf16[1,72,1728]{2,1,0:T(8,128)(2,1)} %bitcast.116), channel_id=1, source_target_pairs={{0,8},{1,9},{2,10},{3,11},{4,12},{5,13},{6,14},{7,15},{8,0},{9,1},... | collective-permute-start | bytes 746504 | tf_op jit(solution)/shard_map/ppermute | solution.py:539
  66.3 26.0 %collective-permute-start.15 = (bf16[8,72,1728]{2,1,0:T(8,128)(2,1)}, bf16[8,72,1728]{2,1,0:T(8,128)(2,1)}, u32[]{:S(2)}, u32[]{:S(2)}) collective-permute-start(bf16[8,72,1728]{2,1,0:T(8,128)(2,1)} %join.11), channel_id=1, source_target_pairs={{0,1},{1,0},{2,6},{3,7},{4,5},{5,4},{6,2},{7,3},{8,9},{9,8},{10,14... | collective-permute-start | bytes 5971976 | tf_op jit(solution)/shard_map/ppermute | solution.py:539
  100.0 26.5 %collective-permute-start.22 = (bf16[2,4,72,1728]{3,2,1,0:T(8,128)(2,1)S(1)}, bf16[2,4,72,1728]{3,2,1,0:T(8,128)(2,1)}, u32[]{:S(2)}, u32[]{:S(2)}) collective-permute-start(bf16[2,4,72,1728]{3,2,1,0:T(8,128)(2,1)S(1)} %bitcast.103), channel_id=1, source_target_pairs={{0,2},{1,3},{2,0},{3,1},{4,6},{5,7},{6,4},{7,5},{8,10},{9,11},{10,... | collective-permute-start | bytes 5971976 | tf_op jit(solution)/shard_map/ppermute | solution.py:539
  131.4 30.2 %collective-permute-start.27 = (bf16[8,72,1536]{2,1,0:T(8,128)(2,1)}, bf16[8,72,1536]{2,1,0:T(8,128)(2,1)}, u32[]{:S(2)}, u32[]{:S(2)}) collective-permute-start(bf16[8,72,1536]{2,1,0:T(8,128)(2,1)} %join.15), channel_id=1, source_target_pairs={{0,1},{1,0},{2,6},{3,7},{4,5},{5,4},{6,2},{7,3},{8,9},{9,8},{10,14... | collective-permute-start | bytes 5308424 | tf_op jit(solution)/shard_map/ppermute | solution.py:539
  207.8 24.5 %collective-permute-start.41 = (bf16[2,4,72,1536]{3,2,1,0:T(8,128)(2,1)}, bf16[2,4,72,1536]{3,2,1,0:T(8,128)(2,1)}, u32[]{:S(2)}, u32[]{:S(2)}) collective-permute-start(bf16[2,4,72,1536]{3,2,1,0:T(8,128)(2,1)} %bitcast.36.s0), channel_id=1, source_target_pairs={{0,2},{1,3},{2,0},{3,1},{4,6},{5,7},{6,4},{7,5},{8,10},{9,11},{10,... | collective-permute-start | bytes 5308424 | tf_op jit(solution)/shard_map/ppermute | solution.py:539
  207.8 24.5 %collective-permute-start.42 = (bf16[2,4,72,1536]{3,2,1,0:T(8,128)(2,1)}, bf16[2,4,72,1536]{3,2,1,0:T(8,128)(2,1)}, u32[]{:S(2)}, u32[]{:S(2)}) collective-permute-start(bf16[2,4,72,1536]{3,2,1,0:T(8,128)(2,1)} %bitcast.37.s1), channel_id=1, source_target_pairs={{0,2},{1,3},{2,0},{3,1},{4,6},{5,7},{6,4},{7,5},{8,10},{9,11},{10,... | collective-permute-start | bytes 5308424 | tf_op jit(solution)/shard_map/ppermute | solution.py:539
  232.4 25.0 %collective-permute-start.45 = (bf16[8,192,576]{2,1,0:T(8,128)(2,1)}, bf16[8,192,576]{2,1,0:T(8,128)(2,1)}, u32[]{:S(2)}, u32[]{:S(2)}) collective-permute-start(bf16[8,192,576]{2,1,0:T(8,128)(2,1)} %join.19), channel_id=1, source_target_pairs={{0,1},{1,0},{2,6},{3,7},{4,5},{5,4},{6,2},{7,3},{8,9},{9,8},{10,14... | collective-permute-start | bytes 5308424 | tf_op jit(solution)/shard_map/ppermute | solution.py:539
  280.5 24.9 %collective-permute-start.49 = (bf16[2,4,192,576]{3,2,1,0:T(8,128)(2,1)}, bf16[2,4,192,576]{3,2,1,0:T(8,128)(2,1)}, u32[]{:S(2)}, u32[]{:S(2)}) collective-permute-start(bf16[2,4,192,576]{3,2,1,0:T(8,128)(2,1)} %add_stacks.7), channel_id=1, source_target_pairs={{0,1},{1,0},{2,6},{3,7},{4,5},{5,4},{6,2},{7,3},{8,9},{9,8},{10,14... | collective-permute-start | bytes 5308424 | tf_op jit(solution)/shard_map/ppermute | solution.py:539
  327.3 29.3 %collective-permute-start.53 = (bf16[2,4,72,1536]{3,2,1,0:T(8,128)(2,1)}, bf16[2,4,72,1536]{3,2,1,0:T(8,128)(2,1)}, u32[]{:S(2)}, u32[]{:S(2)}) collective-permute-start(bf16[2,4,72,1536]{3,2,1,0:T(8,128)(2,1)} %get-tuple-element.245), channel_id=1, source_target_pairs={{0,1},{1,0},{2,6},{3,7},{4,5},{5,4},{6,2},{7,3},{8,9},{9,8},{10,14... | collective-permute-start | bytes 5308424 | tf_op jit(solution)/shard_map/ppermute | solution.py:539
  356.6 34.3 %collective-permute-start.58 = (bf16[1,192,576]{2,1,0:T(8,128)(2,1)}, bf16[1,192,576]{2,1,0:T(8,128)(2,1)}, u32[]{:S(2)}, u32[]{:S(2)}) collective-permute-start(bf16[1,192,576]{2,1,0:T(8,128)(2,1)} %add_slabs.17), channel_id=1, source_target_pairs={{0,8},{1,9},{2,10},{3,11},{4,12},{5,13},{6,14},{7,15},{8,0},{9,1},... | collective-permute-start | bytes 663560 | tf_op jit(solution)/shard_map/ppermute | solution.py:539
  358.9 32.0 %collective-permute-start.56 = (bf16[1,4,72,1536]{3,2,1,0:T(8,128)(2,1)}, bf16[1,4,72,1536]{3,2,1,0:T(8,128)(2,1)}, u32[]{:S(2)}, u32[]{:S(2)}) collective-permute-start(bf16[1,4,72,1536]{3,2,1,0:T(8,128)(2,1)} %add_stacks.9), channel_id=1, source_target_pairs={{0,4},{1,5},{2,3},{3,2},{4,0},{5,1},{6,7},{7,6},{8,12},{9,13},{10,... | collective-permute-start | bytes 2654216 | tf_op jit(solution)/shard_map/ppermute | solution.py:539
  360.4 30.5 %collective-permute-start.57 = (bf16[4,4,72,576]{3,2,1,0:T(8,128)(2,1)}, bf16[4,4,72,576]{3,2,1,0:T(8,128)(2,1)}, u32[]{:S(2)}, u32[]{:S(2)}) collective-permute-start(bf16[4,4,72,576]{3,2,1,0:T(8,128)(2,1)} %get-tuple-element.258), channel_id=1, source_target_pairs={{0,2},{1,3},{2,0},{3,1},{4,6},{5,7},{6,4},{7,5},{8,10},{9,11},{10,... | collective-permute-start | bytes 3981320 | tf_op jit(solution)/shard_map/ppermute | solution.py:539
  360.4 30.5 %collective-permute-start.55 = (bf16[2,4,72,1536]{3,2,1,0:T(8,128)(2,1)}, bf16[2,4,72,1536]{3,2,1,0:T(8,128)(2,1)}, u32[]{:S(2)}, u32[]{:S(2)}) collective-permute-start(bf16[2,4,72,1536]{3,2,1,0:T(8,128)(2,1)} %get-tuple-element.255), channel_id=1, source_target_pairs={{0,1},{1,0},{2,6},{3,7},{4,5},{5,4},{6,2},{7,3},{8,9},{9,8},{10,14... | collective-permute-start | bytes 5308424 | tf_op jit(solution)/shard_map/ppermute | solution.py:539
  396.4 33.8 %collective-permute-start.63 = (bf16[2,72,1536]{2,1,0:T(8,128)(2,1)}, bf16[2,72,1536]{2,1,0:T(8,128)(2,1)}, u32[]{:S(2)}, u32[]{:S(2)}) collective-permute-start(bf16[2,72,1536]{2,1,0:T(8,128)(2,1)} %add_slabs.18), channel_id=1, source_target_pairs={{0,16},{1,17},{2,18},{3,19},{4,20},{5,21},{6,22},{7,23},{8,24},{9,... | collective-permute-start | bytes 1327112 | tf_op jit(solution)/shard_map/ppermute | solution.py:539
  402.3 27.8 %collective-permute-start.62 = (bf16[2,4,72,576]{3,2,1,0:T(8,128)(2,1)}, bf16[2,4,72,576]{3,2,1,0:T(8,128)(2,1)}, u32[]{:S(2)}, u32[]{:S(2)}) collective-permute-start(bf16[2,4,72,576]{3,2,1,0:T(8,128)(2,1)} %add_stacks.11), channel_id=1, source_target_pairs={{0,1},{1,0},{2,6},{3,7},{4,5},{5,4},{6,2},{7,3},{8,9},{9,8},{10,14... | collective-permute-start | bytes 1990664 | tf_op jit(solution)/shard_map/ppermute | solution.py:539
  405.6 24.6 %collective-permute-start.61 = (bf16[1,4,72,1536]{3,2,1,0:T(8,128)(2,1)}, bf16[1,4,72,1536]{3,2,1,0:T(8,128)(2,1)}, u32[]{:S(2)}, u32[]{:S(2)}) collective-permute-start(bf16[1,4,72,1536]{3,2,1,0:T(8,128)(2,1)} %add_stacks.10), channel_id=1, source_target_pairs={{0,4},{1,5},{2,3},{3,2},{4,0},{5,1},{6,7},{7,6},{8,12},{9,13},{10,... | collective-permute-start | bytes 2654216 | tf_op jit(solution)/shard_map/ppermute | solution.py:539
  430.2 30.0 %collective-permute-start.64 = (bf16[2,4,72,1728]{3,2,1,0:T(8,128)(2,1)}, bf16[2,4,72,1728]{3,2,1,0:T(8,128)(2,1)}, u32[]{:S(2)}, u32[]{:S(2)}) collective-permute-start(bf16[2,4,72,1728]{3,2,1,0:T(8,128)(2,1)} %get-tuple-element.279), channel_id=1, source_target_pairs={{0,1},{1,0},{2,6},{3,7},{4,5},{5,4},{6,2},{7,3},{8,9},{9,8},{10,14... | collective-permute-start | bytes 5971976 | tf_op jit(solution)/shard_map/ppermute | solution.py:539
  433.1 29.5 %collective-permute-start.67 = (bf16[1,72,1536]{2,1,0:T(8,128)(2,1)}, bf16[1,72,1536]{2,1,0:T(8,128)(2,1)}, u32[]{:S(2)}, u32[]{:S(2)}) collective-permute-start(bf16[1,72,1536]{2,1,0:T(8,128)(2,1)} %add_slabs.20), channel_id=1, source_target_pairs={{0,8},{1,9},{2,10},{3,11},{4,12},{5,13},{6,14},{7,15},{8,0},{9,1},... | collective-permute-start | bytes 663560 | tf_op jit(solution)/shard_map/ppermute | solution.py:539
  435.2 27.4 %collective-permute-start.65 = (bf16[1,4,72,576]{3,2,1,0:T(8,128)(2,1)}, bf16[1,4,72,576]{3,2,1,0:T(8,128)(2,1)}, u32[]{:S(2)}, u32[]{:S(2)}) collective-permute-start(bf16[1,4,72,576]{3,2,1,0:T(8,128)(2,1)} %add_stacks.12), channel_id=1, source_target_pairs={{0,4},{1,5},{2,3},{3,2},{4,0},{5,1},{6,7},{7,6},{8,12},{9,13},{10,... | collective-permute-start | bytes 995336 | tf_op jit(solution)/shard_map/ppermute | solution.py:539
  511.0 28.5 %collective-permute-start.73 = (bf16[1,72,1728]{2,1,0:T(8,128)(2,1)S(1)}, bf16[1,72,1728]{2,1,0:T(8,128)(2,1)S(1)}, u32[]{:S(2)}, u32[]{:S(2)}) collective-permute-start(bf16[1,72,1728]{2,1,0:T(8,128)(2,1)S(1)} %copy-done.14), channel_id=1, source_target_pairs={{0,24},{1,25},{2,26},{3,27},{4,28},{5,29},{6,30},{7,31},{8,16},{9,... | collective-permute-start | bytes 746504 | tf_op jit(solution)/shard_map/ppermute | solution.py:539
  512.9 26.6 %collective-permute-start.74 = (bf16[1,72,1728]{2,1,0:T(8,128)(2,1)S(1)}, bf16[1,72,1728]{2,1,0:T(8,128)(2,1)}, u32[]{:S(2)}, u32[]{:S(2)}) collective-permute-start(bf16[1,72,1728]{2,1,0:T(8,128)(2,1)S(1)} %copy-done.13), channel_id=1, source_target_pairs={{0,16},{1,17},{2,18},{3,19},{4,20},{5,21},{6,22},{7,23},{8,24},{9,... | collective-permute-start | bytes 746504 | tf_op jit(solution)/shard_map/ppermute | solution.py:539
  512.9 26.6 %collective-permute-start.75 = (bf16[1,72,1728]{2,1,0:T(8,128)(2,1)S(1)}, bf16[1,72,1728]{2,1,0:T(8,128)(2,1)}, u32[]{:S(2)}, u32[]{:S(2)}) collective-permute-start(bf16[1,72,1728]{2,1,0:T(8,128)(2,1)S(1)} %copy-done.15), channel_id=1, source_target_pairs={{0,8},{1,9},{2,10},{3,11},{4,12},{5,13},{6,14},{7,15},{8,0},{9,1},... | collective-permute-start | bytes 746504 | tf_op jit(solution)/shard_map/ppermute | solution.py:539
  (115 other events, 1537.3 us)

commit v6 on v5

--- a/solution.py
+++ b/solution.py
@@ -1083,7 +1083,10 @@
     g_down.step_z(*z_down)
     g_up = ChipScatter(t, mlp_turned, [[t.tie(d_up)], [d_up_got]])
     g_out = Scatter(t, mixed, t.tie(d_attn))
-    t.next(g_up.ready, g_out.to_core)
+    block_output, sums_gate = block_tail(
+        t.tie(hidden_mid), down_b, hidden_one, flat(cotangent), pieces, image_counts, images
+    )
+    t.next(g_up.ready, g_out.to_core, sums_gate)
 
     g_up.first()
     g_gate.last()
@@ -1103,16 +1106,7 @@
     g_out.first()
     g_gate.step_z(*z_down)
     g_qkv = ChipScatter(t, attn_turned, [t.tie(d_packed), d_packed_got])
-    block_output, sums_gate = block_tail(
-        after(hidden_mid, g_qkv.ready),
-        down_b,
-        hidden_one,
-        flat(cotangent),
-        pieces,
-        image_counts,
-        images,
-    )
-    t.next(sums_gate)
+    t.next(g_qkv.ready)
 
     g_qkv.first()
     for grad in (g_out, g_up, g_gate):

time: 554 us -> 549 us (level)
    ppermute x81, waiting for transfers between devices: 115 us -> 110 us  [swap(): return lax.ppermute(value, ALL, pairs)]
  transfers between devices with their start and end apart: 81 -> 81, of which waited for: 28 -> 29; matrix products, arithmetic and copies ran while one was open for 7% -> 7% of each run, Pallas kernels for 50% -> 50%
where the time goes in v6:
time: 549 us; the launch traced here: 538 us
  Pallas kernels  297 us (54%)
  waiting for transfers between devices  110 us (20%)
  starting transfers between devices  81 us (15%)
  other arithmetic  29.7 us (5%)
  local copies, waits for them, and re-layouts  14.1 us (3%)
    ppermute x81, waiting for transfers between devices, swap(): return lax.ppermute(value, ALL, pairs)  110 us
    ppermute x81, starting transfers between devices, swap(): return lax.ppermute(value, ALL, pairs)  81 us
    pallas_call x4, Pallas kernels, per_image(): pl.pallas_call(kernel, grid=(images,), out_shape=[jax.ShapeDtypeStruct((i...  38.7 us
    pallas_call x16, Pallas kernels, add_slabs(): pl.pallas_call(kernel, grid_spec=pltpu.PrefetchScalarGridSpec(num_scalar_...  37.5 us
    pallas_call x5, Pallas kernels, assemble(): pl.pallas_call(kernel, out_shape=jax.ShapeDtypeStruct(shape, BF), in_spec...  33.8 us
    pallas_call x1, Pallas kernels, attention_backward(): pl.pallas_call(kernel, grid=(images,), out_shape=[jax.ShapeDtypeStruct((t...  29.3 us
    pallas_call x3, Pallas kernels, chip_stacks(): pl.pallas_call(kernel, grid=(-(-columns // chunk),), out_shape=[jax.Shape...  25.8 us
    pallas_call x10, Pallas kernels, join(): pl.pallas_call(kernel, grid=(1,), out_shape=shape, in_specs=[whole_block(...  24.5 us
  transfers between devices with their start and end apart: 81, of which 29 were waited for; matrix products, arithmetic and copies ran while one was open for 7% of the time, Pallas kernels for 50%

profile of v6, /device:TPU:0, one launch (start us, length us, event | category | flops | bytes accessed | tf_op | source)
XLA Modules:
  0.0 538.5 jit_solution(17011143591392514962)
XLA Ops:
  12.1 6.3 %fusion.8 = (f32[256,1152]{1,0:T(8,128)}, f32[256,1152]{1,0:T(8,128)}, f32[256,1152]{1,0:T(8,128)}) fusion(f32[1152]{0:T(1024)S(1)} %fusion.29, s32[256]{0:T(256)S(1)} %get-tuple-element.341, s32[256]{0:T(256)S(1)} %get-tuple-element.342, pred[1152]{0:T(1024)(128)(4,1)S(1)} %get-tuple-element.343, pred[1152]{0:T(1024)(128)(4,1)S(1)} %get-tuple-element.344), kind=kLoop, calls=%fused_computation.14 | loop fusion | flops 1769472 | bytes 3547904 | tf_op jit(solution)/shard_map/jit(_where)/select_n | solution.py:39
  72.8 12.0 %collective-permute-done.17.refs_2_ = bf16[1,72,1536]{2,1,0:T(8,128)(2,1)} collective-permute-done((bf16[1,72,1536]{2,1,0:T(8,128)(2,1)S(1)}, bf16[1,72,1536]{2,1,0:T(8,128)(2,1)}, u32[]{:S(2)}, u32[]{:S(2)}) %collective-permute-start.17) | collective-permute-done | bytes 221216 | tf_op jit(solution)/shard_map/ppermute | solution.py:539
  108.7 5.3 collective-permute-done.24.refs_1_
  116.8 6.8 %collective-permute-done.25.refs_1_ = bf16[4,72,1536]{2,1,0:T(8,128)(2,1)} collective-permute-done((bf16[4,72,1536]{2,1,0:T(8,128)(2,1)}, bf16[4,72,1536]{2,1,0:T(8,128)(2,1)}, u32[]{:S(2)}, u32[]{:S(2)}) %collective-permute-start.25) | collective-permute-done | bytes 884768 | tf_op jit(solution)/shard_map/ppermute | solution.py:539
  133.5 7.9 %assemble.5 = bf16[2,4,2,2,72,1728]{5,4,3,2,1,0:T(8,128)(2,1)} custom-call(s32[4]{0:T(128)} %pad_add_fusion.at, bf16[2,4,72,1728]{3,2,1,0:T(8,128)(2,1)} %bitcast.102, bf16[2,4,72,1728]{3,2,1,0:T(8,128)(2,1)} %bitcast.13.s1, bf16[2,4,72,1728]{3,2,1,0:T(8,128)(2,1)} %collective-permute-done.22.t0, bf16[2,4,72,1728]{3,2,1,0:T(8,128)(2,1)} %collective-permute-done.23.t1), custom_call_target="tpu_custom_call" | custom-call | flops 999999995904 | bytes 1 | tf_op jit(solution)/shard_map/assemble/pallas_call | solution.py:645
  150.8 10.7 %collective-permute-done.27 = bf16[8,72,1536]{2,1,0:T(8,128)(2,1)} collective-permute-done((bf16[8,72,1536]{2,1,0:T(8,128)(2,1)}, bf16[8,72,1536]{2,1,0:T(8,128)(2,1)}, u32[]{:S(2)}, u32[]{:S(2)}) %collective-permute-start.27) | collective-permute-done | bytes 1769504 | tf_op jit(solution)/shard_map/ppermute | solution.py:539
  166.8 10.4 %project.1 = (f32[512,1728]{1,0:T(8,128)}, f32[512,1728]{1,0:T(8,128)}) custom-call(bf16[512,1152]{1,0:T(8,128)(2,1)} %bitcast.107, bf16[2,1152,1728]{2,1,0:T(8,128)(2,1)} %bitcast.139, bf16[2,1152,1728]{2,1,0:T(8,128)(2,1)} %bitcast.140), custom_call_target="tpu_custom_call" | custom-call | flops 999999995904 | bytes 1 | tf_op jit(solution)/shard_map/project/pallas_call | solution.py:258
  185.0 15.4 %attention_forward.1 = (bf16[512,1152]{1,0:T(8,128)(2,1)}, bf16[512,1152]{1,0:T(8,128)(2,1)}, bf16[512,1152]{1,0:T(8,128)(2,1)}, bf16[512,1152]{1,0:T(8,128)(2,1)}) custom-call(f32[512,1728]{1,0:T(8,128)} %get-tuple-element.190.refs_0_, f32[512,1728]{1,0:T(8,128)} %get-tuple-element.191.refs_1_, f32[2,1152]{1,0:T(2,128)} %tile.10.refs_2_.refs_6_, ...), custom_call_target="tpu_custom_call" | custom-call | flops 999999995904 | bytes 1 | tf_op jit(solution)/shard_map/attention_forward/pallas_call | solution.py:148
  212.8 6.8 %attention_tail.1 = (f32[512,1152]{1,0:T(8,128)}, f32[512,1152]{1,0:T(8,128)}, bf16[512,1152]{1,0:T(8,128)(2,1)}) custom-call(bf16[512,1152]{1,0:T(8,128)(2,1)} %get-tuple-element.192.mixed_ref.a_ref, bf16[512,1152]{1,0:T(8,128)(2,1)} %bitcast.99, f32[2,6,1152]{2,1,0:T(8,128)} %broadcast_add_fusion.piece.refs_4_, bf16[2,1152,576]{2,1,0:T(8,128)(2,1)} %bitcast.149), custom_call_target="tpu_custom_call" | custom-call | flops 999999995904 | bytes 1 | tf_op jit(solution)/shard_map/attention_tail/pallas_call | solution.py:366
  222.4 7.0 %assemble.7 = bf16[4,2,2,72,3072]{4,3,2,1,0:T(8,128)(2,1)} custom-call(s32[4]{0:T(128)} %pad_add_fusion.at, bf16[2,4,72,1536]{3,2,1,0:T(8,128)(2,1)} %bitcast.30.s0, bf16[2,4,72,1536]{3,2,1,0:T(8,128)(2,1)} %bitcast.31.s1, bf16[2,4,72,1536]{3,2,1,0:T(8,128)(2,1)} %collective-permute-done.33.t0, bf16[2,4,72,1536]{3,2,1,0:T(8,128)(2,1)} %collective-permute-done.34.t1), custom_call_target="tpu_custom_call" | custom-call | flops 999999995904 | bytes 1 | tf_op jit(solution)/shard_map/assemble/pallas_call | solution.py:645
  233.2 7.0 %assemble.8 = bf16[4,2,2,72,3072]{4,3,2,1,0:T(8,128)(2,1)} custom-call(s32[4]{0:T(128)} %pad_add_fusion.at, bf16[2,4,72,1536]{3,2,1,0:T(8,128)(2,1)} %bitcast.36.s0, bf16[2,4,72,1536]{3,2,1,0:T(8,128)(2,1)} %bitcast.37.s1, bf16[2,4,72,1536]{3,2,1,0:T(8,128)(2,1)} %collective-permute-done.41.t0, bf16[2,4,72,1536]{3,2,1,0:T(8,128)(2,1)} %collective-permute-done.42.t1), custom_call_target="tpu_custom_call" | custom-call | flops 999999995904 | bytes 1 | tf_op jit(solution)/shard_map/assemble/pallas_call | solution.py:645
  240.2 15.5 %gated.1 = (f32[512,3072]{1,0:T(8,128)}, f32[512,3072]{1,0:T(8,128)}, bf16[512,3072]{1,0:T(8,128)(2,1)}) custom-call(bf16[512,1152]{1,0:T(8,128)(2,1)} %get-tuple-element.200.a_ref, bf16[1152,3072]{1,0:T(8,128)(2,1)} %bitcast.145, bf16[1152,3072]{1,0:T(8,128)(2,1)} %bitcast.147), custom_call_target="tpu_custom_call" | custom-call | flops 999999995904 | bytes 1 | tf_op jit(solution)/shard_map/gated/pallas_call | solution.py:285
  257.8 10.7 %grad_stacks.2 = (bf16[4,4,192,576]{3,2,1,0:T(8,128)(2,1)}, bf16[4,4,192,576]{3,2,1,0:T(8,128)(2,1)}) custom-call(s32[3]{0:T(128)} %pad_add_fusion.1.at, bf16[512,3072]{1,0:T(8,128)(2,1)} %get-tuple-element.244.a_ref.mid_ref, bf16[512,576]{1,0:T(8,128)(2,1)} %get-tuple-element.224.refs_0_, bf16[512,576]{1,0:T(8,128)(2,1)} %get-tuple-element.225.refs_1_), custom_call_target="tpu_custom_call" | custom-call | flops 999999995904 | bytes 1 | tf_op jit(solution)/shard_map/grad_stacks/pallas_call | solution.py:500
  268.6 7.5 %assemble.9 = bf16[2,4,2,2,192,576]{5,4,3,2,1,0:T(8,128)(2,1)} custom-call(s32[4]{0:T(128)} %pad_add_fusion.at, bf16[2,4,192,576]{3,2,1,0:T(8,128)(2,1)} %bitcast.41.s0, bf16[2,4,192,576]{3,2,1,0:T(8,128)(2,1)} %bitcast.42.s1, bf16[2,4,192,576]{3,2,1,0:T(8,128)(2,1)} %collective-permute-done.46.t0, bf16[2,4,192,576]{3,2,1,0:T(8,128)(2,1)} %collective-permute-done.47.t1), custom_call_target="tpu_custom_call" | custom-call | flops 999999995904 | bytes 1 | tf_op jit(solution)/shard_map/assemble/pallas_call | solution.py:645
  281.2 24.2 %gated_back.1 = (bf16[512,3072]{1,0:T(8,128)(2,1)}, bf16[512,3072]{1,0:T(8,128)(2,1)}, f32[512,1152]{1,0:T(8,128)}) custom-call(bf16[512,576]{1,0:T(8,128)(2,1)} %get-tuple-element.224.refs_0_, bf16[512,576]{1,0:T(8,128)(2,1)} %get-tuple-element.225.refs_1_, bf16[2,3072,576]{2,1,0:T(8,128)(2,1)} %bitcast.142, bf16[2,3072,576]{2,1,0:T(8,128)(2,1)} %bitcast.143, ...), custom_call_target="tpu_custom_call" | custom-call | flops 999999995904 | bytes 1 | tf_op jit(solution)/shard_map/gated_back/pallas_call | solution.py:328
  310.1 8.9 %middle_back.1 = (f32[512,1152]{1,0:T(8,128)}, bf16[512,1152]{1,0:T(8,128)(2,1)}, f32[2,3,1152]{2,1,0:T(4,128)}, bf16[512,576]{1,0:T(8,128)(2,1)}, bf16[512,576]{1,0:T(8,128)(2,1)}) custom-call(f32[512,1152]{1,0:T(8,128)} %get-tuple-element.235.in_ref, f32[512,1152]{1,0:T(8,128)} %get-tuple-element.236.hidden_ref, f32[512,1152]{1,0:T(8,128)} %get-tuple-element.237.attn_ref, ...), custom_call_target="tpu_custom_call" | custom-call | flops 999999995904 | bytes 1 | tf_op jit(solution)/shard_map/middle_back/pallas_call | solution.py:366
  319.0 8.2 %chip_stacks.3 = (bf16[2,4,72,1536]{3,2,1,0:T(8,128)(2,1)}, bf16[2,4,72,1536]{3,2,1,0:T(8,128)(2,1)}) custom-call(s32[3]{0:T(128)} %pad_add_fusion.1.at, bf16[576,512]{1,0:T(8,128)(2,1)} %bitcast.154, bf16[576,512]{1,0:T(8,128)(2,1)} %bitcast.45.got_ref, bf16[512,3072]{1,0:T(8,128)(2,1)} %get-tuple-element.239.refs_0_.refs_1_, ...), custom_call_target="tpu_custom_call" | custom-call | flops 999999995904 | bytes 1 | tf_op jit(solution)/shard_map/chip_stacks/pallas_call | solution.py:720
  331.6 10.9 %block_tail.1 = (bf16[512,1152]{1,0:T(8,128)(2,1)}, f32[2,1,1152]{2,1,0:T(1,128)}) custom-call(bf16[512,3072]{1,0:T(8,128)(2,1)} %get-tuple-element.244.a_ref.mid_ref, f32[512,1152]{1,0:T(8,128)} %get-tuple-element.236.hidden_ref, bf16[512,1152]{1,0:T(8,128)(2,1)} %bitcast.105, f32[2,6,1152]{2,1,0:T(8,128)} %broadcast_add_fusion.piece.refs_4_, ...), custom_call_target="tpu_custom_call" | custom-call | flops 999999995904 | bytes 1 | tf_op jit(solution)/shard_map/block_tail/pallas_call | solution.py:366
  342.5 5.4 %grad_stacks.3 = (bf16[4,4,72,576]{3,2,1,0:T(8,128)(2,1)}, bf16[4,4,72,576]{3,2,1,0:T(8,128)(2,1)}) custom-call(s32[3]{0:T(128)} %pad_add_fusion.1.at, bf16[512,1152]{1,0:T(8,128)(2,1)} %get-tuple-element.192.mixed_ref.a_ref, bf16[512,576]{1,0:T(8,128)(2,1)} %get-tuple-element.253.refs_0_, bf16[512,576]{1,0:T(8,128)(2,1)} %get-tuple-element.254.refs_1_), custom_call_target="tpu_custom_call" | custom-call | flops 999999995904 | bytes 1 | tf_op jit(solution)/shard_map/grad_stacks/pallas_call | solution.py:500
  347.9 8.1 %chip_stacks.4 = (bf16[2,4,72,1536]{3,2,1,0:T(8,128)(2,1)}, bf16[2,4,72,1536]{3,2,1,0:T(8,128)(2,1)}) custom-call(s32[3]{0:T(128)} %pad_add_fusion.1.at, bf16[576,512]{1,0:T(8,128)(2,1)} %bitcast.155, bf16[576,512]{1,0:T(8,128)(2,1)} %bitcast.45.got_ref, bf16[512,3072]{1,0:T(8,128)(2,1)} %get-tuple-element.249.refs_0_.refs_1_, ...), custom_call_target="tpu_custom_call" | custom-call | flops 999999995904 | bytes 1 | tf_op jit(solution)/shard_map/chip_stacks/pallas_call | solution.py:720
  363.8 29.3 %attention_backward.1 = (bf16[512,1728]{1,0:T(8,128)(2,1)}, bf16[512,1728]{1,0:T(8,128)(2,1)}, f32[2,2,1152]{2,1,0:T(2,128)}) custom-call(f32[512,1728]{1,0:T(8,128)} %get-tuple-element.190.refs_0_, f32[512,1728]{1,0:T(8,128)} %get-tuple-element.191.refs_1_, bf16[512,1152]{1,0:T(8,128)(2,1)} %get-tuple-element.246.refs_2_, ...), custom_call_target="tpu_custom_call" | custom-call | flops 999999995904 | bytes 1 | tf_op jit(solution)/shard_map/attention_backward/pallas_call | solution.py:222
  409.8 9.5 %chip_stacks.5 = (bf16[2,4,72,1728]{3,2,1,0:T(8,128)(2,1)}, bf16[2,4,72,1728]{3,2,1,0:T(8,128)(2,1)}) custom-call(s32[3]{0:T(128)} %pad_add_fusion.1.at, bf16[576,512]{1,0:T(8,128)(2,1)} %bitcast.153, bf16[576,512]{1,0:T(8,128)(2,1)} %bitcast.51.got_ref, bf16[512,1728]{1,0:T(8,128)(2,1)} %get-tuple-element.286.refs_0_, ...), custom_call_target="tpu_custom_call" | custom-call | flops 999999995904 | bytes 1 | tf_op jit(solution)/shard_map/chip_stacks/pallas_call | solution.py:720
  434.9 12.1 %block_head_back.1 = (bf16[512,1152]{1,0:T(8,128)(2,1)}, f32[2,2,1152]{2,1,0:T(2,128)}) custom-call(bf16[512,1728]{1,0:T(8,128)(2,1)} %get-tuple-element.286.refs_0_, bf16[512,1728]{1,0:T(8,128)(2,1)} %get-tuple-element.287.refs_1_, f32[512,1152]{1,0:T(8,128)} %get-tuple-element.288.refs_2_, bf16[512,1152]{1,0:T(8,128)(2,1)} %bitcast.100, ...), custom_call_target="tpu_custom_call" | custom-call | flops 999999995904 | bytes 1 | tf_op jit(solution)/shard_map/block_head_back/pallas_call | solution.py:366
  447.8 6.7 %collective-permute-done.64.refs_1_ = bf16[2,4,72,1728]{3,2,1,0:T(8,128)(2,1)} collective-permute-done((bf16[2,4,72,1728]{3,2,1,0:T(8,128)(2,1)}, bf16[2,4,72,1728]{3,2,1,0:T(8,128)(2,1)}, u32[]{:S(2)}, u32[]{:S(2)}) %collective-permute-start.64) | collective-permute-done | bytes 1990688 | tf_op jit(solution)/shard_map/ppermute | solution.py:539
  (409 shorter events, 282.8 us)
Async XLA Ops:
  0.7 36.3 %collective-permute-start.7 = (bf16[1,72,1728]{2,1,0:T(8,128)(2,1)}, bf16[1,72,1728]{2,1,0:T(8,128)(2,1)S(1)}, u32[]{:S(2)}, u32[]{:S(2)}) collective-permute-start(bf16[1,72,1728]{2,1,0:T(8,128)(2,1)} %bitcast.114), channel_id=1, source_target_pairs={{0,24},{1,25},{2,26},{3,27},{4,28},{5,29},{6,30},{7,31},{8,16},{9,... | collective-permute-start | bytes 746504 | tf_op jit(solution)/shard_map/ppermute | solution.py:539
  5.8 31.2 %collective-permute-start.6 = (bf16[1,72,1728]{2,1,0:T(8,128)(2,1)}, bf16[1,72,1728]{2,1,0:T(8,128)(2,1)S(1)}, u32[]{:S(2)}, u32[]{:S(2)}) collective-permute-start(bf16[1,72,1728]{2,1,0:T(8,128)(2,1)} %bitcast.115), channel_id=1, source_target_pairs={{0,16},{1,17},{2,18},{3,19},{4,20},{5,21},{6,22},{7,23},{8,24},{9,... | collective-permute-start | bytes 746504 | tf_op jit(solution)/shard_map/ppermute | solution.py:539
  5.8 31.2 %collective-permute-start.5 = (bf16[1,72,1728]{2,1,0:T(8,128)(2,1)}, bf16[1,72,1728]{2,1,0:T(8,128)(2,1)S(1)}, u32[]{:S(2)}, u32[]{:S(2)}) collective-permute-start(bf16[1,72,1728]{2,1,0:T(8,128)(2,1)} %bitcast.116), channel_id=1, source_target_pairs={{0,8},{1,9},{2,10},{3,11},{4,12},{5,13},{6,14},{7,15},{8,0},{9,1},... | collective-permute-start | bytes 746504 | tf_op jit(solution)/shard_map/ppermute | solution.py:539
  66.3 26.0 %collective-permute-start.15 = (bf16[8,72,1728]{2,1,0:T(8,128)(2,1)}, bf16[8,72,1728]{2,1,0:T(8,128)(2,1)}, u32[]{:S(2)}, u32[]{:S(2)}) collective-permute-start(bf16[8,72,1728]{2,1,0:T(8,128)(2,1)} %join.11), channel_id=1, source_target_pairs={{0,1},{1,0},{2,6},{3,7},{4,5},{5,4},{6,2},{7,3},{8,9},{9,8},{10,14... | collective-permute-start | bytes 5971976 | tf_op jit(solution)/shard_map/ppermute | solution.py:539
  99.9 26.5 %collective-permute-start.22 = (bf16[2,4,72,1728]{3,2,1,0:T(8,128)(2,1)S(1)}, bf16[2,4,72,1728]{3,2,1,0:T(8,128)(2,1)}, u32[]{:S(2)}, u32[]{:S(2)}) collective-permute-start(bf16[2,4,72,1728]{3,2,1,0:T(8,128)(2,1)S(1)} %bitcast.103), channel_id=1, source_target_pairs={{0,2},{1,3},{2,0},{3,1},{4,6},{5,7},{6,4},{7,5},{8,10},{9,11},{10,... | collective-permute-start | bytes 5971976 | tf_op jit(solution)/shard_map/ppermute | solution.py:539
  102.8 23.6 %collective-permute-start.23 = (bf16[2,4,72,1728]{3,2,1,0:T(8,128)(2,1)}, bf16[2,4,72,1728]{3,2,1,0:T(8,128)(2,1)}, u32[]{:S(2)}, u32[]{:S(2)}) collective-permute-start(bf16[2,4,72,1728]{3,2,1,0:T(8,128)(2,1)} %bitcast.13.s1), channel_id=1, source_target_pairs={{0,2},{1,3},{2,0},{3,1},{4,6},{5,7},{6,4},{7,5},{8,10},{9,11},{10,... | collective-permute-start | bytes 5971976 | tf_op jit(solution)/shard_map/ppermute | solution.py:539
  131.3 30.2 %collective-permute-start.27 = (bf16[8,72,1536]{2,1,0:T(8,128)(2,1)}, bf16[8,72,1536]{2,1,0:T(8,128)(2,1)}, u32[]{:S(2)}, u32[]{:S(2)}) collective-permute-start(bf16[8,72,1536]{2,1,0:T(8,128)(2,1)} %join.15), channel_id=1, source_target_pairs={{0,1},{1,0},{2,6},{3,7},{4,5},{5,4},{6,2},{7,3},{8,9},{9,8},{10,14... | collective-permute-start | bytes 5308424 | tf_op jit(solution)/shard_map/ppermute | solution.py:539
  207.8 24.5 %collective-permute-start.41 = (bf16[2,4,72,1536]{3,2,1,0:T(8,128)(2,1)}, bf16[2,4,72,1536]{3,2,1,0:T(8,128)(2,1)}, u32[]{:S(2)}, u32[]{:S(2)}) collective-permute-start(bf16[2,4,72,1536]{3,2,1,0:T(8,128)(2,1)} %bitcast.36.s0), channel_id=1, source_target_pairs={{0,2},{1,3},{2,0},{3,1},{4,6},{5,7},{6,4},{7,5},{8,10},{9,11},{10,... | collective-permute-start | bytes 5308424 | tf_op jit(solution)/shard_map/ppermute | solution.py:539
  207.8 24.5 %collective-permute-start.42 = (bf16[2,4,72,1536]{3,2,1,0:T(8,128)(2,1)}, bf16[2,4,72,1536]{3,2,1,0:T(8,128)(2,1)}, u32[]{:S(2)}, u32[]{:S(2)}) collective-permute-start(bf16[2,4,72,1536]{3,2,1,0:T(8,128)(2,1)} %bitcast.37.s1), channel_id=1, source_target_pairs={{0,2},{1,3},{2,0},{3,1},{4,6},{5,7},{6,4},{7,5},{8,10},{9,11},{10,... | collective-permute-start | bytes 5308424 | tf_op jit(solution)/shard_map/ppermute | solution.py:539
  232.3 23.5 %collective-permute-start.44 = (bf16[8,72,512]{2,1,0:T(8,128)(2,1)}, bf16[8,72,512]{2,1,0:T(8,128)(2,1)}, u32[]{:S(2)}, u32[]{:S(2)}) collective-permute-start(bf16[8,72,512]{2,1,0:T(8,128)(2,1)} %get-tuple-element.206), channel_id=1, source_target_pairs={{0,2},{1,3},{2,0},{3,1},{4,6},{5,7},{6,4},{7,5},{8,10},{9,11},{10,... | collective-permute-start | bytes 1769480 | tf_op jit(solution)/shard_map/ppermute | solution.py:539
  232.3 25.0 %collective-permute-start.45 = (bf16[8,192,576]{2,1,0:T(8,128)(2,1)}, bf16[8,192,576]{2,1,0:T(8,128)(2,1)}, u32[]{:S(2)}, u32[]{:S(2)}) collective-permute-start(bf16[8,192,576]{2,1,0:T(8,128)(2,1)} %join.19), channel_id=1, source_target_pairs={{0,1},{1,0},{2,6},{3,7},{4,5},{5,4},{6,2},{7,3},{8,9},{9,8},{10,14... | collective-permute-start | bytes 5308424 | tf_op jit(solution)/shard_map/ppermute | solution.py:539
  280.4 25.0 %collective-permute-start.49 = (bf16[2,4,192,576]{3,2,1,0:T(8,128)(2,1)}, bf16[2,4,192,576]{3,2,1,0:T(8,128)(2,1)}, u32[]{:S(2)}, u32[]{:S(2)}) collective-permute-start(bf16[2,4,192,576]{3,2,1,0:T(8,128)(2,1)} %add_stacks.7), channel_id=1, source_target_pairs={{0,1},{1,0},{2,6},{3,7},{4,5},{5,4},{6,2},{7,3},{8,9},{9,8},{10,14... | collective-permute-start | bytes 5308424 | tf_op jit(solution)/shard_map/ppermute | solution.py:539
  327.3 30.9 %collective-permute-start.53 = (bf16[2,4,72,1536]{3,2,1,0:T(8,128)(2,1)}, bf16[2,4,72,1536]{3,2,1,0:T(8,128)(2,1)}, u32[]{:S(2)}, u32[]{:S(2)}) collective-permute-start(bf16[2,4,72,1536]{3,2,1,0:T(8,128)(2,1)} %get-tuple-element.241), channel_id=1, source_target_pairs={{0,1},{1,0},{2,6},{3,7},{4,5},{5,4},{6,2},{7,3},{8,9},{9,8},{10,14... | collective-permute-start | bytes 5308424 | tf_op jit(solution)/shard_map/ppermute | solution.py:539
  331.1 24.9 %collective-permute-start.54 = (bf16[2,192,576]{2,1,0:T(8,128)(2,1)}, bf16[2,192,576]{2,1,0:T(8,128)(2,1)}, u32[]{:S(2)}, u32[]{:S(2)}) collective-permute-start(bf16[2,192,576]{2,1,0:T(8,128)(2,1)} %add_slabs.16), channel_id=1, source_target_pairs={{0,16},{1,17},{2,18},{3,19},{4,20},{5,21},{6,22},{7,23},{8,24},{9,... | collective-permute-start | bytes 1327112 | tf_op jit(solution)/shard_map/ppermute | solution.py:539
  358.2 35.0 %collective-permute-start.58 = (bf16[1,192,576]{2,1,0:T(8,128)(2,1)}, bf16[1,192,576]{2,1,0:T(8,128)(2,1)}, u32[]{:S(2)}, u32[]{:S(2)}) collective-permute-start(bf16[1,192,576]{2,1,0:T(8,128)(2,1)} %add_slabs.17), channel_id=1, source_target_pairs={{0,8},{1,9},{2,10},{3,11},{4,12},{5,13},{6,14},{7,15},{8,0},{9,1},... | collective-permute-start | bytes 663560 | tf_op jit(solution)/shard_map/ppermute | solution.py:539
  362.5 30.7 %collective-permute-start.56 = (bf16[1,4,72,1536]{3,2,1,0:T(8,128)(2,1)}, bf16[1,4,72,1536]{3,2,1,0:T(8,128)(2,1)}, u32[]{:S(2)}, u32[]{:S(2)}) collective-permute-start(bf16[1,4,72,1536]{3,2,1,0:T(8,128)(2,1)} %add_stacks.9), channel_id=1, source_target_pairs={{0,4},{1,5},{2,3},{3,2},{4,0},{5,1},{6,7},{7,6},{8,12},{9,13},{10,... | collective-permute-start | bytes 2654216 | tf_op jit(solution)/shard_map/ppermute | solution.py:539
  363.0 30.2 %collective-permute-start.57 = (bf16[4,4,72,576]{3,2,1,0:T(8,128)(2,1)}, bf16[4,4,72,576]{3,2,1,0:T(8,128)(2,1)}, u32[]{:S(2)}, u32[]{:S(2)}) collective-permute-start(bf16[4,4,72,576]{3,2,1,0:T(8,128)(2,1)} %get-tuple-element.260), channel_id=1, source_target_pairs={{0,2},{1,3},{2,0},{3,1},{4,6},{5,7},{6,4},{7,5},{8,10},{9,11},{10,... | collective-permute-start | bytes 3981320 | tf_op jit(solution)/shard_map/ppermute | solution.py:539
  363.0 30.2 %collective-permute-start.55 = (bf16[2,4,72,1536]{3,2,1,0:T(8,128)(2,1)}, bf16[2,4,72,1536]{3,2,1,0:T(8,128)(2,1)}, u32[]{:S(2)}, u32[]{:S(2)}) collective-permute-start(bf16[2,4,72,1536]{3,2,1,0:T(8,128)(2,1)} %get-tuple-element.257), channel_id=1, source_target_pairs={{0,1},{1,0},{2,6},{3,7},{4,5},{5,4},{6,2},{7,3},{8,9},{9,8},{10,14... | collective-permute-start | bytes 5308424 | tf_op jit(solution)/shard_map/ppermute | solution.py:539
  424.6 29.9 %collective-permute-start.64 = (bf16[2,4,72,1728]{3,2,1,0:T(8,128)(2,1)}, bf16[2,4,72,1728]{3,2,1,0:T(8,128)(2,1)}, u32[]{:S(2)}, u32[]{:S(2)}) collective-permute-start(bf16[2,4,72,1728]{3,2,1,0:T(8,128)(2,1)} %get-tuple-element.279), channel_id=1, source_target_pairs={{0,1},{1,0},{2,6},{3,7},{4,5},{5,4},{6,2},{7,3},{8,9},{9,8},{10,14... | collective-permute-start | bytes 5971976 | tf_op jit(solution)/shard_map/ppermute | solution.py:539
  427.4 29.6 %collective-permute-start.67 = (bf16[1,72,1536]{2,1,0:T(8,128)(2,1)}, bf16[1,72,1536]{2,1,0:T(8,128)(2,1)}, u32[]{:S(2)}, u32[]{:S(2)}) collective-permute-start(bf16[1,72,1536]{2,1,0:T(8,128)(2,1)} %add_slabs.20), channel_id=1, source_target_pairs={{0,8},{1,9},{2,10},{3,11},{4,12},{5,13},{6,14},{7,15},{8,0},{9,1},... | collective-permute-start | bytes 663560 | tf_op jit(solution)/shard_map/ppermute | solution.py:539
  431.5 25.5 %collective-permute-start.65 = (bf16[1,4,72,576]{3,2,1,0:T(8,128)(2,1)}, bf16[1,4,72,576]{3,2,1,0:T(8,128)(2,1)}, u32[]{:S(2)}, u32[]{:S(2)}) collective-permute-start(bf16[1,4,72,576]{3,2,1,0:T(8,128)(2,1)} %add_stacks.12), channel_id=1, source_target_pairs={{0,4},{1,5},{2,3},{3,2},{4,0},{5,1},{6,7},{7,6},{8,12},{9,13},{10,... | collective-permute-start | bytes 995336 | tf_op jit(solution)/shard_map/ppermute | solution.py:539
  505.2 28.9 %collective-permute-start.73 = (bf16[1,72,1728]{2,1,0:T(8,128)(2,1)S(1)}, bf16[1,72,1728]{2,1,0:T(8,128)(2,1)S(1)}, u32[]{:S(2)}, u32[]{:S(2)}) collective-permute-start(bf16[1,72,1728]{2,1,0:T(8,128)(2,1)S(1)} %copy-done.14), channel_id=1, source_target_pairs={{0,24},{1,25},{2,26},{3,27},{4,28},{5,29},{6,30},{7,31},{8,16},{9,... | collective-permute-start | bytes 746504 | tf_op jit(solution)/shard_map/ppermute | solution.py:539
  507.2 27.0 %collective-permute-start.74 = (bf16[1,72,1728]{2,1,0:T(8,128)(2,1)S(1)}, bf16[1,72,1728]{2,1,0:T(8,128)(2,1)}, u32[]{:S(2)}, u32[]{:S(2)}) collective-permute-start(bf16[1,72,1728]{2,1,0:T(8,128)(2,1)S(1)} %copy-done.13), channel_id=1, source_target_pairs={{0,16},{1,17},{2,18},{3,19},{4,20},{5,21},{6,22},{7,23},{8,24},{9,... | collective-permute-start | bytes 746504 | tf_op jit(solution)/shard_map/ppermute | solution.py:539
  508.7 25.4 %collective-permute-start.75 = (bf16[1,72,1728]{2,1,0:T(8,128)(2,1)S(1)}, bf16[1,72,1728]{2,1,0:T(8,128)(2,1)}, u32[]{:S(2)}, u32[]{:S(2)}) collective-permute-start(bf16[1,72,1728]{2,1,0:T(8,128)(2,1)S(1)} %copy-done.15), channel_id=1, source_target_pairs={{0,8},{1,9},{2,10},{3,11},{4,12},{5,13},{6,14},{7,15},{8,0},{9,1},... | collective-permute-start | bytes 746504 | tf_op jit(solution)/shard_map/ppermute | solution.py:539
  (116 other events, 1552.2 us)

commit v7 on v6

--- a/solution.py
+++ b/solution.py
@@ -1138,7 +1138,7 @@
 
     g_qkv.direct_z()
     g_out.step_z(*z_low)
-    d_all = places.gather_bits(t.tie(d_all), bits[len(places.z_bits) :])
+    d_all = places.gather_bits(after(d_all, *t.before), bits[len(places.z_bits) :])
     d_all = d_all.reshape(wide * narrow * images, -1)
     gain_sum = d_all[:, 6 * width : 6 * width + 2 * HD].astype(F32)
     gain_sum = jnp.sum(gain_sum, axis=0).reshape(2, HD) / real_count

time: 549 us -> 549 us (level)
  transfers between devices with their start and end apart: 81 -> 81, of which waited for: 29 -> 29; matrix products, arithmetic and copies ran while one was open for 7% -> 7% of each run, Pallas kernels for 50% -> 51%
where the time goes in v7:
time: 549 us; the launch traced here: 538 us
  Pallas kernels  296 us (54%)
  waiting for transfers between devices  113 us (21%)
  starting transfers between devices  80.8 us (15%)
  other arithmetic  29.6 us (5%)
  local copies, waits for them, and re-layouts  11.8 us (2%)
    ppermute x81, waiting for transfers between devices, swap(): return lax.ppermute(value, ALL, pairs)  113 us
    ppermute x81, starting transfers between devices, swap(): return lax.ppermute(value, ALL, pairs)  80.8 us
    pallas_call x4, Pallas kernels, per_image(): pl.pallas_call(kernel, grid=(images,), out_shape=[jax.ShapeDtypeStruct((i...  38.7 us
    pallas_call x16, Pallas kernels, add_slabs(): pl.pallas_call(kernel, grid_spec=pltpu.PrefetchScalarGridSpec(num_scalar_...  37.3 us
    pallas_call x5, Pallas kernels, assemble(): pl.pallas_call(kernel, out_shape=jax.ShapeDtypeStruct(shape, BF), in_spec...  33.8 us
    pallas_call x1, Pallas kernels, attention_backward(): pl.pallas_call(kernel, grid=(images,), out_shape=[jax.ShapeDtypeStruct((t...  29.3 us
    pallas_call x3, Pallas kernels, chip_stacks(): pl.pallas_call(kernel, grid=(-(-columns // chunk),), out_shape=[jax.Shape...  25.8 us
    pallas_call x10, Pallas kernels, join(): pl.pallas_call(kernel, grid=(1,), out_shape=shape, in_specs=[whole_block(...  24.6 us
  transfers between devices with their start and end apart: 81, of which 29 were waited for; matrix products, arithmetic and copies ran while one was open for 7% of the time, Pallas kernels for 51%

profile of v7, /device:TPU:0, one launch (start us, length us, event | category | flops | bytes accessed | tf_op | source)
XLA Modules:
  0.0 538.3 jit_solution(2072556148523817286)
XLA Ops:
  12.1 6.2 %fusion.8 = (f32[256,1152]{1,0:T(8,128)}, f32[256,1152]{1,0:T(8,128)}, f32[256,1152]{1,0:T(8,128)}) fusion(f32[1152]{0:T(1024)S(1)} %fusion.29, s32[256]{0:T(256)S(1)} %get-tuple-element.341, s32[256]{0:T(256)S(1)} %get-tuple-element.342, pred[1152]{0:T(1024)(128)(4,1)S(1)} %get-tuple-element.343, pred[1152]{0:T(1024)(128)(4,1)S(1)} %get-tuple-element.344), kind=kLoop, calls=%fused_computation.14 | loop fusion | flops 1769472 | bytes 3547904 | tf_op jit(solution)/shard_map/jit(_where)/select_n | solution.py:39
  72.8 12.0 %collective-permute-done.17.refs_2_ = bf16[1,72,1536]{2,1,0:T(8,128)(2,1)} collective-permute-done((bf16[1,72,1536]{2,1,0:T(8,128)(2,1)S(1)}, bf16[1,72,1536]{2,1,0:T(8,128)(2,1)}, u32[]{:S(2)}, u32[]{:S(2)}) %collective-permute-start.17) | collective-permute-done | bytes 221216 | tf_op jit(solution)/shard_map/ppermute | solution.py:539
  116.8 6.8 %collective-permute-done.25.refs_1_ = bf16[4,72,1536]{2,1,0:T(8,128)(2,1)} collective-permute-done((bf16[4,72,1536]{2,1,0:T(8,128)(2,1)}, bf16[4,72,1536]{2,1,0:T(8,128)(2,1)}, u32[]{:S(2)}, u32[]{:S(2)}) %collective-permute-start.25) | collective-permute-done | bytes 884768 | tf_op jit(solution)/shard_map/ppermute | solution.py:539
  133.5 7.9 %assemble.5 = bf16[2,4,2,2,72,1728]{5,4,3,2,1,0:T(8,128)(2,1)} custom-call(s32[4]{0:T(128)} %pad_add_fusion.at, bf16[2,4,72,1728]{3,2,1,0:T(8,128)(2,1)} %bitcast.102, bf16[2,4,72,1728]{3,2,1,0:T(8,128)(2,1)} %bitcast.13.s1, bf16[2,4,72,1728]{3,2,1,0:T(8,128)(2,1)} %collective-permute-done.22.t0, bf16[2,4,72,1728]{3,2,1,0:T(8,128)(2,1)} %collective-permute-done.23.t1), custom_call_target="tpu_custom_call" | custom-call | flops 999999995904 | bytes 1 | tf_op jit(solution)/shard_map/assemble/pallas_call | solution.py:645
  150.8 10.7 %collective-permute-done.27 = bf16[8,72,1536]{2,1,0:T(8,128)(2,1)} collective-permute-done((bf16[8,72,1536]{2,1,0:T(8,128)(2,1)}, bf16[8,72,1536]{2,1,0:T(8,128)(2,1)}, u32[]{:S(2)}, u32[]{:S(2)}) %collective-permute-start.27) | collective-permute-done | bytes 1769504 | tf_op jit(solution)/shard_map/ppermute | solution.py:539
  166.8 10.4 %project.1 = (f32[512,1728]{1,0:T(8,128)}, f32[512,1728]{1,0:T(8,128)}) custom-call(bf16[512,1152]{1,0:T(8,128)(2,1)} %bitcast.107, bf16[2,1152,1728]{2,1,0:T(8,128)(2,1)} %bitcast.139, bf16[2,1152,1728]{2,1,0:T(8,128)(2,1)} %bitcast.140), custom_call_target="tpu_custom_call" | custom-call | flops 999999995904 | bytes 1 | tf_op jit(solution)/shard_map/project/pallas_call | solution.py:258
  185.0 15.4 %attention_forward.1 = (bf16[512,1152]{1,0:T(8,128)(2,1)}, bf16[512,1152]{1,0:T(8,128)(2,1)}, bf16[512,1152]{1,0:T(8,128)(2,1)}, bf16[512,1152]{1,0:T(8,128)(2,1)}) custom-call(f32[512,1728]{1,0:T(8,128)} %get-tuple-element.190.refs_0_, f32[512,1728]{1,0:T(8,128)} %get-tuple-element.191.refs_1_, f32[2,1152]{1,0:T(2,128)} %tile.10.refs_2_.refs_6_, ...), custom_call_target="tpu_custom_call" | custom-call | flops 999999995904 | bytes 1 | tf_op jit(solution)/shard_map/attention_forward/pallas_call | solution.py:148
  212.8 6.8 %attention_tail.1 = (f32[512,1152]{1,0:T(8,128)}, f32[512,1152]{1,0:T(8,128)}, bf16[512,1152]{1,0:T(8,128)(2,1)}) custom-call(bf16[512,1152]{1,0:T(8,128)(2,1)} %get-tuple-element.192.mixed_ref.a_ref, bf16[512,1152]{1,0:T(8,128)(2,1)} %bitcast.99, f32[2,6,1152]{2,1,0:T(8,128)} %broadcast_add_fusion.piece.refs_4_, bf16[2,1152,576]{2,1,0:T(8,128)(2,1)} %bitcast.149), custom_call_target="tpu_custom_call" | custom-call | flops 999999995904 | bytes 1 | tf_op jit(solution)/shard_map/attention_tail/pallas_call | solution.py:366
  222.4 7.0 %assemble.7 = bf16[4,2,2,72,3072]{4,3,2,1,0:T(8,128)(2,1)} custom-call(s32[4]{0:T(128)} %pad_add_fusion.at, bf16[2,4,72,1536]{3,2,1,0:T(8,128)(2,1)} %bitcast.30.s0, bf16[2,4,72,1536]{3,2,1,0:T(8,128)(2,1)} %bitcast.31.s1, bf16[2,4,72,1536]{3,2,1,0:T(8,128)(2,1)} %collective-permute-done.33.t0, bf16[2,4,72,1536]{3,2,1,0:T(8,128)(2,1)} %collective-permute-done.34.t1), custom_call_target="tpu_custom_call" | custom-call | flops 999999995904 | bytes 1 | tf_op jit(solution)/shard_map/assemble/pallas_call | solution.py:645
  233.2 7.0 %assemble.8 = bf16[4,2,2,72,3072]{4,3,2,1,0:T(8,128)(2,1)} custom-call(s32[4]{0:T(128)} %pad_add_fusion.at, bf16[2,4,72,1536]{3,2,1,0:T(8,128)(2,1)} %bitcast.36.s0, bf16[2,4,72,1536]{3,2,1,0:T(8,128)(2,1)} %bitcast.37.s1, bf16[2,4,72,1536]{3,2,1,0:T(8,128)(2,1)} %collective-permute-done.41.t0, bf16[2,4,72,1536]{3,2,1,0:T(8,128)(2,1)} %collective-permute-done.42.t1), custom_call_target="tpu_custom_call" | custom-call | flops 999999995904 | bytes 1 | tf_op jit(solution)/shard_map/assemble/pallas_call | solution.py:645
  240.2 15.6 %gated.1 = (f32[512,3072]{1,0:T(8,128)}, f32[512,3072]{1,0:T(8,128)}, bf16[512,3072]{1,0:T(8,128)(2,1)}) custom-call(bf16[512,1152]{1,0:T(8,128)(2,1)} %get-tuple-element.200.a_ref, bf16[1152,3072]{1,0:T(8,128)(2,1)} %bitcast.145, bf16[1152,3072]{1,0:T(8,128)(2,1)} %bitcast.147), custom_call_target="tpu_custom_call" | custom-call | flops 999999995904 | bytes 1 | tf_op jit(solution)/shard_map/gated/pallas_call | solution.py:285
  257.9 10.7 %grad_stacks.2 = (bf16[4,4,192,576]{3,2,1,0:T(8,128)(2,1)}, bf16[4,4,192,576]{3,2,1,0:T(8,128)(2,1)}) custom-call(s32[3]{0:T(128)} %pad_add_fusion.1.at, bf16[512,3072]{1,0:T(8,128)(2,1)} %get-tuple-element.244.a_ref.mid_ref, bf16[512,576]{1,0:T(8,128)(2,1)} %get-tuple-element.224.refs_0_, bf16[512,576]{1,0:T(8,128)(2,1)} %get-tuple-element.225.refs_1_), custom_call_target="tpu_custom_call" | custom-call | flops 999999995904 | bytes 1 | tf_op jit(solution)/shard_map/grad_stacks/pallas_call | solution.py:500
  268.7 7.5 %assemble.9 = bf16[2,4,2,2,192,576]{5,4,3,2,1,0:T(8,128)(2,1)} custom-call(s32[4]{0:T(128)} %pad_add_fusion.at, bf16[2,4,192,576]{3,2,1,0:T(8,128)(2,1)} %bitcast.41.s0, bf16[2,4,192,576]{3,2,1,0:T(8,128)(2,1)} %bitcast.42.s1, bf16[2,4,192,576]{3,2,1,0:T(8,128)(2,1)} %collective-permute-done.46.t0, bf16[2,4,192,576]{3,2,1,0:T(8,128)(2,1)} %collective-permute-done.47.t1), custom_call_target="tpu_custom_call" | custom-call | flops 999999995904 | bytes 1 | tf_op jit(solution)/shard_map/assemble/pallas_call | solution.py:645
  281.2 24.2 %gated_back.1 = (bf16[512,3072]{1,0:T(8,128)(2,1)}, bf16[512,3072]{1,0:T(8,128)(2,1)}, f32[512,1152]{1,0:T(8,128)}) custom-call(bf16[512,576]{1,0:T(8,128)(2,1)} %get-tuple-element.224.refs_0_, bf16[512,576]{1,0:T(8,128)(2,1)} %get-tuple-element.225.refs_1_, bf16[2,3072,576]{2,1,0:T(8,128)(2,1)} %bitcast.142, bf16[2,3072,576]{2,1,0:T(8,128)(2,1)} %bitcast.143, ...), custom_call_target="tpu_custom_call" | custom-call | flops 999999995904 | bytes 1 | tf_op jit(solution)/shard_map/gated_back/pallas_call | solution.py:328
  310.1 8.9 %middle_back.1 = (f32[512,1152]{1,0:T(8,128)}, bf16[512,1152]{1,0:T(8,128)(2,1)}, f32[2,3,1152]{2,1,0:T(4,128)}, bf16[512,576]{1,0:T(8,128)(2,1)}, bf16[512,576]{1,0:T(8,128)(2,1)}) custom-call(f32[512,1152]{1,0:T(8,128)} %get-tuple-element.235.in_ref, f32[512,1152]{1,0:T(8,128)} %get-tuple-element.236.hidden_ref, f32[512,1152]{1,0:T(8,128)} %get-tuple-element.237.attn_ref, ...), custom_call_target="tpu_custom_call" | custom-call | flops 999999995904 | bytes 1 | tf_op jit(solution)/shard_map/middle_back/pallas_call | solution.py:366
  319.0 8.2 %chip_stacks.3 = (bf16[2,4,72,1536]{3,2,1,0:T(8,128)(2,1)}, bf16[2,4,72,1536]{3,2,1,0:T(8,128)(2,1)}) custom-call(s32[3]{0:T(128)} %pad_add_fusion.1.at, bf16[576,512]{1,0:T(8,128)(2,1)} %bitcast.154, bf16[576,512]{1,0:T(8,128)(2,1)} %bitcast.45.got_ref, bf16[512,3072]{1,0:T(8,128)(2,1)} %get-tuple-element.239.refs_0_.refs_1_, ...), custom_call_target="tpu_custom_call" | custom-call | flops 999999995904 | bytes 1 | tf_op jit(solution)/shard_map/chip_stacks/pallas_call | solution.py:720
  331.6 10.9 %block_tail.1 = (bf16[512,1152]{1,0:T(8,128)(2,1)}, f32[2,1,1152]{2,1,0:T(1,128)}) custom-call(bf16[512,3072]{1,0:T(8,128)(2,1)} %get-tuple-element.244.a_ref.mid_ref, f32[512,1152]{1,0:T(8,128)} %get-tuple-element.236.hidden_ref, bf16[512,1152]{1,0:T(8,128)(2,1)} %bitcast.105, f32[2,6,1152]{2,1,0:T(8,128)} %broadcast_add_fusion.piece.refs_4_, ...), custom_call_target="tpu_custom_call" | custom-call | flops 999999995904 | bytes 1 | tf_op jit(solution)/shard_map/block_tail/pallas_call | solution.py:366
  342.5 5.4 %grad_stacks.3 = (bf16[4,4,72,576]{3,2,1,0:T(8,128)(2,1)}, bf16[4,4,72,576]{3,2,1,0:T(8,128)(2,1)}) custom-call(s32[3]{0:T(128)} %pad_add_fusion.1.at, bf16[512,1152]{1,0:T(8,128)(2,1)} %get-tuple-element.192.mixed_ref.a_ref, bf16[512,576]{1,0:T(8,128)(2,1)} %get-tuple-element.253.refs_0_, bf16[512,576]{1,0:T(8,128)(2,1)} %get-tuple-element.254.refs_1_), custom_call_target="tpu_custom_call" | custom-call | flops 999999995904 | bytes 1 | tf_op jit(solution)/shard_map/grad_stacks/pallas_call | solution.py:500
  347.9 8.1 %chip_stacks.4 = (bf16[2,4,72,1536]{3,2,1,0:T(8,128)(2,1)}, bf16[2,4,72,1536]{3,2,1,0:T(8,128)(2,1)}) custom-call(s32[3]{0:T(128)} %pad_add_fusion.1.at, bf16[576,512]{1,0:T(8,128)(2,1)} %bitcast.155, bf16[576,512]{1,0:T(8,128)(2,1)} %bitcast.45.got_ref, bf16[512,3072]{1,0:T(8,128)(2,1)} %get-tuple-element.249.refs_0_.refs_1_, ...), custom_call_target="tpu_custom_call" | custom-call | flops 999999995904 | bytes 1 | tf_op jit(solution)/shard_map/chip_stacks/pallas_call | solution.py:720
  363.8 29.3 %attention_backward.1 = (bf16[512,1728]{1,0:T(8,128)(2,1)}, bf16[512,1728]{1,0:T(8,128)(2,1)}, f32[2,2,1152]{2,1,0:T(2,128)}) custom-call(f32[512,1728]{1,0:T(8,128)} %get-tuple-element.190.refs_0_, f32[512,1728]{1,0:T(8,128)} %get-tuple-element.191.refs_1_, bf16[512,1152]{1,0:T(8,128)(2,1)} %get-tuple-element.246.refs_2_, ...), custom_call_target="tpu_custom_call" | custom-call | flops 999999995904 | bytes 1 | tf_op jit(solution)/shard_map/attention_backward/pallas_call | solution.py:222
  409.8 9.5 %chip_stacks.5 = (bf16[2,4,72,1728]{3,2,1,0:T(8,128)(2,1)}, bf16[2,4,72,1728]{3,2,1,0:T(8,128)(2,1)}) custom-call(s32[3]{0:T(128)} %pad_add_fusion.1.at, bf16[576,512]{1,0:T(8,128)(2,1)} %bitcast.153, bf16[576,512]{1,0:T(8,128)(2,1)} %bitcast.51.got_ref, bf16[512,1728]{1,0:T(8,128)(2,1)} %get-tuple-element.286.refs_0_, ...), custom_call_target="tpu_custom_call" | custom-call | flops 999999995904 | bytes 1 | tf_op jit(solution)/shard_map/chip_stacks/pallas_call | solution.py:720
  434.8 12.1 %block_head_back.1 = (bf16[512,1152]{1,0:T(8,128)(2,1)}, f32[2,2,1152]{2,1,0:T(2,128)}) custom-call(bf16[512,1728]{1,0:T(8,128)(2,1)} %get-tuple-element.286.refs_0_, bf16[512,1728]{1,0:T(8,128)(2,1)} %get-tuple-element.287.refs_1_, f32[512,1152]{1,0:T(8,128)} %get-tuple-element.288.refs_2_, bf16[512,1152]{1,0:T(8,128)(2,1)} %bitcast.100, ...), custom_call_target="tpu_custom_call" | custom-call | flops 999999995904 | bytes 1 | tf_op jit(solution)/shard_map/block_head_back/pallas_call | solution.py:366
  447.8 6.7 %collective-permute-done.64.refs_1_ = bf16[2,4,72,1728]{3,2,1,0:T(8,128)(2,1)} collective-permute-done((bf16[2,4,72,1728]{3,2,1,0:T(8,128)(2,1)}, bf16[2,4,72,1728]{3,2,1,0:T(8,128)(2,1)}, u32[]{:S(2)}, u32[]{:S(2)}) %collective-permute-start.64) | collective-permute-done | bytes 1990688 | tf_op jit(solution)/shard_map/ppermute | solution.py:539
  478.5 6.7 %collective-permute-done.68.refs_2_ = bf16[1,4,72,1728]{3,2,1,0:T(8,128)(2,1)S(1)} collective-permute-done((bf16[1,4,72,1728]{3,2,1,0:T(8,128)(2,1)S(1)}, bf16[1,4,72,1728]{3,2,1,0:T(8,128)(2,1)S(1)}, u32[]{:S(2)}, u32[]{:S(2)}) %collective-permute-start.68) | collective-permute-done | bytes 995360 | tf_op jit(solution)/shard_map/ppermute | solution.py:539
  (403 shorter events, 281.3 us)
Async XLA Ops:
  0.7 36.3 %collective-permute-start.7 = (bf16[1,72,1728]{2,1,0:T(8,128)(2,1)}, bf16[1,72,1728]{2,1,0:T(8,128)(2,1)S(1)}, u32[]{:S(2)}, u32[]{:S(2)}) collective-permute-start(bf16[1,72,1728]{2,1,0:T(8,128)(2,1)} %bitcast.114), channel_id=1, source_target_pairs={{0,24},{1,25},{2,26},{3,27},{4,28},{5,29},{6,30},{7,31},{8,16},{9,... | collective-permute-start | bytes 746504 | tf_op jit(solution)/shard_map/ppermute | solution.py:539
  5.8 31.2 %collective-permute-start.6 = (bf16[1,72,1728]{2,1,0:T(8,128)(2,1)}, bf16[1,72,1728]{2,1,0:T(8,128)(2,1)S(1)}, u32[]{:S(2)}, u32[]{:S(2)}) collective-permute-start(bf16[1,72,1728]{2,1,0:T(8,128)(2,1)} %bitcast.115), channel_id=1, source_target_pairs={{0,16},{1,17},{2,18},{3,19},{4,20},{5,21},{6,22},{7,23},{8,24},{9,... | collective-permute-start | bytes 746504 | tf_op jit(solution)/shard_map/ppermute | solution.py:539
  5.8 31.2 %collective-permute-start.5 = (bf16[1,72,1728]{2,1,0:T(8,128)(2,1)}, bf16[1,72,1728]{2,1,0:T(8,128)(2,1)S(1)}, u32[]{:S(2)}, u32[]{:S(2)}) collective-permute-start(bf16[1,72,1728]{2,1,0:T(8,128)(2,1)} %bitcast.116), channel_id=1, source_target_pairs={{0,8},{1,9},{2,10},{3,11},{4,12},{5,13},{6,14},{7,15},{8,0},{9,1},... | collective-permute-start | bytes 746504 | tf_op jit(solution)/shard_map/ppermute | solution.py:539
  66.3 26.0 %collective-permute-start.15 = (bf16[8,72,1728]{2,1,0:T(8,128)(2,1)}, bf16[8,72,1728]{2,1,0:T(8,128)(2,1)}, u32[]{:S(2)}, u32[]{:S(2)}) collective-permute-start(bf16[8,72,1728]{2,1,0:T(8,128)(2,1)} %join.11), channel_id=1, source_target_pairs={{0,1},{1,0},{2,6},{3,7},{4,5},{5,4},{6,2},{7,3},{8,9},{9,8},{10,14... | collective-permute-start | bytes 5971976 | tf_op jit(solution)/shard_map/ppermute | solution.py:539
  99.9 26.5 %collective-permute-start.22 = (bf16[2,4,72,1728]{3,2,1,0:T(8,128)(2,1)S(1)}, bf16[2,4,72,1728]{3,2,1,0:T(8,128)(2,1)}, u32[]{:S(2)}, u32[]{:S(2)}) collective-permute-start(bf16[2,4,72,1728]{3,2,1,0:T(8,128)(2,1)S(1)} %bitcast.103), channel_id=1, source_target_pairs={{0,2},{1,3},{2,0},{3,1},{4,6},{5,7},{6,4},{7,5},{8,10},{9,11},{10,... | collective-permute-start | bytes 5971976 | tf_op jit(solution)/shard_map/ppermute | solution.py:539
  102.8 23.7 %collective-permute-start.23 = (bf16[2,4,72,1728]{3,2,1,0:T(8,128)(2,1)}, bf16[2,4,72,1728]{3,2,1,0:T(8,128)(2,1)}, u32[]{:S(2)}, u32[]{:S(2)}) collective-permute-start(bf16[2,4,72,1728]{3,2,1,0:T(8,128)(2,1)} %bitcast.13.s1), channel_id=1, source_target_pairs={{0,2},{1,3},{2,0},{3,1},{4,6},{5,7},{6,4},{7,5},{8,10},{9,11},{10,... | collective-permute-start | bytes 5971976 | tf_op jit(solution)/shard_map/ppermute | solution.py:539
  131.4 30.2 %collective-permute-start.27 = (bf16[8,72,1536]{2,1,0:T(8,128)(2,1)}, bf16[8,72,1536]{2,1,0:T(8,128)(2,1)}, u32[]{:S(2)}, u32[]{:S(2)}) collective-permute-start(bf16[8,72,1536]{2,1,0:T(8,128)(2,1)} %join.15), channel_id=1, source_target_pairs={{0,1},{1,0},{2,6},{3,7},{4,5},{5,4},{6,2},{7,3},{8,9},{9,8},{10,14... | collective-permute-start | bytes 5308424 | tf_op jit(solution)/shard_map/ppermute | solution.py:539
  207.8 24.5 %collective-permute-start.41 = (bf16[2,4,72,1536]{3,2,1,0:T(8,128)(2,1)}, bf16[2,4,72,1536]{3,2,1,0:T(8,128)(2,1)}, u32[]{:S(2)}, u32[]{:S(2)}) collective-permute-start(bf16[2,4,72,1536]{3,2,1,0:T(8,128)(2,1)} %bitcast.36.s0), channel_id=1, source_target_pairs={{0,2},{1,3},{2,0},{3,1},{4,6},{5,7},{6,4},{7,5},{8,10},{9,11},{10,... | collective-permute-start | bytes 5308424 | tf_op jit(solution)/shard_map/ppermute | solution.py:539
  207.8 24.5 %collective-permute-start.42 = (bf16[2,4,72,1536]{3,2,1,0:T(8,128)(2,1)}, bf16[2,4,72,1536]{3,2,1,0:T(8,128)(2,1)}, u32[]{:S(2)}, u32[]{:S(2)}) collective-permute-start(bf16[2,4,72,1536]{3,2,1,0:T(8,128)(2,1)} %bitcast.37.s1), channel_id=1, source_target_pairs={{0,2},{1,3},{2,0},{3,1},{4,6},{5,7},{6,4},{7,5},{8,10},{9,11},{10,... | collective-permute-start | bytes 5308424 | tf_op jit(solution)/shard_map/ppermute | solution.py:539
  232.3 25.0 %collective-permute-start.45 = (bf16[8,192,576]{2,1,0:T(8,128)(2,1)}, bf16[8,192,576]{2,1,0:T(8,128)(2,1)}, u32[]{:S(2)}, u32[]{:S(2)}) collective-permute-start(bf16[8,192,576]{2,1,0:T(8,128)(2,1)} %join.19), channel_id=1, source_target_pairs={{0,1},{1,0},{2,6},{3,7},{4,5},{5,4},{6,2},{7,3},{8,9},{9,8},{10,14... | collective-permute-start | bytes 5308424 | tf_op jit(solution)/shard_map/ppermute | solution.py:539
  280.4 25.0 %collective-permute-start.49 = (bf16[2,4,192,576]{3,2,1,0:T(8,128)(2,1)}, bf16[2,4,192,576]{3,2,1,0:T(8,128)(2,1)}, u32[]{:S(2)}, u32[]{:S(2)}) collective-permute-start(bf16[2,4,192,576]{3,2,1,0:T(8,128)(2,1)} %add_stacks.7), channel_id=1, source_target_pairs={{0,1},{1,0},{2,6},{3,7},{4,5},{5,4},{6,2},{7,3},{8,9},{9,8},{10,14... | collective-permute-start | bytes 5308424 | tf_op jit(solution)/shard_map/ppermute | solution.py:539
  327.3 30.9 %collective-permute-start.53 = (bf16[2,4,72,1536]{3,2,1,0:T(8,128)(2,1)}, bf16[2,4,72,1536]{3,2,1,0:T(8,128)(2,1)}, u32[]{:S(2)}, u32[]{:S(2)}) collective-permute-start(bf16[2,4,72,1536]{3,2,1,0:T(8,128)(2,1)} %get-tuple-element.241), channel_id=1, source_target_pairs={{0,1},{1,0},{2,6},{3,7},{4,5},{5,4},{6,2},{7,3},{8,9},{9,8},{10,14... | collective-permute-start | bytes 5308424 | tf_op jit(solution)/shard_map/ppermute | solution.py:539
  331.1 24.9 %collective-permute-start.54 = (bf16[2,192,576]{2,1,0:T(8,128)(2,1)}, bf16[2,192,576]{2,1,0:T(8,128)(2,1)}, u32[]{:S(2)}, u32[]{:S(2)}) collective-permute-start(bf16[2,192,576]{2,1,0:T(8,128)(2,1)} %add_slabs.16), channel_id=1, source_target_pairs={{0,16},{1,17},{2,18},{3,19},{4,20},{5,21},{6,22},{7,23},{8,24},{9,... | collective-permute-start | bytes 1327112 | tf_op jit(solution)/shard_map/ppermute | solution.py:539
  358.2 34.9 %collective-permute-start.58 = (bf16[1,192,576]{2,1,0:T(8,128)(2,1)}, bf16[1,192,576]{2,1,0:T(8,128)(2,1)}, u32[]{:S(2)}, u32[]{:S(2)}) collective-permute-start(bf16[1,192,576]{2,1,0:T(8,128)(2,1)} %add_slabs.17), channel_id=1, source_target_pairs={{0,8},{1,9},{2,10},{3,11},{4,12},{5,13},{6,14},{7,15},{8,0},{9,1},... | collective-permute-start | bytes 663560 | tf_op jit(solution)/shard_map/ppermute | solution.py:539
  362.5 30.7 %collective-permute-start.56 = (bf16[1,4,72,1536]{3,2,1,0:T(8,128)(2,1)}, bf16[1,4,72,1536]{3,2,1,0:T(8,128)(2,1)}, u32[]{:S(2)}, u32[]{:S(2)}) collective-permute-start(bf16[1,4,72,1536]{3,2,1,0:T(8,128)(2,1)} %add_stacks.9), channel_id=1, source_target_pairs={{0,4},{1,5},{2,3},{3,2},{4,0},{5,1},{6,7},{7,6},{8,12},{9,13},{10,... | collective-permute-start | bytes 2654216 | tf_op jit(solution)/shard_map/ppermute | solution.py:539
  363.0 30.2 %collective-permute-start.57 = (bf16[4,4,72,576]{3,2,1,0:T(8,128)(2,1)}, bf16[4,4,72,576]{3,2,1,0:T(8,128)(2,1)}, u32[]{:S(2)}, u32[]{:S(2)}) collective-permute-start(bf16[4,4,72,576]{3,2,1,0:T(8,128)(2,1)} %get-tuple-element.260), channel_id=1, source_target_pairs={{0,2},{1,3},{2,0},{3,1},{4,6},{5,7},{6,4},{7,5},{8,10},{9,11},{10,... | collective-permute-start | bytes 3981320 | tf_op jit(solution)/shard_map/ppermute | solution.py:539
  363.0 30.2 %collective-permute-start.55 = (bf16[2,4,72,1536]{3,2,1,0:T(8,128)(2,1)}, bf16[2,4,72,1536]{3,2,1,0:T(8,128)(2,1)}, u32[]{:S(2)}, u32[]{:S(2)}) collective-permute-start(bf16[2,4,72,1536]{3,2,1,0:T(8,128)(2,1)} %get-tuple-element.257), channel_id=1, source_target_pairs={{0,1},{1,0},{2,6},{3,7},{4,5},{5,4},{6,2},{7,3},{8,9},{9,8},{10,14... | collective-permute-start | bytes 5308424 | tf_op jit(solution)/shard_map/ppermute | solution.py:539
  424.6 29.9 %collective-permute-start.64 = (bf16[2,4,72,1728]{3,2,1,0:T(8,128)(2,1)}, bf16[2,4,72,1728]{3,2,1,0:T(8,128)(2,1)}, u32[]{:S(2)}, u32[]{:S(2)}) collective-permute-start(bf16[2,4,72,1728]{3,2,1,0:T(8,128)(2,1)} %get-tuple-element.279), channel_id=1, source_target_pairs={{0,1},{1,0},{2,6},{3,7},{4,5},{5,4},{6,2},{7,3},{8,9},{9,8},{10,14... | collective-permute-start | bytes 5971976 | tf_op jit(solution)/shard_map/ppermute | solution.py:539
  427.4 29.6 %collective-permute-start.67 = (bf16[1,72,1536]{2,1,0:T(8,128)(2,1)}, bf16[1,72,1536]{2,1,0:T(8,128)(2,1)}, u32[]{:S(2)}, u32[]{:S(2)}) collective-permute-start(bf16[1,72,1536]{2,1,0:T(8,128)(2,1)} %add_slabs.20), channel_id=1, source_target_pairs={{0,8},{1,9},{2,10},{3,11},{4,12},{5,13},{6,14},{7,15},{8,0},{9,1},... | collective-permute-start | bytes 663560 | tf_op jit(solution)/shard_map/ppermute | solution.py:539
  431.4 25.5 %collective-permute-start.65 = (bf16[1,4,72,576]{3,2,1,0:T(8,128)(2,1)}, bf16[1,4,72,576]{3,2,1,0:T(8,128)(2,1)}, u32[]{:S(2)}, u32[]{:S(2)}) collective-permute-start(bf16[1,4,72,576]{3,2,1,0:T(8,128)(2,1)} %add_stacks.12), channel_id=1, source_target_pairs={{0,4},{1,5},{2,3},{3,2},{4,0},{5,1},{6,7},{7,6},{8,12},{9,13},{10,... | collective-permute-start | bytes 995336 | tf_op jit(solution)/shard_map/ppermute | solution.py:539
  497.7 24.9 %collective-permute-start.78 = (bf16[4,2,1,2,2,7056]{5,4,3,2,1,0:T(2,128)(2,1)S(1)}, bf16[4,2,1,2,2,7056]{5,4,3,2,1,0:T(2,128)(2,1)S(1)}, u32[]{:S(2)}, u32[]{:S(2)}) collective-permute-start(bf16[4,2,1,2,2,7056]{5,4,3,2,1,0:T(2,128)(2,1)S(1)} %pad_maximum_fusion.1), channel_id=1, source_target_pairs={{0,2},{1,3},{2,0},{3,1},{4,6},{5,7},{6,4},{7,5},{8,10},{9,11},{10,... | collective-permute-start | bytes 1354760 | tf_op jit(solution)/shard_map/ppermute | solution.py:539
  506.3 28.4 %collective-permute-start.73 = (bf16[1,72,1728]{2,1,0:T(8,128)(2,1)}, bf16[1,72,1728]{2,1,0:T(8,128)(2,1)}, u32[]{:S(2)}, u32[]{:S(2)}) collective-permute-start(bf16[1,72,1728]{2,1,0:T(8,128)(2,1)} %add_slabs.21), channel_id=1, source_target_pairs={{0,24},{1,25},{2,26},{3,27},{4,28},{5,29},{6,30},{7,31},{8,16},{9,... | collective-permute-start | bytes 746504 | tf_op jit(solution)/shard_map/ppermute | solution.py:539
  508.3 26.5 %collective-permute-start.74 = (bf16[1,72,1728]{2,1,0:T(8,128)(2,1)S(1)}, bf16[1,72,1728]{2,1,0:T(8,128)(2,1)}, u32[]{:S(2)}, u32[]{:S(2)}) collective-permute-start(bf16[1,72,1728]{2,1,0:T(8,128)(2,1)S(1)} %copy-done.13), channel_id=1, source_target_pairs={{0,16},{1,17},{2,18},{3,19},{4,20},{5,21},{6,22},{7,23},{8,24},{9,... | collective-permute-start | bytes 746504 | tf_op jit(solution)/shard_map/ppermute | solution.py:539
  509.8 24.9 %collective-permute-start.75 = (bf16[1,72,1728]{2,1,0:T(8,128)(2,1)S(1)}, bf16[1,72,1728]{2,1,0:T(8,128)(2,1)}, u32[]{:S(2)}, u32[]{:S(2)}) collective-permute-start(bf16[1,72,1728]{2,1,0:T(8,128)(2,1)S(1)} %copy-done.14), channel_id=1, source_target_pairs={{0,8},{1,9},{2,10},{3,11},{4,12},{5,13},{6,14},{7,15},{8,0},{9,1},... | collective-permute-start | bytes 746504 | tf_op jit(solution)/shard_map/ppermute | solution.py:539
  (113 other events, 1530.6 us)
